TPU v7x, 32 devices: a whole 2x2x4 slice. The times are simulated.
32 devices in a mesh: grp: 2 (over x), shell: 16 (over z, y, core).
Axes of the slice: x: 2, y: 2, z: 4, core: 2. Of those that a mesh axis runs over, the one named last changes fastest.
Arguments:
- pair_coef: bfloat16 [1024, 8, 16, 1024], P(('grp', 'shell')), parts along dimension 0, may hold values from -6 to 6
- panel_pool: bfloat16 [16, 512, 512], P('shell'), may hold values from -0.0625 to 0.0625
- degree_owner: int32 [16], replicated, may hold values from 0 to 15, as said below
- batch_order: int32 [8], replicated, may hold values from 0 to 7, each once
Outputs:
- scores: float32 [2, 1024, 4, 2, 512], P(None, ('grp', 'shell')), parts along dimension 1
There are 2 independent parts, one for each index of `grp`. A program takes and returns all parts, laid end to end along the dimension named above; an argument that names none is the same for every part. Nothing has to cross between parts.
Inputs may be any that keep to these rules, and one draw needn't show every extreme that they name: `degree_owner`: the entries are distinct slot numbers; slots that no degree names are not read.
All inputs are finite; a program needn't handle non-finite values.
Results may differ from a plain program's by a relative error of at most 0.0003.
Values may be sent and summed in bfloat16 or wider, within the bound.
No kernel may reach another device: no remote copies, remote signals or barrier semaphores. Data moves between devices by JAX's collectives and lax.ppermute only.
A program may use at most 128 MiB of HBM per device.

v0:
```python
import math

import jax
import jax.numpy as jnp
from jax import lax
from jax.sharding import PartitionSpec as P


def broadcast(value, axis, root):
    mine = lax.axis_index(axis) == root
    return lax.psum(jnp.where(mine, value, jnp.zeros_like(value)), axis)


def partner(value, axis, distance):
    mask = 2**distance
    pairs = [(source, source ^ mask) for source in range(lax.axis_size(axis))]
    return lax.ppermute(value, axis, pairs)


def rotate(real_part, imag_part, cosine, sine):
    return (real_part * cosine - imag_part * sine, real_part * sine + imag_part * cosine)


def shards(pair_coef, panel_pool, degree_owner, batch_order):
    local_orders = pair_coef.shape[0]
    degrees = pair_coef.shape[2]
    width = pair_coef.shape[3] // 2
    batch_rows = batch_order.shape[0] // 2
    devices = lax.axis_size("shell")
    total_orders = local_orders * devices
    first = jnp.take(pair_coef, batch_order[:batch_rows], axis=1)
    second = jnp.take(pair_coef, batch_order[batch_rows:], axis=1)
    rows = jnp.stack([first, second])

    def add_degree(degree, total):
        panel = broadcast(panel_pool[0], "shell", degree_owner[degree])
        piece = lax.dynamic_index_in_dim(rows, degree, axis=3, keepdims=False).reshape(-1, width)
        return total + jnp.dot(piece, panel, preferred_element_type=jnp.float32)

    total = lax.fori_loop(
        0, degrees, add_degree, jnp.zeros((2 * local_orders * batch_rows * 2, width), jnp.float32)
    )
    proj = total.reshape(2, local_orders, batch_rows, 2, width)
    nbits = devices.bit_length() - 1
    high = lax.Precision.HIGHEST
    me = lax.axis_index("shell")
    blocks = proj
    for bit in reversed(range(nbits)):
        other = partner(blocks, "shell", bit)
        upper = me >> bit & 1 == 1
        lower_val = jnp.where(upper, other, blocks)
        upper_val = jnp.where(upper, blocks, other)
        summed = lower_val + upper_val
        differ = lower_val - upper_val
        twist = (me % (1 << bit)).astype(jnp.float32)
        angle = -2.0 * math.pi * twist / float(2 << bit)
        new_real, new_imag = rotate(
            differ[:, :, :, 0], differ[:, :, :, 1], jnp.cos(angle), jnp.sin(angle)
        )
        turned = jnp.stack([new_real, new_imag], axis=3)
        blocks = jnp.where(upper, turned, summed)
    flipped = jnp.zeros((), jnp.int32)
    for bit in range(nbits):
        flipped = flipped | (me >> bit & 1) << nbits - 1 - bit
    inner = lax.iota(jnp.int32, local_orders)
    freq = flipped + devices * inner
    phase = inner[None, :] * freq[:, None] % total_orders
    angle = -2.0 * math.pi * phase.astype(jnp.float32) / float(total_orders)
    cosine = jnp.cos(angle)
    sine = jnp.sin(angle)
    real_part = blocks[:, :, :, 0]
    imag_part = blocks[:, :, :, 1]
    out_real = jnp.einsum("gr,brtj->bgtj", cosine, real_part, precision=high) - jnp.einsum(
        "gr,brtj->bgtj", sine, imag_part, precision=high
    )
    out_imag = jnp.einsum("gr,brtj->bgtj", sine, real_part, precision=high) + jnp.einsum(
        "gr,brtj->bgtj", cosine, imag_part, precision=high
    )
    result = jnp.stack([out_real, out_imag], axis=3)
    return result * (1.0 / math.sqrt(total_orders))


def solution(mesh):
    return jax.shard_map(
        shards,
        mesh=mesh,
        in_specs=(P(("grp", "shell"), None, None, None), P("shell", None, None), P(), P()),
        out_specs=P(None, ("grp", "shell"), None, None, None),
        check_vma=False,
    )
```

profile of v0, /device:TPU:0, one launch (start us, length us, event | category | flops | bytes accessed | tf_op | source)
XLA Modules:
  0.0 1708.2 jit_solution(1576196073185448806)
XLA Ops:
  7.4 6.1 gather_fusion
  13.5 6.2 gather_fusion.1
  19.7 7.5 select_bitcast_fusion.1
  27.1 7.5 pad_maximum_fusion
  34.6 12.4 copy.6
  47.0 1543.7 %while.14 = (s32[]{:T(128)}, f32[512,512]{1,0:T(8,128)S(1)}, bf16[2,32,4,16,1024]{4,2,1,0,3:T(4,128)(2,1)}, s32[16]{0:T(128)S(1)}, bf16[1,512,512]{2,1,0:T(8,128)(2,1)S(1)}, /*index=5*/s32[]{:T(128)}, u32[]{:T(128)}, s32[]{:T(128)}) while((s32[]{:T(128)}, f32[512,512]{1,0:T(8,128)S(1)}, bf16[2,32,4,16,1024]{4,2,1,0,3:T(4,128)(2,1)}, ...), condition=%wide.region_2.4_spmd.clone, body=%wide.region_0.3_spmd.clone.sunk | while | flops 269484032 | bytes 9437365 | solution.py:40
  50.5 93.6 %all-reduce.2.cloned.1.call-done = bf16[512,512]{1,0:T(8,128)(2,1)} async-done(((bf16[512,512]{1,0:T(8,128)(2,1)}), bf16[512,512]{1,0:T(8,128)(2,1)}) %all-reduce.2.cloned.1.call-update) | async-done | bytes 524304 | tf_op jit(solution)/shard_map/while/body/eval_jaxpr/psum | solution.py:11
  149.3 91.4 %all-reduce.2.cloned.1.call-done = bf16[512,512]{1,0:T(8,128)(2,1)} async-done(((bf16[512,512]{1,0:T(8,128)(2,1)}), bf16[512,512]{1,0:T(8,128)(2,1)}) %all-reduce.2.cloned.1.call-update) | async-done | bytes 524304 | tf_op jit(solution)/shard_map/while/body/eval_jaxpr/psum | solution.py:11
  245.8 91.3 %all-reduce.2.cloned.1.call-done = bf16[512,512]{1,0:T(8,128)(2,1)} async-done(((bf16[512,512]{1,0:T(8,128)(2,1)}), bf16[512,512]{1,0:T(8,128)(2,1)}) %all-reduce.2.cloned.1.call-update) | async-done | bytes 524304 | tf_op jit(solution)/shard_map/while/body/eval_jaxpr/psum | solution.py:11
  342.3 91.0 %all-reduce.2.cloned.1.call-done = bf16[512,512]{1,0:T(8,128)(2,1)} async-done(((bf16[512,512]{1,0:T(8,128)(2,1)}), bf16[512,512]{1,0:T(8,128)(2,1)}) %all-reduce.2.cloned.1.call-update) | async-done | bytes 524304 | tf_op jit(solution)/shard_map/while/body/eval_jaxpr/psum | solution.py:11
  438.5 91.1 %all-reduce.2.cloned.1.call-done = bf16[512,512]{1,0:T(8,128)(2,1)} async-done(((bf16[512,512]{1,0:T(8,128)(2,1)}), bf16[512,512]{1,0:T(8,128)(2,1)}) %all-reduce.2.cloned.1.call-update) | async-done | bytes 524304 | tf_op jit(solution)/shard_map/while/body/eval_jaxpr/psum | solution.py:11
  534.7 91.0 %all-reduce.2.cloned.1.call-done = bf16[512,512]{1,0:T(8,128)(2,1)} async-done(((bf16[512,512]{1,0:T(8,128)(2,1)}), bf16[512,512]{1,0:T(8,128)(2,1)}) %all-reduce.2.cloned.1.call-update) | async-done | bytes 524304 | tf_op jit(solution)/shard_map/while/body/eval_jaxpr/psum | solution.py:11
  625.7 1.6 convolution_add_fusion.3
  630.8 91.4 %all-reduce.2.cloned.1.call-done = bf16[512,512]{1,0:T(8,128)(2,1)} async-done(((bf16[512,512]{1,0:T(8,128)(2,1)}), bf16[512,512]{1,0:T(8,128)(2,1)}) %all-reduce.2.cloned.1.call-update) | async-done | bytes 524304 | tf_op jit(solution)/shard_map/while/body/eval_jaxpr/psum | solution.py:11
  722.2 1.6 convolution_add_fusion.3
  727.3 91.4 %all-reduce.2.cloned.1.call-done = bf16[512,512]{1,0:T(8,128)(2,1)} async-done(((bf16[512,512]{1,0:T(8,128)(2,1)}), bf16[512,512]{1,0:T(8,128)(2,1)}) %all-reduce.2.cloned.1.call-update) | async-done | bytes 524304 | tf_op jit(solution)/shard_map/while/body/eval_jaxpr/psum | solution.py:11
  818.7 1.6 convolution_add_fusion.3
  823.8 91.3 %all-reduce.2.cloned.1.call-done = bf16[512,512]{1,0:T(8,128)(2,1)} async-done(((bf16[512,512]{1,0:T(8,128)(2,1)}), bf16[512,512]{1,0:T(8,128)(2,1)}) %all-reduce.2.cloned.1.call-update) | async-done | bytes 524304 | tf_op jit(solution)/shard_map/while/body/eval_jaxpr/psum | solution.py:11
  920.3 91.1 %all-reduce.2.cloned.1.call-done = bf16[512,512]{1,0:T(8,128)(2,1)} async-done(((bf16[512,512]{1,0:T(8,128)(2,1)}), bf16[512,512]{1,0:T(8,128)(2,1)}) %all-reduce.2.cloned.1.call-update) | async-done | bytes 524304 | tf_op jit(solution)/shard_map/while/body/eval_jaxpr/psum | solution.py:11
  1016.5 91.3 %all-reduce.2.cloned.1.call-done = bf16[512,512]{1,0:T(8,128)(2,1)} async-done(((bf16[512,512]{1,0:T(8,128)(2,1)}), bf16[512,512]{1,0:T(8,128)(2,1)}) %all-reduce.2.cloned.1.call-update) | async-done | bytes 524304 | tf_op jit(solution)/shard_map/while/body/eval_jaxpr/psum | solution.py:11
  1113.0 91.0 %all-reduce.2.cloned.1.call-done = bf16[512,512]{1,0:T(8,128)(2,1)} async-done(((bf16[512,512]{1,0:T(8,128)(2,1)}), bf16[512,512]{1,0:T(8,128)(2,1)}) %all-reduce.2.cloned.1.call-update) | async-done | bytes 524304 | tf_op jit(solution)/shard_map/while/body/eval_jaxpr/psum | solution.py:11
  1209.2 91.4 %all-reduce.2.cloned.1.call-done = bf16[512,512]{1,0:T(8,128)(2,1)} async-done(((bf16[512,512]{1,0:T(8,128)(2,1)}), bf16[512,512]{1,0:T(8,128)(2,1)}) %all-reduce.2.cloned.1.call-update) | async-done | bytes 524304 | tf_op jit(solution)/shard_map/while/body/eval_jaxpr/psum | solution.py:11
  1305.7 91.0 %all-reduce.2.cloned.1.call-done = bf16[512,512]{1,0:T(8,128)(2,1)} async-done(((bf16[512,512]{1,0:T(8,128)(2,1)}), bf16[512,512]{1,0:T(8,128)(2,1)}) %all-reduce.2.cloned.1.call-update) | async-done | bytes 524304 | tf_op jit(solution)/shard_map/while/body/eval_jaxpr/psum | solution.py:11
  1401.9 91.1 %all-reduce.2.cloned.1.call-done = bf16[512,512]{1,0:T(8,128)(2,1)} async-done(((bf16[512,512]{1,0:T(8,128)(2,1)}), bf16[512,512]{1,0:T(8,128)(2,1)}) %all-reduce.2.cloned.1.call-update) | async-done | bytes 524304 | tf_op jit(solution)/shard_map/while/body/eval_jaxpr/psum | solution.py:11
  1493.0 1.6 convolution_add_fusion.3
  1498.1 91.0 %all-reduce.2.cloned.1.call-done = bf16[512,512]{1,0:T(8,128)(2,1)} async-done(((bf16[512,512]{1,0:T(8,128)(2,1)}), bf16[512,512]{1,0:T(8,128)(2,1)}) %all-reduce.2.cloned.1.call-update) | async-done | bytes 524304 | tf_op jit(solution)/shard_map/while/body/eval_jaxpr/psum | solution.py:11
  1592.0 3.0 collective-permute-start
  1595.1 45.5 %collective-permute-done = f32[2,32,4,2,512]{4,1,2,0,3:T(8,128)S(1)} collective-permute-done((f32[2,32,4,2,512]{4,1,2,0,3:T(8,128)S(1)}, f32[2,32,4,2,512]{4,1,2,0,3:T(8,128)S(1)}, u32[]{:S(2)}, u32[]{:S(2)}) %collective-permute-start) | collective-permute-done | bytes 1048608 | tf_op jit(solution)/shard_map/ppermute | solution.py:17
  1642.4 24.9 %collective-permute-done.1 = f32[2,32,4,2,512]{4,1,2,0,3:T(8,128)S(1)} collective-permute-done((f32[2,32,4,2,512]{4,1,2,0,3:T(8,128)S(1)}, f32[2,32,4,2,512]{4,1,2,0,3:T(8,128)S(1)}, u32[]{:S(2)}, u32[]{:S(2)}) %collective-permute-start.1) | collective-permute-done | bytes 1048608 | tf_op jit(solution)/shard_map/ppermute | solution.py:17
  1668.8 23.7 %collective-permute-done.2 = f32[2,32,4,2,512]{4,1,2,0,3:T(8,128)S(1)} collective-permute-done((f32[2,32,4,2,512]{4,1,2,0,3:T(8,128)S(1)}, f32[2,32,4,2,512]{4,1,2,0,3:T(8,128)S(1)}, u32[]{:S(2)}, u32[]{:S(2)}) %collective-permute-start.2) | collective-permute-done | bytes 1048608 | tf_op jit(solution)/shard_map/ppermute | solution.py:17
  1693.4 2.6 collective-permute-done.3
  1699.8 1.8 copy.10
  (139 shorter events, 74.0 us)
Async XLA Ops:
  34.6 12.4 copy-start
  34.6 12.4 copy-start.1
  47.0 97.2 %all-reduce.2.cloned.1.call-start = ((), (), s32[]{:S(2)}) async-start(), calls=%async_computation | async-start | bytes 1048576 | tf_op jit(solution)/shard_map/while/body/eval_jaxpr/psum | solution.py:11
  145.8 94.9 %all-reduce.2.cloned.1.call-start = ((), (), s32[]{:S(2)}) async-start(), calls=%async_computation | async-start | bytes 1048576 | tf_op jit(solution)/shard_map/while/body/eval_jaxpr/psum | solution.py:11
  242.3 94.9 %all-reduce.2.cloned.1.call-start = ((), (), s32[]{:S(2)}) async-start(), calls=%async_computation | async-start | bytes 1048576 | tf_op jit(solution)/shard_map/while/body/eval_jaxpr/psum | solution.py:11
  338.8 94.6 %all-reduce.2.cloned.1.call-start = ((), (), s32[]{:S(2)}) async-start(), calls=%async_computation | async-start | bytes 1048576 | tf_op jit(solution)/shard_map/while/body/eval_jaxpr/psum | solution.py:11
  434.9 94.6 %all-reduce.2.cloned.1.call-start = ((), (), s32[]{:S(2)}) async-start(), calls=%async_computation | async-start | bytes 1048576 | tf_op jit(solution)/shard_map/while/body/eval_jaxpr/psum | solution.py:11
  531.2 94.5 %all-reduce.2.cloned.1.call-start = ((), (), s32[]{:S(2)}) async-start(), calls=%async_computation | async-start | bytes 1048576 | tf_op jit(solution)/shard_map/while/body/eval_jaxpr/psum | solution.py:11
  627.3 94.9 %all-reduce.2.cloned.1.call-start = ((), (), s32[]{:S(2)}) async-start(), calls=%async_computation | async-start | bytes 1048576 | tf_op jit(solution)/shard_map/while/body/eval_jaxpr/psum | solution.py:11
  723.8 94.9 %all-reduce.2.cloned.1.call-start = ((), (), s32[]{:S(2)}) async-start(), calls=%async_computation | async-start | bytes 1048576 | tf_op jit(solution)/shard_map/while/body/eval_jaxpr/psum | solution.py:11
  820.3 94.9 %all-reduce.2.cloned.1.call-start = ((), (), s32[]{:S(2)}) async-start(), calls=%async_computation | async-start | bytes 1048576 | tf_op jit(solution)/shard_map/while/body/eval_jaxpr/psum | solution.py:11
  916.8 94.6 %all-reduce.2.cloned.1.call-start = ((), (), s32[]{:S(2)}) async-start(), calls=%async_computation | async-start | bytes 1048576 | tf_op jit(solution)/shard_map/while/body/eval_jaxpr/psum | solution.py:11
  1013.0 94.9 %all-reduce.2.cloned.1.call-start = ((), (), s32[]{:S(2)}) async-start(), calls=%async_computation | async-start | bytes 1048576 | tf_op jit(solution)/shard_map/while/body/eval_jaxpr/psum | solution.py:11
  1109.5 94.6 %all-reduce.2.cloned.1.call-start = ((), (), s32[]{:S(2)}) async-start(), calls=%async_computation | async-start | bytes 1048576 | tf_op jit(solution)/shard_map/while/body/eval_jaxpr/psum | solution.py:11
  1205.7 94.9 %all-reduce.2.cloned.1.call-start = ((), (), s32[]{:S(2)}) async-start(), calls=%async_computation | async-start | bytes 1048576 | tf_op jit(solution)/shard_map/while/body/eval_jaxpr/psum | solution.py:11
  1302.2 94.6 %all-reduce.2.cloned.1.call-start = ((), (), s32[]{:S(2)}) async-start(), calls=%async_computation | async-start | bytes 1048576 | tf_op jit(solution)/shard_map/while/body/eval_jaxpr/psum | solution.py:11
  1398.4 94.6 %all-reduce.2.cloned.1.call-start = ((), (), s32[]{:S(2)}) async-start(), calls=%async_computation | async-start | bytes 1048576 | tf_op jit(solution)/shard_map/while/body/eval_jaxpr/psum | solution.py:11
  1494.6 94.5 %all-reduce.2.cloned.1.call-start = ((), (), s32[]{:S(2)}) async-start(), calls=%async_computation | async-start | bytes 1048576 | tf_op jit(solution)/shard_map/while/body/eval_jaxpr/psum | solution.py:11
  1592.0 48.7 %collective-permute-start = (f32[2,32,4,2,512]{4,1,2,0,3:T(8,128)S(1)}, f32[2,32,4,2,512]{4,1,2,0,3:T(8,128)S(1)}, u32[]{:S(2)}, u32[]{:S(2)}) collective-permute-start(f32[2,32,4,2,512]{4,1,2,0,3:T(8,128)S(1)} %copy.7), channel_id=1, source_target_pairs={{0,8},{1,9},{2,10},{3,11},{4,12},{5,13},{6,14},{7,15},{8,0},{9,1},... | collective-permute-start | bytes 3145736 | tf_op jit(solution)/shard_map/ppermute | solution.py:17
  1642.2 25.2 %collective-permute-start.1 = (f32[2,32,4,2,512]{4,1,2,0,3:T(8,128)S(1)}, f32[2,32,4,2,512]{4,1,2,0,3:T(8,128)S(1)}, u32[]{:S(2)}, u32[]{:S(2)}) collective-permute-start(f32[2,32,4,2,512]{4,1,2,0,3:T(8,128)S(1)} %maximum_select_fusion), channel_id=1, source_target_pairs={{0,4},{1,5},{2,6},{3,7},{4,0},{5,1},{6,2},{7,3},{8,12},{9,13},{10,... | collective-permute-start | bytes 3145736 | tf_op jit(solution)/shard_map/ppermute | solution.py:17
  1668.2 24.4 %collective-permute-start.2 = (f32[2,32,4,2,512]{4,1,2,0,3:T(8,128)S(1)}, f32[2,32,4,2,512]{4,1,2,0,3:T(8,128)S(1)}, u32[]{:S(2)}, u32[]{:S(2)}) collective-permute-start(f32[2,32,4,2,512]{4,1,2,0,3:T(8,128)S(1)} %maximum_select_fusion.1), channel_id=1, source_target_pairs={{0,2},{1,3},{2,0},{3,1},{4,6},{5,7},{6,4},{7,5},{8,10},{9,11},{10,... | collective-permute-start | bytes 3145736 | tf_op jit(solution)/shard_map/ppermute | solution.py:17
  1693.3 2.7 collective-permute-start.3
Sparse Core Ops, SparseCore 0:
  51.3 92.8 all-reduce.1
  150.0 90.5 all-reduce.1
  246.5 90.5 all-reduce.1
  342.7 90.5 all-reduce.1
  438.9 90.6 all-reduce.1
  535.1 90.5 all-reduce.1
  631.6 90.5 all-reduce.1
  728.0 90.5 all-reduce.1
  824.5 90.5 all-reduce.1
  920.7 90.6 all-reduce.1
  1017.2 90.5 all-reduce.1
  1113.4 90.5 all-reduce.1
  1209.9 90.6 all-reduce.1
  1306.1 90.5 all-reduce.1
  1402.3 90.6 all-reduce.1
  1498.5 90.5 all-reduce.1
where the time goes:
time: 1710 us
  waiting for transfers between devices  1560 us (91%)
  local copies, waits for them, and re-layouts  58.8 us (3%)
  other arithmetic  32.9 us (2%)
  matrix products  28.5 us (2%)
    psum x16, waiting for transfers between devices, broadcast(): return lax.psum(jnp.where(mine, value, jnp.zeros_like(value)), axis)  1460 us
    ppermute x4, waiting for transfers between devices, partner(): return lax.ppermute(value, axis, pairs)  96.8 us
  transfers between devices with their start and end apart: 20, of which 20 were waited for; matrix products, arithmetic and copies ran while one was open for 1% of the time, Pallas kernels for 0%

commit v1 on v0

--- a/solution.py
+++ b/solution.py
@@ -1,8 +1,11 @@
+import functools
 import math
 
 import jax
 import jax.numpy as jnp
 from jax import lax
+from jax.experimental import pallas as pl
+from jax.experimental.pallas import tpu as pltpu
 from jax.sharding import PartitionSpec as P
 
 
@@ -21,7 +24,7 @@
     return (real_part * cosine - imag_part * sine, real_part * sine + imag_part * cosine)
 
 
-def shards(pair_coef, panel_pool, degree_owner, batch_order):
+def general(pair_coef, panel_pool, degree_owner, batch_order):
     local_orders = pair_coef.shape[0]
     degrees = pair_coef.shape[2]
     width = pair_coef.shape[3] // 2
@@ -80,9 +83,319 @@
     return result * (1.0 / math.sqrt(total_orders))
 
 
+STEPS = 16.0
+TOP = 32000.0
+LANES = 128
+
+
+def bit_reverse(value, nbits):
+    flipped = 0
+    for bit in range(nbits):
+        flipped = flipped | (value >> bit & 1) << nbits - 1 - bit
+    return flipped
+
+
+def sort_kernel(perm_ref, coef_ref, out_ref):
+    moved = jnp.dot(perm_ref[...], coef_ref[...], preferred_element_type=jnp.float32)
+    out_ref[...] = moved.astype(out_ref.dtype).reshape(out_ref.shape)
+
+
+def sort_rows(pair_coef, batch_order):
+    orders, shells, degrees, width = pair_coef.shape
+    group = 16 // shells
+    rows = group * shells * degrees
+    out_at = lax.iota(jnp.int32, rows)
+    in_at = out_at
+    out_degree, out_order, out_t = out_at // (group * shells), out_at // shells % group, out_at % shells
+    in_degree, in_order, in_shell = in_at % degrees, in_at // (degrees * shells), in_at // degrees % shells
+    wanted = jnp.zeros((rows,), jnp.int32)
+    for t in range(shells):
+        wanted = jnp.where(out_t == t, batch_order[t], wanted)
+    perm = (
+        (out_degree[:, None] == in_degree[None, :])
+        & (out_order[:, None] == in_order[None, :])
+        & (wanted[:, None] == in_shell[None, :])
+    ).astype(jnp.bfloat16)
+    return pl.pallas_call(
+        sort_kernel,
+        grid=(orders // group,),
+        in_specs=[
+            pl.BlockSpec((rows, rows), lambda i: (0, 0)),
+            pl.BlockSpec((rows, width), lambda i: (i, 0)),
+        ],
+        out_specs=pl.BlockSpec((degrees, group * shells, width), lambda i: (0, i, 0)),
+        out_shape=jax.ShapeDtypeStruct((degrees, orders * shells, width), pair_coef.dtype),
+        compiler_params=pltpu.CompilerParams(vmem_limit_bytes=24 * 2**20),
+        cost_estimate=pl.CostEstimate(
+            flops=2 * orders * shells * degrees * rows * width,
+            bytes_accessed=4 * orders * shells * degrees * width,
+            transcendentals=0,
+        ),
+    )(perm, pair_coef.reshape(orders * shells * degrees, width))
+
+
+def scale_code(largest):
+    return jnp.ceil(jnp.log2(jnp.maximum(largest, 1e-30)) * STEPS) + 1.0
+
+
+def encode(real_part, imag_part):
+    largest = jnp.max(jnp.maximum(jnp.abs(real_part), jnp.abs(imag_part)), axis=0, keepdims=True)
+    code = scale_code(largest)
+    gain = jnp.exp2(code * (-1.0 / STEPS)) * TOP
+    coded = [
+        jnp.floor(v * gain + 0.5).astype(jnp.int32).astype(jnp.int16) for v in (real_part, imag_part)
+    ]
+    return coded[0], coded[1], code
+
+
+def gains(codes):
+    return jnp.exp2(codes.astype(jnp.int32).astype(jnp.float32) * (1.0 / STEPS)) * (1.0 / TOP)
+
+
+def widen(value):
+    return value.astype(jnp.int32).astype(jnp.float32)
+
+
+def project_kernel(offsets, n_acc, degree_ref, rows_ref, *refs):
+    n = len(offsets)
+    panels = refs[:n]
+    acc_in = refs[n : n + n_acc]
+    acc_out, lhs, rhs, sems = refs[n + n_acc :]
+    width = rhs.shape[1]
+    copies = []
+    at = 0
+    for i, (panel, offset) in enumerate(zip(panels, offsets)):
+        depth = panel.shape[0]
+        copies.append(pltpu.make_async_copy(panel, rhs.at[pl.ds(at, depth), :], sems.at[3 * i]))
+        for c in range(2):
+            copies.append(
+                pltpu.make_async_copy(
+                    rows_ref.at[degree_ref[i], :, pl.ds(c * width + offset, depth)],
+                    lhs.at[c, :, pl.ds(at, depth)],
+                    sems.at[3 * i + 1 + c],
+                )
+            )
+        at += depth
+    for copy in copies:
+        copy.start()
+    for copy in copies:
+        copy.wait()
+    for c in range(2):
+        part = jnp.dot(lhs[c], rhs[...], preferred_element_type=jnp.float32)
+        acc_out[c] = part + acc_in[0][c] if n_acc else part
+
+
+def project(acc, rows, degrees, panels, offsets):
+    count, width = rows.shape[1], panels[0].shape[1]
+    depth = sum(p.shape[0] for p in panels)
+    n_acc = 0 if acc is None else 1
+    return pl.pallas_call(
+        functools.partial(project_kernel, tuple(offsets), n_acc),
+        in_specs=[pl.BlockSpec(memory_space=pltpu.SMEM)]
+        + [pl.BlockSpec(memory_space=pl.ANY)] * (1 + len(panels))
+        + [pl.BlockSpec(memory_space=pltpu.VMEM)] * n_acc,
+        out_specs=pl.BlockSpec(memory_space=pltpu.VMEM),
+        out_shape=jax.ShapeDtypeStruct((2, count, width), jnp.float32),
+        scratch_shapes=[
+            pltpu.VMEM((2, count, depth), rows.dtype),
+            pltpu.VMEM((depth, width), rows.dtype),
+            pltpu.SemaphoreType.DMA((3 * len(panels),)),
+        ],
+        compiler_params=pltpu.CompilerParams(vmem_limit_bytes=24 * 2**20),
+        cost_estimate=pl.CostEstimate(
+            flops=4 * count * depth * width,
+            bytes_accessed=2 * depth * (width + 2 * count) + 8 * count * width * (1 + n_acc),
+            transcendentals=0,
+        ),
+    )(degrees, rows, *panels, *([acc] if n_acc else []))
+
+
+def pack_kernel(proj_ref, out_ref):
+    width = proj_ref.shape[2]
+    blocks = width // LANES
+    line = lax.broadcasted_iota(jnp.int32, (16, LANES), 0)
+    for d in range(out_ref.shape[0]):
+        codes = jnp.zeros((16, LANES), jnp.float32)
+        for jb in range(blocks):
+            lanes = pl.ds(jb * LANES, LANES)
+            real_part, imag_part, code = encode(
+                proj_ref[0, pl.ds(16 * d, 16), lanes], proj_ref[1, pl.ds(16 * d, 16), lanes]
+            )
+            out_ref[d, pl.ds(32 * jb, 16), :] = real_part
+            out_ref[d, pl.ds(32 * jb + 16, 16), :] = imag_part
+            codes = jnp.where(line == jb, code, codes)
+        out_ref[d, pl.ds(32 * blocks, 16), :] = codes.astype(jnp.int32).astype(jnp.int16)
+
+
+def radix2(real_parts, imag_parts):
+    n = len(real_parts)
+    re, im = list(real_parts), list(imag_parts)
+    half = n // 2
+    while half:
+        for start in range(0, n, 2 * half):
+            for k in range(half):
+                a, b = start + k, start + k + half
+                dr, di = re[a] - re[b], im[a] - im[b]
+                re[a], im[a] = re[a] + re[b], im[a] + im[b]
+                angle = -math.pi * k / half
+                if k == 0:
+                    re[b], im[b] = dr, di
+                elif 2 * k == half:
+                    re[b], im[b] = di, -dr
+                elif 4 * k == half:
+                    re[b], im[b] = (dr + di) * math.cos(angle), (di - dr) * math.cos(angle)
+                elif 4 * k == 3 * half:
+                    re[b], im[b] = (di - dr) * math.cos(math.pi / 4), (dr + di) * -math.cos(math.pi / 4)
+                else:
+                    c, s = math.cos(angle), math.sin(angle)
+                    re[b], im[b] = dr * c - di * s, dr * s + di * c
+        half //= 2
+    return re, im
+
+
+def outer_kernel(in_ref, out_ref, gain_ref, code_ref):
+    n = in_ref.shape[0]
+    blocks = in_ref.shape[1] // 32
+    for q in range(n):
+        gain_ref[q] = gains(in_ref[q, pl.ds(32 * blocks, 16), :])
+    code_ref[...] = jnp.zeros_like(code_ref)
+    for jb in range(blocks):
+        re, im = [], []
+        for q in range(n):
+            gain = gain_ref[q, pl.ds(jb, 1), :]
+            re.append(widen(in_ref[q, pl.ds(32 * jb, 16), :]) * gain)
+            im.append(widen(in_ref[q, pl.ds(32 * jb + 16, 16), :]) * gain)
+        re, im = radix2(re, im)
+        for p in range(n):
+            real_part, imag_part, code = encode(re[p], im[p])
+            out_ref[p, pl.ds(32 * jb, 16), :] = real_part
+            out_ref[p, pl.ds(32 * jb + 16, 16), :] = imag_part
+            code_ref[p, pl.ds(jb, 1), :] = code
+    for p in range(n):
+        out_ref[p, pl.ds(32 * blocks, 16), :] = code_ref[p].astype(jnp.int32).astype(jnp.int16)
+
+
+def inner_kernel(twist_ref, in_ref, out_ref, gain_ref):
+    n = in_ref.shape[0]
+    blocks = in_ref.shape[1] // 32
+    orders = 2 * n
+    nbits = orders.bit_length() - 1
+    for d in range(n):
+        gain_ref[d] = gains(in_ref[d, pl.ds(32 * blocks, 16), :])
+    for jb in range(blocks):
+        re, im = [], []
+        for d in range(n):
+            gain = gain_ref[d, pl.ds(jb, 1), :]
+            both_re = widen(in_ref[d, pl.ds(32 * jb, 16), :]) * gain
+            both_im = widen(in_ref[d, pl.ds(32 * jb + 16, 16), :]) * gain
+            for r in range(2):
+                a, b = both_re[8 * r : 8 * r + 8], both_im[8 * r : 8 * r + 8]
+                c, s = twist_ref[0, 2 * d + r], twist_ref[1, 2 * d + r]
+                re.append(a * c - b * s)
+                im.append(a * s + b * c)
+        re, im = radix2(re, im)
+        for p in range(orders):
+            h = bit_reverse(p, nbits)
+            for part, value in enumerate((re[p], im[p])):
+                for b in range(2):
+                    first = (b * orders + h) * 32 + 2 * jb + part
+                    out_ref[pl.ds(first, 4, stride=8), :] = value[4 * b : 4 * b + 4]
+
+
+def local_call(kernel, out, scratch, *args, smem=0):
+    return pl.pallas_call(
+        kernel,
+        in_specs=[pl.BlockSpec(memory_space=pltpu.SMEM)] * smem
+        + [pl.BlockSpec(memory_space=pltpu.VMEM)] * (len(args) - smem),
+        out_specs=pl.BlockSpec(memory_space=pltpu.VMEM),
+        out_shape=out,
+        scratch_shapes=scratch,
+        compiler_params=pltpu.CompilerParams(vmem_limit_bytes=24 * 2**20),
+    )(*args)
+
+
+def ring_of(chips, columns):
+    lines = chips // columns
+    walk = [columns * z for z in range(lines)]
+    if columns == 2:
+        walk += [columns * z + 1 for z in reversed(range(lines))]
+    return walk
+
+
+def shards(pair_coef, panel_pool, degree_owner, batch_order):
+    local_orders, shells = pair_coef.shape[:2]
+    width = panel_pool.shape[2]
+    devices = lax.axis_size("shell")
+    total_orders = local_orders * devices
+    chips = devices // 2
+    me = lax.axis_index("shell")
+    walk = jnp.array(ring_of(chips, 2), jnp.int32)
+    place = jnp.argsort(walk)[me // 2]
+    degree_of = jnp.argsort(degree_owner)
+    steps = [ring_of(chips, 2)[i % chips] for i in range(chips + 1)]
+
+    def around(value, forward):
+        pairs = []
+        for here, there in zip(steps[:-1], steps[1:]):
+            for core in range(2):
+                pair = (2 * here + core, 2 * there + core)
+                pairs.append(pair if forward else pair[::-1])
+        return lax.ppermute(value, "shell", pairs)
+
+    def sibling(value):
+        return lax.ppermute(value, "shell", [(s, s ^ 1) for s in range(devices)])
+
+    def degrees_at(*shifts):
+        slots = []
+        for shift in shifts:
+            chip = walk[(place + shift) % chips]
+            slots += [2 * chip + me % 2, 2 * chip + 1 - me % 2]
+        return degree_of[jnp.stack(slots)]
+
+    rows = sort_rows(pair_coef, batch_order)
+    own = panel_pool[0]
+    acc = project(None, rows, degrees_at(0), [own, sibling(own)], [0, 0])
+    fwd = bwd = own
+    for step in range(1, chips // 2):
+        fwd, bwd = around(fwd, True), around(bwd, False)
+        acc = project(
+            acc,
+            rows,
+            degrees_at(-step, step),
+            [fwd, sibling(fwd), bwd, sibling(bwd)],
+            [0] * 4,
+        )
+    half = own.shape[0] // 2
+    upper, lower = around(fwd[:half], True), around(bwd[half:], False)
+    far = degrees_at(chips // 2)
+    proj = project(
+        acc,
+        rows,
+        jnp.concatenate([far, far]),
+        [upper, sibling(upper), lower, sibling(lower)],
+        [0, 0, half, half],
+    )
+    blocks = width // LANES
+    parcel = jax.ShapeDtypeStruct((devices, 32 * blocks + 16, LANES), jnp.int16)
+    lines = pltpu.VMEM((devices, 16, LANES), jnp.float32)
+    sent = local_call(pack_kernel, parcel, [], proj)
+    sent = lax.all_to_all(sent, "shell", 0, 0)
+    sent = local_call(outer_kernel, parcel, [lines, lines], sent)
+    sent = lax.all_to_all(sent, "shell", 0, 0)
+    first = bit_reverse(me, devices.bit_length() - 1)
+    phase = lax.iota(jnp.int32, local_orders) * first % total_orders
+    angle = -2.0 * math.pi * phase.astype(jnp.float32) / float(total_orders)
+    twist = jnp.stack([jnp.cos(angle), jnp.sin(angle)]) * (1.0 / math.sqrt(total_orders))
+    out = jax.ShapeDtypeStruct((2 * local_orders * shells // 2 * 2 * blocks, LANES), jnp.float32)
+    scores = local_call(inner_kernel, out, [lines], twist, sent, smem=1)
+    scores = scores.reshape(2, local_orders, shells // 2, blocks, 2, LANES)
+    return scores.transpose(0, 1, 2, 4, 3, 5).reshape(2, local_orders, shells // 2, 2, width)
+
+
 def solution(mesh):
+    devices = mesh.shape["shell"]
     return jax.shard_map(
-        shards,
+        shards if devices == 16 else general,
         mesh=mesh,
         in_specs=(P(("grp", "shell"), None, None, None), P("shell", None, None), P(), P()),
         out_specs=P(None, ("grp", "shell"), None, None, None),

time: 1710 us -> 134 us (0.08)
  waiting for transfers between devices: 1560 us -> 36.6 us
  local copies, waits for them, and re-layouts: 58.8 us -> 15.9 us
  matrix products: 28.5 us -> 0 us
  Pallas kernels: 0 us -> 23.1 us
  other arithmetic: 32.9 us -> 9.86 us
  blocking collectives: 0 us -> 21.9 us
    psum x16 -> x0, waiting for transfers between devices: 1460 us -> none  [broadcast(): return lax.psum(jnp.where(mine, value, jnp.zeros_like(value)), axis)]
    ppermute x4 -> x17, waiting for transfers between devices: 96.8 us -> 21.2 us  [the longest x8 21.1 us: around(): return lax.ppermute(value, 'shell', pairs)]
    dot_general x20 -> x0, matrix products: 28.5 us -> none  [the longest x16 25.6 us: add_degree(): return total + jnp.dot(piece, panel, preferred_element_type=jnp.float32)]
    dynamic_slice x32 -> x2, local copies, waits for them, and re-layouts: 29.1 us -> 2.89 us  [the longest x1 1.65 us: degrees_at(): chip = walk[(place + shift) % chips]]
    pallas_call x0 -> x9, Pallas kernels: none -> 23.1 us  [the longest x5 13.4 us: project(): pl.pallas_call(functools.partial(project_kernel, tuple(offsets), n_acc),...]
    all_to_all x0 -> x1, blocking collectives: none -> 21.9 us  [shards(): sent = lax.all_to_all(sent, 'shell', 0, 0)]
  transfers between devices with their start and end apart: 20 -> 18, of which waited for: 20 -> 4; matrix products, arithmetic and copies ran while one was open for 1% -> 15% of each run, Pallas kernels for 0% -> 12%
where the time goes in v1:
time: 134 us
  waiting for transfers between devices  36.6 us (27%)
  Pallas kernels  23.1 us (17%)
  blocking collectives  21.9 us (16%)
  local copies, waits for them, and re-layouts  15.9 us (12%)
  starting transfers between devices  14.3 us (11%)
  between operations  12 us (9%)
  other arithmetic  9.86 us (7%)
    all_to_all x1, blocking collectives, shards(): sent = lax.all_to_all(sent, 'shell', 0, 0)  21.9 us
    ppermute x8, waiting for transfers between devices, around(): return lax.ppermute(value, 'shell', pairs)  21.1 us
    all_to_all x1, waiting for transfers between devices, shards(): sent = lax.all_to_all(sent, 'shell', 0, 0)  15.4 us
    pallas_call x5, Pallas kernels, project(): pl.pallas_call(functools.partial(project_kernel, tuple(offsets), n_acc),...  13.4 us
    ppermute x8, starting transfers between devices, around(): return lax.ppermute(value, 'shell', pairs)  9.16 us
    unnamed x20, local copies, waits for them, and re-layouts  5.79 us
    pallas_call x1, Pallas kernels, sort_rows(): pl.pallas_call(sort_kernel, grid=(orders // group,), in_specs=[pl.BlockSp...  5.53 us
    select_n x1, other arithmetic, sort_rows(): in_at // degrees % shells  4.94 us
  transfers between devices with their start and end apart: 18, of which 4 were waited for; matrix products, arithmetic and copies ran while one was open for 15% of the time, Pallas kernels for 12%

profile of v1, /device:TPU:0, one launch (start us, length us, event | category | flops | bytes accessed | tf_op | source)
XLA Modules:
  0.0 133.6 jit_solution(3843108340423381768)
XLA Ops:
  0.0 3.0 %collective-permute-start = (bf16[512,512]{1,0:T(8,128)(2,1)}, bf16[512,512]{1,0:T(8,128)(2,1)S(1)}, u32[]{:S(2)}, u32[]{:S(2)}) collective-permute-start(bf16[512,512]{1,0:T(8,128)(2,1)} %bitcast.51), channel_id=1, source_target_pairs={{0,4},{1,5},{4,8},{5,9},{8,12},{9,13},{12,14},{13,15},{14,10},{15,... | collective-permute-start | bytes 1572872 | tf_op jit(solution)/shard_map/ppermute | solution.py:343
  3.0 1.2 dynamic_slice.27
  10.9 1.7 %fusion.16 = (s32[1]{0:T(128)}, s32[1]{0:T(128)}, s32[1]{0:T(128)}, s32[1]{0:T(128)}, s32[1]{0:T(128)}, /*index=5*/s32[1]{0:T(128)}, s32[1]{0:T(128)}, s32[1]{0:T(128)}) fusion(s32[8]{0:T(128)} %constant.222.clone, s32[]{:T(128)S(6)} %select_n.340, s32[]{:T(128)S(6)} %select_n.332, s32[]{:T(128)S(6)} %select_n.330, s32[]{:T(128)S(6)} %select_n.327, ...), kind=kLoop, calls=%fused_computation.63 | loop fusion | bytes 96 | tf_op jit(solution)/shard_map/dynamic_slice | solution.py:351
  17.7 1.9 %sort.34 = (s32[16]{0:T(128)}, s32[16]{0:T(128)S(1)}) sort(s32[16]{0:T(128)} %param.7, s32[16]{0:T(128)S(1)} %iota.53), dimensions={0}, to_apply=%region_0.0 | sort | flops 64 | bytes 256 | tf_op jit(solution)/shard_map/jit(argsort)/sort | solution.py:334
  19.6 2.0 %collective-permute-start.1 = (bf16[512,512]{1,0:T(8,128)(2,1)S(1)}, bf16[512,512]{1,0:T(8,128)(2,1)S(1)}, u32[]{:S(2)}, u32[]{:S(2)}) collective-permute-start(bf16[512,512]{1,0:T(8,128)(2,1)S(1)} %collective-permute-done.refs_0_), channel_id=1, source_target_pairs={{0,4},{1,5},{4,8},{5,9},{8,12},{9,13},{12,14},{13,15},{14,10},{15,... | collective-permute-start | bytes 1572872 | tf_op jit(solution)/shard_map/ppermute | solution.py:343
  22.3 1.6 %fusion.17 = (s32[1]{0:T(128)}, s32[1]{0:T(128)}, s32[1]{0:T(128)}, s32[1]{0:T(128)}, s32[1]{0:T(128)}, /*index=5*/s32[1]{0:T(128)}, s32[1]{0:T(128)}, s32[1]{0:T(128)}) fusion(s32[8]{0:T(128)} %param.8), kind=kLoop, calls=%fused_computation.64 | loop fusion | bytes 64 | tf_op jit(solution)/shard_map/slice | solution.py:113
  24.1 9.9 %collective-permute-done.1.refs_0_ = bf16[512,512]{1,0:T(8,128)(2,1)S(1)} collective-permute-done((bf16[512,512]{1,0:T(8,128)(2,1)S(1)}, bf16[512,512]{1,0:T(8,128)(2,1)S(1)}, u32[]{:S(2)}, u32[]{:S(2)}) %collective-permute-start.1) | collective-permute-done | bytes 524320 | tf_op jit(solution)/shard_map/ppermute | solution.py:343
  34.0 1.7 %collective-permute-start.2 = (bf16[512,512]{1,0:T(8,128)(2,1)S(1)}, bf16[512,512]{1,0:T(8,128)(2,1)S(1)}, u32[]{:S(2)}, u32[]{:S(2)}) collective-permute-start(bf16[512,512]{1,0:T(8,128)(2,1)S(1)} %collective-permute-done.1.refs_0_), channel_id=1, source_target_pairs={{0,4},{1,5},{4,8},{5,9},{8,12},{9,13},{12,14},{13,15},{14,10},{15,... | collective-permute-start | bytes 1572872 | tf_op jit(solution)/shard_map/ppermute | solution.py:343
  35.8 4.9 %and_select_fusion = (s32[256]{0:T(256)S(1)}, s32[256]{0:T(256)S(1)}) fusion(s32[]{:T(128)} %bitcast.12, s32[]{:T(128)} %bitcast.11, s32[]{:T(128)} %bitcast.10, s32[]{:T(128)} %bitcast.9, s32[]{:T(128)} %bitcast.8, s32[]{:T(128)} %bitcast.7, s32[]{:T(128)} %bitcast.6, s32[]{:T(128)} %bitcast.5), kind=kLoop, calls=%fused_computation.25 | loop fusion | flops 10496 | bytes 2080 | tf_op jit(solution)/shard_map/jit(remainder)/select_n | solution.py:110
  42.2 5.3 %collective-permute-done.2.refs_0_ = bf16[512,512]{1,0:T(8,128)(2,1)S(1)} collective-permute-done((bf16[512,512]{1,0:T(8,128)(2,1)S(1)}, bf16[512,512]{1,0:T(8,128)(2,1)S(1)}, u32[]{:S(2)}, u32[]{:S(2)}) %collective-permute-start.2) | collective-permute-done | bytes 524320 | tf_op jit(solution)/shard_map/ppermute | solution.py:343
  48.4 5.9 %collective-permute-done.7.refs_2_ = bf16[512,512]{1,0:T(8,128)(2,1)S(1)} collective-permute-done((bf16[512,512]{1,0:T(8,128)(2,1)S(1)}, bf16[512,512]{1,0:T(8,128)(2,1)S(1)}, u32[]{:S(2)}, u32[]{:S(2)}) %collective-permute-start.7) | collective-permute-done | bytes 524320 | tf_op jit(solution)/shard_map/ppermute | solution.py:343
  54.9 0.7 slice.50
  55.6 0.7 slice.51
  56.4 1.6 %collective-permute-start.3 = (bf16[256,512]{1,0:T(8,128)(2,1)}, bf16[256,512]{1,0:T(8,128)(2,1)S(1)}, u32[]{:S(2)}, u32[]{:S(2)}) collective-permute-start(bf16[256,512]{1,0:T(8,128)(2,1)} %slice.50), channel_id=1, source_target_pairs={{0,4},{1,5},{4,8},{5,9},{8,12},{9,13},{12,14},{13,15},{14,10},{15,... | collective-permute-start | bytes 786440 | tf_op jit(solution)/shard_map/ppermute | solution.py:343
  57.9 0.8 copy-done.1
  59.2 0.8 copy-done.5
  60.0 0.8 copy-done.3
  62.5 0.8 gather_fusion.3
  63.3 0.8 gather_fusion.2
  64.0 1.3 gather_fusion.1
  65.4 3.4 %copy-done = bf16[32,8,16,1024]{3,2,1,0:T(8,128)(2,1)S(1)} copy-done((bf16[32,8,16,1024]{3,2,1,0:T(8,128)(2,1)S(1)}, bf16[32,8,16,1024]{3,2,1,0:T(8,128)(2,1)}, u32[]{:S(2)}) %copy-start) | copy-done | bytes 8388632
  68.8 5.5 %shard_map.55.rows_ref = bf16[16,256,1024]{2,1,0:T(8,128)(2,1)S(1)} custom-call(bf16[256,256]{1,0:T(8,128)(2,1)S(1)} %and_convert_fusion.perm_ref, bf16[4096,1024]{1,0:T(8,128)(2,1)S(1)} %bitcast.50), custom_call_target="tpu_custom_call" | custom-call | flops 2147483648 | bytes 16777216 | tf_op jit(solution)/shard_map/pallas_call | solution.py:119
  74.3 2.4 %shard_map.56.refs_4_ = f32[2,256,512]{2,1,0:T(8,128)S(1)} custom-call(s32[2]{0:T(128)S(1)} %gather_fusion.4, bf16[16,256,1024]{2,1,0:T(8,128)(2,1)S(1)} %shard_map.55.rows_ref, bf16[512,512]{1,0:T(8,128)(2,1)S(1)} %bitcast.54, bf16[512,512]{1,0:T(8,128)(2,1)} %collective-permute-done.16.refs_1_), custom_call_target="tpu_custom_call" | custom-call | flops 536870912 | bytes 3145728 | tf_op jit(solution)/shard_map/pallas_call | solution.py:192
  77.4 2.2 %shard_map.57.refs_4_ = f32[2,256,512]{2,1,0:T(8,128)S(1)} custom-call(s32[4]{0:T(128)S(1)} %gather_fusion.3, bf16[16,256,1024]{2,1,0:T(8,128)(2,1)S(1)} %shard_map.55.rows_ref, bf16[512,512]{1,0:T(8,128)(2,1)S(1)} %collective-permute-done.refs_0_, bf16[512,512]{1,0:T(8,128)(2,1)S(1)} %copy-done.2, bf16[512,512]{1,0:T(8,128)(2,1)S(1)} %collective-permute-done.5.refs_2_, ...), custom_call_target="tpu_custom_call" | custom-call | flops 1073741824 | bytes 6291456 | tf_op jit(solution)/shard_map/pallas_call | solution.py:192
  79.6 3.2 %shard_map.58.refs_4_ = f32[2,256,512]{2,1,0:T(8,128)S(1)} custom-call(s32[4]{0:T(128)S(1)} %gather_fusion.2, bf16[16,256,1024]{2,1,0:T(8,128)(2,1)S(1)} %shard_map.55.rows_ref, bf16[512,512]{1,0:T(8,128)(2,1)S(1)} %collective-permute-done.1.refs_0_, bf16[512,512]{1,0:T(8,128)(2,1)S(1)} %copy-done.4, bf16[512,512]{1,0:T(8,128)(2,1)S(1)} %collective-permute-done.6.refs_2_, ...), custom_call_target="tpu_custom_call" | custom-call | flops 1073741824 | bytes 6291456 | tf_op jit(solution)/shard_map/pallas_call | solution.py:192
  82.8 3.2 %shard_map.59.refs_4_ = f32[2,256,512]{2,1,0:T(8,128)S(1)} custom-call(s32[4]{0:T(128)S(1)} %gather_fusion.1, bf16[16,256,1024]{2,1,0:T(8,128)(2,1)S(1)} %shard_map.55.rows_ref, bf16[512,512]{1,0:T(8,128)(2,1)S(1)} %collective-permute-done.2.refs_0_, bf16[512,512]{1,0:T(8,128)(2,1)} %collective-permute-done.10.refs_1_, ...), custom_call_target="tpu_custom_call" | custom-call | flops 1073741824 | bytes 6291456 | tf_op jit(solution)/shard_map/pallas_call | solution.py:192
  86.1 2.4 %shard_map.60.proj_ref = f32[2,256,512]{2,1,0:T(8,128)S(1)} custom-call(s32[4]{0:T(128)S(1)} %copy-done.8, bf16[16,256,1024]{2,1,0:T(8,128)(2,1)S(1)} %shard_map.55.rows_ref, bf16[256,512]{1,0:T(8,128)(2,1)S(1)} %collective-permute-done.3.refs_0_, bf16[256,512]{1,0:T(8,128)(2,1)S(1)} %collective-permute-done.4.refs_1_, ...), custom_call_target="tpu_custom_call" | custom-call | flops 536870912 | bytes 4194304 | tf_op jit(solution)/shard_map/pallas_call | solution.py:192
  88.9 21.9 %all_to_all.10.in_ref = s16[16,144,128]{2,1,0:T(8,128)(2,1)S(1)} all-to-all(s16[16,144,128]{2,1,0:T(8,128)(2,1)S(1)} %shard_map.61), channel_id=1, replica_groups=mesh['grp'=2,'shell'=16] {'shell'}, dimensions={0} | all-to-all | bytes 1179648 | tf_op jit(solution)/shard_map/all_to_all | solution.py:382
  110.8 1.5 %shard_map.62 = s16[16,144,128]{2,1,0:T(8,128)(2,1)} custom-call(s16[16,144,128]{2,1,0:T(8,128)(2,1)S(1)} %all_to_all.10.in_ref), custom_call_target="tpu_custom_call" | custom-call | tf_op jit(solution)/shard_map/pallas_call | solution.py:306
  112.3 3.6 %all-to-all-start.1 = ((s16[16,144,128]{2,1,0:T(8,128)(2,1)}), s16[16,144,128]{2,1,0:T(8,128)(2,1)S(1)}, u32[]{:S(2)}, u32[]{:S(2)}) async-start(s16[16,144,128]{2,1,0:T(8,128)(2,1)} %shard_map.62), calls=%async_computation.1 | async-start | bytes 1179648 | tf_op jit(solution)/shard_map/all_to_all | solution.py:384
  116.0 15.4 %all-to-all-done.1.in_ref = s16[16,144,128]{2,1,0:T(8,128)(2,1)S(1)} async-done(((s16[16,144,128]{2,1,0:T(8,128)(2,1)}), s16[16,144,128]{2,1,0:T(8,128)(2,1)S(1)}, u32[]{:S(2)}, u32[]{:S(2)}) %all-to-all-start.1) | async-done | bytes 589856 | tf_op jit(solution)/shard_map/all_to_all | solution.py:384
  131.4 2.2 %shard_map.63 = f32[2048,128]{1,0:T(8,128)} custom-call(f32[2,32]{1,0:T(2,128)S(1)} %maximum_multiply_fusion.twist_ref, s16[16,144,128]{2,1,0:T(8,128)(2,1)S(1)} %all-to-all-done.1.in_ref), custom_call_target="tpu_custom_call" | custom-call | tf_op jit(solution)/shard_map/pallas_call | solution.py:306
  (63 shorter events, 7.1 us)
Async XLA Ops:
  0.0 19.6 %collective-permute-start = (bf16[512,512]{1,0:T(8,128)(2,1)}, bf16[512,512]{1,0:T(8,128)(2,1)S(1)}, u32[]{:S(2)}, u32[]{:S(2)}) collective-permute-start(bf16[512,512]{1,0:T(8,128)(2,1)} %bitcast.51), channel_id=1, source_target_pairs={{0,4},{1,5},{4,8},{5,9},{8,12},{9,13},{12,14},{13,15},{14,10},{15,... | collective-permute-start | bytes 1572872 | tf_op jit(solution)/shard_map/ppermute | solution.py:343
  3.0 53.3 %collective-permute-start.16 = (bf16[512,512]{1,0:T(8,128)(2,1)}, bf16[512,512]{1,0:T(8,128)(2,1)}, u32[]{:S(2)}, u32[]{:S(2)}) collective-permute-start(bf16[512,512]{1,0:T(8,128)(2,1)} %bitcast.52), channel_id=1, source_target_pairs={{0,1},{1,0},{2,3},{3,2},{4,5},{5,4},{6,7},{7,6},{8,9},{9,8},{10,11... | collective-permute-start | bytes 1572872 | tf_op jit(solution)/shard_map/ppermute | solution.py:346
  3.0 20.9 %collective-permute-start.5 = (bf16[512,512]{1,0:T(8,128)(2,1)}, bf16[512,512]{1,0:T(8,128)(2,1)S(1)}, u32[]{:S(2)}, u32[]{:S(2)}) collective-permute-start(bf16[512,512]{1,0:T(8,128)(2,1)} %bitcast.53), channel_id=1, source_target_pairs={{4,0},{5,1},{8,4},{9,5},{12,8},{13,9},{14,12},{15,13},{10,14},{11,... | collective-permute-start | bytes 1572872 | tf_op jit(solution)/shard_map/ppermute | solution.py:343
  19.6 43.7 %copy-start.9 = (s32[16]{0:T(128)}, s32[16]{0:T(128)S(1)}, u32[]{:S(2)}) copy-start(s32[16]{0:T(128)S(1)} %get-tuple-element.7) | copy-start | bytes 196
  19.6 14.3 %collective-permute-start.1 = (bf16[512,512]{1,0:T(8,128)(2,1)S(1)}, bf16[512,512]{1,0:T(8,128)(2,1)S(1)}, u32[]{:S(2)}, u32[]{:S(2)}) collective-permute-start(bf16[512,512]{1,0:T(8,128)(2,1)S(1)} %collective-permute-done.refs_0_), channel_id=1, source_target_pairs={{0,4},{1,5},{4,8},{5,9},{8,12},{9,13},{12,14},{13,15},{14,10},{15,... | collective-permute-start | bytes 1572872 | tf_op jit(solution)/shard_map/ppermute | solution.py:343
  23.9 17.4 %collective-permute-start.6 = (bf16[512,512]{1,0:T(8,128)(2,1)S(1)}, bf16[512,512]{1,0:T(8,128)(2,1)S(1)}, u32[]{:S(2)}, u32[]{:S(2)}) collective-permute-start(bf16[512,512]{1,0:T(8,128)(2,1)S(1)} %collective-permute-done.5.refs_2_), channel_id=1, source_target_pairs={{4,0},{5,1},{8,4},{9,5},{12,8},{13,9},{14,12},{15,13},{10,14},{11,... | collective-permute-start | bytes 1572872 | tf_op jit(solution)/shard_map/ppermute | solution.py:343
  34.0 13.6 %collective-permute-start.2 = (bf16[512,512]{1,0:T(8,128)(2,1)S(1)}, bf16[512,512]{1,0:T(8,128)(2,1)S(1)}, u32[]{:S(2)}, u32[]{:S(2)}) collective-permute-start(bf16[512,512]{1,0:T(8,128)(2,1)S(1)} %collective-permute-done.1.refs_0_), channel_id=1, source_target_pairs={{0,4},{1,5},{4,8},{5,9},{8,12},{9,13},{12,14},{13,15},{14,10},{15,... | collective-permute-start | bytes 1572872 | tf_op jit(solution)/shard_map/ppermute | solution.py:343
  41.4 13.0 %collective-permute-start.7 = (bf16[512,512]{1,0:T(8,128)(2,1)S(1)}, bf16[512,512]{1,0:T(8,128)(2,1)S(1)}, u32[]{:S(2)}, u32[]{:S(2)}) collective-permute-start(bf16[512,512]{1,0:T(8,128)(2,1)S(1)} %collective-permute-done.6.refs_2_), channel_id=1, source_target_pairs={{4,0},{5,1},{8,4},{9,5},{12,8},{13,9},{14,12},{15,13},{10,14},{11,... | collective-permute-start | bytes 1572872 | tf_op jit(solution)/shard_map/ppermute | solution.py:343
  41.7 16.2 %collective-permute-start.14 = (bf16[512,512]{1,0:T(8,128)(2,1)S(1)}, bf16[512,512]{1,0:T(8,128)(2,1)S(1)}, u32[]{:S(2)}, u32[]{:S(2)}) collective-permute-start(bf16[512,512]{1,0:T(8,128)(2,1)S(1)} %collective-permute-done.refs_0_), channel_id=1, source_target_pairs={{0,1},{1,0},{2,3},{3,2},{4,5},{5,4},{6,7},{7,6},{8,9},{9,8},{10,11... | collective-permute-start | bytes 1572872 | tf_op jit(solution)/shard_map/ppermute | solution.py:346
  41.7 17.5 %collective-permute-start.15 = (bf16[512,512]{1,0:T(8,128)(2,1)S(1)}, bf16[512,512]{1,0:T(8,128)(2,1)S(1)}, u32[]{:S(2)}, u32[]{:S(2)}) collective-permute-start(bf16[512,512]{1,0:T(8,128)(2,1)S(1)} %collective-permute-done.5.refs_2_), channel_id=1, source_target_pairs={{0,1},{1,0},{2,3},{3,2},{4,5},{5,4},{6,7},{7,6},{8,9},{9,8},{10,11... | collective-permute-start | bytes 1572872 | tf_op jit(solution)/shard_map/ppermute | solution.py:346
  47.5 12.5 %collective-permute-start.12 = (bf16[512,512]{1,0:T(8,128)(2,1)S(1)}, bf16[512,512]{1,0:T(8,128)(2,1)S(1)}, u32[]{:S(2)}, u32[]{:S(2)}) collective-permute-start(bf16[512,512]{1,0:T(8,128)(2,1)S(1)} %collective-permute-done.1.refs_0_), channel_id=1, source_target_pairs={{0,1},{1,0},{2,3},{3,2},{4,5},{5,4},{6,7},{7,6},{8,9},{9,8},{10,11... | collective-permute-start | bytes 1572872 | tf_op jit(solution)/shard_map/ppermute | solution.py:346
  54.3 25.3 %collective-permute-start.13 = (bf16[512,512]{1,0:T(8,128)(2,1)S(1)}, bf16[512,512]{1,0:T(8,128)(2,1)}, u32[]{:S(2)}, u32[]{:S(2)}) collective-permute-start(bf16[512,512]{1,0:T(8,128)(2,1)S(1)} %collective-permute-done.6.refs_2_), channel_id=1, source_target_pairs={{0,1},{1,0},{2,3},{3,2},{4,5},{5,4},{6,7},{7,6},{8,9},{9,8},{10,11... | collective-permute-start | bytes 1572872 | tf_op jit(solution)/shard_map/ppermute | solution.py:346
  56.4 20.4 %collective-permute-start.3 = (bf16[256,512]{1,0:T(8,128)(2,1)}, bf16[256,512]{1,0:T(8,128)(2,1)S(1)}, u32[]{:S(2)}, u32[]{:S(2)}) collective-permute-start(bf16[256,512]{1,0:T(8,128)(2,1)} %slice.50), channel_id=1, source_target_pairs={{0,4},{1,5},{4,8},{5,9},{8,12},{9,13},{12,14},{13,15},{14,10},{15,... | collective-permute-start | bytes 786440 | tf_op jit(solution)/shard_map/ppermute | solution.py:343
  57.9 0.8 copy-start.1
  58.7 18.1 %collective-permute-start.8 = (bf16[256,512]{1,0:T(8,128)(2,1)}, bf16[256,512]{1,0:T(8,128)(2,1)}, u32[]{:S(2)}, u32[]{:S(2)}) collective-permute-start(bf16[256,512]{1,0:T(8,128)(2,1)} %slice.51), channel_id=1, source_target_pairs={{4,0},{5,1},{8,4},{9,5},{12,8},{13,9},{14,12},{15,13},{10,14},{11,... | collective-permute-start | bytes 786440 | tf_op jit(solution)/shard_map/ppermute | solution.py:343
  59.2 0.8 copy-start.5
  60.0 22.8 %collective-permute-start.10 = (bf16[512,512]{1,0:T(8,128)(2,1)S(1)}, bf16[512,512]{1,0:T(8,128)(2,1)}, u32[]{:S(2)}, u32[]{:S(2)}) collective-permute-start(bf16[512,512]{1,0:T(8,128)(2,1)S(1)} %collective-permute-done.2.refs_0_), channel_id=1, source_target_pairs={{0,1},{1,0},{2,3},{3,2},{4,5},{5,4},{6,7},{7,6},{8,9},{9,8},{10,11... | collective-permute-start | bytes 1572872 | tf_op jit(solution)/shard_map/ppermute | solution.py:346
  60.0 0.8 copy-start.3
  60.8 22.0 %collective-permute-start.11 = (bf16[512,512]{1,0:T(8,128)(2,1)S(1)}, bf16[512,512]{1,0:T(8,128)(2,1)}, u32[]{:S(2)}, u32[]{:S(2)}) collective-permute-start(bf16[512,512]{1,0:T(8,128)(2,1)S(1)} %collective-permute-done.7.refs_2_), channel_id=1, source_target_pairs={{0,1},{1,0},{2,3},{3,2},{4,5},{5,4},{6,7},{7,6},{8,9},{9,8},{10,11... | collective-permute-start | bytes 1572872 | tf_op jit(solution)/shard_map/ppermute | solution.py:346
  65.4 3.4 %copy-start = (bf16[32,8,16,1024]{3,2,1,0:T(8,128)(2,1)S(1)}, bf16[32,8,16,1024]{3,2,1,0:T(8,128)(2,1)}, u32[]{:S(2)}) copy-start(bf16[32,8,16,1024]{3,2,1,0:T(8,128)(2,1)} %param.5) | copy-start | bytes 25165828
  68.8 5.5 %copy-start.7 = (bf16[1,512,512]{2,1,0:T(8,128)(2,1)S(1)}, bf16[1,512,512]{2,1,0:T(8,128)(2,1)}, u32[]{:S(2)}) copy-start(bf16[1,512,512]{2,1,0:T(8,128)(2,1)} %param.6) | copy-start | bytes 1572868
  74.3 3.1 %copy-start.2 = (bf16[512,512]{1,0:T(8,128)(2,1)S(1)}, bf16[512,512]{1,0:T(8,128)(2,1)}, u32[]{:S(2)}) copy-start(bf16[512,512]{1,0:T(8,128)(2,1)} %copy-done.1) | copy-start | bytes 1572868
  74.3 3.0 %copy-start.6 = (bf16[512,512]{1,0:T(8,128)(2,1)S(1)}, bf16[512,512]{1,0:T(8,128)(2,1)}, u32[]{:S(2)}) copy-start(bf16[512,512]{1,0:T(8,128)(2,1)} %copy-done.5) | copy-start | bytes 1572868
  76.8 2.9 %copy-start.4 = (bf16[512,512]{1,0:T(8,128)(2,1)S(1)}, bf16[512,512]{1,0:T(8,128)(2,1)}, u32[]{:S(2)}) copy-start(bf16[512,512]{1,0:T(8,128)(2,1)} %copy-done.3) | copy-start | bytes 1572868
  76.8 9.3 %collective-permute-start.4 = (bf16[256,512]{1,0:T(8,128)(2,1)S(1)}, bf16[256,512]{1,0:T(8,128)(2,1)S(1)}, u32[]{:S(2)}, u32[]{:S(2)}) collective-permute-start(bf16[256,512]{1,0:T(8,128)(2,1)S(1)} %collective-permute-done.3.refs_0_), channel_id=1, source_target_pairs={{0,1},{1,0},{2,3},{3,2},{4,5},{5,4},{6,7},{7,6},{8,9},{9,8},{10,11... | collective-permute-start | bytes 786440 | tf_op jit(solution)/shard_map/ppermute | solution.py:346
  76.9 9.2 %collective-permute-start.9 = (bf16[256,512]{1,0:T(8,128)(2,1)}, bf16[256,512]{1,0:T(8,128)(2,1)S(1)}, u32[]{:S(2)}, u32[]{:S(2)}) collective-permute-start(bf16[256,512]{1,0:T(8,128)(2,1)} %collective-permute-done.8.refs_2_), channel_id=1, source_target_pairs={{0,1},{1,0},{2,3},{3,2},{4,5},{5,4},{6,7},{7,6},{8,9},{9,8},{10,11... | collective-permute-start | bytes 786440 | tf_op jit(solution)/shard_map/ppermute | solution.py:346
  82.8 3.3 %copy-start.8 = (s32[4]{0:T(128)S(1)}, s32[4]{0:T(128)}, u32[]{:S(2)}) copy-start(s32[4]{0:T(128)} %pad_add_fusion.degree_ref) | copy-start | bytes 52
  112.3 19.1 %all-to-all-start.1 = ((s16[16,144,128]{2,1,0:T(8,128)(2,1)}), s16[16,144,128]{2,1,0:T(8,128)(2,1)S(1)}, u32[]{:S(2)}, u32[]{:S(2)}) async-start(s16[16,144,128]{2,1,0:T(8,128)(2,1)} %shard_map.62), calls=%async_computation.1 | async-start | bytes 1179648 | tf_op jit(solution)/shard_map/all_to_all | solution.py:384

commit v2 on v1

--- a/solution.py
+++ b/solution.py
@@ -95,7 +95,20 @@
     return flipped
 
 
-def sort_kernel(perm_ref, coef_ref, out_ref):
+def sort_kernel(shells, order_ref, coef_ref, out_ref, perm_ref):
+    @pl.when(pl.program_id(0) == 0)
+    def _():
+        degrees, group = out_ref.shape[0], out_ref.shape[1] // shells
+        shape = perm_ref.shape
+        out_at = lax.broadcasted_iota(jnp.int32, shape, 0)
+        in_at = lax.broadcasted_iota(jnp.int32, shape, 1)
+        out_t = out_at % shells
+        wanted = jnp.zeros(shape, jnp.int32)
+        for t in range(shells):
+            wanted = jnp.where(out_t == t, order_ref[t], wanted)
+        source = (out_at // shells % group * shells + wanted) * degrees + out_at // (group * shells)
+        perm_ref[...] = jnp.where(in_at == source, 1.0, 0.0).astype(perm_ref.dtype)
+
     moved = jnp.dot(perm_ref[...], coef_ref[...], preferred_element_type=jnp.float32)
     out_ref[...] = moved.astype(out_ref.dtype).reshape(out_ref.shape)
 
@@ -104,34 +117,23 @@
     orders, shells, degrees, width = pair_coef.shape
     group = 16 // shells
     rows = group * shells * degrees
-    out_at = lax.iota(jnp.int32, rows)
-    in_at = out_at
-    out_degree, out_order, out_t = out_at // (group * shells), out_at // shells % group, out_at % shells
-    in_degree, in_order, in_shell = in_at % degrees, in_at // (degrees * shells), in_at // degrees % shells
-    wanted = jnp.zeros((rows,), jnp.int32)
-    for t in range(shells):
-        wanted = jnp.where(out_t == t, batch_order[t], wanted)
-    perm = (
-        (out_degree[:, None] == in_degree[None, :])
-        & (out_order[:, None] == in_order[None, :])
-        & (wanted[:, None] == in_shell[None, :])
-    ).astype(jnp.bfloat16)
     return pl.pallas_call(
-        sort_kernel,
+        functools.partial(sort_kernel, shells),
         grid=(orders // group,),
         in_specs=[
-            pl.BlockSpec((rows, rows), lambda i: (0, 0)),
+            pl.BlockSpec(memory_space=pltpu.SMEM),
             pl.BlockSpec((rows, width), lambda i: (i, 0)),
         ],
         out_specs=pl.BlockSpec((degrees, group * shells, width), lambda i: (0, i, 0)),
         out_shape=jax.ShapeDtypeStruct((degrees, orders * shells, width), pair_coef.dtype),
+        scratch_shapes=[pltpu.VMEM((rows, rows), pair_coef.dtype)],
         compiler_params=pltpu.CompilerParams(vmem_limit_bytes=24 * 2**20),
         cost_estimate=pl.CostEstimate(
             flops=2 * orders * shells * degrees * rows * width,
             bytes_accessed=4 * orders * shells * degrees * width,
             transcendentals=0,
         ),
-    )(perm, pair_coef.reshape(orders * shells * degrees, width))
+    )(batch_order, pair_coef.reshape(orders * shells * degrees, width))
 
 
 def scale_code(largest):
@@ -156,21 +158,40 @@
     return value.astype(jnp.int32).astype(jnp.float32)
 
 
-def project_kernel(offsets, n_acc, degree_ref, rows_ref, *refs):
-    n = len(offsets)
+def walk_at(place, chips):
+    lines = chips // 2
+    return jnp.where(place < lines, 2 * place, 2 * (chips - 1 - place) + 1)
+
+
+def place_of(chip, chips):
+    return jnp.where(chip % 2 == 0, chip // 2, chips - 1 - chip // 2)
+
+
+def project_kernel(devices, sources, n_acc, owner_ref, rows_ref, *refs):
+    n = len(sources)
     panels = refs[:n]
     acc_in = refs[n : n + n_acc]
     acc_out, lhs, rhs, sems = refs[n + n_acc :]
     width = rhs.shape[1]
+    chips = devices // 2
+    me = lax.axis_index("shell")
     copies = []
     at = 0
-    for i, (panel, offset) in enumerate(zip(panels, offsets)):
+    part = lax.axis_index("grp")
+    for i, (panel, (shift, flip, half)) in enumerate(zip(panels, sources)):
         depth = panel.shape[0]
+        ahead = jnp.where(me % 2 == 0, shift, -shift)
+        place = lax.rem(place_of(me // 2, chips) + ahead + chips, chips)
+        slot = 2 * walk_at(place, chips) + (me + flip) % 2
+        offset = 0 if half is None else pl.multiple_of(depth * (part + half) % (2 * depth), 128)
+        degree = jnp.zeros((), jnp.int32)
+        for l in range(rows_ref.shape[0]):
+            degree = jnp.where(owner_ref[l] == slot, l, degree)
         copies.append(pltpu.make_async_copy(panel, rhs.at[pl.ds(at, depth), :], sems.at[3 * i]))
         for c in range(2):
             copies.append(
                 pltpu.make_async_copy(
-                    rows_ref.at[degree_ref[i], :, pl.ds(c * width + offset, depth)],
+                    rows_ref.at[degree, :, pl.ds(pl.multiple_of(c * width + offset, 128), depth)],
                     lhs.at[c, :, pl.ds(at, depth)],
                     sems.at[3 * i + 1 + c],
                 )
@@ -185,12 +206,12 @@
         acc_out[c] = part + acc_in[0][c] if n_acc else part
 
 
-def project(acc, rows, degrees, panels, offsets):
+def project(acc, rows, owner, panels, sources):
     count, width = rows.shape[1], panels[0].shape[1]
     depth = sum(p.shape[0] for p in panels)
     n_acc = 0 if acc is None else 1
     return pl.pallas_call(
-        functools.partial(project_kernel, tuple(offsets), n_acc),
+        functools.partial(project_kernel, lax.axis_size("shell"), tuple(sources), n_acc),
         in_specs=[pl.BlockSpec(memory_space=pltpu.SMEM)]
         + [pl.BlockSpec(memory_space=pl.ANY)] * (1 + len(panels))
         + [pl.BlockSpec(memory_space=pltpu.VMEM)] * n_acc,
@@ -207,7 +228,7 @@
             bytes_accessed=2 * depth * (width + 2 * count) + 8 * count * width * (1 + n_acc),
             transcendentals=0,
         ),
-    )(degrees, rows, *panels, *([acc] if n_acc else []))
+    )(owner, rows, *panels, *([acc] if n_acc else []))
 
 
 def pack_kernel(proj_ref, out_ref):
@@ -314,14 +335,6 @@
     )(*args)
 
 
-def ring_of(chips, columns):
-    lines = chips // columns
-    walk = [columns * z for z in range(lines)]
-    if columns == 2:
-        walk += [columns * z + 1 for z in reversed(range(lines))]
-    return walk
-
-
 def shards(pair_coef, panel_pool, degree_owner, batch_order):
     local_orders, shells = pair_coef.shape[:2]
     width = panel_pool.shape[2]
@@ -329,51 +342,50 @@
     total_orders = local_orders * devices
     chips = devices // 2
     me = lax.axis_index("shell")
-    walk = jnp.array(ring_of(chips, 2), jnp.int32)
-    place = jnp.argsort(walk)[me // 2]
-    degree_of = jnp.argsort(degree_owner)
-    steps = [ring_of(chips, 2)[i % chips] for i in range(chips + 1)]
-
-    def around(value, forward):
+    lines = chips // 2
+    walk = [2 * z for z in range(lines)] + [2 * z + 1 for z in reversed(range(lines))]
+
+    def around(value):
         pairs = []
-        for here, there in zip(steps[:-1], steps[1:]):
-            for core in range(2):
-                pair = (2 * here + core, 2 * there + core)
-                pairs.append(pair if forward else pair[::-1])
+        for here, there in zip(walk, walk[1:] + walk[:1]):
+            pairs += [(2 * here, 2 * there), (2 * there + 1, 2 * here + 1)]
         return lax.ppermute(value, "shell", pairs)
 
     def sibling(value):
         return lax.ppermute(value, "shell", [(s, s ^ 1) for s in range(devices)])
 
-    def degrees_at(*shifts):
-        slots = []
-        for shift in shifts:
-            chip = walk[(place + shift) % chips]
-            slots += [2 * chip + me % 2, 2 * chip + 1 - me % 2]
-        return degree_of[jnp.stack(slots)]
-
+    def across(value):
+        return lax.ppermute(value, "grp", [(0, 1), (1, 0)])
+
+    own = panel_pool[0]
+    half = own.shape[0] // 2
+    other = sibling(own)
+    whole = around(own)
+    part = around(lax.dynamic_slice_in_dim(other, half * lax.axis_index("grp"), half))
     rows = sort_rows(pair_coef, batch_order)
-    own = panel_pool[0]
-    acc = project(None, rows, degrees_at(0), [own, sibling(own)], [0, 0])
-    fwd = bwd = own
+    acc = project(None, rows, degree_owner, [own, other], [(0, 0, None), (0, 1, None)])
+    late, late_from = [], []
     for step in range(1, chips // 2):
-        fwd, bwd = around(fwd, True), around(bwd, False)
+        whole, acc = lax.optimization_barrier((whole, acc))
+        next_whole = around(whole)
+        next_part = around(part) if step + 1 < chips // 2 else None
+        rest = across(part)
         acc = project(
             acc,
             rows,
-            degrees_at(-step, step),
-            [fwd, sibling(fwd), bwd, sibling(bwd)],
-            [0] * 4,
+            degree_owner,
+            [whole, sibling(whole), part, sibling(part), *late],
+            [(-step, 0, None), (step, 1, None), (-step, 1, 0), (step, 0, 0), *late_from],
         )
-    half = own.shape[0] // 2
-    upper, lower = around(fwd[:half], True), around(bwd[half:], False)
-    far = degrees_at(chips // 2)
+        late, late_from = [rest, sibling(rest)], [(-step, 1, 1), (step, 0, 1)]
+        whole, part = next_whole, next_part
+    whole, acc = lax.optimization_barrier((whole, acc))
     proj = project(
         acc,
         rows,
-        jnp.concatenate([far, far]),
-        [upper, sibling(upper), lower, sibling(lower)],
-        [0, 0, half, half],
+        degree_owner,
+        [whole, sibling(whole), *late],
+        [(-(chips // 2), 0, None), (chips // 2, 1, None), *late_from],
     )
     blocks = width // LANES
     parcel = jax.ShapeDtypeStruct((devices, 32 * blocks + 16, LANES), jnp.int16)
@@ -395,7 +407,7 @@
 def solution(mesh):
     devices = mesh.shape["shell"]
     return jax.shard_map(
-        shards if devices == 16 else general,
+        shards if (devices, mesh.shape["grp"]) == (16, 2) else general,
         mesh=mesh,
         in_specs=(P(("grp", "shell"), None, None, None), P("shell", None, None), P(), P()),
         out_specs=P(None, ("grp", "shell"), None, None, None),

time: 134 us -> 96.4 us (0.72)
  between operations: 12 us -> 0.13 us
  local copies, waits for them, and re-layouts: 15.9 us -> 4.07 us
  other arithmetic: 9.86 us -> 0.06 us
  waiting for transfers between devices: 36.6 us -> 27.8 us
  starting transfers between devices: 14.3 us -> 21.2 us
  Pallas kernels: 23.1 us -> 20.8 us
    ppermute x8 -> x7, waiting for transfers between devices: 21.1 us -> 6.76 us  [around(): return lax.ppermute(value, 'shell', pairs)]
    select_n x8 -> x0, other arithmetic: 5.34 us -> none  [the longest x1 4.94 us: sort_rows(): in_at // degrees % shells]
    ppermute x0 -> x3, starting transfers between devices: none -> 4.47 us  [across(): return lax.ppermute(value, 'grp', [(0, 1), (1, 0)])]
    gather x5 -> x0, local copies, waits for them, and re-layouts: 4.13 us -> none  [degrees_at(): return degree_of[jnp.stack(slots)]]
    ppermute x0 -> x3, waiting for transfers between devices: none -> 3.98 us  [across(): return lax.ppermute(value, 'grp', [(0, 1), (1, 0)])]
    slice x3 -> x0, local copies, waits for them, and re-layouts: 3.05 us -> none  [the longest x1 1.62 us: sort_rows(): wanted = jnp.where(out_t == t, batch_order[t], wanted)]
    ppermute x8 -> x7, starting transfers between devices: 9.16 us -> 12.1 us  [around(): return lax.ppermute(value, 'shell', pairs)]
    dynamic_slice x2 -> x1, local copies, waits for them, and re-layouts: 2.89 us -> 0.03 us  [shards(): lax.dynamic_slice_in_dim(other, half * lax.axis_index('grp'), half)]
  transfers between devices with their start and end apart: 18 -> 22, of which waited for: 4 -> 10; matrix products, arithmetic and copies ran while one was open for 15% -> 0% of each run, Pallas kernels for 12% -> 15%
where the time goes in v2:
time: 96.4 us; the launch traced here: 96.1 us
  waiting for transfers between devices  27.8 us (29%)
  blocking collectives  22 us (23%)
  starting transfers between devices  21.2 us (22%)
  Pallas kernels  20.8 us (22%)
  local copies, waits for them, and re-layouts  4.07 us (4%)
    all_to_all x1, blocking collectives, shards(): sent = lax.all_to_all(sent, 'shell', 0, 0)  22 us
    all_to_all x1, waiting for transfers between devices, shards(): sent = lax.all_to_all(sent, 'shell', 0, 0)  15.4 us
    ppermute x7, starting transfers between devices, around(): return lax.ppermute(value, 'shell', pairs)  12.1 us
    pallas_call x5, Pallas kernels, project(): pl.pallas_call(functools.partial(project_kernel, lax.axis_size('shell'),...  10.5 us
    ppermute x7, waiting for transfers between devices, around(): return lax.ppermute(value, 'shell', pairs)  6.76 us
    pallas_call x1, Pallas kernels, sort_rows(): pl.pallas_call(functools.partial(sort_kernel, shells), grid=(orders // gr...  6.19 us
    ppermute x3, starting transfers between devices, across(): return lax.ppermute(value, 'grp', [(0, 1), (1, 0)])  4.47 us
    pallas_call x3, Pallas kernels, local_call(): pl.pallas_call(kernel, in_specs=[pl.BlockSpec(memory_space=pltpu.SMEM)] *...  4.13 us
  transfers between devices with their start and end apart: 22, of which 10 were waited for; matrix products, arithmetic and copies ran while one was open for 0% of the time, Pallas kernels for 15%

profile of v2, /device:TPU:0, one launch (start us, length us, event | category | flops | bytes accessed | tf_op | source)
XLA Modules:
  0.0 96.1 jit_solution(18249240620154691354)
XLA Ops:
  0.5 2.6 %collective-permute-start = (bf16[512,512]{1,0:T(8,128)(2,1)}, bf16[512,512]{1,0:T(8,128)(2,1)S(1)}, u32[]{:S(2)}, u32[]{:S(2)}) collective-permute-start(bf16[512,512]{1,0:T(8,128)(2,1)} %bitcast.9), channel_id=1, source_target_pairs={{0,4},{5,1},{4,8},{9,5},{8,12},{13,9},{12,14},{15,13},{14,10},{11,... | collective-permute-start | bytes 1572872 | tf_op jit(solution)/shard_map/ppermute | solution.py:352
  3.0 3.4 %copy-done = bf16[32,8,16,1024]{3,2,1,0:T(8,128)(2,1)S(1)} copy-done((bf16[32,8,16,1024]{3,2,1,0:T(8,128)(2,1)S(1)}, bf16[32,8,16,1024]{3,2,1,0:T(8,128)(2,1)}, u32[]{:S(2)}) %copy-start) | copy-done | bytes 8388632
  6.4 0.7 copy-done.3
  7.1 6.2 %shard_map.46.rows_ref = bf16[16,256,1024]{2,1,0:T(8,128)(2,1)S(1)} custom-call(s32[8]{0:T(128)S(1)} %copy-done.3, bf16[4096,1024]{1,0:T(8,128)(2,1)S(1)} %bitcast.7), custom_call_target="tpu_custom_call" | custom-call | flops 2147483648 | bytes 16777216 | tf_op jit(solution)/shard_map/pallas_call | solution.py:120
  13.3 1.6 %collective-permute-start.4 = (bf16[256,512]{1,0:T(8,128)(2,1)S(1)}, bf16[256,512]{1,0:T(8,128)(2,1)S(1)}, u32[]{:S(2)}, u32[]{:S(2)}) collective-permute-start(bf16[256,512]{1,0:T(8,128)(2,1)S(1)} %constant_dynamic-slice_fusion), channel_id=1, source_target_pairs={{0,4},{5,1},{4,8},{9,5},{8,12},{13,9},{12,14},{15,13},{14,10},{11,... | collective-permute-start | bytes 786440 | tf_op jit(solution)/shard_map/ppermute | solution.py:352
  15.0 1.5 %shard_map.47.refs_4_ = f32[2,256,512]{2,1,0:T(8,128)S(1)} custom-call(s32[16]{0:T(128)S(1)} %copy-done.2, bf16[16,256,1024]{2,1,0:T(8,128)(2,1)S(1)} %shard_map.46.rows_ref, bf16[512,512]{1,0:T(8,128)(2,1)S(1)} %bitcast.10, bf16[512,512]{1,0:T(8,128)(2,1)S(1)} %collective-permute-done.1.refs_1_), custom_call_target="tpu_custom_call" | custom-call | flops 536870912 | bytes 3145728 | tf_op jit(solution)/shard_map/pallas_call | solution.py:213
  16.6 1.6 %collective-permute-start.2 = (bf16[512,512]{1,0:T(8,128)(2,1)S(1)}, bf16[512,512]{1,0:T(8,128)(2,1)S(1)}, u32[]{:S(2)}, u32[]{:S(2)}) collective-permute-start(bf16[512,512]{1,0:T(8,128)(2,1)S(1)} %collective-permute-done.refs_0_), channel_id=1, source_target_pairs={{0,4},{5,1},{4,8},{9,5},{8,12},{13,9},{12,14},{15,13},{14,10},{11,... | collective-permute-start | bytes 1572872 | tf_op jit(solution)/shard_map/ppermute | solution.py:352
  18.2 1.6 %collective-permute-done.4.refs_2_ = bf16[256,512]{1,0:T(8,128)(2,1)S(1)} collective-permute-done((bf16[256,512]{1,0:T(8,128)(2,1)S(1)}, bf16[256,512]{1,0:T(8,128)(2,1)S(1)}, u32[]{:S(2)}, u32[]{:S(2)}) %collective-permute-start.4) | collective-permute-done | bytes 262176 | tf_op jit(solution)/shard_map/ppermute | solution.py:352
  19.7 1.6 %collective-permute-start.8 = (bf16[256,512]{1,0:T(8,128)(2,1)S(1)}, bf16[256,512]{1,0:T(8,128)(2,1)S(1)}, u32[]{:S(2)}, u32[]{:S(2)}) collective-permute-start(bf16[256,512]{1,0:T(8,128)(2,1)S(1)} %collective-permute-done.4.refs_2_), channel_id=1, source_target_pairs={{0,4},{5,1},{4,8},{9,5},{8,12},{13,9},{12,14},{15,13},{14,10},{11,... | collective-permute-start | bytes 786440 | tf_op jit(solution)/shard_map/ppermute | solution.py:352
  21.3 1.5 %collective-permute-start.10 = (bf16[256,512]{1,0:T(8,128)(2,1)S(1)}, bf16[256,512]{1,0:T(8,128)(2,1)S(1)}, u32[]{:S(2)}, u32[]{:S(2)}) collective-permute-start(bf16[256,512]{1,0:T(8,128)(2,1)S(1)} %collective-permute-done.4.refs_2_), channel_id=1, source_target_pairs={{0,16},{16,0},{1,17},{17,1},{2,18},{18,2},{3,19},{19,3},{4,20},{20... | collective-permute-start | bytes 786440 | tf_op jit(solution)/shard_map/ppermute | solution.py:358
  22.8 2.0 %shard_map.48.refs_6_ = f32[2,256,512]{2,1,0:T(8,128)S(1)} custom-call(s32[16]{0:T(128)S(1)} %copy-done.2, bf16[16,256,1024]{2,1,0:T(8,128)(2,1)S(1)} %shard_map.46.rows_ref, bf16[512,512]{1,0:T(8,128)(2,1)S(1)} %collective-permute-done.refs_0_, bf16[512,512]{1,0:T(8,128)(2,1)S(1)} %collective-permute-done.3.refs_1_, ...), custom_call_target="tpu_custom_call" | custom-call | flops 805306368 | bytes 5242880 | tf_op jit(solution)/shard_map/pallas_call | solution.py:213
  24.8 1.0 collective-permute-done.2.refs_0_
  25.8 1.6 %collective-permute-start.6 = (bf16[512,512]{1,0:T(8,128)(2,1)S(1)}, bf16[512,512]{1,0:T(8,128)(2,1)S(1)}, u32[]{:S(2)}, u32[]{:S(2)}) collective-permute-start(bf16[512,512]{1,0:T(8,128)(2,1)S(1)} %collective-permute-done.2.refs_0_), channel_id=1, source_target_pairs={{0,4},{5,1},{4,8},{9,5},{8,12},{13,9},{12,14},{15,13},{14,10},{11,... | collective-permute-start | bytes 1572872 | tf_op jit(solution)/shard_map/ppermute | solution.py:352
  27.4 1.2 %collective-permute-done.8.refs_2_ = bf16[256,512]{1,0:T(8,128)(2,1)S(1)} collective-permute-done((bf16[256,512]{1,0:T(8,128)(2,1)S(1)}, bf16[256,512]{1,0:T(8,128)(2,1)S(1)}, u32[]{:S(2)}, u32[]{:S(2)}) %collective-permute-start.8) | collective-permute-done | bytes 262176 | tf_op jit(solution)/shard_map/ppermute | solution.py:352
  28.6 0.5 collective-permute-start.11
  29.1 1.6 %collective-permute-start.14 = (bf16[256,512]{1,0:T(8,128)(2,1)S(1)}, bf16[256,512]{1,0:T(8,128)(2,1)S(1)}, u32[]{:S(2)}, u32[]{:S(2)}) collective-permute-start(bf16[256,512]{1,0:T(8,128)(2,1)S(1)} %collective-permute-done.8.refs_2_), channel_id=1, source_target_pairs={{0,4},{5,1},{4,8},{9,5},{8,12},{13,9},{12,14},{15,13},{14,10},{11,... | collective-permute-start | bytes 786440 | tf_op jit(solution)/shard_map/ppermute | solution.py:352
  30.7 1.5 %collective-permute-start.16 = (bf16[256,512]{1,0:T(8,128)(2,1)S(1)}, bf16[256,512]{1,0:T(8,128)(2,1)S(1)}, u32[]{:S(2)}, u32[]{:S(2)}) collective-permute-start(bf16[256,512]{1,0:T(8,128)(2,1)S(1)} %collective-permute-done.8.refs_2_), channel_id=1, source_target_pairs={{0,16},{16,0},{1,17},{17,1},{2,18},{18,2},{3,19},{19,3},{4,20},{20... | collective-permute-start | bytes 786440 | tf_op jit(solution)/shard_map/ppermute | solution.py:358
  32.2 2.5 %shard_map.49.refs_6_ = f32[2,256,512]{2,1,0:T(8,128)S(1)} custom-call(s32[16]{0:T(128)S(1)} %copy-done.2, bf16[16,256,1024]{2,1,0:T(8,128)(2,1)S(1)} %shard_map.46.rows_ref, bf16[512,512]{1,0:T(8,128)(2,1)S(1)} %collective-permute-done.2.refs_0_, bf16[512,512]{1,0:T(8,128)(2,1)S(1)} %collective-permute-done.7.refs_1_, ...), custom_call_target="tpu_custom_call" | custom-call | flops 1073741824 | bytes 6291456 | tf_op jit(solution)/shard_map/pallas_call | solution.py:213
  35.0 1.6 %collective-permute-start.12 = (bf16[512,512]{1,0:T(8,128)(2,1)S(1)}, bf16[512,512]{1,0:T(8,128)(2,1)S(1)}, u32[]{:S(2)}, u32[]{:S(2)}) collective-permute-start(bf16[512,512]{1,0:T(8,128)(2,1)S(1)} %collective-permute-done.6.refs_0_), channel_id=1, source_target_pairs={{0,4},{5,1},{4,8},{9,5},{8,12},{13,9},{12,14},{15,13},{14,10},{11,... | collective-permute-start | bytes 1572872 | tf_op jit(solution)/shard_map/ppermute | solution.py:352
  36.6 1.2 %collective-permute-done.14.refs_2_ = bf16[256,512]{1,0:T(8,128)(2,1)S(1)} collective-permute-done((bf16[256,512]{1,0:T(8,128)(2,1)S(1)}, bf16[256,512]{1,0:T(8,128)(2,1)S(1)}, u32[]{:S(2)}, u32[]{:S(2)}) %collective-permute-start.14) | collective-permute-done | bytes 262176 | tf_op jit(solution)/shard_map/ppermute | solution.py:352
  37.8 0.8 collective-permute-done.16.refs_4_
  38.6 1.5 %collective-permute-start.19 = (bf16[256,512]{1,0:T(8,128)(2,1)S(1)}, bf16[256,512]{1,0:T(8,128)(2,1)S(1)}, u32[]{:S(2)}, u32[]{:S(2)}) collective-permute-start(bf16[256,512]{1,0:T(8,128)(2,1)S(1)} %collective-permute-done.14.refs_2_), channel_id=1, source_target_pairs={{0,16},{16,0},{1,17},{17,1},{2,18},{18,2},{3,19},{19,3},{4,20},{20... | collective-permute-start | bytes 786440 | tf_op jit(solution)/shard_map/ppermute | solution.py:358
  40.1 2.5 %shard_map.50.refs_4_ = f32[2,256,512]{2,1,0:T(8,128)S(1)} custom-call(s32[16]{0:T(128)S(1)} %copy-done.2, bf16[16,256,1024]{2,1,0:T(8,128)(2,1)S(1)} %shard_map.46.rows_ref, bf16[512,512]{1,0:T(8,128)(2,1)S(1)} %collective-permute-done.6.refs_0_, bf16[512,512]{1,0:T(8,128)(2,1)S(1)} %collective-permute-done.13.refs_1_, ...), custom_call_target="tpu_custom_call" | custom-call | flops 1073741824 | bytes 6291456 | tf_op jit(solution)/shard_map/pallas_call | solution.py:213
  42.7 1.5 %collective-permute-done.12.refs_0_ = bf16[512,512]{1,0:T(8,128)(2,1)S(1)} collective-permute-done((bf16[512,512]{1,0:T(8,128)(2,1)S(1)}, bf16[512,512]{1,0:T(8,128)(2,1)S(1)}, u32[]{:S(2)}, u32[]{:S(2)}) %collective-permute-start.12) | collective-permute-done | bytes 524320 | tf_op jit(solution)/shard_map/ppermute | solution.py:352
  44.2 3.2 %collective-permute-done.19.refs_2_ = bf16[256,512]{1,0:T(8,128)(2,1)S(1)} collective-permute-done((bf16[256,512]{1,0:T(8,128)(2,1)S(1)}, bf16[256,512]{1,0:T(8,128)(2,1)S(1)}, u32[]{:S(2)}, u32[]{:S(2)}) %collective-permute-start.19) | collective-permute-done | bytes 262176 | tf_op jit(solution)/shard_map/ppermute | solution.py:358
  47.3 1.5 %collective-permute-done.20.refs_3_ = bf16[256,512]{1,0:T(8,128)(2,1)S(1)} collective-permute-done((bf16[256,512]{1,0:T(8,128)(2,1)S(1)}, bf16[256,512]{1,0:T(8,128)(2,1)S(1)}, u32[]{:S(2)}, u32[]{:S(2)}) %collective-permute-start.20) | collective-permute-done | bytes 262176 | tf_op jit(solution)/shard_map/ppermute | solution.py:355
  48.9 2.0 %shard_map.51.proj_ref = f32[2,256,512]{2,1,0:T(8,128)S(1)} custom-call(s32[16]{0:T(128)S(1)} %copy-done.2, bf16[16,256,1024]{2,1,0:T(8,128)(2,1)S(1)} %shard_map.46.rows_ref, bf16[512,512]{1,0:T(8,128)(2,1)S(1)} %collective-permute-done.12.refs_0_, bf16[512,512]{1,0:T(8,128)(2,1)S(1)} %collective-permute-done.18.refs_1_, ...), custom_call_target="tpu_custom_call" | custom-call | flops 805306368 | bytes 5242880 | tf_op jit(solution)/shard_map/pallas_call | solution.py:213
  51.2 22.0 %all_to_all.10.in_ref = s16[16,144,128]{2,1,0:T(8,128)(2,1)S(1)} all-to-all(s16[16,144,128]{2,1,0:T(8,128)(2,1)S(1)} %shard_map.52), channel_id=1, replica_groups=mesh['grp'=2,'shell'=16] {'shell'}, dimensions={0} | all-to-all | bytes 1179648 | tf_op jit(solution)/shard_map/all_to_all | solution.py:394
  73.3 1.5 %shard_map.53 = s16[16,144,128]{2,1,0:T(8,128)(2,1)} custom-call(s16[16,144,128]{2,1,0:T(8,128)(2,1)S(1)} %all_to_all.10.in_ref), custom_call_target="tpu_custom_call" | custom-call | tf_op jit(solution)/shard_map/pallas_call | solution.py:327
  74.8 3.6 %all-to-all-start.1 = ((s16[16,144,128]{2,1,0:T(8,128)(2,1)}), s16[16,144,128]{2,1,0:T(8,128)(2,1)S(1)}, u32[]{:S(2)}, u32[]{:S(2)}) async-start(s16[16,144,128]{2,1,0:T(8,128)(2,1)} %shard_map.53), calls=%async_computation.1 | async-start | bytes 1179648 | tf_op jit(solution)/shard_map/all_to_all | solution.py:396
  78.5 15.4 %all-to-all-done.1.in_ref = s16[16,144,128]{2,1,0:T(8,128)(2,1)S(1)} async-done(((s16[16,144,128]{2,1,0:T(8,128)(2,1)}), s16[16,144,128]{2,1,0:T(8,128)(2,1)S(1)}, u32[]{:S(2)}, u32[]{:S(2)}) %all-to-all-start.1) | async-done | bytes 589856 | tf_op jit(solution)/shard_map/all_to_all | solution.py:396
  93.9 2.2 %shard_map.54 = f32[2048,128]{1,0:T(8,128)} custom-call(f32[2,32]{1,0:T(2,128)S(1)} %maximum_multiply_fusion.twist_ref, s16[16,144,128]{2,1,0:T(8,128)(2,1)S(1)} %all-to-all-done.1.in_ref), custom_call_target="tpu_custom_call" | custom-call | tf_op jit(solution)/shard_map/pallas_call | solution.py:327
  (33 shorter events, 1.4 us)
Async XLA Ops:
  0.0 13.3 %collective-permute-start.1 = (bf16[512,512]{1,0:T(8,128)(2,1)}, bf16[512,512]{1,0:T(8,128)(2,1)S(1)}, u32[]{:S(2)}, u32[]{:S(2)}) collective-permute-start(bf16[512,512]{1,0:T(8,128)(2,1)} %bitcast.8), channel_id=1, source_target_pairs={{0,1},{1,0},{2,3},{3,2},{4,5},{5,4},{6,7},{7,6},{8,9},{9,8},{10,11... | collective-permute-start | bytes 1572872 | tf_op jit(solution)/shard_map/ppermute | solution.py:355
  0.5 16.0 %collective-permute-start = (bf16[512,512]{1,0:T(8,128)(2,1)}, bf16[512,512]{1,0:T(8,128)(2,1)S(1)}, u32[]{:S(2)}, u32[]{:S(2)}) collective-permute-start(bf16[512,512]{1,0:T(8,128)(2,1)} %bitcast.9), channel_id=1, source_target_pairs={{0,4},{5,1},{4,8},{9,5},{8,12},{13,9},{12,14},{15,13},{14,10},{11,... | collective-permute-start | bytes 1572872 | tf_op jit(solution)/shard_map/ppermute | solution.py:352
  3.0 3.4 %copy-start = (bf16[32,8,16,1024]{3,2,1,0:T(8,128)(2,1)S(1)}, bf16[32,8,16,1024]{3,2,1,0:T(8,128)(2,1)}, u32[]{:S(2)}) copy-start(bf16[32,8,16,1024]{3,2,1,0:T(8,128)(2,1)} %param.4) | copy-start | bytes 25165828
  6.4 0.7 copy-start.3
  7.1 7.9 %copy-start.1 = (bf16[1,512,512]{2,1,0:T(8,128)(2,1)S(1)}, bf16[1,512,512]{2,1,0:T(8,128)(2,1)}, u32[]{:S(2)}) copy-start(bf16[1,512,512]{2,1,0:T(8,128)(2,1)} %param.5) | copy-start | bytes 1572868
  7.1 7.9 %copy-start.2 = (s32[16]{0:T(128)S(1)}, s32[16]{0:T(128)}, u32[]{:S(2)}) copy-start(s32[16]{0:T(128)} %owner_ref.9) | copy-start | bytes 196
  13.3 6.4 %collective-permute-start.4 = (bf16[256,512]{1,0:T(8,128)(2,1)S(1)}, bf16[256,512]{1,0:T(8,128)(2,1)S(1)}, u32[]{:S(2)}, u32[]{:S(2)}) collective-permute-start(bf16[256,512]{1,0:T(8,128)(2,1)S(1)} %constant_dynamic-slice_fusion), channel_id=1, source_target_pairs={{0,4},{5,1},{4,8},{9,5},{8,12},{13,9},{12,14},{15,13},{14,10},{11,... | collective-permute-start | bytes 786440 | tf_op jit(solution)/shard_map/ppermute | solution.py:352
  16.5 6.3 %collective-permute-start.3 = (bf16[512,512]{1,0:T(8,128)(2,1)S(1)}, bf16[512,512]{1,0:T(8,128)(2,1)S(1)}, u32[]{:S(2)}, u32[]{:S(2)}) collective-permute-start(bf16[512,512]{1,0:T(8,128)(2,1)S(1)} %collective-permute-done.refs_0_), channel_id=1, source_target_pairs={{0,1},{1,0},{2,3},{3,2},{4,5},{5,4},{6,7},{7,6},{8,9},{9,8},{10,11... | collective-permute-start | bytes 1572872 | tf_op jit(solution)/shard_map/ppermute | solution.py:355
  16.6 9.2 %collective-permute-start.2 = (bf16[512,512]{1,0:T(8,128)(2,1)S(1)}, bf16[512,512]{1,0:T(8,128)(2,1)S(1)}, u32[]{:S(2)}, u32[]{:S(2)}) collective-permute-start(bf16[512,512]{1,0:T(8,128)(2,1)S(1)} %collective-permute-done.refs_0_), channel_id=1, source_target_pairs={{0,4},{5,1},{4,8},{9,5},{8,12},{13,9},{12,14},{15,13},{14,10},{11,... | collective-permute-start | bytes 1572872 | tf_op jit(solution)/shard_map/ppermute | solution.py:352
  19.7 3.1 %collective-permute-start.5 = (bf16[256,512]{1,0:T(8,128)(2,1)S(1)}, bf16[256,512]{1,0:T(8,128)(2,1)S(1)}, u32[]{:S(2)}, u32[]{:S(2)}) collective-permute-start(bf16[256,512]{1,0:T(8,128)(2,1)S(1)} %collective-permute-done.4.refs_2_), channel_id=1, source_target_pairs={{0,1},{1,0},{2,3},{3,2},{4,5},{5,4},{6,7},{7,6},{8,9},{9,8},{10,11... | collective-permute-start | bytes 786440 | tf_op jit(solution)/shard_map/ppermute | solution.py:355
  19.7 8.8 %collective-permute-start.8 = (bf16[256,512]{1,0:T(8,128)(2,1)S(1)}, bf16[256,512]{1,0:T(8,128)(2,1)S(1)}, u32[]{:S(2)}, u32[]{:S(2)}) collective-permute-start(bf16[256,512]{1,0:T(8,128)(2,1)S(1)} %collective-permute-done.4.refs_2_), channel_id=1, source_target_pairs={{0,4},{5,1},{4,8},{9,5},{8,12},{13,9},{12,14},{15,13},{14,10},{11,... | collective-permute-start | bytes 786440 | tf_op jit(solution)/shard_map/ppermute | solution.py:352
  21.3 7.3 %collective-permute-start.10 = (bf16[256,512]{1,0:T(8,128)(2,1)S(1)}, bf16[256,512]{1,0:T(8,128)(2,1)S(1)}, u32[]{:S(2)}, u32[]{:S(2)}) collective-permute-start(bf16[256,512]{1,0:T(8,128)(2,1)S(1)} %collective-permute-done.4.refs_2_), channel_id=1, source_target_pairs={{0,16},{16,0},{1,17},{17,1},{2,18},{18,2},{3,19},{19,3},{4,20},{20... | collective-permute-start | bytes 786440 | tf_op jit(solution)/shard_map/ppermute | solution.py:358
  25.8 6.4 %collective-permute-start.7 = (bf16[512,512]{1,0:T(8,128)(2,1)S(1)}, bf16[512,512]{1,0:T(8,128)(2,1)S(1)}, u32[]{:S(2)}, u32[]{:S(2)}) collective-permute-start(bf16[512,512]{1,0:T(8,128)(2,1)S(1)} %collective-permute-done.2.refs_0_), channel_id=1, source_target_pairs={{0,1},{1,0},{2,3},{3,2},{4,5},{5,4},{6,7},{7,6},{8,9},{9,8},{10,11... | collective-permute-start | bytes 1572872 | tf_op jit(solution)/shard_map/ppermute | solution.py:355
  25.8 9.2 %collective-permute-start.6 = (bf16[512,512]{1,0:T(8,128)(2,1)S(1)}, bf16[512,512]{1,0:T(8,128)(2,1)S(1)}, u32[]{:S(2)}, u32[]{:S(2)}) collective-permute-start(bf16[512,512]{1,0:T(8,128)(2,1)S(1)} %collective-permute-done.2.refs_0_), channel_id=1, source_target_pairs={{0,4},{5,1},{4,8},{9,5},{8,12},{13,9},{12,14},{15,13},{14,10},{11,... | collective-permute-start | bytes 1572872 | tf_op jit(solution)/shard_map/ppermute | solution.py:352
  28.6 2.1 %collective-permute-start.9 = (bf16[256,512]{1,0:T(8,128)(2,1)S(1)}, bf16[256,512]{1,0:T(8,128)(2,1)S(1)}, u32[]{:S(2)}, u32[]{:S(2)}) collective-permute-start(bf16[256,512]{1,0:T(8,128)(2,1)S(1)} %collective-permute-done.8.refs_2_), channel_id=1, source_target_pairs={{0,1},{1,0},{2,3},{3,2},{4,5},{5,4},{6,7},{7,6},{8,9},{9,8},{10,11... | collective-permute-start | bytes 786440 | tf_op jit(solution)/shard_map/ppermute | solution.py:355
  28.6 3.6 %collective-permute-start.11 = (bf16[256,512]{1,0:T(8,128)(2,1)S(1)}, bf16[256,512]{1,0:T(8,128)(2,1)S(1)}, u32[]{:S(2)}, u32[]{:S(2)}) collective-permute-start(bf16[256,512]{1,0:T(8,128)(2,1)S(1)} %collective-permute-done.10.refs_4_), channel_id=1, source_target_pairs={{0,1},{1,0},{2,3},{3,2},{4,5},{5,4},{6,7},{7,6},{8,9},{9,8},{10,11... | collective-permute-start | bytes 786440 | tf_op jit(solution)/shard_map/ppermute | solution.py:355
  29.1 8.7 %collective-permute-start.14 = (bf16[256,512]{1,0:T(8,128)(2,1)S(1)}, bf16[256,512]{1,0:T(8,128)(2,1)S(1)}, u32[]{:S(2)}, u32[]{:S(2)}) collective-permute-start(bf16[256,512]{1,0:T(8,128)(2,1)S(1)} %collective-permute-done.8.refs_2_), channel_id=1, source_target_pairs={{0,4},{5,1},{4,8},{9,5},{8,12},{13,9},{12,14},{15,13},{14,10},{11,... | collective-permute-start | bytes 786440 | tf_op jit(solution)/shard_map/ppermute | solution.py:352
  30.7 7.9 %collective-permute-start.16 = (bf16[256,512]{1,0:T(8,128)(2,1)S(1)}, bf16[256,512]{1,0:T(8,128)(2,1)S(1)}, u32[]{:S(2)}, u32[]{:S(2)}) collective-permute-start(bf16[256,512]{1,0:T(8,128)(2,1)S(1)} %collective-permute-done.8.refs_2_), channel_id=1, source_target_pairs={{0,16},{16,0},{1,17},{17,1},{2,18},{18,2},{3,19},{19,3},{4,20},{20... | collective-permute-start | bytes 786440 | tf_op jit(solution)/shard_map/ppermute | solution.py:358
  35.0 5.2 %collective-permute-start.13 = (bf16[512,512]{1,0:T(8,128)(2,1)S(1)}, bf16[512,512]{1,0:T(8,128)(2,1)S(1)}, u32[]{:S(2)}, u32[]{:S(2)}) collective-permute-start(bf16[512,512]{1,0:T(8,128)(2,1)S(1)} %collective-permute-done.6.refs_0_), channel_id=1, source_target_pairs={{0,1},{1,0},{2,3},{3,2},{4,5},{5,4},{6,7},{7,6},{8,9},{9,8},{10,11... | collective-permute-start | bytes 1572872 | tf_op jit(solution)/shard_map/ppermute | solution.py:355
  35.0 9.2 %collective-permute-start.12 = (bf16[512,512]{1,0:T(8,128)(2,1)S(1)}, bf16[512,512]{1,0:T(8,128)(2,1)S(1)}, u32[]{:S(2)}, u32[]{:S(2)}) collective-permute-start(bf16[512,512]{1,0:T(8,128)(2,1)S(1)} %collective-permute-done.6.refs_0_), channel_id=1, source_target_pairs={{0,4},{5,1},{4,8},{9,5},{8,12},{13,9},{12,14},{15,13},{14,10},{11,... | collective-permute-start | bytes 1572872 | tf_op jit(solution)/shard_map/ppermute | solution.py:352
  37.8 2.3 %collective-permute-start.15 = (bf16[256,512]{1,0:T(8,128)(2,1)S(1)}, bf16[256,512]{1,0:T(8,128)(2,1)S(1)}, u32[]{:S(2)}, u32[]{:S(2)}) collective-permute-start(bf16[256,512]{1,0:T(8,128)(2,1)S(1)} %collective-permute-done.14.refs_2_), channel_id=1, source_target_pairs={{0,1},{1,0},{2,3},{3,2},{4,5},{5,4},{6,7},{7,6},{8,9},{9,8},{10,11... | collective-permute-start | bytes 786440 | tf_op jit(solution)/shard_map/ppermute | solution.py:355
  38.6 1.5 %collective-permute-start.17 = (bf16[256,512]{1,0:T(8,128)(2,1)S(1)}, bf16[256,512]{1,0:T(8,128)(2,1)S(1)}, u32[]{:S(2)}, u32[]{:S(2)}) collective-permute-start(bf16[256,512]{1,0:T(8,128)(2,1)S(1)} %collective-permute-done.16.refs_4_), channel_id=1, source_target_pairs={{0,1},{1,0},{2,3},{3,2},{4,5},{5,4},{6,7},{7,6},{8,9},{9,8},{10,11... | collective-permute-start | bytes 786440 | tf_op jit(solution)/shard_map/ppermute | solution.py:355
  38.6 8.7 %collective-permute-start.19 = (bf16[256,512]{1,0:T(8,128)(2,1)S(1)}, bf16[256,512]{1,0:T(8,128)(2,1)S(1)}, u32[]{:S(2)}, u32[]{:S(2)}) collective-permute-start(bf16[256,512]{1,0:T(8,128)(2,1)S(1)} %collective-permute-done.14.refs_2_), channel_id=1, source_target_pairs={{0,16},{16,0},{1,17},{17,1},{2,18},{18,2},{3,19},{19,3},{4,20},{20... | collective-permute-start | bytes 786440 | tf_op jit(solution)/shard_map/ppermute | solution.py:358
  44.2 4.7 %collective-permute-start.18 = (bf16[512,512]{1,0:T(8,128)(2,1)S(1)}, bf16[512,512]{1,0:T(8,128)(2,1)S(1)}, u32[]{:S(2)}, u32[]{:S(2)}) collective-permute-start(bf16[512,512]{1,0:T(8,128)(2,1)S(1)} %collective-permute-done.12.refs_0_), channel_id=1, source_target_pairs={{0,1},{1,0},{2,3},{3,2},{4,5},{5,4},{6,7},{7,6},{8,9},{9,8},{10,11... | collective-permute-start | bytes 1572872 | tf_op jit(solution)/shard_map/ppermute | solution.py:355
  47.3 1.5 %collective-permute-start.20 = (bf16[256,512]{1,0:T(8,128)(2,1)S(1)}, bf16[256,512]{1,0:T(8,128)(2,1)S(1)}, u32[]{:S(2)}, u32[]{:S(2)}) collective-permute-start(bf16[256,512]{1,0:T(8,128)(2,1)S(1)} %collective-permute-done.19.refs_2_), channel_id=1, source_target_pairs={{0,1},{1,0},{2,3},{3,2},{4,5},{5,4},{6,7},{7,6},{8,9},{9,8},{10,11... | collective-permute-start | bytes 786440 | tf_op jit(solution)/shard_map/ppermute | solution.py:355
  74.8 19.1 %all-to-all-start.1 = ((s16[16,144,128]{2,1,0:T(8,128)(2,1)}), s16[16,144,128]{2,1,0:T(8,128)(2,1)S(1)}, u32[]{:S(2)}, u32[]{:S(2)}) async-start(s16[16,144,128]{2,1,0:T(8,128)(2,1)} %shard_map.53), calls=%async_computation.1 | async-start | bytes 1179648 | tf_op jit(solution)/shard_map/all_to_all | solution.py:396

commit v3 on v2

--- a/solution.py
+++ b/solution.py
@@ -86,6 +86,7 @@
 STEPS = 16.0
 TOP = 32000.0
 LANES = 128
+SORT_LIMIT = 42
 
 
 def bit_reverse(value, nbits):
@@ -95,42 +96,55 @@
     return flipped
 
 
-def sort_kernel(shells, order_ref, coef_ref, out_ref, perm_ref):
-    @pl.when(pl.program_id(0) == 0)
-    def _():
-        degrees, group = out_ref.shape[0], out_ref.shape[1] // shells
-        shape = perm_ref.shape
-        out_at = lax.broadcasted_iota(jnp.int32, shape, 0)
-        in_at = lax.broadcasted_iota(jnp.int32, shape, 1)
-        out_t = out_at % shells
-        wanted = jnp.zeros(shape, jnp.int32)
-        for t in range(shells):
-            wanted = jnp.where(out_t == t, order_ref[t], wanted)
-        source = (out_at // shells % group * shells + wanted) * degrees + out_at // (group * shells)
-        perm_ref[...] = jnp.where(in_at == source, 1.0, 0.0).astype(perm_ref.dtype)
-
-    moved = jnp.dot(perm_ref[...], coef_ref[...], preferred_element_type=jnp.float32)
-    out_ref[...] = moved.astype(out_ref.dtype).reshape(out_ref.shape)
+def sort_kernel(order_ref, coef_ref, out_ref, perm_ref, held_ref, sems):
+    blocks, rows, _ = held_ref.shape
+    degrees = out_ref.shape[0]
+    shells = order_ref.shape[0]
+    slab = rows // degrees
+
+    def copy(i):
+        block = coef_ref.at[pl.ds(i * rows, rows), :]
+        return pltpu.make_async_copy(block, held_ref.at[i], sems.at[i])
+
+    for i in range(blocks):
+        copy(i).start()
+    line = lax.broadcasted_iota(jnp.int32, (slab, rows), 0)
+    in_at = lax.broadcasted_iota(jnp.int32, (slab, rows), 1)
+    wanted = jnp.zeros(line.shape, jnp.int32)
+    for at in range(slab):
+        source = (at // shells * shells + order_ref[at % shells]) * degrees
+        wanted = jnp.where(line == at, source, wanted)
+    for l in range(degrees):
+        chosen = jnp.where(in_at == wanted + l, 1.0, 0.0).astype(perm_ref.dtype)
+        perm_ref[pl.ds(l * slab, slab), :] = chosen
+
+    for i in range(blocks):
+        copy(i).wait()
+        moved = jnp.dot(perm_ref[...], held_ref[i], preferred_element_type=jnp.float32)
+        out_ref[:, pl.ds(i * slab, slab), :] = moved.astype(out_ref.dtype).reshape(
+            degrees, slab, moved.shape[1]
+        )
 
 
 def sort_rows(pair_coef, batch_order):
     orders, shells, degrees, width = pair_coef.shape
     group = 16 // shells
     rows = group * shells * degrees
+    blocks = orders // group
     return pl.pallas_call(
-        functools.partial(sort_kernel, shells),
-        grid=(orders // group,),
-        in_specs=[
-            pl.BlockSpec(memory_space=pltpu.SMEM),
-            pl.BlockSpec((rows, width), lambda i: (i, 0)),
+        sort_kernel,
+        in_specs=[pl.BlockSpec(memory_space=pltpu.SMEM), pl.BlockSpec(memory_space=pltpu.HBM)],
+        out_specs=pl.BlockSpec(memory_space=pltpu.VMEM),
+        out_shape=jax.ShapeDtypeStruct((degrees, orders * shells, width), pair_coef.dtype),
+        scratch_shapes=[
+            pltpu.VMEM((rows, rows), pair_coef.dtype),
+            pltpu.VMEM((blocks, rows, width), pair_coef.dtype),
+            pltpu.SemaphoreType.DMA((blocks,)),
         ],
-        out_specs=pl.BlockSpec((degrees, group * shells, width), lambda i: (0, i, 0)),
-        out_shape=jax.ShapeDtypeStruct((degrees, orders * shells, width), pair_coef.dtype),
-        scratch_shapes=[pltpu.VMEM((rows, rows), pair_coef.dtype)],
-        compiler_params=pltpu.CompilerParams(vmem_limit_bytes=24 * 2**20),
+        compiler_params=pltpu.CompilerParams(vmem_limit_bytes=SORT_LIMIT * 2**20),
         cost_estimate=pl.CostEstimate(
-            flops=2 * orders * shells * degrees * rows * width,
-            bytes_accessed=4 * orders * shells * degrees * width,
+            flops=2 * blocks * rows * rows * width,
+            bytes_accessed=4 * blocks * rows * width,
             transcendentals=0,
         ),
     )(batch_order, pair_coef.reshape(orders * shells * degrees, width))
@@ -167,61 +181,51 @@
     return jnp.where(chip % 2 == 0, chip // 2, chips - 1 - chip // 2)
 
 
-def project_kernel(devices, sources, n_acc, owner_ref, rows_ref, *refs):
+def project_kernel(devices, sources, n_acc, packed, owner_ref, rows_ref, *refs):
     n = len(sources)
     panels = refs[:n]
     acc_in = refs[n : n + n_acc]
-    acc_out, lhs, rhs, sems = refs[n + n_acc :]
-    width = rhs.shape[1]
+    acc_out = refs[-1]
     chips = devices // 2
     me = lax.axis_index("shell")
-    copies = []
-    at = 0
     part = lax.axis_index("grp")
-    for i, (panel, (shift, flip, half)) in enumerate(zip(panels, sources)):
+    width = rows_ref.shape[2] // 2
+    started = n_acc
+    if n_acc:
+        acc_out[...] = acc_in[0][...]
+    for panel, (shift, flip, half) in zip(panels, sources):
         depth = panel.shape[0]
         ahead = jnp.where(me % 2 == 0, shift, -shift)
         place = lax.rem(place_of(me // 2, chips) + ahead + chips, chips)
         slot = 2 * walk_at(place, chips) + (me + flip) % 2
-        offset = 0 if half is None else pl.multiple_of(depth * (part + half) % (2 * depth), 128)
         degree = jnp.zeros((), jnp.int32)
         for l in range(rows_ref.shape[0]):
             degree = jnp.where(owner_ref[l] == slot, l, degree)
-        copies.append(pltpu.make_async_copy(panel, rhs.at[pl.ds(at, depth), :], sems.at[3 * i]))
-        for c in range(2):
-            copies.append(
-                pltpu.make_async_copy(
-                    rows_ref.at[degree, :, pl.ds(pl.multiple_of(c * width + offset, 128), depth)],
-                    lhs.at[c, :, pl.ds(at, depth)],
-                    sems.at[3 * i + 1 + c],
-                )
-            )
-        at += depth
-    for copy in copies:
-        copy.start()
-    for copy in copies:
-        copy.wait()
-    for c in range(2):
-        part = jnp.dot(lhs[c], rhs[...], preferred_element_type=jnp.float32)
-        acc_out[c] = part + acc_in[0][c] if n_acc else part
-
-
-def project(acc, rows, owner, panels, sources):
+        offset = 0 if half is None else depth * (part + half) % (2 * depth)
+        left = jnp.concatenate(
+            [rows_ref[degree, :, pl.ds(pl.multiple_of(c * width + offset, 128), depth)] for c in range(2)]
+        )
+        product = jnp.dot(left, panel[...], preferred_element_type=jnp.float32)
+        acc_out[...] = acc_out[...] + product if started else product
+        started = 1
+    if packed:
+        pack(acc_out, refs[-2])
+
+
+def project(acc, rows, owner, panels, sources, packed=None):
     count, width = rows.shape[1], panels[0].shape[1]
     depth = sum(p.shape[0] for p in panels)
     n_acc = 0 if acc is None else 1
+    total = jax.ShapeDtypeStruct((2 * count, width), jnp.float32)
     return pl.pallas_call(
-        functools.partial(project_kernel, lax.axis_size("shell"), tuple(sources), n_acc),
+        functools.partial(
+            project_kernel, lax.axis_size("shell"), tuple(sources), n_acc, packed is not None
+        ),
         in_specs=[pl.BlockSpec(memory_space=pltpu.SMEM)]
-        + [pl.BlockSpec(memory_space=pl.ANY)] * (1 + len(panels))
-        + [pl.BlockSpec(memory_space=pltpu.VMEM)] * n_acc,
+        + [pl.BlockSpec(memory_space=pltpu.VMEM)] * (1 + len(panels) + n_acc),
         out_specs=pl.BlockSpec(memory_space=pltpu.VMEM),
-        out_shape=jax.ShapeDtypeStruct((2, count, width), jnp.float32),
-        scratch_shapes=[
-            pltpu.VMEM((2, count, depth), rows.dtype),
-            pltpu.VMEM((depth, width), rows.dtype),
-            pltpu.SemaphoreType.DMA((3 * len(panels),)),
-        ],
+        out_shape=total if packed is None else packed,
+        scratch_shapes=[] if packed is None else [pltpu.VMEM(total.shape, total.dtype)],
         compiler_params=pltpu.CompilerParams(vmem_limit_bytes=24 * 2**20),
         cost_estimate=pl.CostEstimate(
             flops=4 * count * depth * width,
@@ -231,8 +235,8 @@
     )(owner, rows, *panels, *([acc] if n_acc else []))
 
 
-def pack_kernel(proj_ref, out_ref):
-    width = proj_ref.shape[2]
+def pack(proj_ref, out_ref):
+    count, width = proj_ref.shape[0] // 2, proj_ref.shape[1]
     blocks = width // LANES
     line = lax.broadcasted_iota(jnp.int32, (16, LANES), 0)
     for d in range(out_ref.shape[0]):
@@ -240,7 +244,7 @@
         for jb in range(blocks):
             lanes = pl.ds(jb * LANES, LANES)
             real_part, imag_part, code = encode(
-                proj_ref[0, pl.ds(16 * d, 16), lanes], proj_ref[1, pl.ds(16 * d, 16), lanes]
+                proj_ref[pl.ds(16 * d, 16), lanes], proj_ref[pl.ds(count + 16 * d, 16), lanes]
             )
             out_ref[d, pl.ds(32 * jb, 16), :] = real_part
             out_ref[d, pl.ds(32 * jb + 16, 16), :] = imag_part
@@ -345,11 +349,15 @@
     lines = chips // 2
     walk = [2 * z for z in range(lines)] + [2 * z + 1 for z in reversed(range(lines))]
 
+    onward = []
+    for here, there in zip(walk, walk[1:] + walk[:1]):
+        onward += [(2 * here, 2 * there), (2 * there + 1, 2 * here + 1)]
+
     def around(value):
-        pairs = []
-        for here, there in zip(walk, walk[1:] + walk[:1]):
-            pairs += [(2 * here, 2 * there), (2 * there + 1, 2 * here + 1)]
-        return lax.ppermute(value, "shell", pairs)
+        return lax.ppermute(value, "shell", onward)
+
+    def crosswise(value):
+        return lax.ppermute(value, "shell", [(source ^ 1, target) for source, target in onward])
 
     def sibling(value):
         return lax.ppermute(value, "shell", [(s, s ^ 1) for s in range(devices)])
@@ -357,16 +365,21 @@
     def across(value):
         return lax.ppermute(value, "grp", [(0, 1), (1, 0)])
 
+    blocks = width // LANES
+    parcel = jax.ShapeDtypeStruct((devices, 32 * blocks + 16, LANES), jnp.int16)
+    lines = pltpu.VMEM((devices, 16, LANES), jnp.float32)
     own = panel_pool[0]
     half = own.shape[0] // 2
+    whole = around(own)
+    part = crosswise(lax.dynamic_slice_in_dim(own, half * lax.axis_index("grp"), half))
     other = sibling(own)
-    whole = around(own)
-    part = around(lax.dynamic_slice_in_dim(other, half * lax.axis_index("grp"), half))
     rows = sort_rows(pair_coef, batch_order)
     acc = project(None, rows, degree_owner, [own, other], [(0, 0, None), (0, 1, None)])
+    whole, part, rows = lax.optimization_barrier((whole, part, rows))
     late, late_from = [], []
     for step in range(1, chips // 2):
-        whole, acc = lax.optimization_barrier((whole, acc))
+        if step > 1:
+            whole, acc = lax.optimization_barrier((whole, acc))
         next_whole = around(whole)
         next_part = around(part) if step + 1 < chips // 2 else None
         rest = across(part)
@@ -380,17 +393,14 @@
         late, late_from = [rest, sibling(rest)], [(-step, 1, 1), (step, 0, 1)]
         whole, part = next_whole, next_part
     whole, acc = lax.optimization_barrier((whole, acc))
-    proj = project(
+    sent = project(
         acc,
         rows,
         degree_owner,
         [whole, sibling(whole), *late],
         [(-(chips // 2), 0, None), (chips // 2, 1, None), *late_from],
+        packed=parcel,
     )
-    blocks = width // LANES
-    parcel = jax.ShapeDtypeStruct((devices, 32 * blocks + 16, LANES), jnp.int16)
-    lines = pltpu.VMEM((devices, 16, LANES), jnp.float32)
-    sent = local_call(pack_kernel, parcel, [], proj)
     sent = lax.all_to_all(sent, "shell", 0, 0)
     sent = local_call(outer_kernel, parcel, [lines, lines], sent)
     sent = lax.all_to_all(sent, "shell", 0, 0)

time: 96.4 us -> 93.8 us (0.973)
  local copies, waits for them, and re-layouts: 4.07 us -> 1.66 us
  Pallas kernels: 20.8 us -> 18.6 us
  starting transfers between devices: 21.2 us -> 23.1 us
    unnamed x8 -> x6, local copies, waits for them, and re-layouts: 4.04 us -> 0.66 us
    pallas_call x5, Pallas kernels: 10.5 us -> 8.26 us  [project(): pl.pallas_call(functools.partial(project_kernel, lax.axis_size('shell'),...]
    ppermute x7, waiting for transfers between devices: 6.76 us -> 5.23 us  [the longest x6 5.23 us: around(): return lax.ppermute(value, 'shell', onward)]
    ppermute x7, starting transfers between devices: 12.1 us -> 13.3 us  [the longest x6 12.6 us: around(): return lax.ppermute(value, 'shell', onward)]
    dynamic_slice x1, local copies, waits for them, and re-layouts: 0.03 us -> 1 us  [shards(): lax.dynamic_slice_in_dim(own, half * lax.axis_index('grp'), half)]
    pallas_call x3 -> x2, Pallas kernels: 4.13 us -> 3.74 us  [local_call(): pl.pallas_call(kernel, in_specs=[pl.BlockSpec(memory_space=pltpu.SMEM)] *...]
  transfers between devices with their start and end apart: 22 -> 22, of which waited for: 10 -> 10; matrix products, arithmetic and copies ran while one was open for 0% -> 1% of each run, Pallas kernels for 15% -> 14%
where the time goes in v3:
time: 93.8 us; the launch traced here: 93.5 us
  waiting for transfers between devices  27.1 us (29%)
  starting transfers between devices  23.1 us (25%)
  blocking collectives  22.9 us (24%)
  Pallas kernels  18.6 us (20%)
  local copies, waits for them, and re-layouts  1.66 us (2%)
    all_to_all x1, blocking collectives, shards(): sent = lax.all_to_all(sent, 'shell', 0, 0)  22.9 us
    all_to_all x1, waiting for transfers between devices, shards(): sent = lax.all_to_all(sent, 'shell', 0, 0)  15.4 us
    ppermute x6, starting transfers between devices, around(): return lax.ppermute(value, 'shell', onward)  12.6 us
    pallas_call x5, Pallas kernels, project(): pl.pallas_call(functools.partial(project_kernel, lax.axis_size('shell'),...  8.26 us
    pallas_call x1, Pallas kernels, sort_rows(): pl.pallas_call(sort_kernel, in_specs=[pl.BlockSpec(memory_space=pltpu.SME...  6.6 us
    ppermute x6, waiting for transfers between devices, around(): return lax.ppermute(value, 'shell', onward)  5.23 us
    ppermute x3, waiting for transfers between devices, across(): return lax.ppermute(value, 'grp', [(0, 1), (1, 0)])  4.82 us
    ppermute x3, starting transfers between devices, across(): return lax.ppermute(value, 'grp', [(0, 1), (1, 0)])  4.47 us
  transfers between devices with their start and end apart: 22, of which 10 were waited for; matrix products, arithmetic and copies ran while one was open for 1% of the time, Pallas kernels for 14%

profile of v3, /device:TPU:0, one launch (start us, length us, event | category | flops | bytes accessed | tf_op | source)
XLA Modules:
  0.0 93.5 jit_solution(15892687657351393125)
XLA Ops:
  0.0 3.0 %collective-permute-start = (bf16[512,512]{1,0:T(8,128)(2,1)}, bf16[512,512]{1,0:T(8,128)(2,1)S(1)}, u32[]{:S(2)}, u32[]{:S(2)}) collective-permute-start(bf16[512,512]{1,0:T(8,128)(2,1)} %bitcast.9), channel_id=1, source_target_pairs={{0,4},{5,1},{4,8},{9,5},{8,12},{13,9},{12,14},{15,13},{14,10},{11,... | collective-permute-start | bytes 1572872 | tf_op jit(solution)/shard_map/ppermute | solution.py:357
  3.0 1.0 %dynamic-slice_bitcast_fusion = bf16[256,512]{1,0:T(8,128)(2,1)S(1)} fusion(bf16[1,512,512]{2,1,0:T(8,128)(2,1)} %param.5, s32[]{:T(128)S(6)} %select_n.22), kind=kLoop, calls=%fused_computation | loop fusion | bytes 524292 | tf_op jit(solution)/shard_map/dynamic_slice | solution.py:374
  4.0 0.7 collective-permute-start.1
  4.8 1.0 %collective-permute-start.5 = (bf16[512,512]{1,0:T(8,128)(2,1)}, bf16[512,512]{1,0:T(8,128)(2,1)S(1)}, u32[]{:S(2)}, u32[]{:S(2)}) collective-permute-start(bf16[512,512]{1,0:T(8,128)(2,1)} %bitcast.10), channel_id=1, source_target_pairs={{0,1},{1,0},{2,3},{3,2},{4,5},{5,4},{6,7},{7,6},{8,9},{9,8},{10,11... | collective-permute-start | bytes 1572872 | tf_op jit(solution)/shard_map/ppermute | solution.py:363
  5.8 0.7 copy-done.2
  6.4 6.6 %shard_map.46.rows_ref = bf16[16,256,1024]{2,1,0:T(8,128)(2,1)S(1)} custom-call(s32[8]{0:T(128)S(1)} %copy-done.2, bf16[4096,1024]{1,0:T(8,128)(2,1)} %bitcast.12), custom_call_target="tpu_custom_call" | custom-call | flops 2147483648 | bytes 16777216 | tf_op jit(solution)/shard_map/pallas_call | solution.py:134
  13.2 2.1 %collective-permute-start.2 = (bf16[512,512]{1,0:T(8,128)(2,1)S(1)}, bf16[512,512]{1,0:T(8,128)(2,1)S(1)}, u32[]{:S(2)}, u32[]{:S(2)}) collective-permute-start(bf16[512,512]{1,0:T(8,128)(2,1)S(1)} %collective-permute-done.refs_0_), channel_id=1, source_target_pairs={{0,4},{5,1},{4,8},{9,5},{8,12},{13,9},{12,14},{15,13},{14,10},{11,... | collective-permute-start | bytes 1572872 | tf_op jit(solution)/shard_map/ppermute | solution.py:357
  15.4 1.4 %collective-permute-start.8 = (bf16[256,512]{1,0:T(8,128)(2,1)S(1)}, bf16[256,512]{1,0:T(8,128)(2,1)S(1)}, u32[]{:S(2)}, u32[]{:S(2)}) collective-permute-start(bf16[256,512]{1,0:T(8,128)(2,1)S(1)} %collective-permute-done.1.refs_2_), channel_id=1, source_target_pairs={{0,4},{5,1},{4,8},{9,5},{8,12},{13,9},{12,14},{15,13},{14,10},{11,... | collective-permute-start | bytes 786440 | tf_op jit(solution)/shard_map/ppermute | solution.py:357
  16.8 1.5 %collective-permute-start.10 = (bf16[256,512]{1,0:T(8,128)(2,1)S(1)}, bf16[256,512]{1,0:T(8,128)(2,1)S(1)}, u32[]{:S(2)}, u32[]{:S(2)}) collective-permute-start(bf16[256,512]{1,0:T(8,128)(2,1)S(1)} %collective-permute-done.1.refs_2_), channel_id=1, source_target_pairs={{0,16},{16,0},{1,17},{17,1},{2,18},{18,2},{3,19},{19,3},{4,20},{20... | collective-permute-start | bytes 786440 | tf_op jit(solution)/shard_map/ppermute | solution.py:366
  18.3 1.3 %shard_map.47.refs_4_ = f32[512,512]{1,0:T(8,128)S(1)} custom-call(s32[16]{0:T(128)S(1)} %copy-done.1, bf16[16,256,1024]{2,1,0:T(8,128)(2,1)S(1)} %shard_map.46.rows_ref, bf16[512,512]{1,0:T(8,128)(2,1)S(1)} %bitcast.11, bf16[512,512]{1,0:T(8,128)(2,1)S(1)} %collective-permute-done.5.refs_1_), custom_call_target="tpu_custom_call" | custom-call | flops 536870912 | bytes 3145728 | tf_op jit(solution)/shard_map/pallas_call | solution.py:220
  19.6 1.5 %shard_map.48.refs_6_ = f32[512,512]{1,0:T(8,128)S(1)} custom-call(s32[16]{0:T(128)S(1)} %copy-done.1, bf16[16,256,1024]{2,1,0:T(8,128)(2,1)S(1)} %shard_map.46.rows_ref, bf16[512,512]{1,0:T(8,128)(2,1)S(1)} %collective-permute-done.refs_0_, bf16[512,512]{1,0:T(8,128)(2,1)S(1)} %collective-permute-done.3.refs_1_, ...), custom_call_target="tpu_custom_call" | custom-call | flops 805306368 | bytes 5242880 | tf_op jit(solution)/shard_map/pallas_call | solution.py:220
  21.1 1.3 %collective-permute-done.2.refs_0_ = bf16[512,512]{1,0:T(8,128)(2,1)S(1)} collective-permute-done((bf16[512,512]{1,0:T(8,128)(2,1)S(1)}, bf16[512,512]{1,0:T(8,128)(2,1)S(1)}, u32[]{:S(2)}, u32[]{:S(2)}) %collective-permute-start.2) | collective-permute-done | bytes 524320 | tf_op jit(solution)/shard_map/ppermute | solution.py:357
  22.4 2.0 %collective-permute-start.6 = (bf16[512,512]{1,0:T(8,128)(2,1)S(1)}, bf16[512,512]{1,0:T(8,128)(2,1)S(1)}, u32[]{:S(2)}, u32[]{:S(2)}) collective-permute-start(bf16[512,512]{1,0:T(8,128)(2,1)S(1)} %collective-permute-done.2.refs_0_), channel_id=1, source_target_pairs={{0,4},{5,1},{4,8},{9,5},{8,12},{13,9},{12,14},{15,13},{14,10},{11,... | collective-permute-start | bytes 1572872 | tf_op jit(solution)/shard_map/ppermute | solution.py:357
  24.4 0.8 collective-permute-done.8.refs_2_
  25.7 2.0 %collective-permute-start.14 = (bf16[256,512]{1,0:T(8,128)(2,1)S(1)}, bf16[256,512]{1,0:T(8,128)(2,1)S(1)}, u32[]{:S(2)}, u32[]{:S(2)}) collective-permute-start(bf16[256,512]{1,0:T(8,128)(2,1)S(1)} %collective-permute-done.8.refs_2_), channel_id=1, source_target_pairs={{0,4},{5,1},{4,8},{9,5},{8,12},{13,9},{12,14},{15,13},{14,10},{11,... | collective-permute-start | bytes 786440 | tf_op jit(solution)/shard_map/ppermute | solution.py:357
  27.7 1.5 %collective-permute-start.16 = (bf16[256,512]{1,0:T(8,128)(2,1)S(1)}, bf16[256,512]{1,0:T(8,128)(2,1)S(1)}, u32[]{:S(2)}, u32[]{:S(2)}) collective-permute-start(bf16[256,512]{1,0:T(8,128)(2,1)S(1)} %collective-permute-done.8.refs_2_), channel_id=1, source_target_pairs={{0,16},{16,0},{1,17},{17,1},{2,18},{18,2},{3,19},{19,3},{4,20},{20... | collective-permute-start | bytes 786440 | tf_op jit(solution)/shard_map/ppermute | solution.py:366
  29.2 1.8 %shard_map.49.refs_6_ = f32[512,512]{1,0:T(8,128)S(1)} custom-call(s32[16]{0:T(128)S(1)} %copy-done.1, bf16[16,256,1024]{2,1,0:T(8,128)(2,1)S(1)} %shard_map.46.rows_ref, bf16[512,512]{1,0:T(8,128)(2,1)S(1)} %collective-permute-done.2.refs_0_, bf16[512,512]{1,0:T(8,128)(2,1)S(1)} %collective-permute-done.7.refs_1_, ...), custom_call_target="tpu_custom_call" | custom-call | flops 1073741824 | bytes 6291456 | tf_op jit(solution)/shard_map/pallas_call | solution.py:220
  31.0 0.5 collective-permute-done.6.refs_0_
  31.6 2.0 %collective-permute-start.12 = (bf16[512,512]{1,0:T(8,128)(2,1)S(1)}, bf16[512,512]{1,0:T(8,128)(2,1)S(1)}, u32[]{:S(2)}, u32[]{:S(2)}) collective-permute-start(bf16[512,512]{1,0:T(8,128)(2,1)S(1)} %collective-permute-done.6.refs_0_), channel_id=1, source_target_pairs={{0,4},{5,1},{4,8},{9,5},{8,12},{13,9},{12,14},{15,13},{14,10},{11,... | collective-permute-start | bytes 1572872 | tf_op jit(solution)/shard_map/ppermute | solution.py:357
  33.6 0.8 collective-permute-done.14.refs_2_
  34.4 1.2 %collective-permute-done.16.refs_4_ = bf16[256,512]{1,0:T(8,128)(2,1)S(1)} collective-permute-done((bf16[256,512]{1,0:T(8,128)(2,1)S(1)}, bf16[256,512]{1,0:T(8,128)(2,1)S(1)}, u32[]{:S(2)}, u32[]{:S(2)}) %collective-permute-start.16) | collective-permute-done | bytes 262176 | tf_op jit(solution)/shard_map/ppermute | solution.py:366
  35.6 1.5 %collective-permute-start.19 = (bf16[256,512]{1,0:T(8,128)(2,1)S(1)}, bf16[256,512]{1,0:T(8,128)(2,1)S(1)}, u32[]{:S(2)}, u32[]{:S(2)}) collective-permute-start(bf16[256,512]{1,0:T(8,128)(2,1)S(1)} %collective-permute-done.14.refs_2_), channel_id=1, source_target_pairs={{0,16},{16,0},{1,17},{17,1},{2,18},{18,2},{3,19},{19,3},{4,20},{20... | collective-permute-start | bytes 786440 | tf_op jit(solution)/shard_map/ppermute | solution.py:366
  37.2 1.8 %shard_map.50.refs_4_ = f32[512,512]{1,0:T(8,128)S(1)} custom-call(s32[16]{0:T(128)S(1)} %copy-done.1, bf16[16,256,1024]{2,1,0:T(8,128)(2,1)S(1)} %shard_map.46.rows_ref, bf16[512,512]{1,0:T(8,128)(2,1)S(1)} %collective-permute-done.6.refs_0_, bf16[512,512]{1,0:T(8,128)(2,1)S(1)} %collective-permute-done.13.refs_1_, ...), custom_call_target="tpu_custom_call" | custom-call | flops 1073741824 | bytes 6291456 | tf_op jit(solution)/shard_map/pallas_call | solution.py:220
  39.0 1.8 %collective-permute-done.12.refs_0_ = bf16[512,512]{1,0:T(8,128)(2,1)S(1)} collective-permute-done((bf16[512,512]{1,0:T(8,128)(2,1)S(1)}, bf16[512,512]{1,0:T(8,128)(2,1)S(1)}, u32[]{:S(2)}, u32[]{:S(2)}) %collective-permute-start.12) | collective-permute-done | bytes 524320 | tf_op jit(solution)/shard_map/ppermute | solution.py:357
  40.8 3.6 %collective-permute-done.19.refs_2_ = bf16[256,512]{1,0:T(8,128)(2,1)S(1)} collective-permute-done((bf16[256,512]{1,0:T(8,128)(2,1)S(1)}, bf16[256,512]{1,0:T(8,128)(2,1)S(1)}, u32[]{:S(2)}, u32[]{:S(2)}) %collective-permute-start.19) | collective-permute-done | bytes 262176 | tf_op jit(solution)/shard_map/ppermute | solution.py:366
  44.3 1.5 %collective-permute-done.20.refs_3_ = bf16[256,512]{1,0:T(8,128)(2,1)S(1)} collective-permute-done((bf16[256,512]{1,0:T(8,128)(2,1)S(1)}, bf16[256,512]{1,0:T(8,128)(2,1)S(1)}, u32[]{:S(2)}, u32[]{:S(2)}) %collective-permute-start.20) | collective-permute-done | bytes 262176 | tf_op jit(solution)/shard_map/ppermute | solution.py:363
  45.9 1.9 %shard_map.51 = s16[16,144,128]{2,1,0:T(8,128)(2,1)S(1)} custom-call(s32[16]{0:T(128)S(1)} %copy-done.1, bf16[16,256,1024]{2,1,0:T(8,128)(2,1)S(1)} %shard_map.46.rows_ref, bf16[512,512]{1,0:T(8,128)(2,1)S(1)} %collective-permute-done.12.refs_0_, bf16[512,512]{1,0:T(8,128)(2,1)S(1)} %collective-permute-done.18.refs_1_, ...), custom_call_target="tpu_custom_call" | custom-call | flops 805306368 | bytes 5242880 | tf_op jit(solution)/shard_map/pallas_call | solution.py:220
  47.8 22.9 %all_to_all.10.in_ref = s16[16,144,128]{2,1,0:T(8,128)(2,1)S(1)} all-to-all(s16[16,144,128]{2,1,0:T(8,128)(2,1)S(1)} %shard_map.51), channel_id=1, replica_groups=mesh['grp'=2,'shell'=16] {'shell'}, dimensions={0} | all-to-all | bytes 1179648 | tf_op jit(solution)/shard_map/all_to_all | solution.py:404
  70.7 1.5 %shard_map.52 = s16[16,144,128]{2,1,0:T(8,128)(2,1)} custom-call(s16[16,144,128]{2,1,0:T(8,128)(2,1)S(1)} %all_to_all.10.in_ref), custom_call_target="tpu_custom_call" | custom-call | tf_op jit(solution)/shard_map/pallas_call | solution.py:331
  72.2 3.6 %all-to-all-start.1 = ((s16[16,144,128]{2,1,0:T(8,128)(2,1)}), s16[16,144,128]{2,1,0:T(8,128)(2,1)S(1)}, u32[]{:S(2)}, u32[]{:S(2)}) async-start(s16[16,144,128]{2,1,0:T(8,128)(2,1)} %shard_map.52), calls=%async_computation.1 | async-start | bytes 1179648 | tf_op jit(solution)/shard_map/all_to_all | solution.py:406
  75.9 15.4 %all-to-all-done.1.in_ref = s16[16,144,128]{2,1,0:T(8,128)(2,1)S(1)} async-done(((s16[16,144,128]{2,1,0:T(8,128)(2,1)}), s16[16,144,128]{2,1,0:T(8,128)(2,1)S(1)}, u32[]{:S(2)}, u32[]{:S(2)}) %all-to-all-start.1) | async-done | bytes 589856 | tf_op jit(solution)/shard_map/all_to_all | solution.py:406
  91.3 2.2 %shard_map.53 = f32[2048,128]{1,0:T(8,128)} custom-call(f32[2,32]{1,0:T(2,128)S(1)} %maximum_multiply_fusion.twist_ref, s16[16,144,128]{2,1,0:T(8,128)(2,1)S(1)} %all-to-all-done.1.in_ref), custom_call_target="tpu_custom_call" | custom-call | tf_op jit(solution)/shard_map/pallas_call | solution.py:331
  (30 shorter events, 0.9 us)
Async XLA Ops:
  0.0 13.1 %collective-permute-start = (bf16[512,512]{1,0:T(8,128)(2,1)}, bf16[512,512]{1,0:T(8,128)(2,1)S(1)}, u32[]{:S(2)}, u32[]{:S(2)}) collective-permute-start(bf16[512,512]{1,0:T(8,128)(2,1)} %bitcast.9), channel_id=1, source_target_pairs={{0,4},{5,1},{4,8},{9,5},{8,12},{13,9},{12,14},{15,13},{14,10},{11,... | collective-permute-start | bytes 1572872 | tf_op jit(solution)/shard_map/ppermute | solution.py:357
  4.0 9.0 %collective-permute-start.1 = (bf16[256,512]{1,0:T(8,128)(2,1)S(1)}, bf16[256,512]{1,0:T(8,128)(2,1)S(1)}, u32[]{:S(2)}, u32[]{:S(2)}) collective-permute-start(bf16[256,512]{1,0:T(8,128)(2,1)S(1)} %dynamic-slice_bitcast_fusion), channel_id=1, source_target_pairs={{1,4},{4,1},{5,8},{8,5},{9,12},{12,9},{13,14},{14,13},{15,10},{10,... | collective-permute-start | bytes 786440 | tf_op jit(solution)/shard_map/ppermute | solution.py:360
  4.8 12.0 %collective-permute-start.5 = (bf16[512,512]{1,0:T(8,128)(2,1)}, bf16[512,512]{1,0:T(8,128)(2,1)S(1)}, u32[]{:S(2)}, u32[]{:S(2)}) collective-permute-start(bf16[512,512]{1,0:T(8,128)(2,1)} %bitcast.10), channel_id=1, source_target_pairs={{0,1},{1,0},{2,3},{3,2},{4,5},{5,4},{6,7},{7,6},{8,9},{9,8},{10,11... | collective-permute-start | bytes 1572872 | tf_op jit(solution)/shard_map/ppermute | solution.py:363
  5.8 0.7 copy-start.2
  6.4 11.9 %copy-start = (bf16[1,512,512]{2,1,0:T(8,128)(2,1)S(1)}, bf16[1,512,512]{2,1,0:T(8,128)(2,1)}, u32[]{:S(2)}) copy-start(bf16[1,512,512]{2,1,0:T(8,128)(2,1)} %param.5) | copy-start | bytes 1572868
  6.4 11.9 %copy-start.1 = (s32[16]{0:T(128)S(1)}, s32[16]{0:T(128)}, u32[]{:S(2)}) copy-start(s32[16]{0:T(128)} %owner_ref.9) | copy-start | bytes 196
  13.1 6.4 %collective-permute-start.3 = (bf16[512,512]{1,0:T(8,128)(2,1)S(1)}, bf16[512,512]{1,0:T(8,128)(2,1)S(1)}, u32[]{:S(2)}, u32[]{:S(2)}) collective-permute-start(bf16[512,512]{1,0:T(8,128)(2,1)S(1)} %collective-permute-done.refs_0_), channel_id=1, source_target_pairs={{0,1},{1,0},{2,3},{3,2},{4,5},{5,4},{6,7},{7,6},{8,9},{9,8},{10,11... | collective-permute-start | bytes 1572872 | tf_op jit(solution)/shard_map/ppermute | solution.py:363
  13.2 9.2 %collective-permute-start.2 = (bf16[512,512]{1,0:T(8,128)(2,1)S(1)}, bf16[512,512]{1,0:T(8,128)(2,1)S(1)}, u32[]{:S(2)}, u32[]{:S(2)}) collective-permute-start(bf16[512,512]{1,0:T(8,128)(2,1)S(1)} %collective-permute-done.refs_0_), channel_id=1, source_target_pairs={{0,4},{5,1},{4,8},{9,5},{8,12},{13,9},{12,14},{15,13},{14,10},{11,... | collective-permute-start | bytes 1572872 | tf_op jit(solution)/shard_map/ppermute | solution.py:357
  15.2 4.3 %collective-permute-start.4 = (bf16[256,512]{1,0:T(8,128)(2,1)S(1)}, bf16[256,512]{1,0:T(8,128)(2,1)S(1)}, u32[]{:S(2)}, u32[]{:S(2)}) collective-permute-start(bf16[256,512]{1,0:T(8,128)(2,1)S(1)} %collective-permute-done.1.refs_2_), channel_id=1, source_target_pairs={{0,1},{1,0},{2,3},{3,2},{4,5},{5,4},{6,7},{7,6},{8,9},{9,8},{10,11... | collective-permute-start | bytes 786440 | tf_op jit(solution)/shard_map/ppermute | solution.py:363
  15.4 9.8 %collective-permute-start.8 = (bf16[256,512]{1,0:T(8,128)(2,1)S(1)}, bf16[256,512]{1,0:T(8,128)(2,1)S(1)}, u32[]{:S(2)}, u32[]{:S(2)}) collective-permute-start(bf16[256,512]{1,0:T(8,128)(2,1)S(1)} %collective-permute-done.1.refs_2_), channel_id=1, source_target_pairs={{0,4},{5,1},{4,8},{9,5},{8,12},{13,9},{12,14},{15,13},{14,10},{11,... | collective-permute-start | bytes 786440 | tf_op jit(solution)/shard_map/ppermute | solution.py:357
  16.8 8.4 %collective-permute-start.10 = (bf16[256,512]{1,0:T(8,128)(2,1)S(1)}, bf16[256,512]{1,0:T(8,128)(2,1)S(1)}, u32[]{:S(2)}, u32[]{:S(2)}) collective-permute-start(bf16[256,512]{1,0:T(8,128)(2,1)S(1)} %collective-permute-done.1.refs_2_), channel_id=1, source_target_pairs={{0,16},{16,0},{1,17},{17,1},{2,18},{18,2},{3,19},{19,3},{4,20},{20... | collective-permute-start | bytes 786440 | tf_op jit(solution)/shard_map/ppermute | solution.py:366
  22.4 6.9 %collective-permute-start.7 = (bf16[512,512]{1,0:T(8,128)(2,1)S(1)}, bf16[512,512]{1,0:T(8,128)(2,1)S(1)}, u32[]{:S(2)}, u32[]{:S(2)}) collective-permute-start(bf16[512,512]{1,0:T(8,128)(2,1)S(1)} %collective-permute-done.2.refs_0_), channel_id=1, source_target_pairs={{0,1},{1,0},{2,3},{3,2},{4,5},{5,4},{6,7},{7,6},{8,9},{9,8},{10,11... | collective-permute-start | bytes 1572872 | tf_op jit(solution)/shard_map/ppermute | solution.py:363
  22.4 9.2 %collective-permute-start.6 = (bf16[512,512]{1,0:T(8,128)(2,1)S(1)}, bf16[512,512]{1,0:T(8,128)(2,1)S(1)}, u32[]{:S(2)}, u32[]{:S(2)}) collective-permute-start(bf16[512,512]{1,0:T(8,128)(2,1)S(1)} %collective-permute-done.2.refs_0_), channel_id=1, source_target_pairs={{0,4},{5,1},{4,8},{9,5},{8,12},{13,9},{12,14},{15,13},{14,10},{11,... | collective-permute-start | bytes 1572872 | tf_op jit(solution)/shard_map/ppermute | solution.py:357
  25.2 2.5 %collective-permute-start.9 = (bf16[256,512]{1,0:T(8,128)(2,1)S(1)}, bf16[256,512]{1,0:T(8,128)(2,1)S(1)}, u32[]{:S(2)}, u32[]{:S(2)}) collective-permute-start(bf16[256,512]{1,0:T(8,128)(2,1)S(1)} %collective-permute-done.8.refs_2_), channel_id=1, source_target_pairs={{0,1},{1,0},{2,3},{3,2},{4,5},{5,4},{6,7},{7,6},{8,9},{9,8},{10,11... | collective-permute-start | bytes 786440 | tf_op jit(solution)/shard_map/ppermute | solution.py:363
  25.2 4.0 %collective-permute-start.11 = (bf16[256,512]{1,0:T(8,128)(2,1)S(1)}, bf16[256,512]{1,0:T(8,128)(2,1)S(1)}, u32[]{:S(2)}, u32[]{:S(2)}) collective-permute-start(bf16[256,512]{1,0:T(8,128)(2,1)S(1)} %collective-permute-done.10.refs_4_), channel_id=1, source_target_pairs={{0,1},{1,0},{2,3},{3,2},{4,5},{5,4},{6,7},{7,6},{8,9},{9,8},{10,11... | collective-permute-start | bytes 786440 | tf_op jit(solution)/shard_map/ppermute | solution.py:363
  25.7 8.7 %collective-permute-start.14 = (bf16[256,512]{1,0:T(8,128)(2,1)S(1)}, bf16[256,512]{1,0:T(8,128)(2,1)S(1)}, u32[]{:S(2)}, u32[]{:S(2)}) collective-permute-start(bf16[256,512]{1,0:T(8,128)(2,1)S(1)} %collective-permute-done.8.refs_2_), channel_id=1, source_target_pairs={{0,4},{5,1},{4,8},{9,5},{8,12},{13,9},{12,14},{15,13},{14,10},{11,... | collective-permute-start | bytes 786440 | tf_op jit(solution)/shard_map/ppermute | solution.py:357
  27.7 7.9 %collective-permute-start.16 = (bf16[256,512]{1,0:T(8,128)(2,1)S(1)}, bf16[256,512]{1,0:T(8,128)(2,1)S(1)}, u32[]{:S(2)}, u32[]{:S(2)}) collective-permute-start(bf16[256,512]{1,0:T(8,128)(2,1)S(1)} %collective-permute-done.8.refs_2_), channel_id=1, source_target_pairs={{0,16},{16,0},{1,17},{17,1},{2,18},{18,2},{3,19},{19,3},{4,20},{20... | collective-permute-start | bytes 786440 | tf_op jit(solution)/shard_map/ppermute | solution.py:366
  31.6 5.6 %collective-permute-start.13 = (bf16[512,512]{1,0:T(8,128)(2,1)S(1)}, bf16[512,512]{1,0:T(8,128)(2,1)S(1)}, u32[]{:S(2)}, u32[]{:S(2)}) collective-permute-start(bf16[512,512]{1,0:T(8,128)(2,1)S(1)} %collective-permute-done.6.refs_0_), channel_id=1, source_target_pairs={{0,1},{1,0},{2,3},{3,2},{4,5},{5,4},{6,7},{7,6},{8,9},{9,8},{10,11... | collective-permute-start | bytes 1572872 | tf_op jit(solution)/shard_map/ppermute | solution.py:363
  31.6 9.2 %collective-permute-start.12 = (bf16[512,512]{1,0:T(8,128)(2,1)S(1)}, bf16[512,512]{1,0:T(8,128)(2,1)S(1)}, u32[]{:S(2)}, u32[]{:S(2)}) collective-permute-start(bf16[512,512]{1,0:T(8,128)(2,1)S(1)} %collective-permute-done.6.refs_0_), channel_id=1, source_target_pairs={{0,4},{5,1},{4,8},{9,5},{8,12},{13,9},{12,14},{15,13},{14,10},{11,... | collective-permute-start | bytes 1572872 | tf_op jit(solution)/shard_map/ppermute | solution.py:357
  34.4 2.7 %collective-permute-start.15 = (bf16[256,512]{1,0:T(8,128)(2,1)S(1)}, bf16[256,512]{1,0:T(8,128)(2,1)S(1)}, u32[]{:S(2)}, u32[]{:S(2)}) collective-permute-start(bf16[256,512]{1,0:T(8,128)(2,1)S(1)} %collective-permute-done.14.refs_2_), channel_id=1, source_target_pairs={{0,1},{1,0},{2,3},{3,2},{4,5},{5,4},{6,7},{7,6},{8,9},{9,8},{10,11... | collective-permute-start | bytes 786440 | tf_op jit(solution)/shard_map/ppermute | solution.py:363
  35.6 1.5 %collective-permute-start.17 = (bf16[256,512]{1,0:T(8,128)(2,1)S(1)}, bf16[256,512]{1,0:T(8,128)(2,1)S(1)}, u32[]{:S(2)}, u32[]{:S(2)}) collective-permute-start(bf16[256,512]{1,0:T(8,128)(2,1)S(1)} %collective-permute-done.16.refs_4_), channel_id=1, source_target_pairs={{0,1},{1,0},{2,3},{3,2},{4,5},{5,4},{6,7},{7,6},{8,9},{9,8},{10,11... | collective-permute-start | bytes 786440 | tf_op jit(solution)/shard_map/ppermute | solution.py:363
  35.6 8.7 %collective-permute-start.19 = (bf16[256,512]{1,0:T(8,128)(2,1)S(1)}, bf16[256,512]{1,0:T(8,128)(2,1)S(1)}, u32[]{:S(2)}, u32[]{:S(2)}) collective-permute-start(bf16[256,512]{1,0:T(8,128)(2,1)S(1)} %collective-permute-done.14.refs_2_), channel_id=1, source_target_pairs={{0,16},{16,0},{1,17},{17,1},{2,18},{18,2},{3,19},{19,3},{4,20},{20... | collective-permute-start | bytes 786440 | tf_op jit(solution)/shard_map/ppermute | solution.py:366
  40.8 5.1 %collective-permute-start.18 = (bf16[512,512]{1,0:T(8,128)(2,1)S(1)}, bf16[512,512]{1,0:T(8,128)(2,1)S(1)}, u32[]{:S(2)}, u32[]{:S(2)}) collective-permute-start(bf16[512,512]{1,0:T(8,128)(2,1)S(1)} %collective-permute-done.12.refs_0_), channel_id=1, source_target_pairs={{0,1},{1,0},{2,3},{3,2},{4,5},{5,4},{6,7},{7,6},{8,9},{9,8},{10,11... | collective-permute-start | bytes 1572872 | tf_op jit(solution)/shard_map/ppermute | solution.py:363
  44.3 1.5 %collective-permute-start.20 = (bf16[256,512]{1,0:T(8,128)(2,1)S(1)}, bf16[256,512]{1,0:T(8,128)(2,1)S(1)}, u32[]{:S(2)}, u32[]{:S(2)}) collective-permute-start(bf16[256,512]{1,0:T(8,128)(2,1)S(1)} %collective-permute-done.19.refs_2_), channel_id=1, source_target_pairs={{0,1},{1,0},{2,3},{3,2},{4,5},{5,4},{6,7},{7,6},{8,9},{9,8},{10,11... | collective-permute-start | bytes 786440 | tf_op jit(solution)/shard_map/ppermute | solution.py:363
  72.2 19.1 %all-to-all-start.1 = ((s16[16,144,128]{2,1,0:T(8,128)(2,1)}), s16[16,144,128]{2,1,0:T(8,128)(2,1)S(1)}, u32[]{:S(2)}, u32[]{:S(2)}) async-start(s16[16,144,128]{2,1,0:T(8,128)(2,1)} %shard_map.52), calls=%async_computation.1 | async-start | bytes 1179648 | tf_op jit(solution)/shard_map/all_to_all | solution.py:406

commit v4 on v3

--- a/solution.py
+++ b/solution.py
@@ -86,6 +86,7 @@
 STEPS = 16.0
 TOP = 32000.0
 LANES = 128
+GROUP = 4
 SORT_LIMIT = 42
 
 
@@ -97,16 +98,17 @@
 
 
 def sort_kernel(order_ref, coef_ref, out_ref, perm_ref, held_ref, sems):
-    blocks, rows, _ = held_ref.shape
+    rows = perm_ref.shape[0]
+    blocks = held_ref.shape[0] // rows
     degrees = out_ref.shape[0]
     shells = order_ref.shape[0]
     slab = rows // degrees
 
     def copy(i):
-        block = coef_ref.at[pl.ds(i * rows, rows), :]
-        return pltpu.make_async_copy(block, held_ref.at[i], sems.at[i])
-
-    for i in range(blocks):
+        block = coef_ref.at[pl.ds(i * rows, GROUP * rows), :]
+        return pltpu.make_async_copy(block, held_ref.at[pl.ds(i * rows, GROUP * rows), :], sems.at[i])
+
+    for i in range(0, blocks, GROUP):
         copy(i).start()
     line = lax.broadcasted_iota(jnp.int32, (slab, rows), 0)
     in_at = lax.broadcasted_iota(jnp.int32, (slab, rows), 1)
@@ -119,8 +121,9 @@
         perm_ref[pl.ds(l * slab, slab), :] = chosen
 
     for i in range(blocks):
-        copy(i).wait()
-        moved = jnp.dot(perm_ref[...], held_ref[i], preferred_element_type=jnp.float32)
+        if i % GROUP == 0:
+            copy(i).wait()
+        moved = jnp.dot(perm_ref[...], held_ref[pl.ds(i * rows, rows), :], preferred_element_type=jnp.float32)
         out_ref[:, pl.ds(i * slab, slab), :] = moved.astype(out_ref.dtype).reshape(
             degrees, slab, moved.shape[1]
         )
@@ -138,7 +141,7 @@
         out_shape=jax.ShapeDtypeStruct((degrees, orders * shells, width), pair_coef.dtype),
         scratch_shapes=[
             pltpu.VMEM((rows, rows), pair_coef.dtype),
-            pltpu.VMEM((blocks, rows, width), pair_coef.dtype),
+            pltpu.VMEM((blocks * rows, width), pair_coef.dtype),
             pltpu.SemaphoreType.DMA((blocks,)),
         ],
         compiler_params=pltpu.CompilerParams(vmem_limit_bytes=SORT_LIMIT * 2**20),
@@ -158,10 +161,40 @@
     largest = jnp.max(jnp.maximum(jnp.abs(real_part), jnp.abs(imag_part)), axis=0, keepdims=True)
     code = scale_code(largest)
     gain = jnp.exp2(code * (-1.0 / STEPS)) * TOP
-    coded = [
-        jnp.floor(v * gain + 0.5).astype(jnp.int32).astype(jnp.int16) for v in (real_part, imag_part)
-    ]
+    coded = [jnp.floor(v * gain + 0.5).astype(jnp.int32) for v in (real_part, imag_part)]
     return coded[0], coded[1], code
+
+
+EIGHTS = 17
+
+
+def stage_block(stage_ref, piece, jb, coded, code):
+    odd = lax.axis_index("shell") % 2
+    first = EIGHTS * piece + odd + 4 * jb
+    for part in range(2):
+        stage_ref[pl.ds(first + 2 * part, 2)] = coded[part].reshape(2, 8, LANES)
+    stage_ref[EIGHTS * piece + (EIGHTS - 1) * (1 - odd), pl.ds(jb, 1), :] = code.astype(jnp.int32)
+
+
+def clear_codes(stage_ref, pieces):
+    odd = lax.axis_index("shell") % 2
+    for piece in range(pieces):
+        stage_ref[EIGHTS * piece + (EIGHTS - 1) * (1 - odd)] = jnp.zeros((8, LANES), jnp.int32)
+
+
+def ship(stage_ref, out_ref):
+    for pair in range(stage_ref.shape[0] // 2):
+        both = stage_ref[pl.ds(2 * pair, 2)].reshape(16, LANES)
+        out_ref[pl.ds(16 * pair, 16), :] = both.astype(jnp.int16)
+
+
+def value_rows(piece, jb, part):
+    return pl.ds((EIGHTS * piece + piece % 2 + 4 * jb + 2 * part) * 8, 16)
+
+
+def read_gains(in_ref, gain_ref):
+    for pair in range(gain_ref.shape[0]):
+        gain_ref[pair] = gains(in_ref[pl.ds((2 * EIGHTS * pair + EIGHTS - 1) * 8, 16), :])
 
 
 def gains(codes):
@@ -185,7 +218,7 @@
     n = len(sources)
     panels = refs[:n]
     acc_in = refs[n : n + n_acc]
-    acc_out = refs[-1]
+    acc_out = refs[-2] if packed else refs[-1]
     chips = devices // 2
     me = lax.axis_index("shell")
     part = lax.axis_index("grp")
@@ -209,7 +242,7 @@
         acc_out[...] = acc_out[...] + product if started else product
         started = 1
     if packed:
-        pack(acc_out, refs[-2])
+        pack(acc_out, refs[-1], refs[-3])
 
 
 def project(acc, rows, owner, panels, sources, packed=None):
@@ -225,7 +258,12 @@
         + [pl.BlockSpec(memory_space=pltpu.VMEM)] * (1 + len(panels) + n_acc),
         out_specs=pl.BlockSpec(memory_space=pltpu.VMEM),
         out_shape=total if packed is None else packed,
-        scratch_shapes=[] if packed is None else [pltpu.VMEM(total.shape, total.dtype)],
+        scratch_shapes=[]
+        if packed is None
+        else [
+            pltpu.VMEM(total.shape, total.dtype),
+            pltpu.VMEM((packed.shape[0] // 8, 8, LANES), jnp.int32),
+        ],
         compiler_params=pltpu.CompilerParams(vmem_limit_bytes=24 * 2**20),
         cost_estimate=pl.CostEstimate(
             flops=4 * count * depth * width,
@@ -235,21 +273,18 @@
     )(owner, rows, *panels, *([acc] if n_acc else []))
 
 
-def pack(proj_ref, out_ref):
+def pack(proj_ref, stage_ref, out_ref):
     count, width = proj_ref.shape[0] // 2, proj_ref.shape[1]
-    blocks = width // LANES
-    line = lax.broadcasted_iota(jnp.int32, (16, LANES), 0)
-    for d in range(out_ref.shape[0]):
-        codes = jnp.zeros((16, LANES), jnp.float32)
-        for jb in range(blocks):
+    pieces = count // 16
+    clear_codes(stage_ref, pieces)
+    for d in range(pieces):
+        for jb in range(width // LANES):
             lanes = pl.ds(jb * LANES, LANES)
-            real_part, imag_part, code = encode(
+            *coded, code = encode(
                 proj_ref[pl.ds(16 * d, 16), lanes], proj_ref[pl.ds(count + 16 * d, 16), lanes]
             )
-            out_ref[d, pl.ds(32 * jb, 16), :] = real_part
-            out_ref[d, pl.ds(32 * jb + 16, 16), :] = imag_part
-            codes = jnp.where(line == jb, code, codes)
-        out_ref[d, pl.ds(32 * blocks, 16), :] = codes.astype(jnp.int32).astype(jnp.int16)
+            stage_block(stage_ref, d, jb, coded, code)
+    ship(stage_ref, out_ref)
 
 
 def radix2(real_parts, imag_parts):
@@ -278,41 +313,34 @@
     return re, im
 
 
-def outer_kernel(in_ref, out_ref, gain_ref, code_ref):
-    n = in_ref.shape[0]
-    blocks = in_ref.shape[1] // 32
-    for q in range(n):
-        gain_ref[q] = gains(in_ref[q, pl.ds(32 * blocks, 16), :])
-    code_ref[...] = jnp.zeros_like(code_ref)
-    for jb in range(blocks):
+def outer_kernel(in_ref, out_ref, gain_ref, stage_ref):
+    n = 2 * gain_ref.shape[0]
+    read_gains(in_ref, gain_ref)
+    clear_codes(stage_ref, n)
+    for jb in range((EIGHTS - 1) // 4):
         re, im = [], []
         for q in range(n):
-            gain = gain_ref[q, pl.ds(jb, 1), :]
-            re.append(widen(in_ref[q, pl.ds(32 * jb, 16), :]) * gain)
-            im.append(widen(in_ref[q, pl.ds(32 * jb + 16, 16), :]) * gain)
+            gain = gain_ref[q // 2, pl.ds(8 * (q % 2) + jb, 1), :]
+            re.append(widen(in_ref[value_rows(q, jb, 0), :]) * gain)
+            im.append(widen(in_ref[value_rows(q, jb, 1), :]) * gain)
         re, im = radix2(re, im)
         for p in range(n):
-            real_part, imag_part, code = encode(re[p], im[p])
-            out_ref[p, pl.ds(32 * jb, 16), :] = real_part
-            out_ref[p, pl.ds(32 * jb + 16, 16), :] = imag_part
-            code_ref[p, pl.ds(jb, 1), :] = code
-    for p in range(n):
-        out_ref[p, pl.ds(32 * blocks, 16), :] = code_ref[p].astype(jnp.int32).astype(jnp.int16)
+            *coded, code = encode(re[p], im[p])
+            stage_block(stage_ref, p, jb, coded, code)
+    ship(stage_ref, out_ref)
 
 
 def inner_kernel(twist_ref, in_ref, out_ref, gain_ref):
-    n = in_ref.shape[0]
-    blocks = in_ref.shape[1] // 32
+    n = 2 * gain_ref.shape[0]
     orders = 2 * n
     nbits = orders.bit_length() - 1
-    for d in range(n):
-        gain_ref[d] = gains(in_ref[d, pl.ds(32 * blocks, 16), :])
-    for jb in range(blocks):
+    read_gains(in_ref, gain_ref)
+    for jb in range((EIGHTS - 1) // 4):
         re, im = [], []
         for d in range(n):
-            gain = gain_ref[d, pl.ds(jb, 1), :]
-            both_re = widen(in_ref[d, pl.ds(32 * jb, 16), :]) * gain
-            both_im = widen(in_ref[d, pl.ds(32 * jb + 16, 16), :]) * gain
+            gain = gain_ref[d // 2, pl.ds(8 * (d % 2) + jb, 1), :]
+            both_re = widen(in_ref[value_rows(d, jb, 0), :]) * gain
+            both_im = widen(in_ref[value_rows(d, jb, 1), :]) * gain
             for r in range(2):
                 a, b = both_re[8 * r : 8 * r + 8], both_im[8 * r : 8 * r + 8]
                 c, s = twist_ref[0, 2 * d + r], twist_ref[1, 2 * d + r]
@@ -366,8 +394,14 @@
         return lax.ppermute(value, "grp", [(0, 1), (1, 0)])
 
     blocks = width // LANES
-    parcel = jax.ShapeDtypeStruct((devices, 32 * blocks + 16, LANES), jnp.int16)
-    lines = pltpu.VMEM((devices, 16, LANES), jnp.float32)
+    parcels = jax.ShapeDtypeStruct((devices * EIGHTS * 8, LANES), jnp.int16)
+    lines = pltpu.VMEM((devices // 2, 16, LANES), jnp.float32)
+    stage = pltpu.VMEM((devices * EIGHTS, 8, LANES), jnp.int32)
+
+    def exchange(value):
+        value = value.reshape(devices, EIGHTS * 8, LANES)
+        return lax.all_to_all(value, "shell", 0, 0).reshape(parcels.shape)
+
     own = panel_pool[0]
     half = own.shape[0] // 2
     whole = around(own)
@@ -399,11 +433,10 @@
         degree_owner,
         [whole, sibling(whole), *late],
         [(-(chips // 2), 0, None), (chips // 2, 1, None), *late_from],
-        packed=parcel,
+        packed=parcels,
     )
-    sent = lax.all_to_all(sent, "shell", 0, 0)
-    sent = local_call(outer_kernel, parcel, [lines, lines], sent)
-    sent = lax.all_to_all(sent, "shell", 0, 0)
+    sent = local_call(outer_kernel, parcels, [lines, stage], exchange(sent))
+    sent = exchange(sent)
     first = bit_reverse(me, devices.bit_length() - 1)
     phase = lax.iota(jnp.int32, local_orders) * first % total_orders
     angle = -2.0 * math.pi * phase.astype(jnp.float32) / float(total_orders)

time: 93.8 us -> 93.1 us (level)
  Pallas kernels: 18.6 us -> 17.5 us
    pallas_call x1, Pallas kernels: 6.6 us -> 5.14 us  [sort_rows(): pl.pallas_call(sort_kernel, in_specs=[pl.BlockSpec(memory_space=pltpu.SME...]
    ppermute x1, waiting for transfers between devices: 0.01 us -> 1.17 us  [crosswise(): lax.ppermute(value, 'shell', [(source ^ 1, target) for source, target in...]
  transfers between devices with their start and end apart: 22 -> 22, of which waited for: 10 -> 11; matrix products, arithmetic and copies ran while one was open for 1% -> 1% of each run, Pallas kernels for 14% -> 12%
where the time goes in v4:
time: 93.1 us; the launch traced here: 92.8 us
  waiting for transfers between devices  27.9 us (30%)
  starting transfers between devices  23.3 us (25%)
  blocking collectives  22.4 us (24%)
  Pallas kernels  17.5 us (19%)
  local copies, waits for them, and re-layouts  1.66 us (2%)
    all_to_all x1, blocking collectives, exchange(): return lax.all_to_all(value, 'shell', 0, 0).reshape(parcels.shape)  22.4 us
    all_to_all x1, waiting for transfers between devices, exchange(): return lax.all_to_all(value, 'shell', 0, 0).reshape(parcels.shape)  14.9 us
    ppermute x6, starting transfers between devices, around(): return lax.ppermute(value, 'shell', onward)  12.8 us
    pallas_call x5, Pallas kernels, project(): pl.pallas_call(functools.partial(project_kernel, lax.axis_size('shell'),...  8.44 us
    ppermute x6, waiting for transfers between devices, around(): return lax.ppermute(value, 'shell', onward)  5.26 us
    pallas_call x1, Pallas kernels, sort_rows(): pl.pallas_call(sort_kernel, in_specs=[pl.BlockSpec(memory_space=pltpu.SME...  5.14 us
    ppermute x3, waiting for transfers between devices, across(): return lax.ppermute(value, 'grp', [(0, 1), (1, 0)])  4.92 us
    ppermute x3, starting transfers between devices, across(): return lax.ppermute(value, 'grp', [(0, 1), (1, 0)])  4.47 us
  transfers between devices with their start and end apart: 22, of which 11 were waited for; matrix products, arithmetic and copies ran while one was open for 1% of the time, Pallas kernels for 12%

profile of v4, /device:TPU:0, one launch (start us, length us, event | category | flops | bytes accessed | tf_op | source)
XLA Modules:
  0.0 92.8 jit_solution(7773162337050886509)
XLA Ops:
  0.0 3.0 %collective-permute-start = (bf16[512,512]{1,0:T(8,128)(2,1)}, bf16[512,512]{1,0:T(8,128)(2,1)S(1)}, u32[]{:S(2)}, u32[]{:S(2)}) collective-permute-start(bf16[512,512]{1,0:T(8,128)(2,1)} %bitcast.16), channel_id=1, source_target_pairs={{0,4},{5,1},{4,8},{9,5},{8,12},{13,9},{12,14},{15,13},{14,10},{11,... | collective-permute-start | bytes 1572872 | tf_op jit(solution)/shard_map/ppermute | solution.py:385
  3.0 1.0 %dynamic-slice_bitcast_fusion = bf16[256,512]{1,0:T(8,128)(2,1)S(1)} fusion(bf16[1,512,512]{2,1,0:T(8,128)(2,1)} %param.5, s32[]{:T(128)S(6)} %select_n.22), kind=kLoop, calls=%fused_computation | loop fusion | bytes 524292 | tf_op jit(solution)/shard_map/dynamic_slice | solution.py:408
  4.0 0.7 collective-permute-start.1
  4.8 1.0 %collective-permute-start.5 = (bf16[512,512]{1,0:T(8,128)(2,1)}, bf16[512,512]{1,0:T(8,128)(2,1)S(1)}, u32[]{:S(2)}, u32[]{:S(2)}) collective-permute-start(bf16[512,512]{1,0:T(8,128)(2,1)} %bitcast.17), channel_id=1, source_target_pairs={{0,1},{1,0},{2,3},{3,2},{4,5},{5,4},{6,7},{7,6},{8,9},{9,8},{10,11... | collective-permute-start | bytes 1572872 | tf_op jit(solution)/shard_map/ppermute | solution.py:391
  5.8 0.7 copy-done.2
  6.4 5.1 %shard_map.46.rows_ref = bf16[16,256,1024]{2,1,0:T(8,128)(2,1)S(1)} custom-call(s32[8]{0:T(128)S(1)} %copy-done.2, bf16[4096,1024]{1,0:T(8,128)(2,1)} %bitcast.19), custom_call_target="tpu_custom_call" | custom-call | flops 2147483648 | bytes 16777216 | tf_op jit(solution)/shard_map/pallas_call | solution.py:137
  11.6 1.2 %collective-permute-done.1.refs_2_ = bf16[256,512]{1,0:T(8,128)(2,1)S(1)} collective-permute-done((bf16[256,512]{1,0:T(8,128)(2,1)S(1)}, bf16[256,512]{1,0:T(8,128)(2,1)S(1)}, u32[]{:S(2)}, u32[]{:S(2)}) %collective-permute-start.1) | collective-permute-done | bytes 262176 | tf_op jit(solution)/shard_map/ppermute | solution.py:388
  13.1 2.1 %collective-permute-start.2 = (bf16[512,512]{1,0:T(8,128)(2,1)S(1)}, bf16[512,512]{1,0:T(8,128)(2,1)S(1)}, u32[]{:S(2)}, u32[]{:S(2)}) collective-permute-start(bf16[512,512]{1,0:T(8,128)(2,1)S(1)} %collective-permute-done.refs_0_), channel_id=1, source_target_pairs={{0,4},{5,1},{4,8},{9,5},{8,12},{13,9},{12,14},{15,13},{14,10},{11,... | collective-permute-start | bytes 1572872 | tf_op jit(solution)/shard_map/ppermute | solution.py:385
  15.4 1.4 %collective-permute-start.8 = (bf16[256,512]{1,0:T(8,128)(2,1)S(1)}, bf16[256,512]{1,0:T(8,128)(2,1)S(1)}, u32[]{:S(2)}, u32[]{:S(2)}) collective-permute-start(bf16[256,512]{1,0:T(8,128)(2,1)S(1)} %collective-permute-done.1.refs_2_), channel_id=1, source_target_pairs={{0,4},{5,1},{4,8},{9,5},{8,12},{13,9},{12,14},{15,13},{14,10},{11,... | collective-permute-start | bytes 786440 | tf_op jit(solution)/shard_map/ppermute | solution.py:385
  16.8 1.5 %collective-permute-start.10 = (bf16[256,512]{1,0:T(8,128)(2,1)S(1)}, bf16[256,512]{1,0:T(8,128)(2,1)S(1)}, u32[]{:S(2)}, u32[]{:S(2)}) collective-permute-start(bf16[256,512]{1,0:T(8,128)(2,1)S(1)} %collective-permute-done.1.refs_2_), channel_id=1, source_target_pairs={{0,16},{16,0},{1,17},{17,1},{2,18},{18,2},{3,19},{19,3},{4,20},{20... | collective-permute-start | bytes 786440 | tf_op jit(solution)/shard_map/ppermute | solution.py:394
  18.3 1.3 %shard_map.47.refs_4_ = f32[512,512]{1,0:T(8,128)S(1)} custom-call(s32[16]{0:T(128)S(1)} %copy-done.1, bf16[16,256,1024]{2,1,0:T(8,128)(2,1)S(1)} %shard_map.46.rows_ref, bf16[512,512]{1,0:T(8,128)(2,1)S(1)} %bitcast.18, bf16[512,512]{1,0:T(8,128)(2,1)S(1)} %collective-permute-done.5.refs_1_), custom_call_target="tpu_custom_call" | custom-call | flops 536870912 | bytes 3145728 | tf_op jit(solution)/shard_map/pallas_call | solution.py:253
  19.6 1.5 %shard_map.48.refs_6_ = f32[512,512]{1,0:T(8,128)S(1)} custom-call(s32[16]{0:T(128)S(1)} %copy-done.1, bf16[16,256,1024]{2,1,0:T(8,128)(2,1)S(1)} %shard_map.46.rows_ref, bf16[512,512]{1,0:T(8,128)(2,1)S(1)} %collective-permute-done.refs_0_, bf16[512,512]{1,0:T(8,128)(2,1)S(1)} %collective-permute-done.3.refs_1_, ...), custom_call_target="tpu_custom_call" | custom-call | flops 805306368 | bytes 5242880 | tf_op jit(solution)/shard_map/pallas_call | solution.py:253
  21.1 1.2 %collective-permute-done.2.refs_0_ = bf16[512,512]{1,0:T(8,128)(2,1)S(1)} collective-permute-done((bf16[512,512]{1,0:T(8,128)(2,1)S(1)}, bf16[512,512]{1,0:T(8,128)(2,1)S(1)}, u32[]{:S(2)}, u32[]{:S(2)}) %collective-permute-start.2) | collective-permute-done | bytes 524320 | tf_op jit(solution)/shard_map/ppermute | solution.py:385
  22.3 2.1 %collective-permute-start.6 = (bf16[512,512]{1,0:T(8,128)(2,1)S(1)}, bf16[512,512]{1,0:T(8,128)(2,1)S(1)}, u32[]{:S(2)}, u32[]{:S(2)}) collective-permute-start(bf16[512,512]{1,0:T(8,128)(2,1)S(1)} %collective-permute-done.2.refs_0_), channel_id=1, source_target_pairs={{0,4},{5,1},{4,8},{9,5},{8,12},{13,9},{12,14},{15,13},{14,10},{11,... | collective-permute-start | bytes 1572872 | tf_op jit(solution)/shard_map/ppermute | solution.py:385
  24.4 0.7 collective-permute-done.8.refs_2_
  25.7 2.1 %collective-permute-start.14 = (bf16[256,512]{1,0:T(8,128)(2,1)S(1)}, bf16[256,512]{1,0:T(8,128)(2,1)S(1)}, u32[]{:S(2)}, u32[]{:S(2)}) collective-permute-start(bf16[256,512]{1,0:T(8,128)(2,1)S(1)} %collective-permute-done.8.refs_2_), channel_id=1, source_target_pairs={{0,4},{5,1},{4,8},{9,5},{8,12},{13,9},{12,14},{15,13},{14,10},{11,... | collective-permute-start | bytes 786440 | tf_op jit(solution)/shard_map/ppermute | solution.py:385
  27.7 1.5 %collective-permute-start.16 = (bf16[256,512]{1,0:T(8,128)(2,1)S(1)}, bf16[256,512]{1,0:T(8,128)(2,1)S(1)}, u32[]{:S(2)}, u32[]{:S(2)}) collective-permute-start(bf16[256,512]{1,0:T(8,128)(2,1)S(1)} %collective-permute-done.8.refs_2_), channel_id=1, source_target_pairs={{0,16},{16,0},{1,17},{17,1},{2,18},{18,2},{3,19},{19,3},{4,20},{20... | collective-permute-start | bytes 786440 | tf_op jit(solution)/shard_map/ppermute | solution.py:394
  29.2 1.8 %shard_map.49.refs_6_ = f32[512,512]{1,0:T(8,128)S(1)} custom-call(s32[16]{0:T(128)S(1)} %copy-done.1, bf16[16,256,1024]{2,1,0:T(8,128)(2,1)S(1)} %shard_map.46.rows_ref, bf16[512,512]{1,0:T(8,128)(2,1)S(1)} %collective-permute-done.2.refs_0_, bf16[512,512]{1,0:T(8,128)(2,1)S(1)} %collective-permute-done.7.refs_1_, ...), custom_call_target="tpu_custom_call" | custom-call | flops 1073741824 | bytes 6291456 | tf_op jit(solution)/shard_map/pallas_call | solution.py:253
  31.5 2.1 %collective-permute-start.12 = (bf16[512,512]{1,0:T(8,128)(2,1)S(1)}, bf16[512,512]{1,0:T(8,128)(2,1)S(1)}, u32[]{:S(2)}, u32[]{:S(2)}) collective-permute-start(bf16[512,512]{1,0:T(8,128)(2,1)S(1)} %collective-permute-done.6.refs_0_), channel_id=1, source_target_pairs={{0,4},{5,1},{4,8},{9,5},{8,12},{13,9},{12,14},{15,13},{14,10},{11,... | collective-permute-start | bytes 1572872 | tf_op jit(solution)/shard_map/ppermute | solution.py:385
  33.6 0.7 collective-permute-done.14.refs_2_
  34.3 1.3 %collective-permute-done.16.refs_4_ = bf16[256,512]{1,0:T(8,128)(2,1)S(1)} collective-permute-done((bf16[256,512]{1,0:T(8,128)(2,1)S(1)}, bf16[256,512]{1,0:T(8,128)(2,1)S(1)}, u32[]{:S(2)}, u32[]{:S(2)}) %collective-permute-start.16) | collective-permute-done | bytes 262176 | tf_op jit(solution)/shard_map/ppermute | solution.py:394
  35.6 1.5 %collective-permute-start.19 = (bf16[256,512]{1,0:T(8,128)(2,1)S(1)}, bf16[256,512]{1,0:T(8,128)(2,1)S(1)}, u32[]{:S(2)}, u32[]{:S(2)}) collective-permute-start(bf16[256,512]{1,0:T(8,128)(2,1)S(1)} %collective-permute-done.14.refs_2_), channel_id=1, source_target_pairs={{0,16},{16,0},{1,17},{17,1},{2,18},{18,2},{3,19},{19,3},{4,20},{20... | collective-permute-start | bytes 786440 | tf_op jit(solution)/shard_map/ppermute | solution.py:394
  37.2 1.8 %shard_map.50.refs_4_ = f32[512,512]{1,0:T(8,128)S(1)} custom-call(s32[16]{0:T(128)S(1)} %copy-done.1, bf16[16,256,1024]{2,1,0:T(8,128)(2,1)S(1)} %shard_map.46.rows_ref, bf16[512,512]{1,0:T(8,128)(2,1)S(1)} %collective-permute-done.6.refs_0_, bf16[512,512]{1,0:T(8,128)(2,1)S(1)} %collective-permute-done.13.refs_1_, ...), custom_call_target="tpu_custom_call" | custom-call | flops 1073741824 | bytes 6291456 | tf_op jit(solution)/shard_map/pallas_call | solution.py:253
  39.0 1.7 %collective-permute-done.12.refs_0_ = bf16[512,512]{1,0:T(8,128)(2,1)S(1)} collective-permute-done((bf16[512,512]{1,0:T(8,128)(2,1)S(1)}, bf16[512,512]{1,0:T(8,128)(2,1)S(1)}, u32[]{:S(2)}, u32[]{:S(2)}) %collective-permute-start.12) | collective-permute-done | bytes 524320 | tf_op jit(solution)/shard_map/ppermute | solution.py:385
  40.7 3.6 %collective-permute-done.19.refs_2_ = bf16[256,512]{1,0:T(8,128)(2,1)S(1)} collective-permute-done((bf16[256,512]{1,0:T(8,128)(2,1)S(1)}, bf16[256,512]{1,0:T(8,128)(2,1)S(1)}, u32[]{:S(2)}, u32[]{:S(2)}) %collective-permute-start.19) | collective-permute-done | bytes 262176 | tf_op jit(solution)/shard_map/ppermute | solution.py:394
  44.3 1.5 %collective-permute-done.20.refs_3_ = bf16[256,512]{1,0:T(8,128)(2,1)S(1)} collective-permute-done((bf16[256,512]{1,0:T(8,128)(2,1)S(1)}, bf16[256,512]{1,0:T(8,128)(2,1)S(1)}, u32[]{:S(2)}, u32[]{:S(2)}) %collective-permute-start.20) | collective-permute-done | bytes 262176 | tf_op jit(solution)/shard_map/ppermute | solution.py:391
  45.9 2.1 %shard_map.51 = s16[2176,128]{1,0:T(8,128)(2,1)S(1)} custom-call(s32[16]{0:T(128)S(1)} %copy-done.1, bf16[16,256,1024]{2,1,0:T(8,128)(2,1)S(1)} %shard_map.46.rows_ref, bf16[512,512]{1,0:T(8,128)(2,1)S(1)} %collective-permute-done.12.refs_0_, bf16[512,512]{1,0:T(8,128)(2,1)S(1)} %collective-permute-done.18.refs_1_, ...), custom_call_target="tpu_custom_call" | custom-call | flops 805306368 | bytes 5242880 | tf_op jit(solution)/shard_map/pallas_call | solution.py:253
  48.0 22.4 %all_to_all.10 = s16[16,136,128]{2,1,0:T(8,128)(2,1)S(1)} all-to-all(s16[16,136,128]{2,1,0:T(8,128)(2,1)S(1)} %bitcast.13), channel_id=1, replica_groups=mesh['grp'=2,'shell'=16] {'shell'}, dimensions={0} | all-to-all | bytes 1114112 | tf_op jit(solution)/shard_map/all_to_all | solution.py:403
  70.3 1.7 %shard_map.52 = s16[2176,128]{1,0:T(8,128)(2,1)} custom-call(s16[2176,128]{1,0:T(8,128)(2,1)S(1)} %bitcast.15), custom_call_target="tpu_custom_call" | custom-call | tf_op jit(solution)/shard_map/pallas_call | solution.py:359
  72.0 3.6 %all-to-all-start.1 = ((s16[16,136,128]{2,1,0:T(8,128)(2,1)}), s16[16,136,128]{2,1,0:T(8,128)(2,1)S(1)}, u32[]{:S(2)}, u32[]{:S(2)}) async-start(s16[16,136,128]{2,1,0:T(8,128)(2,1)} %bitcast.5), calls=%async_computation.1 | async-start | bytes 1114112 | tf_op jit(solution)/shard_map/all_to_all | solution.py:403
  75.7 14.9 %all-to-all-done.1 = s16[16,136,128]{2,1,0:T(8,128)(2,1)S(1)} async-done(((s16[16,136,128]{2,1,0:T(8,128)(2,1)}), s16[16,136,128]{2,1,0:T(8,128)(2,1)S(1)}, u32[]{:S(2)}, u32[]{:S(2)}) %all-to-all-start.1) | async-done | bytes 557088 | tf_op jit(solution)/shard_map/all_to_all | solution.py:403
  90.6 2.2 %shard_map.53 = f32[2048,128]{1,0:T(8,128)} custom-call(f32[2,32]{1,0:T(2,128)S(1)} %maximum_multiply_fusion.twist_ref, s16[2176,128]{1,0:T(8,128)(2,1)S(1)} %bitcast.14), custom_call_target="tpu_custom_call" | custom-call | tf_op jit(solution)/shard_map/pallas_call | solution.py:359
  (30 shorter events, 1.7 us)
Async XLA Ops:
  0.0 13.1 %collective-permute-start = (bf16[512,512]{1,0:T(8,128)(2,1)}, bf16[512,512]{1,0:T(8,128)(2,1)S(1)}, u32[]{:S(2)}, u32[]{:S(2)}) collective-permute-start(bf16[512,512]{1,0:T(8,128)(2,1)} %bitcast.16), channel_id=1, source_target_pairs={{0,4},{5,1},{4,8},{9,5},{8,12},{13,9},{12,14},{15,13},{14,10},{11,... | collective-permute-start | bytes 1572872 | tf_op jit(solution)/shard_map/ppermute | solution.py:385
  4.0 8.7 %collective-permute-start.1 = (bf16[256,512]{1,0:T(8,128)(2,1)S(1)}, bf16[256,512]{1,0:T(8,128)(2,1)S(1)}, u32[]{:S(2)}, u32[]{:S(2)}) collective-permute-start(bf16[256,512]{1,0:T(8,128)(2,1)S(1)} %dynamic-slice_bitcast_fusion), channel_id=1, source_target_pairs={{1,4},{4,1},{5,8},{8,5},{9,12},{12,9},{13,14},{14,13},{15,10},{10,... | collective-permute-start | bytes 786440 | tf_op jit(solution)/shard_map/ppermute | solution.py:388
  4.8 12.0 %collective-permute-start.5 = (bf16[512,512]{1,0:T(8,128)(2,1)}, bf16[512,512]{1,0:T(8,128)(2,1)S(1)}, u32[]{:S(2)}, u32[]{:S(2)}) collective-permute-start(bf16[512,512]{1,0:T(8,128)(2,1)} %bitcast.17), channel_id=1, source_target_pairs={{0,1},{1,0},{2,3},{3,2},{4,5},{5,4},{6,7},{7,6},{8,9},{9,8},{10,11... | collective-permute-start | bytes 1572872 | tf_op jit(solution)/shard_map/ppermute | solution.py:391
  5.8 0.7 copy-start.2
  6.4 11.9 %copy-start = (bf16[1,512,512]{2,1,0:T(8,128)(2,1)S(1)}, bf16[1,512,512]{2,1,0:T(8,128)(2,1)}, u32[]{:S(2)}) copy-start(bf16[1,512,512]{2,1,0:T(8,128)(2,1)} %param.5) | copy-start | bytes 1572868
  6.4 11.9 %copy-start.1 = (s32[16]{0:T(128)S(1)}, s32[16]{0:T(128)}, u32[]{:S(2)}) copy-start(s32[16]{0:T(128)} %owner_ref.9) | copy-start | bytes 196
  13.1 6.4 %collective-permute-start.3 = (bf16[512,512]{1,0:T(8,128)(2,1)S(1)}, bf16[512,512]{1,0:T(8,128)(2,1)S(1)}, u32[]{:S(2)}, u32[]{:S(2)}) collective-permute-start(bf16[512,512]{1,0:T(8,128)(2,1)S(1)} %collective-permute-done.refs_0_), channel_id=1, source_target_pairs={{0,1},{1,0},{2,3},{3,2},{4,5},{5,4},{6,7},{7,6},{8,9},{9,8},{10,11... | collective-permute-start | bytes 1572872 | tf_op jit(solution)/shard_map/ppermute | solution.py:391
  13.1 9.2 %collective-permute-start.2 = (bf16[512,512]{1,0:T(8,128)(2,1)S(1)}, bf16[512,512]{1,0:T(8,128)(2,1)S(1)}, u32[]{:S(2)}, u32[]{:S(2)}) collective-permute-start(bf16[512,512]{1,0:T(8,128)(2,1)S(1)} %collective-permute-done.refs_0_), channel_id=1, source_target_pairs={{0,4},{5,1},{4,8},{9,5},{8,12},{13,9},{12,14},{15,13},{14,10},{11,... | collective-permute-start | bytes 1572872 | tf_op jit(solution)/shard_map/ppermute | solution.py:385
  15.2 4.3 %collective-permute-start.4 = (bf16[256,512]{1,0:T(8,128)(2,1)S(1)}, bf16[256,512]{1,0:T(8,128)(2,1)S(1)}, u32[]{:S(2)}, u32[]{:S(2)}) collective-permute-start(bf16[256,512]{1,0:T(8,128)(2,1)S(1)} %collective-permute-done.1.refs_2_), channel_id=1, source_target_pairs={{0,1},{1,0},{2,3},{3,2},{4,5},{5,4},{6,7},{7,6},{8,9},{9,8},{10,11... | collective-permute-start | bytes 786440 | tf_op jit(solution)/shard_map/ppermute | solution.py:391
  15.4 9.7 %collective-permute-start.8 = (bf16[256,512]{1,0:T(8,128)(2,1)S(1)}, bf16[256,512]{1,0:T(8,128)(2,1)S(1)}, u32[]{:S(2)}, u32[]{:S(2)}) collective-permute-start(bf16[256,512]{1,0:T(8,128)(2,1)S(1)} %collective-permute-done.1.refs_2_), channel_id=1, source_target_pairs={{0,4},{5,1},{4,8},{9,5},{8,12},{13,9},{12,14},{15,13},{14,10},{11,... | collective-permute-start | bytes 786440 | tf_op jit(solution)/shard_map/ppermute | solution.py:385
  16.8 8.3 %collective-permute-start.10 = (bf16[256,512]{1,0:T(8,128)(2,1)S(1)}, bf16[256,512]{1,0:T(8,128)(2,1)S(1)}, u32[]{:S(2)}, u32[]{:S(2)}) collective-permute-start(bf16[256,512]{1,0:T(8,128)(2,1)S(1)} %collective-permute-done.1.refs_2_), channel_id=1, source_target_pairs={{0,16},{16,0},{1,17},{17,1},{2,18},{18,2},{3,19},{19,3},{4,20},{20... | collective-permute-start | bytes 786440 | tf_op jit(solution)/shard_map/ppermute | solution.py:394
  22.3 6.9 %collective-permute-start.7 = (bf16[512,512]{1,0:T(8,128)(2,1)S(1)}, bf16[512,512]{1,0:T(8,128)(2,1)S(1)}, u32[]{:S(2)}, u32[]{:S(2)}) collective-permute-start(bf16[512,512]{1,0:T(8,128)(2,1)S(1)} %collective-permute-done.2.refs_0_), channel_id=1, source_target_pairs={{0,1},{1,0},{2,3},{3,2},{4,5},{5,4},{6,7},{7,6},{8,9},{9,8},{10,11... | collective-permute-start | bytes 1572872 | tf_op jit(solution)/shard_map/ppermute | solution.py:391
  22.3 9.2 %collective-permute-start.6 = (bf16[512,512]{1,0:T(8,128)(2,1)S(1)}, bf16[512,512]{1,0:T(8,128)(2,1)S(1)}, u32[]{:S(2)}, u32[]{:S(2)}) collective-permute-start(bf16[512,512]{1,0:T(8,128)(2,1)S(1)} %collective-permute-done.2.refs_0_), channel_id=1, source_target_pairs={{0,4},{5,1},{4,8},{9,5},{8,12},{13,9},{12,14},{15,13},{14,10},{11,... | collective-permute-start | bytes 1572872 | tf_op jit(solution)/shard_map/ppermute | solution.py:385
  25.1 2.6 %collective-permute-start.9 = (bf16[256,512]{1,0:T(8,128)(2,1)S(1)}, bf16[256,512]{1,0:T(8,128)(2,1)S(1)}, u32[]{:S(2)}, u32[]{:S(2)}) collective-permute-start(bf16[256,512]{1,0:T(8,128)(2,1)S(1)} %collective-permute-done.8.refs_2_), channel_id=1, source_target_pairs={{0,1},{1,0},{2,3},{3,2},{4,5},{5,4},{6,7},{7,6},{8,9},{9,8},{10,11... | collective-permute-start | bytes 786440 | tf_op jit(solution)/shard_map/ppermute | solution.py:391
  25.1 4.1 %collective-permute-start.11 = (bf16[256,512]{1,0:T(8,128)(2,1)S(1)}, bf16[256,512]{1,0:T(8,128)(2,1)S(1)}, u32[]{:S(2)}, u32[]{:S(2)}) collective-permute-start(bf16[256,512]{1,0:T(8,128)(2,1)S(1)} %collective-permute-done.10.refs_4_), channel_id=1, source_target_pairs={{0,1},{1,0},{2,3},{3,2},{4,5},{5,4},{6,7},{7,6},{8,9},{9,8},{10,11... | collective-permute-start | bytes 786440 | tf_op jit(solution)/shard_map/ppermute | solution.py:391
  25.7 8.7 %collective-permute-start.14 = (bf16[256,512]{1,0:T(8,128)(2,1)S(1)}, bf16[256,512]{1,0:T(8,128)(2,1)S(1)}, u32[]{:S(2)}, u32[]{:S(2)}) collective-permute-start(bf16[256,512]{1,0:T(8,128)(2,1)S(1)} %collective-permute-done.8.refs_2_), channel_id=1, source_target_pairs={{0,4},{5,1},{4,8},{9,5},{8,12},{13,9},{12,14},{15,13},{14,10},{11,... | collective-permute-start | bytes 786440 | tf_op jit(solution)/shard_map/ppermute | solution.py:385
  27.7 7.9 %collective-permute-start.16 = (bf16[256,512]{1,0:T(8,128)(2,1)S(1)}, bf16[256,512]{1,0:T(8,128)(2,1)S(1)}, u32[]{:S(2)}, u32[]{:S(2)}) collective-permute-start(bf16[256,512]{1,0:T(8,128)(2,1)S(1)} %collective-permute-done.8.refs_2_), channel_id=1, source_target_pairs={{0,16},{16,0},{1,17},{17,1},{2,18},{18,2},{3,19},{19,3},{4,20},{20... | collective-permute-start | bytes 786440 | tf_op jit(solution)/shard_map/ppermute | solution.py:394
  31.5 5.6 %collective-permute-start.13 = (bf16[512,512]{1,0:T(8,128)(2,1)S(1)}, bf16[512,512]{1,0:T(8,128)(2,1)S(1)}, u32[]{:S(2)}, u32[]{:S(2)}) collective-permute-start(bf16[512,512]{1,0:T(8,128)(2,1)S(1)} %collective-permute-done.6.refs_0_), channel_id=1, source_target_pairs={{0,1},{1,0},{2,3},{3,2},{4,5},{5,4},{6,7},{7,6},{8,9},{9,8},{10,11... | collective-permute-start | bytes 1572872 | tf_op jit(solution)/shard_map/ppermute | solution.py:391
  31.5 9.2 %collective-permute-start.12 = (bf16[512,512]{1,0:T(8,128)(2,1)S(1)}, bf16[512,512]{1,0:T(8,128)(2,1)S(1)}, u32[]{:S(2)}, u32[]{:S(2)}) collective-permute-start(bf16[512,512]{1,0:T(8,128)(2,1)S(1)} %collective-permute-done.6.refs_0_), channel_id=1, source_target_pairs={{0,4},{5,1},{4,8},{9,5},{8,12},{13,9},{12,14},{15,13},{14,10},{11,... | collective-permute-start | bytes 1572872 | tf_op jit(solution)/shard_map/ppermute | solution.py:385
  34.3 2.8 %collective-permute-start.15 = (bf16[256,512]{1,0:T(8,128)(2,1)S(1)}, bf16[256,512]{1,0:T(8,128)(2,1)S(1)}, u32[]{:S(2)}, u32[]{:S(2)}) collective-permute-start(bf16[256,512]{1,0:T(8,128)(2,1)S(1)} %collective-permute-done.14.refs_2_), channel_id=1, source_target_pairs={{0,1},{1,0},{2,3},{3,2},{4,5},{5,4},{6,7},{7,6},{8,9},{9,8},{10,11... | collective-permute-start | bytes 786440 | tf_op jit(solution)/shard_map/ppermute | solution.py:391
  35.6 1.5 %collective-permute-start.17 = (bf16[256,512]{1,0:T(8,128)(2,1)S(1)}, bf16[256,512]{1,0:T(8,128)(2,1)S(1)}, u32[]{:S(2)}, u32[]{:S(2)}) collective-permute-start(bf16[256,512]{1,0:T(8,128)(2,1)S(1)} %collective-permute-done.16.refs_4_), channel_id=1, source_target_pairs={{0,1},{1,0},{2,3},{3,2},{4,5},{5,4},{6,7},{7,6},{8,9},{9,8},{10,11... | collective-permute-start | bytes 786440 | tf_op jit(solution)/shard_map/ppermute | solution.py:391
  35.6 8.7 %collective-permute-start.19 = (bf16[256,512]{1,0:T(8,128)(2,1)S(1)}, bf16[256,512]{1,0:T(8,128)(2,1)S(1)}, u32[]{:S(2)}, u32[]{:S(2)}) collective-permute-start(bf16[256,512]{1,0:T(8,128)(2,1)S(1)} %collective-permute-done.14.refs_2_), channel_id=1, source_target_pairs={{0,16},{16,0},{1,17},{17,1},{2,18},{18,2},{3,19},{19,3},{4,20},{20... | collective-permute-start | bytes 786440 | tf_op jit(solution)/shard_map/ppermute | solution.py:394
  40.7 5.2 %collective-permute-start.18 = (bf16[512,512]{1,0:T(8,128)(2,1)S(1)}, bf16[512,512]{1,0:T(8,128)(2,1)S(1)}, u32[]{:S(2)}, u32[]{:S(2)}) collective-permute-start(bf16[512,512]{1,0:T(8,128)(2,1)S(1)} %collective-permute-done.12.refs_0_), channel_id=1, source_target_pairs={{0,1},{1,0},{2,3},{3,2},{4,5},{5,4},{6,7},{7,6},{8,9},{9,8},{10,11... | collective-permute-start | bytes 1572872 | tf_op jit(solution)/shard_map/ppermute | solution.py:391
  44.3 1.5 %collective-permute-start.20 = (bf16[256,512]{1,0:T(8,128)(2,1)S(1)}, bf16[256,512]{1,0:T(8,128)(2,1)S(1)}, u32[]{:S(2)}, u32[]{:S(2)}) collective-permute-start(bf16[256,512]{1,0:T(8,128)(2,1)S(1)} %collective-permute-done.19.refs_2_), channel_id=1, source_target_pairs={{0,1},{1,0},{2,3},{3,2},{4,5},{5,4},{6,7},{7,6},{8,9},{9,8},{10,11... | collective-permute-start | bytes 786440 | tf_op jit(solution)/shard_map/ppermute | solution.py:391
  72.0 18.6 %all-to-all-start.1 = ((s16[16,136,128]{2,1,0:T(8,128)(2,1)}), s16[16,136,128]{2,1,0:T(8,128)(2,1)S(1)}, u32[]{:S(2)}, u32[]{:S(2)}) async-start(s16[16,136,128]{2,1,0:T(8,128)(2,1)} %bitcast.5), calls=%async_computation.1 | async-start | bytes 1114112 | tf_op jit(solution)/shard_map/all_to_all | solution.py:403

commit v5 on v4

--- a/solution.py
+++ b/solution.py
@@ -416,7 +416,7 @@
             whole, acc = lax.optimization_barrier((whole, acc))
         next_whole = around(whole)
         next_part = around(part) if step + 1 < chips // 2 else None
-        rest = across(part)
+        rest = across(part) if next_part is not None else around(late[0])
         acc = project(
             acc,
             rows,

time: 93.1 us -> 92.8 us (level)
  waiting for transfers between devices: 27.9 us -> 26.4 us
    ppermute x3 -> x2, waiting for transfers between devices: 4.92 us -> 0.52 us  [across(): return lax.ppermute(value, 'grp', [(0, 1), (1, 0)])]
    ppermute x6 -> x7, waiting for transfers between devices: 5.26 us -> 8.22 us  [around(): return lax.ppermute(value, 'shell', onward)]
    ppermute x6 -> x7, starting transfers between devices: 12.8 us -> 14.1 us  [around(): return lax.ppermute(value, 'shell', onward)]
    ppermute x3 -> x2, starting transfers between devices: 4.47 us -> 3.49 us  [across(): return lax.ppermute(value, 'grp', [(0, 1), (1, 0)])]
where the time goes in v5:
time: 92.8 us; the launch traced here: 92.6 us
  waiting for transfers between devices  26.4 us (28%)
  starting transfers between devices  23.9 us (26%)
  blocking collectives  23 us (25%)
  Pallas kernels  17.5 us (19%)
  local copies, waits for them, and re-layouts  1.66 us (2%)
    all_to_all x1, blocking collectives, exchange(): return lax.all_to_all(value, 'shell', 0, 0).reshape(parcels.shape)  23 us
    all_to_all x1, waiting for transfers between devices, exchange(): return lax.all_to_all(value, 'shell', 0, 0).reshape(parcels.shape)  14.9 us
    ppermute x7, starting transfers between devices, around(): return lax.ppermute(value, 'shell', onward)  14.1 us
    pallas_call x5, Pallas kernels, project(): pl.pallas_call(functools.partial(project_kernel, lax.axis_size('shell'),...  8.45 us
    ppermute x7, waiting for transfers between devices, around(): return lax.ppermute(value, 'shell', onward)  8.22 us
    pallas_call x1, Pallas kernels, sort_rows(): pl.pallas_call(sort_kernel, in_specs=[pl.BlockSpec(memory_space=pltpu.SME...  5.14 us
    pallas_call x2, Pallas kernels, local_call(): pl.pallas_call(kernel, in_specs=[pl.BlockSpec(memory_space=pltpu.SMEM)] *...  3.89 us
    all_to_all x1, starting transfers between devices, exchange(): return lax.all_to_all(value, 'shell', 0, 0).reshape(parcels.shape)  3.58 us
  transfers between devices with their start and end apart: 22, of which 11 were waited for; matrix products, arithmetic and copies ran while one was open for 1% of the time, Pallas kernels for 12%

profile of v5, /device:TPU:0, one launch (start us, length us, event | category | flops | bytes accessed | tf_op | source)
XLA Modules:
  0.0 92.6 jit_solution(1586855012145813925)
XLA Ops:
  0.0 3.0 %collective-permute-start = (bf16[512,512]{1,0:T(8,128)(2,1)}, bf16[512,512]{1,0:T(8,128)(2,1)S(1)}, u32[]{:S(2)}, u32[]{:S(2)}) collective-permute-start(bf16[512,512]{1,0:T(8,128)(2,1)} %bitcast.16), channel_id=1, source_target_pairs={{0,4},{5,1},{4,8},{9,5},{8,12},{13,9},{12,14},{15,13},{14,10},{11,... | collective-permute-start | bytes 1572872 | tf_op jit(solution)/shard_map/ppermute | solution.py:385
  3.0 1.0 %dynamic-slice_bitcast_fusion = bf16[256,512]{1,0:T(8,128)(2,1)S(1)} fusion(bf16[1,512,512]{2,1,0:T(8,128)(2,1)} %param.5, s32[]{:T(128)S(6)} %select_n.22), kind=kLoop, calls=%fused_computation | loop fusion | bytes 524292 | tf_op jit(solution)/shard_map/dynamic_slice | solution.py:408
  4.0 0.7 collective-permute-start.1
  4.8 1.0 %collective-permute-start.5 = (bf16[512,512]{1,0:T(8,128)(2,1)}, bf16[512,512]{1,0:T(8,128)(2,1)S(1)}, u32[]{:S(2)}, u32[]{:S(2)}) collective-permute-start(bf16[512,512]{1,0:T(8,128)(2,1)} %bitcast.17), channel_id=1, source_target_pairs={{0,1},{1,0},{2,3},{3,2},{4,5},{5,4},{6,7},{7,6},{8,9},{9,8},{10,11... | collective-permute-start | bytes 1572872 | tf_op jit(solution)/shard_map/ppermute | solution.py:391
  5.8 0.7 copy-done.2
  6.4 5.1 %shard_map.46.rows_ref = bf16[16,256,1024]{2,1,0:T(8,128)(2,1)S(1)} custom-call(s32[8]{0:T(128)S(1)} %copy-done.2, bf16[4096,1024]{1,0:T(8,128)(2,1)} %bitcast.19), custom_call_target="tpu_custom_call" | custom-call | flops 2147483648 | bytes 16777216 | tf_op jit(solution)/shard_map/pallas_call | solution.py:137
  11.6 1.2 %collective-permute-done.1.refs_2_ = bf16[256,512]{1,0:T(8,128)(2,1)S(1)} collective-permute-done((bf16[256,512]{1,0:T(8,128)(2,1)S(1)}, bf16[256,512]{1,0:T(8,128)(2,1)S(1)}, u32[]{:S(2)}, u32[]{:S(2)}) %collective-permute-start.1) | collective-permute-done | bytes 262176 | tf_op jit(solution)/shard_map/ppermute | solution.py:388
  13.1 2.1 %collective-permute-start.2 = (bf16[512,512]{1,0:T(8,128)(2,1)S(1)}, bf16[512,512]{1,0:T(8,128)(2,1)S(1)}, u32[]{:S(2)}, u32[]{:S(2)}) collective-permute-start(bf16[512,512]{1,0:T(8,128)(2,1)S(1)} %collective-permute-done.refs_0_), channel_id=1, source_target_pairs={{0,4},{5,1},{4,8},{9,5},{8,12},{13,9},{12,14},{15,13},{14,10},{11,... | collective-permute-start | bytes 1572872 | tf_op jit(solution)/shard_map/ppermute | solution.py:385
  15.4 1.4 %collective-permute-start.8 = (bf16[256,512]{1,0:T(8,128)(2,1)S(1)}, bf16[256,512]{1,0:T(8,128)(2,1)S(1)}, u32[]{:S(2)}, u32[]{:S(2)}) collective-permute-start(bf16[256,512]{1,0:T(8,128)(2,1)S(1)} %collective-permute-done.1.refs_2_), channel_id=1, source_target_pairs={{0,4},{5,1},{4,8},{9,5},{8,12},{13,9},{12,14},{15,13},{14,10},{11,... | collective-permute-start | bytes 786440 | tf_op jit(solution)/shard_map/ppermute | solution.py:385
  16.8 1.5 %collective-permute-start.10 = (bf16[256,512]{1,0:T(8,128)(2,1)S(1)}, bf16[256,512]{1,0:T(8,128)(2,1)S(1)}, u32[]{:S(2)}, u32[]{:S(2)}) collective-permute-start(bf16[256,512]{1,0:T(8,128)(2,1)S(1)} %collective-permute-done.1.refs_2_), channel_id=1, source_target_pairs={{0,16},{16,0},{1,17},{17,1},{2,18},{18,2},{3,19},{19,3},{4,20},{20... | collective-permute-start | bytes 786440 | tf_op jit(solution)/shard_map/ppermute | solution.py:394
  18.3 1.3 %shard_map.47.refs_4_ = f32[512,512]{1,0:T(8,128)S(1)} custom-call(s32[16]{0:T(128)S(1)} %copy-done.1, bf16[16,256,1024]{2,1,0:T(8,128)(2,1)S(1)} %shard_map.46.rows_ref, bf16[512,512]{1,0:T(8,128)(2,1)S(1)} %bitcast.18, bf16[512,512]{1,0:T(8,128)(2,1)S(1)} %collective-permute-done.5.refs_1_), custom_call_target="tpu_custom_call" | custom-call | flops 536870912 | bytes 3145728 | tf_op jit(solution)/shard_map/pallas_call | solution.py:253
  19.6 1.5 %shard_map.48.refs_6_ = f32[512,512]{1,0:T(8,128)S(1)} custom-call(s32[16]{0:T(128)S(1)} %copy-done.1, bf16[16,256,1024]{2,1,0:T(8,128)(2,1)S(1)} %shard_map.46.rows_ref, bf16[512,512]{1,0:T(8,128)(2,1)S(1)} %collective-permute-done.refs_0_, bf16[512,512]{1,0:T(8,128)(2,1)S(1)} %collective-permute-done.3.refs_1_, ...), custom_call_target="tpu_custom_call" | custom-call | flops 805306368 | bytes 5242880 | tf_op jit(solution)/shard_map/pallas_call | solution.py:253
  21.1 1.2 %collective-permute-done.2.refs_0_ = bf16[512,512]{1,0:T(8,128)(2,1)S(1)} collective-permute-done((bf16[512,512]{1,0:T(8,128)(2,1)S(1)}, bf16[512,512]{1,0:T(8,128)(2,1)S(1)}, u32[]{:S(2)}, u32[]{:S(2)}) %collective-permute-start.2) | collective-permute-done | bytes 524320 | tf_op jit(solution)/shard_map/ppermute | solution.py:385
  22.3 2.1 %collective-permute-start.6 = (bf16[512,512]{1,0:T(8,128)(2,1)S(1)}, bf16[512,512]{1,0:T(8,128)(2,1)S(1)}, u32[]{:S(2)}, u32[]{:S(2)}) collective-permute-start(bf16[512,512]{1,0:T(8,128)(2,1)S(1)} %collective-permute-done.2.refs_0_), channel_id=1, source_target_pairs={{0,4},{5,1},{4,8},{9,5},{8,12},{13,9},{12,14},{15,13},{14,10},{11,... | collective-permute-start | bytes 1572872 | tf_op jit(solution)/shard_map/ppermute | solution.py:385
  24.4 0.7 collective-permute-done.8.refs_2_
  25.1 0.5 collective-permute-start.11
  25.7 2.0 %collective-permute-start.16 = (bf16[256,512]{1,0:T(8,128)(2,1)S(1)}, bf16[256,512]{1,0:T(8,128)(2,1)S(1)}, u32[]{:S(2)}, u32[]{:S(2)}) collective-permute-start(bf16[256,512]{1,0:T(8,128)(2,1)S(1)} %collective-permute-done.8.refs_2_), channel_id=1, source_target_pairs={{0,16},{16,0},{1,17},{17,1},{2,18},{18,2},{3,19},{19,3},{4,20},{20... | collective-permute-start | bytes 786440 | tf_op jit(solution)/shard_map/ppermute | solution.py:394
  27.7 1.6 %collective-permute-start.14 = (bf16[256,512]{1,0:T(8,128)(2,1)S(1)}, bf16[256,512]{1,0:T(8,128)(2,1)S(1)}, u32[]{:S(2)}, u32[]{:S(2)}) collective-permute-start(bf16[256,512]{1,0:T(8,128)(2,1)S(1)} %collective-permute-done.8.refs_2_), channel_id=1, source_target_pairs={{0,4},{5,1},{4,8},{9,5},{8,12},{13,9},{12,14},{15,13},{14,10},{11,... | collective-permute-start | bytes 786440 | tf_op jit(solution)/shard_map/ppermute | solution.py:385
  29.2 1.8 %shard_map.49.refs_6_ = f32[512,512]{1,0:T(8,128)S(1)} custom-call(s32[16]{0:T(128)S(1)} %copy-done.1, bf16[16,256,1024]{2,1,0:T(8,128)(2,1)S(1)} %shard_map.46.rows_ref, bf16[512,512]{1,0:T(8,128)(2,1)S(1)} %collective-permute-done.2.refs_0_, bf16[512,512]{1,0:T(8,128)(2,1)S(1)} %collective-permute-done.7.refs_1_, ...), custom_call_target="tpu_custom_call" | custom-call | flops 1073741824 | bytes 6291456 | tf_op jit(solution)/shard_map/pallas_call | solution.py:253
  31.5 2.1 %collective-permute-start.12 = (bf16[512,512]{1,0:T(8,128)(2,1)S(1)}, bf16[512,512]{1,0:T(8,128)(2,1)S(1)}, u32[]{:S(2)}, u32[]{:S(2)}) collective-permute-start(bf16[512,512]{1,0:T(8,128)(2,1)S(1)} %collective-permute-done.6.refs_0_), channel_id=1, source_target_pairs={{0,4},{5,1},{4,8},{9,5},{8,12},{13,9},{12,14},{15,13},{14,10},{11,... | collective-permute-start | bytes 1572872 | tf_op jit(solution)/shard_map/ppermute | solution.py:385
  33.6 0.5 collective-permute-done.16.refs_4_
  34.6 1.8 %collective-permute-start.19 = (bf16[256,512]{1,0:T(8,128)(2,1)S(1)}, bf16[256,512]{1,0:T(8,128)(2,1)S(1)}, u32[]{:S(2)}, u32[]{:S(2)}) collective-permute-start(bf16[256,512]{1,0:T(8,128)(2,1)S(1)} %collective-permute-done.16.refs_4_), channel_id=1, source_target_pairs={{0,4},{5,1},{4,8},{9,5},{8,12},{13,9},{12,14},{15,13},{14,10},{11,... | collective-permute-start | bytes 786440 | tf_op jit(solution)/shard_map/ppermute | solution.py:385
  36.5 1.8 %shard_map.50.refs_4_ = f32[512,512]{1,0:T(8,128)S(1)} custom-call(s32[16]{0:T(128)S(1)} %copy-done.1, bf16[16,256,1024]{2,1,0:T(8,128)(2,1)S(1)} %shard_map.46.rows_ref, bf16[512,512]{1,0:T(8,128)(2,1)S(1)} %collective-permute-done.6.refs_0_, bf16[512,512]{1,0:T(8,128)(2,1)S(1)} %collective-permute-done.13.refs_1_, ...), custom_call_target="tpu_custom_call" | custom-call | flops 1073741824 | bytes 6291456 | tf_op jit(solution)/shard_map/pallas_call | solution.py:253
  38.3 2.4 %collective-permute-done.12.refs_0_ = bf16[512,512]{1,0:T(8,128)(2,1)S(1)} collective-permute-done((bf16[512,512]{1,0:T(8,128)(2,1)S(1)}, bf16[512,512]{1,0:T(8,128)(2,1)S(1)}, u32[]{:S(2)}, u32[]{:S(2)}) %collective-permute-start.12) | collective-permute-done | bytes 524320 | tf_op jit(solution)/shard_map/ppermute | solution.py:385
  40.7 2.8 %collective-permute-done.19.refs_2_ = bf16[256,512]{1,0:T(8,128)(2,1)S(1)} collective-permute-done((bf16[256,512]{1,0:T(8,128)(2,1)S(1)}, bf16[256,512]{1,0:T(8,128)(2,1)S(1)}, u32[]{:S(2)}, u32[]{:S(2)}) %collective-permute-start.19) | collective-permute-done | bytes 262176 | tf_op jit(solution)/shard_map/ppermute | solution.py:385
  43.5 1.5 %collective-permute-done.20.refs_3_ = bf16[256,512]{1,0:T(8,128)(2,1)S(1)} collective-permute-done((bf16[256,512]{1,0:T(8,128)(2,1)S(1)}, bf16[256,512]{1,0:T(8,128)(2,1)S(1)}, u32[]{:S(2)}, u32[]{:S(2)}) %collective-permute-start.20) | collective-permute-done | bytes 262176 | tf_op jit(solution)/shard_map/ppermute | solution.py:391
  45.0 2.1 %shard_map.51 = s16[2176,128]{1,0:T(8,128)(2,1)S(1)} custom-call(s32[16]{0:T(128)S(1)} %copy-done.1, bf16[16,256,1024]{2,1,0:T(8,128)(2,1)S(1)} %shard_map.46.rows_ref, bf16[512,512]{1,0:T(8,128)(2,1)S(1)} %collective-permute-done.12.refs_0_, bf16[512,512]{1,0:T(8,128)(2,1)S(1)} %collective-permute-done.18.refs_1_, ...), custom_call_target="tpu_custom_call" | custom-call | flops 805306368 | bytes 5242880 | tf_op jit(solution)/shard_map/pallas_call | solution.py:253
  47.1 23.0 %all_to_all.10 = s16[16,136,128]{2,1,0:T(8,128)(2,1)S(1)} all-to-all(s16[16,136,128]{2,1,0:T(8,128)(2,1)S(1)} %bitcast.13), channel_id=1, replica_groups=mesh['grp'=2,'shell'=16] {'shell'}, dimensions={0} | all-to-all | bytes 1114112 | tf_op jit(solution)/shard_map/all_to_all | solution.py:403
  70.1 1.7 %shard_map.52 = s16[2176,128]{1,0:T(8,128)(2,1)} custom-call(s16[2176,128]{1,0:T(8,128)(2,1)S(1)} %bitcast.15), custom_call_target="tpu_custom_call" | custom-call | tf_op jit(solution)/shard_map/pallas_call | solution.py:359
  71.8 3.6 %all-to-all-start.1 = ((s16[16,136,128]{2,1,0:T(8,128)(2,1)}), s16[16,136,128]{2,1,0:T(8,128)(2,1)S(1)}, u32[]{:S(2)}, u32[]{:S(2)}) async-start(s16[16,136,128]{2,1,0:T(8,128)(2,1)} %bitcast.5), calls=%async_computation.1 | async-start | bytes 1114112 | tf_op jit(solution)/shard_map/all_to_all | solution.py:403
  75.5 14.9 %all-to-all-done.1 = s16[16,136,128]{2,1,0:T(8,128)(2,1)S(1)} async-done(((s16[16,136,128]{2,1,0:T(8,128)(2,1)}), s16[16,136,128]{2,1,0:T(8,128)(2,1)S(1)}, u32[]{:S(2)}, u32[]{:S(2)}) %all-to-all-start.1) | async-done | bytes 557088 | tf_op jit(solution)/shard_map/all_to_all | solution.py:403
  90.4 2.2 %shard_map.53 = f32[2048,128]{1,0:T(8,128)} custom-call(f32[2,32]{1,0:T(2,128)S(1)} %maximum_multiply_fusion.twist_ref, s16[2176,128]{1,0:T(8,128)(2,1)S(1)} %bitcast.14), custom_call_target="tpu_custom_call" | custom-call | tf_op jit(solution)/shard_map/pallas_call | solution.py:359
  (30 shorter events, 1.7 us)
Async XLA Ops:
  0.0 13.1 %collective-permute-start = (bf16[512,512]{1,0:T(8,128)(2,1)}, bf16[512,512]{1,0:T(8,128)(2,1)S(1)}, u32[]{:S(2)}, u32[]{:S(2)}) collective-permute-start(bf16[512,512]{1,0:T(8,128)(2,1)} %bitcast.16), channel_id=1, source_target_pairs={{0,4},{5,1},{4,8},{9,5},{8,12},{13,9},{12,14},{15,13},{14,10},{11,... | collective-permute-start | bytes 1572872 | tf_op jit(solution)/shard_map/ppermute | solution.py:385
  4.0 8.7 %collective-permute-start.1 = (bf16[256,512]{1,0:T(8,128)(2,1)S(1)}, bf16[256,512]{1,0:T(8,128)(2,1)S(1)}, u32[]{:S(2)}, u32[]{:S(2)}) collective-permute-start(bf16[256,512]{1,0:T(8,128)(2,1)S(1)} %dynamic-slice_bitcast_fusion), channel_id=1, source_target_pairs={{1,4},{4,1},{5,8},{8,5},{9,12},{12,9},{13,14},{14,13},{15,10},{10,... | collective-permute-start | bytes 786440 | tf_op jit(solution)/shard_map/ppermute | solution.py:388
  4.8 12.0 %collective-permute-start.5 = (bf16[512,512]{1,0:T(8,128)(2,1)}, bf16[512,512]{1,0:T(8,128)(2,1)S(1)}, u32[]{:S(2)}, u32[]{:S(2)}) collective-permute-start(bf16[512,512]{1,0:T(8,128)(2,1)} %bitcast.17), channel_id=1, source_target_pairs={{0,1},{1,0},{2,3},{3,2},{4,5},{5,4},{6,7},{7,6},{8,9},{9,8},{10,11... | collective-permute-start | bytes 1572872 | tf_op jit(solution)/shard_map/ppermute | solution.py:391
  5.8 0.7 copy-start.2
  6.4 11.9 %copy-start = (bf16[1,512,512]{2,1,0:T(8,128)(2,1)S(1)}, bf16[1,512,512]{2,1,0:T(8,128)(2,1)}, u32[]{:S(2)}) copy-start(bf16[1,512,512]{2,1,0:T(8,128)(2,1)} %param.5) | copy-start | bytes 1572868
  6.4 11.9 %copy-start.1 = (s32[16]{0:T(128)S(1)}, s32[16]{0:T(128)}, u32[]{:S(2)}) copy-start(s32[16]{0:T(128)} %owner_ref.9) | copy-start | bytes 196
  13.1 6.4 %collective-permute-start.3 = (bf16[512,512]{1,0:T(8,128)(2,1)S(1)}, bf16[512,512]{1,0:T(8,128)(2,1)S(1)}, u32[]{:S(2)}, u32[]{:S(2)}) collective-permute-start(bf16[512,512]{1,0:T(8,128)(2,1)S(1)} %collective-permute-done.refs_0_), channel_id=1, source_target_pairs={{0,1},{1,0},{2,3},{3,2},{4,5},{5,4},{6,7},{7,6},{8,9},{9,8},{10,11... | collective-permute-start | bytes 1572872 | tf_op jit(solution)/shard_map/ppermute | solution.py:391
  13.1 9.2 %collective-permute-start.2 = (bf16[512,512]{1,0:T(8,128)(2,1)S(1)}, bf16[512,512]{1,0:T(8,128)(2,1)S(1)}, u32[]{:S(2)}, u32[]{:S(2)}) collective-permute-start(bf16[512,512]{1,0:T(8,128)(2,1)S(1)} %collective-permute-done.refs_0_), channel_id=1, source_target_pairs={{0,4},{5,1},{4,8},{9,5},{8,12},{13,9},{12,14},{15,13},{14,10},{11,... | collective-permute-start | bytes 1572872 | tf_op jit(solution)/shard_map/ppermute | solution.py:385
  15.2 4.3 %collective-permute-start.4 = (bf16[256,512]{1,0:T(8,128)(2,1)S(1)}, bf16[256,512]{1,0:T(8,128)(2,1)S(1)}, u32[]{:S(2)}, u32[]{:S(2)}) collective-permute-start(bf16[256,512]{1,0:T(8,128)(2,1)S(1)} %collective-permute-done.1.refs_2_), channel_id=1, source_target_pairs={{0,1},{1,0},{2,3},{3,2},{4,5},{5,4},{6,7},{7,6},{8,9},{9,8},{10,11... | collective-permute-start | bytes 786440 | tf_op jit(solution)/shard_map/ppermute | solution.py:391
  15.4 9.7 %collective-permute-start.8 = (bf16[256,512]{1,0:T(8,128)(2,1)S(1)}, bf16[256,512]{1,0:T(8,128)(2,1)S(1)}, u32[]{:S(2)}, u32[]{:S(2)}) collective-permute-start(bf16[256,512]{1,0:T(8,128)(2,1)S(1)} %collective-permute-done.1.refs_2_), channel_id=1, source_target_pairs={{0,4},{5,1},{4,8},{9,5},{8,12},{13,9},{12,14},{15,13},{14,10},{11,... | collective-permute-start | bytes 786440 | tf_op jit(solution)/shard_map/ppermute | solution.py:385
  16.8 8.3 %collective-permute-start.10 = (bf16[256,512]{1,0:T(8,128)(2,1)S(1)}, bf16[256,512]{1,0:T(8,128)(2,1)S(1)}, u32[]{:S(2)}, u32[]{:S(2)}) collective-permute-start(bf16[256,512]{1,0:T(8,128)(2,1)S(1)} %collective-permute-done.1.refs_2_), channel_id=1, source_target_pairs={{0,16},{16,0},{1,17},{17,1},{2,18},{18,2},{3,19},{19,3},{4,20},{20... | collective-permute-start | bytes 786440 | tf_op jit(solution)/shard_map/ppermute | solution.py:394
  22.3 6.9 %collective-permute-start.7 = (bf16[512,512]{1,0:T(8,128)(2,1)S(1)}, bf16[512,512]{1,0:T(8,128)(2,1)S(1)}, u32[]{:S(2)}, u32[]{:S(2)}) collective-permute-start(bf16[512,512]{1,0:T(8,128)(2,1)S(1)} %collective-permute-done.2.refs_0_), channel_id=1, source_target_pairs={{0,1},{1,0},{2,3},{3,2},{4,5},{5,4},{6,7},{7,6},{8,9},{9,8},{10,11... | collective-permute-start | bytes 1572872 | tf_op jit(solution)/shard_map/ppermute | solution.py:391
  22.3 9.2 %collective-permute-start.6 = (bf16[512,512]{1,0:T(8,128)(2,1)S(1)}, bf16[512,512]{1,0:T(8,128)(2,1)S(1)}, u32[]{:S(2)}, u32[]{:S(2)}) collective-permute-start(bf16[512,512]{1,0:T(8,128)(2,1)S(1)} %collective-permute-done.2.refs_0_), channel_id=1, source_target_pairs={{0,4},{5,1},{4,8},{9,5},{8,12},{13,9},{12,14},{15,13},{14,10},{11,... | collective-permute-start | bytes 1572872 | tf_op jit(solution)/shard_map/ppermute | solution.py:385
  25.1 2.5 %collective-permute-start.9 = (bf16[256,512]{1,0:T(8,128)(2,1)S(1)}, bf16[256,512]{1,0:T(8,128)(2,1)S(1)}, u32[]{:S(2)}, u32[]{:S(2)}) collective-permute-start(bf16[256,512]{1,0:T(8,128)(2,1)S(1)} %collective-permute-done.8.refs_2_), channel_id=1, source_target_pairs={{0,1},{1,0},{2,3},{3,2},{4,5},{5,4},{6,7},{7,6},{8,9},{9,8},{10,11... | collective-permute-start | bytes 786440 | tf_op jit(solution)/shard_map/ppermute | solution.py:391
  25.1 4.1 %collective-permute-start.11 = (bf16[256,512]{1,0:T(8,128)(2,1)S(1)}, bf16[256,512]{1,0:T(8,128)(2,1)S(1)}, u32[]{:S(2)}, u32[]{:S(2)}) collective-permute-start(bf16[256,512]{1,0:T(8,128)(2,1)S(1)} %collective-permute-done.10.refs_4_), channel_id=1, source_target_pairs={{0,1},{1,0},{2,3},{3,2},{4,5},{5,4},{6,7},{7,6},{8,9},{9,8},{10,11... | collective-permute-start | bytes 786440 | tf_op jit(solution)/shard_map/ppermute | solution.py:391
  25.7 8.5 %collective-permute-start.16 = (bf16[256,512]{1,0:T(8,128)(2,1)S(1)}, bf16[256,512]{1,0:T(8,128)(2,1)S(1)}, u32[]{:S(2)}, u32[]{:S(2)}) collective-permute-start(bf16[256,512]{1,0:T(8,128)(2,1)S(1)} %collective-permute-done.8.refs_2_), channel_id=1, source_target_pairs={{0,16},{16,0},{1,17},{17,1},{2,18},{18,2},{3,19},{19,3},{4,20},{20... | collective-permute-start | bytes 786440 | tf_op jit(solution)/shard_map/ppermute | solution.py:394
  27.7 6.7 %collective-permute-start.14 = (bf16[256,512]{1,0:T(8,128)(2,1)S(1)}, bf16[256,512]{1,0:T(8,128)(2,1)S(1)}, u32[]{:S(2)}, u32[]{:S(2)}) collective-permute-start(bf16[256,512]{1,0:T(8,128)(2,1)S(1)} %collective-permute-done.8.refs_2_), channel_id=1, source_target_pairs={{0,4},{5,1},{4,8},{9,5},{8,12},{13,9},{12,14},{15,13},{14,10},{11,... | collective-permute-start | bytes 786440 | tf_op jit(solution)/shard_map/ppermute | solution.py:385
  31.5 5.0 %collective-permute-start.13 = (bf16[512,512]{1,0:T(8,128)(2,1)S(1)}, bf16[512,512]{1,0:T(8,128)(2,1)S(1)}, u32[]{:S(2)}, u32[]{:S(2)}) collective-permute-start(bf16[512,512]{1,0:T(8,128)(2,1)S(1)} %collective-permute-done.6.refs_0_), channel_id=1, source_target_pairs={{0,1},{1,0},{2,3},{3,2},{4,5},{5,4},{6,7},{7,6},{8,9},{9,8},{10,11... | collective-permute-start | bytes 1572872 | tf_op jit(solution)/shard_map/ppermute | solution.py:391
  31.5 9.2 %collective-permute-start.12 = (bf16[512,512]{1,0:T(8,128)(2,1)S(1)}, bf16[512,512]{1,0:T(8,128)(2,1)S(1)}, u32[]{:S(2)}, u32[]{:S(2)}) collective-permute-start(bf16[512,512]{1,0:T(8,128)(2,1)S(1)} %collective-permute-done.6.refs_0_), channel_id=1, source_target_pairs={{0,4},{5,1},{4,8},{9,5},{8,12},{13,9},{12,14},{15,13},{14,10},{11,... | collective-permute-start | bytes 1572872 | tf_op jit(solution)/shard_map/ppermute | solution.py:385
  34.1 2.3 %collective-permute-start.17 = (bf16[256,512]{1,0:T(8,128)(2,1)S(1)}, bf16[256,512]{1,0:T(8,128)(2,1)S(1)}, u32[]{:S(2)}, u32[]{:S(2)}) collective-permute-start(bf16[256,512]{1,0:T(8,128)(2,1)S(1)} %collective-permute-done.16.refs_4_), channel_id=1, source_target_pairs={{0,1},{1,0},{2,3},{3,2},{4,5},{5,4},{6,7},{7,6},{8,9},{9,8},{10,11... | collective-permute-start | bytes 786440 | tf_op jit(solution)/shard_map/ppermute | solution.py:391
  34.3 2.1 %collective-permute-start.15 = (bf16[256,512]{1,0:T(8,128)(2,1)S(1)}, bf16[256,512]{1,0:T(8,128)(2,1)S(1)}, u32[]{:S(2)}, u32[]{:S(2)}) collective-permute-start(bf16[256,512]{1,0:T(8,128)(2,1)S(1)} %collective-permute-done.14.refs_2_), channel_id=1, source_target_pairs={{0,1},{1,0},{2,3},{3,2},{4,5},{5,4},{6,7},{7,6},{8,9},{9,8},{10,11... | collective-permute-start | bytes 786440 | tf_op jit(solution)/shard_map/ppermute | solution.py:391
  34.6 8.9 %collective-permute-start.19 = (bf16[256,512]{1,0:T(8,128)(2,1)S(1)}, bf16[256,512]{1,0:T(8,128)(2,1)S(1)}, u32[]{:S(2)}, u32[]{:S(2)}) collective-permute-start(bf16[256,512]{1,0:T(8,128)(2,1)S(1)} %collective-permute-done.16.refs_4_), channel_id=1, source_target_pairs={{0,4},{5,1},{4,8},{9,5},{8,12},{13,9},{12,14},{15,13},{14,10},{11,... | collective-permute-start | bytes 786440 | tf_op jit(solution)/shard_map/ppermute | solution.py:385
  40.7 4.3 %collective-permute-start.18 = (bf16[512,512]{1,0:T(8,128)(2,1)S(1)}, bf16[512,512]{1,0:T(8,128)(2,1)S(1)}, u32[]{:S(2)}, u32[]{:S(2)}) collective-permute-start(bf16[512,512]{1,0:T(8,128)(2,1)S(1)} %collective-permute-done.12.refs_0_), channel_id=1, source_target_pairs={{0,1},{1,0},{2,3},{3,2},{4,5},{5,4},{6,7},{7,6},{8,9},{9,8},{10,11... | collective-permute-start | bytes 1572872 | tf_op jit(solution)/shard_map/ppermute | solution.py:391
  43.5 1.5 %collective-permute-start.20 = (bf16[256,512]{1,0:T(8,128)(2,1)S(1)}, bf16[256,512]{1,0:T(8,128)(2,1)S(1)}, u32[]{:S(2)}, u32[]{:S(2)}) collective-permute-start(bf16[256,512]{1,0:T(8,128)(2,1)S(1)} %collective-permute-done.19.refs_2_), channel_id=1, source_target_pairs={{0,1},{1,0},{2,3},{3,2},{4,5},{5,4},{6,7},{7,6},{8,9},{9,8},{10,11... | collective-permute-start | bytes 786440 | tf_op jit(solution)/shard_map/ppermute | solution.py:391
  71.8 18.6 %all-to-all-start.1 = ((s16[16,136,128]{2,1,0:T(8,128)(2,1)}), s16[16,136,128]{2,1,0:T(8,128)(2,1)S(1)}, u32[]{:S(2)}, u32[]{:S(2)}) async-start(s16[16,136,128]{2,1,0:T(8,128)(2,1)} %bitcast.5), calls=%async_computation.1 | async-start | bytes 1114112 | tf_op jit(solution)/shard_map/all_to_all | solution.py:403

commit v6 on v5

--- a/solution.py
+++ b/solution.py
@@ -427,12 +427,14 @@
         late, late_from = [rest, sibling(rest)], [(-step, 1, 1), (step, 0, 1)]
         whole, part = next_whole, next_part
     whole, acc = lax.optimization_barrier((whole, acc))
+    far = chips // 2
+    acc = project(acc, rows, degree_owner, [whole, late[0]], [(-far, 0, None), late_from[0]])
     sent = project(
         acc,
         rows,
         degree_owner,
-        [whole, sibling(whole), *late],
-        [(-(chips // 2), 0, None), (chips // 2, 1, None), *late_from],
+        [sibling(whole), late[1]],
+        [(far, 1, None), late_from[1]],
         packed=parcels,
     )
     sent = local_call(outer_kernel, parcels, [lines, stage], exchange(sent))

time: 92.8 us -> 92.4 us (level)
  waiting for transfers between devices: 26.4 us -> 25.2 us
    ppermute x11, waiting for transfers between devices: 1.56 us -> 0.43 us  [sibling(): return lax.ppermute(value, 'shell', [(s, s ^ 1) for s in range(devices)])]
    pallas_call x5 -> x6, Pallas kernels: 8.45 us -> 9.16 us  [project(): pl.pallas_call(functools.partial(project_kernel, lax.axis_size('shell'),...]
  transfers between devices with their start and end apart: 22 -> 22, of which waited for: 11 -> 11; matrix products, arithmetic and copies ran while one was open for 1% -> 1% of each run, Pallas kernels for 12% -> 14%
where the time goes in v6:
time: 92.4 us; the launch traced here: 92.2 us
  waiting for transfers between devices  25.2 us (27%)
  starting transfers between devices  23.9 us (26%)
  blocking collectives  23 us (25%)
  Pallas kernels  18.2 us (20%)
  local copies, waits for them, and re-layouts  1.66 us (2%)
    all_to_all x1, blocking collectives, exchange(): return lax.all_to_all(value, 'shell', 0, 0).reshape(parcels.shape)  23 us
    all_to_all x1, waiting for transfers between devices, exchange(): return lax.all_to_all(value, 'shell', 0, 0).reshape(parcels.shape)  14.9 us
    ppermute x7, starting transfers between devices, around(): return lax.ppermute(value, 'shell', onward)  14.1 us
    pallas_call x6, Pallas kernels, project(): pl.pallas_call(functools.partial(project_kernel, lax.axis_size('shell'),...  9.16 us
    ppermute x7, waiting for transfers between devices, around(): return lax.ppermute(value, 'shell', onward)  8.22 us
    pallas_call x1, Pallas kernels, sort_rows(): pl.pallas_call(sort_kernel, in_specs=[pl.BlockSpec(memory_space=pltpu.SME...  5.14 us
    pallas_call x2, Pallas kernels, local_call(): pl.pallas_call(kernel, in_specs=[pl.BlockSpec(memory_space=pltpu.SMEM)] *...  3.89 us
    all_to_all x1, starting transfers between devices, exchange(): return lax.all_to_all(value, 'shell', 0, 0).reshape(parcels.shape)  3.58 us
  transfers between devices with their start and end apart: 22, of which 11 were waited for; matrix products, arithmetic and copies ran while one was open for 1% of the time, Pallas kernels for 14%

profile of v6, /device:TPU:0, one launch (start us, length us, event | category | flops | bytes accessed | tf_op | source)
XLA Modules:
  0.0 92.2 jit_solution(1364304678496651423)
XLA Ops:
  0.0 3.0 %collective-permute-start = (bf16[512,512]{1,0:T(8,128)(2,1)}, bf16[512,512]{1,0:T(8,128)(2,1)S(1)}, u32[]{:S(2)}, u32[]{:S(2)}) collective-permute-start(bf16[512,512]{1,0:T(8,128)(2,1)} %bitcast.16), channel_id=1, source_target_pairs={{0,4},{5,1},{4,8},{9,5},{8,12},{13,9},{12,14},{15,13},{14,10},{11,... | collective-permute-start | bytes 1572872 | tf_op jit(solution)/shard_map/ppermute | solution.py:385
  3.0 1.0 %dynamic-slice_bitcast_fusion = bf16[256,512]{1,0:T(8,128)(2,1)S(1)} fusion(bf16[1,512,512]{2,1,0:T(8,128)(2,1)} %param.5, s32[]{:T(128)S(6)} %select_n.22), kind=kLoop, calls=%fused_computation | loop fusion | bytes 524292 | tf_op jit(solution)/shard_map/dynamic_slice | solution.py:408
  4.0 0.7 collective-permute-start.1
  4.8 1.0 %collective-permute-start.5 = (bf16[512,512]{1,0:T(8,128)(2,1)}, bf16[512,512]{1,0:T(8,128)(2,1)S(1)}, u32[]{:S(2)}, u32[]{:S(2)}) collective-permute-start(bf16[512,512]{1,0:T(8,128)(2,1)} %bitcast.17), channel_id=1, source_target_pairs={{0,1},{1,0},{2,3},{3,2},{4,5},{5,4},{6,7},{7,6},{8,9},{9,8},{10,11... | collective-permute-start | bytes 1572872 | tf_op jit(solution)/shard_map/ppermute | solution.py:391
  5.8 0.7 copy-done.2
  6.4 5.1 %shard_map.46.rows_ref = bf16[16,256,1024]{2,1,0:T(8,128)(2,1)S(1)} custom-call(s32[8]{0:T(128)S(1)} %copy-done.2, bf16[4096,1024]{1,0:T(8,128)(2,1)} %bitcast.19), custom_call_target="tpu_custom_call" | custom-call | flops 2147483648 | bytes 16777216 | tf_op jit(solution)/shard_map/pallas_call | solution.py:137
  11.6 1.2 %collective-permute-done.1.refs_2_ = bf16[256,512]{1,0:T(8,128)(2,1)S(1)} collective-permute-done((bf16[256,512]{1,0:T(8,128)(2,1)S(1)}, bf16[256,512]{1,0:T(8,128)(2,1)S(1)}, u32[]{:S(2)}, u32[]{:S(2)}) %collective-permute-start.1) | collective-permute-done | bytes 262176 | tf_op jit(solution)/shard_map/ppermute | solution.py:388
  13.1 2.1 %collective-permute-start.2 = (bf16[512,512]{1,0:T(8,128)(2,1)S(1)}, bf16[512,512]{1,0:T(8,128)(2,1)S(1)}, u32[]{:S(2)}, u32[]{:S(2)}) collective-permute-start(bf16[512,512]{1,0:T(8,128)(2,1)S(1)} %collective-permute-done.refs_0_), channel_id=1, source_target_pairs={{0,4},{5,1},{4,8},{9,5},{8,12},{13,9},{12,14},{15,13},{14,10},{11,... | collective-permute-start | bytes 1572872 | tf_op jit(solution)/shard_map/ppermute | solution.py:385
  15.4 1.4 %collective-permute-start.8 = (bf16[256,512]{1,0:T(8,128)(2,1)S(1)}, bf16[256,512]{1,0:T(8,128)(2,1)S(1)}, u32[]{:S(2)}, u32[]{:S(2)}) collective-permute-start(bf16[256,512]{1,0:T(8,128)(2,1)S(1)} %collective-permute-done.1.refs_2_), channel_id=1, source_target_pairs={{0,4},{5,1},{4,8},{9,5},{8,12},{13,9},{12,14},{15,13},{14,10},{11,... | collective-permute-start | bytes 786440 | tf_op jit(solution)/shard_map/ppermute | solution.py:385
  16.8 1.5 %collective-permute-start.10 = (bf16[256,512]{1,0:T(8,128)(2,1)S(1)}, bf16[256,512]{1,0:T(8,128)(2,1)S(1)}, u32[]{:S(2)}, u32[]{:S(2)}) collective-permute-start(bf16[256,512]{1,0:T(8,128)(2,1)S(1)} %collective-permute-done.1.refs_2_), channel_id=1, source_target_pairs={{0,16},{16,0},{1,17},{17,1},{2,18},{18,2},{3,19},{19,3},{4,20},{20... | collective-permute-start | bytes 786440 | tf_op jit(solution)/shard_map/ppermute | solution.py:394
  18.3 1.3 %shard_map.47.refs_4_ = f32[512,512]{1,0:T(8,128)S(1)} custom-call(s32[16]{0:T(128)S(1)} %copy-done.1, bf16[16,256,1024]{2,1,0:T(8,128)(2,1)S(1)} %shard_map.46.rows_ref, bf16[512,512]{1,0:T(8,128)(2,1)S(1)} %bitcast.18, bf16[512,512]{1,0:T(8,128)(2,1)S(1)} %collective-permute-done.5.refs_1_), custom_call_target="tpu_custom_call" | custom-call | flops 536870912 | bytes 3145728 | tf_op jit(solution)/shard_map/pallas_call | solution.py:253
  19.6 1.5 %shard_map.48.refs_6_ = f32[512,512]{1,0:T(8,128)S(1)} custom-call(s32[16]{0:T(128)S(1)} %copy-done.1, bf16[16,256,1024]{2,1,0:T(8,128)(2,1)S(1)} %shard_map.46.rows_ref, bf16[512,512]{1,0:T(8,128)(2,1)S(1)} %collective-permute-done.refs_0_, bf16[512,512]{1,0:T(8,128)(2,1)S(1)} %collective-permute-done.3.refs_1_, ...), custom_call_target="tpu_custom_call" | custom-call | flops 805306368 | bytes 5242880 | tf_op jit(solution)/shard_map/pallas_call | solution.py:253
  21.1 1.2 %collective-permute-done.2.refs_0_ = bf16[512,512]{1,0:T(8,128)(2,1)S(1)} collective-permute-done((bf16[512,512]{1,0:T(8,128)(2,1)S(1)}, bf16[512,512]{1,0:T(8,128)(2,1)S(1)}, u32[]{:S(2)}, u32[]{:S(2)}) %collective-permute-start.2) | collective-permute-done | bytes 524320 | tf_op jit(solution)/shard_map/ppermute | solution.py:385
  22.3 2.1 %collective-permute-start.6 = (bf16[512,512]{1,0:T(8,128)(2,1)S(1)}, bf16[512,512]{1,0:T(8,128)(2,1)S(1)}, u32[]{:S(2)}, u32[]{:S(2)}) collective-permute-start(bf16[512,512]{1,0:T(8,128)(2,1)S(1)} %collective-permute-done.2.refs_0_), channel_id=1, source_target_pairs={{0,4},{5,1},{4,8},{9,5},{8,12},{13,9},{12,14},{15,13},{14,10},{11,... | collective-permute-start | bytes 1572872 | tf_op jit(solution)/shard_map/ppermute | solution.py:385
  24.4 0.7 collective-permute-done.8.refs_2_
  25.1 0.5 collective-permute-start.11
  25.7 2.0 %collective-permute-start.16 = (bf16[256,512]{1,0:T(8,128)(2,1)S(1)}, bf16[256,512]{1,0:T(8,128)(2,1)S(1)}, u32[]{:S(2)}, u32[]{:S(2)}) collective-permute-start(bf16[256,512]{1,0:T(8,128)(2,1)S(1)} %collective-permute-done.8.refs_2_), channel_id=1, source_target_pairs={{0,16},{16,0},{1,17},{17,1},{2,18},{18,2},{3,19},{19,3},{4,20},{20... | collective-permute-start | bytes 786440 | tf_op jit(solution)/shard_map/ppermute | solution.py:394
  27.7 1.6 %collective-permute-start.14 = (bf16[256,512]{1,0:T(8,128)(2,1)S(1)}, bf16[256,512]{1,0:T(8,128)(2,1)S(1)}, u32[]{:S(2)}, u32[]{:S(2)}) collective-permute-start(bf16[256,512]{1,0:T(8,128)(2,1)S(1)} %collective-permute-done.8.refs_2_), channel_id=1, source_target_pairs={{0,4},{5,1},{4,8},{9,5},{8,12},{13,9},{12,14},{15,13},{14,10},{11,... | collective-permute-start | bytes 786440 | tf_op jit(solution)/shard_map/ppermute | solution.py:385
  29.2 1.8 %shard_map.49.refs_6_ = f32[512,512]{1,0:T(8,128)S(1)} custom-call(s32[16]{0:T(128)S(1)} %copy-done.1, bf16[16,256,1024]{2,1,0:T(8,128)(2,1)S(1)} %shard_map.46.rows_ref, bf16[512,512]{1,0:T(8,128)(2,1)S(1)} %collective-permute-done.2.refs_0_, bf16[512,512]{1,0:T(8,128)(2,1)S(1)} %collective-permute-done.7.refs_1_, ...), custom_call_target="tpu_custom_call" | custom-call | flops 1073741824 | bytes 6291456 | tf_op jit(solution)/shard_map/pallas_call | solution.py:253
  31.5 2.1 %collective-permute-start.12 = (bf16[512,512]{1,0:T(8,128)(2,1)S(1)}, bf16[512,512]{1,0:T(8,128)(2,1)S(1)}, u32[]{:S(2)}, u32[]{:S(2)}) collective-permute-start(bf16[512,512]{1,0:T(8,128)(2,1)S(1)} %collective-permute-done.6.refs_0_), channel_id=1, source_target_pairs={{0,4},{5,1},{4,8},{9,5},{8,12},{13,9},{12,14},{15,13},{14,10},{11,... | collective-permute-start | bytes 1572872 | tf_op jit(solution)/shard_map/ppermute | solution.py:385
  33.6 0.5 collective-permute-done.16.refs_4_
  34.6 1.8 %collective-permute-start.19 = (bf16[256,512]{1,0:T(8,128)(2,1)S(1)}, bf16[256,512]{1,0:T(8,128)(2,1)S(1)}, u32[]{:S(2)}, u32[]{:S(2)}) collective-permute-start(bf16[256,512]{1,0:T(8,128)(2,1)S(1)} %collective-permute-done.16.refs_4_), channel_id=1, source_target_pairs={{0,4},{5,1},{4,8},{9,5},{8,12},{13,9},{12,14},{15,13},{14,10},{11,... | collective-permute-start | bytes 786440 | tf_op jit(solution)/shard_map/ppermute | solution.py:385
  36.5 1.8 %shard_map.50.refs_2_ = f32[512,512]{1,0:T(8,128)S(1)} custom-call(s32[16]{0:T(128)S(1)} %copy-done.1, bf16[16,256,1024]{2,1,0:T(8,128)(2,1)S(1)} %shard_map.46.rows_ref, bf16[512,512]{1,0:T(8,128)(2,1)S(1)} %collective-permute-done.6.refs_0_, bf16[512,512]{1,0:T(8,128)(2,1)S(1)} %collective-permute-done.13.refs_1_, ...), custom_call_target="tpu_custom_call" | custom-call | flops 1073741824 | bytes 6291456 | tf_op jit(solution)/shard_map/pallas_call | solution.py:253
  38.3 2.4 %collective-permute-done.12.refs_0_ = bf16[512,512]{1,0:T(8,128)(2,1)S(1)} collective-permute-done((bf16[512,512]{1,0:T(8,128)(2,1)S(1)}, bf16[512,512]{1,0:T(8,128)(2,1)S(1)}, u32[]{:S(2)}, u32[]{:S(2)}) %collective-permute-start.12) | collective-permute-done | bytes 524320 | tf_op jit(solution)/shard_map/ppermute | solution.py:385
  40.7 2.8 %collective-permute-done.19.refs_1_ = bf16[256,512]{1,0:T(8,128)(2,1)S(1)} collective-permute-done((bf16[256,512]{1,0:T(8,128)(2,1)S(1)}, bf16[256,512]{1,0:T(8,128)(2,1)S(1)}, u32[]{:S(2)}, u32[]{:S(2)}) %collective-permute-start.19) | collective-permute-done | bytes 262176 | tf_op jit(solution)/shard_map/ppermute | solution.py:385
  43.5 1.1 %shard_map.51.refs_2_ = f32[512,512]{1,0:T(8,128)S(1)} custom-call(s32[16]{0:T(128)S(1)} %copy-done.1, bf16[16,256,1024]{2,1,0:T(8,128)(2,1)S(1)} %shard_map.46.rows_ref, bf16[512,512]{1,0:T(8,128)(2,1)S(1)} %collective-permute-done.12.refs_0_, bf16[256,512]{1,0:T(8,128)(2,1)S(1)} %collective-permute-done.19.refs_1_, f32[512,512]{1,0:T(8,128)S(1)} %shard_map.50.refs_2_), custom_call_target="tpu_custom_call" | custom-call | flops 402653184 | bytes 3670016 | tf_op jit(solution)/shard_map/pallas_call | solution.py:253
  45.0 1.7 %shard_map.52 = s16[2176,128]{1,0:T(8,128)(2,1)S(1)} custom-call(s32[16]{0:T(128)S(1)} %copy-done.1, bf16[16,256,1024]{2,1,0:T(8,128)(2,1)S(1)} %shard_map.46.rows_ref, bf16[512,512]{1,0:T(8,128)(2,1)S(1)} %collective-permute-done.18.refs_0_, bf16[256,512]{1,0:T(8,128)(2,1)S(1)} %collective-permute-done.20.refs_1_, f32[512,512]{1,0:T(8,128)S(1)} %shard_map.51.refs_2_), custom_call_target="tpu_custom_call" | custom-call | flops 402653184 | bytes 3670016 | tf_op jit(solution)/shard_map/pallas_call | solution.py:253
  46.7 23.0 %all_to_all.10 = s16[16,136,128]{2,1,0:T(8,128)(2,1)S(1)} all-to-all(s16[16,136,128]{2,1,0:T(8,128)(2,1)S(1)} %bitcast.15), channel_id=1, replica_groups=mesh['grp'=2,'shell'=16] {'shell'}, dimensions={0} | all-to-all | bytes 1114112 | tf_op jit(solution)/shard_map/all_to_all | solution.py:403
  69.7 1.7 %shard_map.53 = s16[2176,128]{1,0:T(8,128)(2,1)} custom-call(s16[2176,128]{1,0:T(8,128)(2,1)S(1)} %bitcast.14), custom_call_target="tpu_custom_call" | custom-call | tf_op jit(solution)/shard_map/pallas_call | solution.py:359
  71.4 3.6 %all-to-all-start.1 = ((s16[16,136,128]{2,1,0:T(8,128)(2,1)}), s16[16,136,128]{2,1,0:T(8,128)(2,1)S(1)}, u32[]{:S(2)}, u32[]{:S(2)}) async-start(s16[16,136,128]{2,1,0:T(8,128)(2,1)} %bitcast.5), calls=%async_computation.1 | async-start | bytes 1114112 | tf_op jit(solution)/shard_map/all_to_all | solution.py:403
  75.1 14.9 %all-to-all-done.1 = s16[16,136,128]{2,1,0:T(8,128)(2,1)S(1)} async-done(((s16[16,136,128]{2,1,0:T(8,128)(2,1)}), s16[16,136,128]{2,1,0:T(8,128)(2,1)S(1)}, u32[]{:S(2)}, u32[]{:S(2)}) %all-to-all-start.1) | async-done | bytes 557088 | tf_op jit(solution)/shard_map/all_to_all | solution.py:403
  90.0 2.2 %shard_map.54 = f32[2048,128]{1,0:T(8,128)} custom-call(f32[2,32]{1,0:T(2,128)S(1)} %maximum_multiply_fusion.twist_ref, s16[2176,128]{1,0:T(8,128)(2,1)S(1)} %bitcast.13), custom_call_target="tpu_custom_call" | custom-call | tf_op jit(solution)/shard_map/pallas_call | solution.py:359
  (31 shorter events, 2.1 us)
Async XLA Ops:
  0.0 13.1 %collective-permute-start = (bf16[512,512]{1,0:T(8,128)(2,1)}, bf16[512,512]{1,0:T(8,128)(2,1)S(1)}, u32[]{:S(2)}, u32[]{:S(2)}) collective-permute-start(bf16[512,512]{1,0:T(8,128)(2,1)} %bitcast.16), channel_id=1, source_target_pairs={{0,4},{5,1},{4,8},{9,5},{8,12},{13,9},{12,14},{15,13},{14,10},{11,... | collective-permute-start | bytes 1572872 | tf_op jit(solution)/shard_map/ppermute | solution.py:385
  4.0 8.7 %collective-permute-start.1 = (bf16[256,512]{1,0:T(8,128)(2,1)S(1)}, bf16[256,512]{1,0:T(8,128)(2,1)S(1)}, u32[]{:S(2)}, u32[]{:S(2)}) collective-permute-start(bf16[256,512]{1,0:T(8,128)(2,1)S(1)} %dynamic-slice_bitcast_fusion), channel_id=1, source_target_pairs={{1,4},{4,1},{5,8},{8,5},{9,12},{12,9},{13,14},{14,13},{15,10},{10,... | collective-permute-start | bytes 786440 | tf_op jit(solution)/shard_map/ppermute | solution.py:388
  4.8 12.0 %collective-permute-start.5 = (bf16[512,512]{1,0:T(8,128)(2,1)}, bf16[512,512]{1,0:T(8,128)(2,1)S(1)}, u32[]{:S(2)}, u32[]{:S(2)}) collective-permute-start(bf16[512,512]{1,0:T(8,128)(2,1)} %bitcast.17), channel_id=1, source_target_pairs={{0,1},{1,0},{2,3},{3,2},{4,5},{5,4},{6,7},{7,6},{8,9},{9,8},{10,11... | collective-permute-start | bytes 1572872 | tf_op jit(solution)/shard_map/ppermute | solution.py:391
  5.8 0.7 copy-start.2
  6.4 11.9 %copy-start = (bf16[1,512,512]{2,1,0:T(8,128)(2,1)S(1)}, bf16[1,512,512]{2,1,0:T(8,128)(2,1)}, u32[]{:S(2)}) copy-start(bf16[1,512,512]{2,1,0:T(8,128)(2,1)} %param.5) | copy-start | bytes 1572868
  6.4 11.9 %copy-start.1 = (s32[16]{0:T(128)S(1)}, s32[16]{0:T(128)}, u32[]{:S(2)}) copy-start(s32[16]{0:T(128)} %owner_ref.11) | copy-start | bytes 196
  13.1 6.4 %collective-permute-start.3 = (bf16[512,512]{1,0:T(8,128)(2,1)S(1)}, bf16[512,512]{1,0:T(8,128)(2,1)S(1)}, u32[]{:S(2)}, u32[]{:S(2)}) collective-permute-start(bf16[512,512]{1,0:T(8,128)(2,1)S(1)} %collective-permute-done.refs_0_), channel_id=1, source_target_pairs={{0,1},{1,0},{2,3},{3,2},{4,5},{5,4},{6,7},{7,6},{8,9},{9,8},{10,11... | collective-permute-start | bytes 1572872 | tf_op jit(solution)/shard_map/ppermute | solution.py:391
  13.1 9.2 %collective-permute-start.2 = (bf16[512,512]{1,0:T(8,128)(2,1)S(1)}, bf16[512,512]{1,0:T(8,128)(2,1)S(1)}, u32[]{:S(2)}, u32[]{:S(2)}) collective-permute-start(bf16[512,512]{1,0:T(8,128)(2,1)S(1)} %collective-permute-done.refs_0_), channel_id=1, source_target_pairs={{0,4},{5,1},{4,8},{9,5},{8,12},{13,9},{12,14},{15,13},{14,10},{11,... | collective-permute-start | bytes 1572872 | tf_op jit(solution)/shard_map/ppermute | solution.py:385
  15.2 4.3 %collective-permute-start.4 = (bf16[256,512]{1,0:T(8,128)(2,1)S(1)}, bf16[256,512]{1,0:T(8,128)(2,1)S(1)}, u32[]{:S(2)}, u32[]{:S(2)}) collective-permute-start(bf16[256,512]{1,0:T(8,128)(2,1)S(1)} %collective-permute-done.1.refs_2_), channel_id=1, source_target_pairs={{0,1},{1,0},{2,3},{3,2},{4,5},{5,4},{6,7},{7,6},{8,9},{9,8},{10,11... | collective-permute-start | bytes 786440 | tf_op jit(solution)/shard_map/ppermute | solution.py:391
  15.4 9.7 %collective-permute-start.8 = (bf16[256,512]{1,0:T(8,128)(2,1)S(1)}, bf16[256,512]{1,0:T(8,128)(2,1)S(1)}, u32[]{:S(2)}, u32[]{:S(2)}) collective-permute-start(bf16[256,512]{1,0:T(8,128)(2,1)S(1)} %collective-permute-done.1.refs_2_), channel_id=1, source_target_pairs={{0,4},{5,1},{4,8},{9,5},{8,12},{13,9},{12,14},{15,13},{14,10},{11,... | collective-permute-start | bytes 786440 | tf_op jit(solution)/shard_map/ppermute | solution.py:385
  16.8 8.3 %collective-permute-start.10 = (bf16[256,512]{1,0:T(8,128)(2,1)S(1)}, bf16[256,512]{1,0:T(8,128)(2,1)S(1)}, u32[]{:S(2)}, u32[]{:S(2)}) collective-permute-start(bf16[256,512]{1,0:T(8,128)(2,1)S(1)} %collective-permute-done.1.refs_2_), channel_id=1, source_target_pairs={{0,16},{16,0},{1,17},{17,1},{2,18},{18,2},{3,19},{19,3},{4,20},{20... | collective-permute-start | bytes 786440 | tf_op jit(solution)/shard_map/ppermute | solution.py:394
  22.3 6.9 %collective-permute-start.7 = (bf16[512,512]{1,0:T(8,128)(2,1)S(1)}, bf16[512,512]{1,0:T(8,128)(2,1)S(1)}, u32[]{:S(2)}, u32[]{:S(2)}) collective-permute-start(bf16[512,512]{1,0:T(8,128)(2,1)S(1)} %collective-permute-done.2.refs_0_), channel_id=1, source_target_pairs={{0,1},{1,0},{2,3},{3,2},{4,5},{5,4},{6,7},{7,6},{8,9},{9,8},{10,11... | collective-permute-start | bytes 1572872 | tf_op jit(solution)/shard_map/ppermute | solution.py:391
  22.3 9.2 %collective-permute-start.6 = (bf16[512,512]{1,0:T(8,128)(2,1)S(1)}, bf16[512,512]{1,0:T(8,128)(2,1)S(1)}, u32[]{:S(2)}, u32[]{:S(2)}) collective-permute-start(bf16[512,512]{1,0:T(8,128)(2,1)S(1)} %collective-permute-done.2.refs_0_), channel_id=1, source_target_pairs={{0,4},{5,1},{4,8},{9,5},{8,12},{13,9},{12,14},{15,13},{14,10},{11,... | collective-permute-start | bytes 1572872 | tf_op jit(solution)/shard_map/ppermute | solution.py:385
  25.1 2.5 %collective-permute-start.9 = (bf16[256,512]{1,0:T(8,128)(2,1)S(1)}, bf16[256,512]{1,0:T(8,128)(2,1)S(1)}, u32[]{:S(2)}, u32[]{:S(2)}) collective-permute-start(bf16[256,512]{1,0:T(8,128)(2,1)S(1)} %collective-permute-done.8.refs_2_), channel_id=1, source_target_pairs={{0,1},{1,0},{2,3},{3,2},{4,5},{5,4},{6,7},{7,6},{8,9},{9,8},{10,11... | collective-permute-start | bytes 786440 | tf_op jit(solution)/shard_map/ppermute | solution.py:391
  25.1 4.1 %collective-permute-start.11 = (bf16[256,512]{1,0:T(8,128)(2,1)S(1)}, bf16[256,512]{1,0:T(8,128)(2,1)S(1)}, u32[]{:S(2)}, u32[]{:S(2)}) collective-permute-start(bf16[256,512]{1,0:T(8,128)(2,1)S(1)} %collective-permute-done.10.refs_4_), channel_id=1, source_target_pairs={{0,1},{1,0},{2,3},{3,2},{4,5},{5,4},{6,7},{7,6},{8,9},{9,8},{10,11... | collective-permute-start | bytes 786440 | tf_op jit(solution)/shard_map/ppermute | solution.py:391
  25.7 8.5 %collective-permute-start.16 = (bf16[256,512]{1,0:T(8,128)(2,1)S(1)}, bf16[256,512]{1,0:T(8,128)(2,1)S(1)}, u32[]{:S(2)}, u32[]{:S(2)}) collective-permute-start(bf16[256,512]{1,0:T(8,128)(2,1)S(1)} %collective-permute-done.8.refs_2_), channel_id=1, source_target_pairs={{0,16},{16,0},{1,17},{17,1},{2,18},{18,2},{3,19},{19,3},{4,20},{20... | collective-permute-start | bytes 786440 | tf_op jit(solution)/shard_map/ppermute | solution.py:394
  27.7 6.7 %collective-permute-start.14 = (bf16[256,512]{1,0:T(8,128)(2,1)S(1)}, bf16[256,512]{1,0:T(8,128)(2,1)S(1)}, u32[]{:S(2)}, u32[]{:S(2)}) collective-permute-start(bf16[256,512]{1,0:T(8,128)(2,1)S(1)} %collective-permute-done.8.refs_2_), channel_id=1, source_target_pairs={{0,4},{5,1},{4,8},{9,5},{8,12},{13,9},{12,14},{15,13},{14,10},{11,... | collective-permute-start | bytes 786440 | tf_op jit(solution)/shard_map/ppermute | solution.py:385
  31.5 5.0 %collective-permute-start.13 = (bf16[512,512]{1,0:T(8,128)(2,1)S(1)}, bf16[512,512]{1,0:T(8,128)(2,1)S(1)}, u32[]{:S(2)}, u32[]{:S(2)}) collective-permute-start(bf16[512,512]{1,0:T(8,128)(2,1)S(1)} %collective-permute-done.6.refs_0_), channel_id=1, source_target_pairs={{0,1},{1,0},{2,3},{3,2},{4,5},{5,4},{6,7},{7,6},{8,9},{9,8},{10,11... | collective-permute-start | bytes 1572872 | tf_op jit(solution)/shard_map/ppermute | solution.py:391
  31.5 9.2 %collective-permute-start.12 = (bf16[512,512]{1,0:T(8,128)(2,1)S(1)}, bf16[512,512]{1,0:T(8,128)(2,1)S(1)}, u32[]{:S(2)}, u32[]{:S(2)}) collective-permute-start(bf16[512,512]{1,0:T(8,128)(2,1)S(1)} %collective-permute-done.6.refs_0_), channel_id=1, source_target_pairs={{0,4},{5,1},{4,8},{9,5},{8,12},{13,9},{12,14},{15,13},{14,10},{11,... | collective-permute-start | bytes 1572872 | tf_op jit(solution)/shard_map/ppermute | solution.py:385
  34.1 2.3 %collective-permute-start.17 = (bf16[256,512]{1,0:T(8,128)(2,1)S(1)}, bf16[256,512]{1,0:T(8,128)(2,1)S(1)}, u32[]{:S(2)}, u32[]{:S(2)}) collective-permute-start(bf16[256,512]{1,0:T(8,128)(2,1)S(1)} %collective-permute-done.16.refs_4_), channel_id=1, source_target_pairs={{0,1},{1,0},{2,3},{3,2},{4,5},{5,4},{6,7},{7,6},{8,9},{9,8},{10,11... | collective-permute-start | bytes 786440 | tf_op jit(solution)/shard_map/ppermute | solution.py:391
  34.3 2.1 %collective-permute-start.15 = (bf16[256,512]{1,0:T(8,128)(2,1)S(1)}, bf16[256,512]{1,0:T(8,128)(2,1)S(1)}, u32[]{:S(2)}, u32[]{:S(2)}) collective-permute-start(bf16[256,512]{1,0:T(8,128)(2,1)S(1)} %collective-permute-done.14.refs_2_), channel_id=1, source_target_pairs={{0,1},{1,0},{2,3},{3,2},{4,5},{5,4},{6,7},{7,6},{8,9},{9,8},{10,11... | collective-permute-start | bytes 786440 | tf_op jit(solution)/shard_map/ppermute | solution.py:391
  34.6 8.9 %collective-permute-start.19 = (bf16[256,512]{1,0:T(8,128)(2,1)S(1)}, bf16[256,512]{1,0:T(8,128)(2,1)S(1)}, u32[]{:S(2)}, u32[]{:S(2)}) collective-permute-start(bf16[256,512]{1,0:T(8,128)(2,1)S(1)} %collective-permute-done.16.refs_4_), channel_id=1, source_target_pairs={{0,4},{5,1},{4,8},{9,5},{8,12},{13,9},{12,14},{15,13},{14,10},{11,... | collective-permute-start | bytes 786440 | tf_op jit(solution)/shard_map/ppermute | solution.py:385
  40.7 4.3 %collective-permute-start.18 = (bf16[512,512]{1,0:T(8,128)(2,1)S(1)}, bf16[512,512]{1,0:T(8,128)(2,1)S(1)}, u32[]{:S(2)}, u32[]{:S(2)}) collective-permute-start(bf16[512,512]{1,0:T(8,128)(2,1)S(1)} %collective-permute-done.12.refs_0_), channel_id=1, source_target_pairs={{0,1},{1,0},{2,3},{3,2},{4,5},{5,4},{6,7},{7,6},{8,9},{9,8},{10,11... | collective-permute-start | bytes 1572872 | tf_op jit(solution)/shard_map/ppermute | solution.py:391
  43.5 1.5 %collective-permute-start.20 = (bf16[256,512]{1,0:T(8,128)(2,1)S(1)}, bf16[256,512]{1,0:T(8,128)(2,1)S(1)}, u32[]{:S(2)}, u32[]{:S(2)}) collective-permute-start(bf16[256,512]{1,0:T(8,128)(2,1)S(1)} %collective-permute-done.19.refs_1_), channel_id=1, source_target_pairs={{0,1},{1,0},{2,3},{3,2},{4,5},{5,4},{6,7},{7,6},{8,9},{9,8},{10,11... | collective-permute-start | bytes 786440 | tf_op jit(solution)/shard_map/ppermute | solution.py:391
  71.4 18.6 %all-to-all-start.1 = ((s16[16,136,128]{2,1,0:T(8,128)(2,1)}), s16[16,136,128]{2,1,0:T(8,128)(2,1)S(1)}, u32[]{:S(2)}, u32[]{:S(2)}) async-start(s16[16,136,128]{2,1,0:T(8,128)(2,1)} %bitcast.5), calls=%async_computation.1 | async-start | bytes 1114112 | tf_op jit(solution)/shard_map/all_to_all | solution.py:403

commit v7 on v6

--- a/solution.py
+++ b/solution.py
@@ -234,7 +234,7 @@
         degree = jnp.zeros((), jnp.int32)
         for l in range(rows_ref.shape[0]):
             degree = jnp.where(owner_ref[l] == slot, l, degree)
-        offset = 0 if half is None else depth * (part + half) % (2 * depth)
+        offset = 0 if half is None else width // 2 * ((part + half[0]) % 2) + half[1]
         left = jnp.concatenate(
             [rows_ref[degree, :, pl.ds(pl.multiple_of(c * width + offset, 128), depth)] for c in range(2)]
         )
@@ -416,25 +416,37 @@
             whole, acc = lax.optimization_barrier((whole, acc))
         next_whole = around(whole)
         next_part = around(part) if step + 1 < chips // 2 else None
-        rest = across(part) if next_part is not None else around(late[0])
+        if next_part is None:
+            cut = half // 2
+            front, back, acc = lax.optimization_barrier((late[0][:cut], part[cut:], acc))
+            ends = [around(front), across(back)]
+        else:
+            rest = across(part)
         acc = project(
             acc,
             rows,
             degree_owner,
             [whole, sibling(whole), part, sibling(part), *late],
-            [(-step, 0, None), (step, 1, None), (-step, 1, 0), (step, 0, 0), *late_from],
+            [(-step, 0, None), (step, 1, None), (-step, 1, (0, 0)), (step, 0, (0, 0)), *late_from],
         )
-        late, late_from = [rest, sibling(rest)], [(-step, 1, 1), (step, 0, 1)]
+        if next_part is not None:
+            late, late_from = [rest, sibling(rest)], [(-step, 1, (1, 0)), (step, 0, (1, 0))]
         whole, part = next_whole, next_part
-    whole, acc = lax.optimization_barrier((whole, acc))
+    whole, acc, *ends = lax.optimization_barrier((whole, acc, *ends))
     far = chips // 2
-    acc = project(acc, rows, degree_owner, [whole, late[0]], [(-far, 0, None), late_from[0]])
+    acc = project(
+        acc,
+        rows,
+        degree_owner,
+        [whole, *ends],
+        [(-far, 0, None), (1 - far, 1, (1, 0)), (1 - far, 1, (1, cut))],
+    )
     sent = project(
         acc,
         rows,
         degree_owner,
-        [sibling(whole), late[1]],
-        [(far, 1, None), late_from[1]],
+        [sibling(whole), *map(sibling, ends)],
+        [(far, 1, None), (far - 1, 0, (1, 0)), (far - 1, 0, (1, cut))],
         packed=parcels,
     )
     sent = local_call(outer_kernel, parcels, [lines, stage], exchange(sent))

time: 92.4 us -> 91.9 us (level)
  waiting for transfers between devices: 25.2 us -> 21.9 us
  starting transfers between devices: 23.9 us -> 26.5 us
    ppermute x7, waiting for transfers between devices: 8.22 us -> 5.32 us  [around(): return lax.ppermute(value, 'shell', onward)]
    ppermute x2 -> x3, starting transfers between devices: 3.49 us -> 4.98 us  [across(): return lax.ppermute(value, 'grp', [(0, 1), (1, 0)])]
    ppermute x11 -> x12, starting transfers between devices: 2.02 us -> 2.79 us  [sibling(): return lax.ppermute(value, 'shell', [(s, s ^ 1) for s in range(devices)])]
  transfers between devices with their start and end apart: 22 -> 24, of which waited for: 11 -> 10; matrix products, arithmetic and copies ran while one was open for 1% -> 1% of each run, Pallas kernels for 14% -> 14%
where the time goes in v7:
time: 91.9 us; the launch traced here: 91.6 us
  starting transfers between devices  26.5 us (29%)
  blocking collectives  23 us (25%)
  waiting for transfers between devices  21.9 us (24%)
  Pallas kernels  18.5 us (20%)
  local copies, waits for them, and re-layouts  1.68 us (2%)
    all_to_all x1, blocking collectives, exchange(): return lax.all_to_all(value, 'shell', 0, 0).reshape(parcels.shape)  23 us
    all_to_all x1, waiting for transfers between devices, exchange(): return lax.all_to_all(value, 'shell', 0, 0).reshape(parcels.shape)  14.9 us
    ppermute x7, starting transfers between devices, around(): return lax.ppermute(value, 'shell', onward)  14.4 us
    pallas_call x6, Pallas kernels, project(): pl.pallas_call(functools.partial(project_kernel, lax.axis_size('shell'),...  9.43 us
    ppermute x7, waiting for transfers between devices, around(): return lax.ppermute(value, 'shell', onward)  5.32 us
    pallas_call x1, Pallas kernels, sort_rows(): pl.pallas_call(sort_kernel, in_specs=[pl.BlockSpec(memory_space=pltpu.SME...  5.14 us
    ppermute x3, starting transfers between devices, across(): return lax.ppermute(value, 'grp', [(0, 1), (1, 0)])  4.98 us
    pallas_call x2, Pallas kernels, local_call(): pl.pallas_call(kernel, in_specs=[pl.BlockSpec(memory_space=pltpu.SMEM)] *...  3.89 us
  transfers between devices with their start and end apart: 24, of which 10 were waited for; matrix products, arithmetic and copies ran while one was open for 1% of the time, Pallas kernels for 14%

profile of v7, /device:TPU:0, one launch (start us, length us, event | category | flops | bytes accessed | tf_op | source)
XLA Modules:
  0.0 91.6 jit_solution(4206964337454637322)
XLA Ops:
  0.0 3.0 %collective-permute-start = (bf16[512,512]{1,0:T(8,128)(2,1)}, bf16[512,512]{1,0:T(8,128)(2,1)S(1)}, u32[]{:S(2)}, u32[]{:S(2)}) collective-permute-start(bf16[512,512]{1,0:T(8,128)(2,1)} %bitcast.16), channel_id=1, source_target_pairs={{0,4},{5,1},{4,8},{9,5},{8,12},{13,9},{12,14},{15,13},{14,10},{11,... | collective-permute-start | bytes 1572872 | tf_op jit(solution)/shard_map/ppermute | solution.py:385
  3.0 1.0 %dynamic-slice_bitcast_fusion = bf16[256,512]{1,0:T(8,128)(2,1)S(1)} fusion(bf16[1,512,512]{2,1,0:T(8,128)(2,1)} %param.5, s32[]{:T(128)S(6)} %select_n.22), kind=kLoop, calls=%fused_computation | loop fusion | bytes 524292 | tf_op jit(solution)/shard_map/dynamic_slice | solution.py:408
  4.0 0.7 collective-permute-start.1
  4.8 1.0 %collective-permute-start.5 = (bf16[512,512]{1,0:T(8,128)(2,1)}, bf16[512,512]{1,0:T(8,128)(2,1)S(1)}, u32[]{:S(2)}, u32[]{:S(2)}) collective-permute-start(bf16[512,512]{1,0:T(8,128)(2,1)} %bitcast.17), channel_id=1, source_target_pairs={{0,1},{1,0},{2,3},{3,2},{4,5},{5,4},{6,7},{7,6},{8,9},{9,8},{10,11... | collective-permute-start | bytes 1572872 | tf_op jit(solution)/shard_map/ppermute | solution.py:391
  5.8 0.7 copy-done.2
  6.4 5.1 %shard_map.46.rows_ref = bf16[16,256,1024]{2,1,0:T(8,128)(2,1)S(1)} custom-call(s32[8]{0:T(128)S(1)} %copy-done.2, bf16[4096,1024]{1,0:T(8,128)(2,1)} %bitcast.19), custom_call_target="tpu_custom_call" | custom-call | flops 2147483648 | bytes 16777216 | tf_op jit(solution)/shard_map/pallas_call | solution.py:137
  11.6 1.2 %collective-permute-done.1.refs_2_ = bf16[256,512]{1,0:T(8,128)(2,1)S(1)} collective-permute-done((bf16[256,512]{1,0:T(8,128)(2,1)S(1)}, bf16[256,512]{1,0:T(8,128)(2,1)S(1)}, u32[]{:S(2)}, u32[]{:S(2)}) %collective-permute-start.1) | collective-permute-done | bytes 262176 | tf_op jit(solution)/shard_map/ppermute | solution.py:388
  13.1 2.1 %collective-permute-start.2 = (bf16[512,512]{1,0:T(8,128)(2,1)S(1)}, bf16[512,512]{1,0:T(8,128)(2,1)S(1)}, u32[]{:S(2)}, u32[]{:S(2)}) collective-permute-start(bf16[512,512]{1,0:T(8,128)(2,1)S(1)} %collective-permute-done.refs_0_), channel_id=1, source_target_pairs={{0,4},{5,1},{4,8},{9,5},{8,12},{13,9},{12,14},{15,13},{14,10},{11,... | collective-permute-start | bytes 1572872 | tf_op jit(solution)/shard_map/ppermute | solution.py:385
  15.4 1.4 %collective-permute-start.8 = (bf16[256,512]{1,0:T(8,128)(2,1)S(1)}, bf16[256,512]{1,0:T(8,128)(2,1)S(1)}, u32[]{:S(2)}, u32[]{:S(2)}) collective-permute-start(bf16[256,512]{1,0:T(8,128)(2,1)S(1)} %collective-permute-done.1.refs_2_), channel_id=1, source_target_pairs={{0,4},{5,1},{4,8},{9,5},{8,12},{13,9},{12,14},{15,13},{14,10},{11,... | collective-permute-start | bytes 786440 | tf_op jit(solution)/shard_map/ppermute | solution.py:385
  16.8 1.5 %collective-permute-start.10 = (bf16[256,512]{1,0:T(8,128)(2,1)S(1)}, bf16[256,512]{1,0:T(8,128)(2,1)S(1)}, u32[]{:S(2)}, u32[]{:S(2)}) collective-permute-start(bf16[256,512]{1,0:T(8,128)(2,1)S(1)} %collective-permute-done.1.refs_2_), channel_id=1, source_target_pairs={{0,16},{16,0},{1,17},{17,1},{2,18},{18,2},{3,19},{19,3},{4,20},{20... | collective-permute-start | bytes 786440 | tf_op jit(solution)/shard_map/ppermute | solution.py:394
  18.3 1.3 %shard_map.47.refs_4_ = f32[512,512]{1,0:T(8,128)S(1)} custom-call(s32[16]{0:T(128)S(1)} %copy-done.1, bf16[16,256,1024]{2,1,0:T(8,128)(2,1)S(1)} %shard_map.46.rows_ref, bf16[512,512]{1,0:T(8,128)(2,1)S(1)} %bitcast.18, bf16[512,512]{1,0:T(8,128)(2,1)S(1)} %collective-permute-done.5.refs_1_), custom_call_target="tpu_custom_call" | custom-call | flops 536870912 | bytes 3145728 | tf_op jit(solution)/shard_map/pallas_call | solution.py:253
  19.6 1.5 %shard_map.48.refs_6_ = f32[512,512]{1,0:T(8,128)S(1)} custom-call(s32[16]{0:T(128)S(1)} %copy-done.1, bf16[16,256,1024]{2,1,0:T(8,128)(2,1)S(1)} %shard_map.46.rows_ref, bf16[512,512]{1,0:T(8,128)(2,1)S(1)} %collective-permute-done.refs_0_, bf16[512,512]{1,0:T(8,128)(2,1)S(1)} %collective-permute-done.3.refs_1_, ...), custom_call_target="tpu_custom_call" | custom-call | flops 805306368 | bytes 5242880 | tf_op jit(solution)/shard_map/pallas_call | solution.py:253
  21.1 1.2 %collective-permute-done.2.refs_0_ = bf16[512,512]{1,0:T(8,128)(2,1)S(1)} collective-permute-done((bf16[512,512]{1,0:T(8,128)(2,1)S(1)}, bf16[512,512]{1,0:T(8,128)(2,1)S(1)}, u32[]{:S(2)}, u32[]{:S(2)}) %collective-permute-start.2) | collective-permute-done | bytes 524320 | tf_op jit(solution)/shard_map/ppermute | solution.py:385
  22.3 2.1 %collective-permute-start.6 = (bf16[512,512]{1,0:T(8,128)(2,1)S(1)}, bf16[512,512]{1,0:T(8,128)(2,1)S(1)}, u32[]{:S(2)}, u32[]{:S(2)}) collective-permute-start(bf16[512,512]{1,0:T(8,128)(2,1)S(1)} %collective-permute-done.2.refs_0_), channel_id=1, source_target_pairs={{0,4},{5,1},{4,8},{9,5},{8,12},{13,9},{12,14},{15,13},{14,10},{11,... | collective-permute-start | bytes 1572872 | tf_op jit(solution)/shard_map/ppermute | solution.py:385
  24.4 0.7 collective-permute-done.8.refs_2_
  25.1 0.5 collective-permute-start.11
  25.7 2.0 %collective-permute-start.16 = (bf16[256,512]{1,0:T(8,128)(2,1)S(1)}, bf16[256,512]{1,0:T(8,128)(2,1)S(1)}, u32[]{:S(2)}, u32[]{:S(2)}) collective-permute-start(bf16[256,512]{1,0:T(8,128)(2,1)S(1)} %collective-permute-done.8.refs_2_), channel_id=1, source_target_pairs={{0,16},{16,0},{1,17},{17,1},{2,18},{18,2},{3,19},{19,3},{4,20},{20... | collective-permute-start | bytes 786440 | tf_op jit(solution)/shard_map/ppermute | solution.py:394
  27.7 1.6 %collective-permute-start.14 = (bf16[256,512]{1,0:T(8,128)(2,1)S(1)}, bf16[256,512]{1,0:T(8,128)(2,1)S(1)}, u32[]{:S(2)}, u32[]{:S(2)}) collective-permute-start(bf16[256,512]{1,0:T(8,128)(2,1)S(1)} %collective-permute-done.8.refs_2_), channel_id=1, source_target_pairs={{0,4},{5,1},{4,8},{9,5},{8,12},{13,9},{12,14},{15,13},{14,10},{11,... | collective-permute-start | bytes 786440 | tf_op jit(solution)/shard_map/ppermute | solution.py:385
  29.2 1.8 %shard_map.49.refs_6_ = f32[512,512]{1,0:T(8,128)S(1)} custom-call(s32[16]{0:T(128)S(1)} %copy-done.1, bf16[16,256,1024]{2,1,0:T(8,128)(2,1)S(1)} %shard_map.46.rows_ref, bf16[512,512]{1,0:T(8,128)(2,1)S(1)} %collective-permute-done.2.refs_0_, bf16[512,512]{1,0:T(8,128)(2,1)S(1)} %collective-permute-done.7.refs_1_, ...), custom_call_target="tpu_custom_call" | custom-call | flops 1073741824 | bytes 6291456 | tf_op jit(solution)/shard_map/pallas_call | solution.py:253
  31.5 2.1 %collective-permute-start.12 = (bf16[512,512]{1,0:T(8,128)(2,1)S(1)}, bf16[512,512]{1,0:T(8,128)(2,1)S(1)}, u32[]{:S(2)}, u32[]{:S(2)}) collective-permute-start(bf16[512,512]{1,0:T(8,128)(2,1)S(1)} %collective-permute-done.6.refs_0_), channel_id=1, source_target_pairs={{0,4},{5,1},{4,8},{9,5},{8,12},{13,9},{12,14},{15,13},{14,10},{11,... | collective-permute-start | bytes 1572872 | tf_op jit(solution)/shard_map/ppermute | solution.py:385
  33.6 0.7 collective-permute-done.14.refs_2_
  34.9 2.1 %collective-permute-start.18 = (bf16[128,512]{1,0:T(8,128)(2,1)S(1)}, bf16[128,512]{1,0:T(8,128)(2,1)S(1)}, u32[]{:S(2)}, u32[]{:S(2)}) collective-permute-start(bf16[128,512]{1,0:T(8,128)(2,1)S(1)} %slice.8), channel_id=1, source_target_pairs={{0,4},{5,1},{4,8},{9,5},{8,12},{13,9},{12,14},{15,13},{14,10},{11,... | collective-permute-start | bytes 393224 | tf_op jit(solution)/shard_map/ppermute | solution.py:385
  37.0 1.5 %collective-permute-start.19 = (bf16[128,512]{1,0:T(8,128)(2,1)S(1)}, bf16[128,512]{1,0:T(8,128)(2,1)S(1)}, u32[]{:S(2)}, u32[]{:S(2)}) collective-permute-start(bf16[128,512]{1,0:T(8,128)(2,1)S(1)} %slice.9), channel_id=1, source_target_pairs={{0,16},{16,0},{1,17},{17,1},{2,18},{18,2},{3,19},{19,3},{4,20},{20... | collective-permute-start | bytes 393224 | tf_op jit(solution)/shard_map/ppermute | solution.py:394
  38.5 1.8 %shard_map.50.refs_3_ = f32[512,512]{1,0:T(8,128)S(1)} custom-call(s32[16]{0:T(128)S(1)} %copy-done.1, bf16[16,256,1024]{2,1,0:T(8,128)(2,1)S(1)} %shard_map.46.rows_ref, bf16[512,512]{1,0:T(8,128)(2,1)S(1)} %collective-permute-done.6.refs_0_, bf16[512,512]{1,0:T(8,128)(2,1)S(1)} %collective-permute-done.13.refs_1_, ...), custom_call_target="tpu_custom_call" | custom-call | flops 1073741824 | bytes 6291456 | tf_op jit(solution)/shard_map/pallas_call | solution.py:253
  40.3 1.8 %collective-permute-done.18.refs_1_ = bf16[128,512]{1,0:T(8,128)(2,1)S(1)} collective-permute-done((bf16[128,512]{1,0:T(8,128)(2,1)S(1)}, bf16[128,512]{1,0:T(8,128)(2,1)S(1)}, u32[]{:S(2)}, u32[]{:S(2)}) %collective-permute-start.18) | collective-permute-done | bytes 131104 | tf_op jit(solution)/shard_map/ppermute | solution.py:385
  42.7 1.3 %shard_map.51.refs_3_ = f32[512,512]{1,0:T(8,128)S(1)} custom-call(s32[16]{0:T(128)S(1)} %copy-done.1, bf16[16,256,1024]{2,1,0:T(8,128)(2,1)S(1)} %shard_map.46.rows_ref, bf16[512,512]{1,0:T(8,128)(2,1)S(1)} %collective-permute-done.12.refs_0_, bf16[128,512]{1,0:T(8,128)(2,1)S(1)} %collective-permute-done.18.refs_1_, ...), custom_call_target="tpu_custom_call" | custom-call | flops 402653184 | bytes 3670016 | tf_op jit(solution)/shard_map/pallas_call | solution.py:253
  44.4 1.8 %shard_map.52 = s16[2176,128]{1,0:T(8,128)(2,1)S(1)} custom-call(s32[16]{0:T(128)S(1)} %copy-done.1, bf16[16,256,1024]{2,1,0:T(8,128)(2,1)S(1)} %shard_map.46.rows_ref, bf16[512,512]{1,0:T(8,128)(2,1)S(1)} %collective-permute-done.20.refs_0_, bf16[128,512]{1,0:T(8,128)(2,1)S(1)} %collective-permute-done.21.refs_1_, ...), custom_call_target="tpu_custom_call" | custom-call | flops 402653184 | bytes 3670016 | tf_op jit(solution)/shard_map/pallas_call | solution.py:253
  46.2 23.0 %all_to_all.10 = s16[16,136,128]{2,1,0:T(8,128)(2,1)S(1)} all-to-all(s16[16,136,128]{2,1,0:T(8,128)(2,1)S(1)} %bitcast.15), channel_id=1, replica_groups=mesh['grp'=2,'shell'=16] {'shell'}, dimensions={0} | all-to-all | bytes 1114112 | tf_op jit(solution)/shard_map/all_to_all | solution.py:403
  69.2 1.7 %shard_map.53 = s16[2176,128]{1,0:T(8,128)(2,1)} custom-call(s16[2176,128]{1,0:T(8,128)(2,1)S(1)} %bitcast.14), custom_call_target="tpu_custom_call" | custom-call | tf_op jit(solution)/shard_map/pallas_call | solution.py:359
  70.9 3.6 %all-to-all-start.1 = ((s16[16,136,128]{2,1,0:T(8,128)(2,1)}), s16[16,136,128]{2,1,0:T(8,128)(2,1)S(1)}, u32[]{:S(2)}, u32[]{:S(2)}) async-start(s16[16,136,128]{2,1,0:T(8,128)(2,1)} %bitcast.5), calls=%async_computation.1 | async-start | bytes 1114112 | tf_op jit(solution)/shard_map/all_to_all | solution.py:403
  74.6 14.9 %all-to-all-done.1 = s16[16,136,128]{2,1,0:T(8,128)(2,1)S(1)} async-done(((s16[16,136,128]{2,1,0:T(8,128)(2,1)}), s16[16,136,128]{2,1,0:T(8,128)(2,1)S(1)}, u32[]{:S(2)}, u32[]{:S(2)}) %all-to-all-start.1) | async-done | bytes 557088 | tf_op jit(solution)/shard_map/all_to_all | solution.py:403
  89.5 2.2 %shard_map.54 = f32[2048,128]{1,0:T(8,128)} custom-call(f32[2,32]{1,0:T(2,128)S(1)} %maximum_multiply_fusion.twist_ref, s16[2176,128]{1,0:T(8,128)(2,1)S(1)} %bitcast.13), custom_call_target="tpu_custom_call" | custom-call | tf_op jit(solution)/shard_map/pallas_call | solution.py:359
  (37 shorter events, 2.7 us)
Async XLA Ops:
  0.0 13.1 %collective-permute-start = (bf16[512,512]{1,0:T(8,128)(2,1)}, bf16[512,512]{1,0:T(8,128)(2,1)S(1)}, u32[]{:S(2)}, u32[]{:S(2)}) collective-permute-start(bf16[512,512]{1,0:T(8,128)(2,1)} %bitcast.16), channel_id=1, source_target_pairs={{0,4},{5,1},{4,8},{9,5},{8,12},{13,9},{12,14},{15,13},{14,10},{11,... | collective-permute-start | bytes 1572872 | tf_op jit(solution)/shard_map/ppermute | solution.py:385
  4.0 8.7 %collective-permute-start.1 = (bf16[256,512]{1,0:T(8,128)(2,1)S(1)}, bf16[256,512]{1,0:T(8,128)(2,1)S(1)}, u32[]{:S(2)}, u32[]{:S(2)}) collective-permute-start(bf16[256,512]{1,0:T(8,128)(2,1)S(1)} %dynamic-slice_bitcast_fusion), channel_id=1, source_target_pairs={{1,4},{4,1},{5,8},{8,5},{9,12},{12,9},{13,14},{14,13},{15,10},{10,... | collective-permute-start | bytes 786440 | tf_op jit(solution)/shard_map/ppermute | solution.py:388
  4.8 12.0 %collective-permute-start.5 = (bf16[512,512]{1,0:T(8,128)(2,1)}, bf16[512,512]{1,0:T(8,128)(2,1)S(1)}, u32[]{:S(2)}, u32[]{:S(2)}) collective-permute-start(bf16[512,512]{1,0:T(8,128)(2,1)} %bitcast.17), channel_id=1, source_target_pairs={{0,1},{1,0},{2,3},{3,2},{4,5},{5,4},{6,7},{7,6},{8,9},{9,8},{10,11... | collective-permute-start | bytes 1572872 | tf_op jit(solution)/shard_map/ppermute | solution.py:391
  5.8 0.7 copy-start.2
  6.4 11.9 %copy-start = (bf16[1,512,512]{2,1,0:T(8,128)(2,1)S(1)}, bf16[1,512,512]{2,1,0:T(8,128)(2,1)}, u32[]{:S(2)}) copy-start(bf16[1,512,512]{2,1,0:T(8,128)(2,1)} %param.5) | copy-start | bytes 1572868
  6.4 11.9 %copy-start.1 = (s32[16]{0:T(128)S(1)}, s32[16]{0:T(128)}, u32[]{:S(2)}) copy-start(s32[16]{0:T(128)} %owner_ref.11) | copy-start | bytes 196
  13.1 6.4 %collective-permute-start.3 = (bf16[512,512]{1,0:T(8,128)(2,1)S(1)}, bf16[512,512]{1,0:T(8,128)(2,1)S(1)}, u32[]{:S(2)}, u32[]{:S(2)}) collective-permute-start(bf16[512,512]{1,0:T(8,128)(2,1)S(1)} %collective-permute-done.refs_0_), channel_id=1, source_target_pairs={{0,1},{1,0},{2,3},{3,2},{4,5},{5,4},{6,7},{7,6},{8,9},{9,8},{10,11... | collective-permute-start | bytes 1572872 | tf_op jit(solution)/shard_map/ppermute | solution.py:391
  13.1 9.2 %collective-permute-start.2 = (bf16[512,512]{1,0:T(8,128)(2,1)S(1)}, bf16[512,512]{1,0:T(8,128)(2,1)S(1)}, u32[]{:S(2)}, u32[]{:S(2)}) collective-permute-start(bf16[512,512]{1,0:T(8,128)(2,1)S(1)} %collective-permute-done.refs_0_), channel_id=1, source_target_pairs={{0,4},{5,1},{4,8},{9,5},{8,12},{13,9},{12,14},{15,13},{14,10},{11,... | collective-permute-start | bytes 1572872 | tf_op jit(solution)/shard_map/ppermute | solution.py:385
  15.2 4.3 %collective-permute-start.4 = (bf16[256,512]{1,0:T(8,128)(2,1)S(1)}, bf16[256,512]{1,0:T(8,128)(2,1)S(1)}, u32[]{:S(2)}, u32[]{:S(2)}) collective-permute-start(bf16[256,512]{1,0:T(8,128)(2,1)S(1)} %collective-permute-done.1.refs_2_), channel_id=1, source_target_pairs={{0,1},{1,0},{2,3},{3,2},{4,5},{5,4},{6,7},{7,6},{8,9},{9,8},{10,11... | collective-permute-start | bytes 786440 | tf_op jit(solution)/shard_map/ppermute | solution.py:391
  15.4 9.7 %collective-permute-start.8 = (bf16[256,512]{1,0:T(8,128)(2,1)S(1)}, bf16[256,512]{1,0:T(8,128)(2,1)S(1)}, u32[]{:S(2)}, u32[]{:S(2)}) collective-permute-start(bf16[256,512]{1,0:T(8,128)(2,1)S(1)} %collective-permute-done.1.refs_2_), channel_id=1, source_target_pairs={{0,4},{5,1},{4,8},{9,5},{8,12},{13,9},{12,14},{15,13},{14,10},{11,... | collective-permute-start | bytes 786440 | tf_op jit(solution)/shard_map/ppermute | solution.py:385
  16.8 8.3 %collective-permute-start.10 = (bf16[256,512]{1,0:T(8,128)(2,1)S(1)}, bf16[256,512]{1,0:T(8,128)(2,1)S(1)}, u32[]{:S(2)}, u32[]{:S(2)}) collective-permute-start(bf16[256,512]{1,0:T(8,128)(2,1)S(1)} %collective-permute-done.1.refs_2_), channel_id=1, source_target_pairs={{0,16},{16,0},{1,17},{17,1},{2,18},{18,2},{3,19},{19,3},{4,20},{20... | collective-permute-start | bytes 786440 | tf_op jit(solution)/shard_map/ppermute | solution.py:394
  22.3 6.9 %collective-permute-start.7 = (bf16[512,512]{1,0:T(8,128)(2,1)S(1)}, bf16[512,512]{1,0:T(8,128)(2,1)S(1)}, u32[]{:S(2)}, u32[]{:S(2)}) collective-permute-start(bf16[512,512]{1,0:T(8,128)(2,1)S(1)} %collective-permute-done.2.refs_0_), channel_id=1, source_target_pairs={{0,1},{1,0},{2,3},{3,2},{4,5},{5,4},{6,7},{7,6},{8,9},{9,8},{10,11... | collective-permute-start | bytes 1572872 | tf_op jit(solution)/shard_map/ppermute | solution.py:391
  22.3 9.2 %collective-permute-start.6 = (bf16[512,512]{1,0:T(8,128)(2,1)S(1)}, bf16[512,512]{1,0:T(8,128)(2,1)S(1)}, u32[]{:S(2)}, u32[]{:S(2)}) collective-permute-start(bf16[512,512]{1,0:T(8,128)(2,1)S(1)} %collective-permute-done.2.refs_0_), channel_id=1, source_target_pairs={{0,4},{5,1},{4,8},{9,5},{8,12},{13,9},{12,14},{15,13},{14,10},{11,... | collective-permute-start | bytes 1572872 | tf_op jit(solution)/shard_map/ppermute | solution.py:385
  25.1 2.5 %collective-permute-start.9 = (bf16[256,512]{1,0:T(8,128)(2,1)S(1)}, bf16[256,512]{1,0:T(8,128)(2,1)S(1)}, u32[]{:S(2)}, u32[]{:S(2)}) collective-permute-start(bf16[256,512]{1,0:T(8,128)(2,1)S(1)} %collective-permute-done.8.refs_2_), channel_id=1, source_target_pairs={{0,1},{1,0},{2,3},{3,2},{4,5},{5,4},{6,7},{7,6},{8,9},{9,8},{10,11... | collective-permute-start | bytes 786440 | tf_op jit(solution)/shard_map/ppermute | solution.py:391
  25.1 4.1 %collective-permute-start.11 = (bf16[256,512]{1,0:T(8,128)(2,1)S(1)}, bf16[256,512]{1,0:T(8,128)(2,1)S(1)}, u32[]{:S(2)}, u32[]{:S(2)}) collective-permute-start(bf16[256,512]{1,0:T(8,128)(2,1)S(1)} %collective-permute-done.10.refs_4_), channel_id=1, source_target_pairs={{0,1},{1,0},{2,3},{3,2},{4,5},{5,4},{6,7},{7,6},{8,9},{9,8},{10,11... | collective-permute-start | bytes 786440 | tf_op jit(solution)/shard_map/ppermute | solution.py:391
  25.7 8.7 %collective-permute-start.16 = (bf16[256,512]{1,0:T(8,128)(2,1)S(1)}, bf16[256,512]{1,0:T(8,128)(2,1)S(1)}, u32[]{:S(2)}, u32[]{:S(2)}) collective-permute-start(bf16[256,512]{1,0:T(8,128)(2,1)S(1)} %collective-permute-done.8.refs_2_), channel_id=1, source_target_pairs={{0,16},{16,0},{1,17},{17,1},{2,18},{18,2},{3,19},{19,3},{4,20},{20... | collective-permute-start | bytes 786440 | tf_op jit(solution)/shard_map/ppermute | solution.py:394
  27.7 6.7 %collective-permute-start.14 = (bf16[256,512]{1,0:T(8,128)(2,1)S(1)}, bf16[256,512]{1,0:T(8,128)(2,1)S(1)}, u32[]{:S(2)}, u32[]{:S(2)}) collective-permute-start(bf16[256,512]{1,0:T(8,128)(2,1)S(1)} %collective-permute-done.8.refs_2_), channel_id=1, source_target_pairs={{0,4},{5,1},{4,8},{9,5},{8,12},{13,9},{12,14},{15,13},{14,10},{11,... | collective-permute-start | bytes 786440 | tf_op jit(solution)/shard_map/ppermute | solution.py:385
  31.5 7.0 %collective-permute-start.13 = (bf16[512,512]{1,0:T(8,128)(2,1)S(1)}, bf16[512,512]{1,0:T(8,128)(2,1)S(1)}, u32[]{:S(2)}, u32[]{:S(2)}) collective-permute-start(bf16[512,512]{1,0:T(8,128)(2,1)S(1)} %collective-permute-done.6.refs_0_), channel_id=1, source_target_pairs={{0,1},{1,0},{2,3},{3,2},{4,5},{5,4},{6,7},{7,6},{8,9},{9,8},{10,11... | collective-permute-start | bytes 1572872 | tf_op jit(solution)/shard_map/ppermute | solution.py:391
  31.5 10.6 %collective-permute-start.12 = (bf16[512,512]{1,0:T(8,128)(2,1)S(1)}, bf16[512,512]{1,0:T(8,128)(2,1)S(1)}, u32[]{:S(2)}, u32[]{:S(2)}) collective-permute-start(bf16[512,512]{1,0:T(8,128)(2,1)S(1)} %collective-permute-done.6.refs_0_), channel_id=1, source_target_pairs={{0,4},{5,1},{4,8},{9,5},{8,12},{13,9},{12,14},{15,13},{14,10},{11,... | collective-permute-start | bytes 1572872 | tf_op jit(solution)/shard_map/ppermute | solution.py:385
  34.3 2.7 %collective-permute-start.15 = (bf16[256,512]{1,0:T(8,128)(2,1)S(1)}, bf16[256,512]{1,0:T(8,128)(2,1)S(1)}, u32[]{:S(2)}, u32[]{:S(2)}) collective-permute-start(bf16[256,512]{1,0:T(8,128)(2,1)S(1)} %collective-permute-done.14.refs_2_), channel_id=1, source_target_pairs={{0,1},{1,0},{2,3},{3,2},{4,5},{5,4},{6,7},{7,6},{8,9},{9,8},{10,11... | collective-permute-start | bytes 786440 | tf_op jit(solution)/shard_map/ppermute | solution.py:391
  34.3 4.2 %collective-permute-start.17 = (bf16[256,512]{1,0:T(8,128)(2,1)S(1)}, bf16[256,512]{1,0:T(8,128)(2,1)S(1)}, u32[]{:S(2)}, u32[]{:S(2)}) collective-permute-start(bf16[256,512]{1,0:T(8,128)(2,1)S(1)} %collective-permute-done.16.refs_4_), channel_id=1, source_target_pairs={{0,1},{1,0},{2,3},{3,2},{4,5},{5,4},{6,7},{7,6},{8,9},{9,8},{10,11... | collective-permute-start | bytes 786440 | tf_op jit(solution)/shard_map/ppermute | solution.py:391
  34.9 7.2 %collective-permute-start.18 = (bf16[128,512]{1,0:T(8,128)(2,1)S(1)}, bf16[128,512]{1,0:T(8,128)(2,1)S(1)}, u32[]{:S(2)}, u32[]{:S(2)}) collective-permute-start(bf16[128,512]{1,0:T(8,128)(2,1)S(1)} %slice.8), channel_id=1, source_target_pairs={{0,4},{5,1},{4,8},{9,5},{8,12},{13,9},{12,14},{15,13},{14,10},{11,... | collective-permute-start | bytes 393224 | tf_op jit(solution)/shard_map/ppermute | solution.py:385
  37.0 5.1 %collective-permute-start.19 = (bf16[128,512]{1,0:T(8,128)(2,1)S(1)}, bf16[128,512]{1,0:T(8,128)(2,1)S(1)}, u32[]{:S(2)}, u32[]{:S(2)}) collective-permute-start(bf16[128,512]{1,0:T(8,128)(2,1)S(1)} %slice.9), channel_id=1, source_target_pairs={{0,16},{16,0},{1,17},{17,1},{2,18},{18,2},{3,19},{19,3},{4,20},{20... | collective-permute-start | bytes 393224 | tf_op jit(solution)/shard_map/ppermute | solution.py:394
  42.1 2.3 %collective-permute-start.20 = (bf16[512,512]{1,0:T(8,128)(2,1)S(1)}, bf16[512,512]{1,0:T(8,128)(2,1)S(1)}, u32[]{:S(2)}, u32[]{:S(2)}) collective-permute-start(bf16[512,512]{1,0:T(8,128)(2,1)S(1)} %collective-permute-done.12.refs_0_), channel_id=1, source_target_pairs={{0,1},{1,0},{2,3},{3,2},{4,5},{5,4},{6,7},{7,6},{8,9},{9,8},{10,11... | collective-permute-start | bytes 1572872 | tf_op jit(solution)/shard_map/ppermute | solution.py:391
  42.1 2.1 %collective-permute-start.21 = (bf16[128,512]{1,0:T(8,128)(2,1)S(1)}, bf16[128,512]{1,0:T(8,128)(2,1)S(1)}, u32[]{:S(2)}, u32[]{:S(2)}) collective-permute-start(bf16[128,512]{1,0:T(8,128)(2,1)S(1)} %collective-permute-done.18.refs_1_), channel_id=1, source_target_pairs={{0,1},{1,0},{2,3},{3,2},{4,5},{5,4},{6,7},{7,6},{8,9},{9,8},{10,11... | collective-permute-start | bytes 393224 | tf_op jit(solution)/shard_map/ppermute | solution.py:391
  42.6 1.8 %collective-permute-start.22 = (bf16[128,512]{1,0:T(8,128)(2,1)S(1)}, bf16[128,512]{1,0:T(8,128)(2,1)S(1)}, u32[]{:S(2)}, u32[]{:S(2)}) collective-permute-start(bf16[128,512]{1,0:T(8,128)(2,1)S(1)} %collective-permute-done.19.refs_2_), channel_id=1, source_target_pairs={{0,1},{1,0},{2,3},{3,2},{4,5},{5,4},{6,7},{7,6},{8,9},{9,8},{10,11... | collective-permute-start | bytes 393224 | tf_op jit(solution)/shard_map/ppermute | solution.py:391
  70.9 18.6 %all-to-all-start.1 = ((s16[16,136,128]{2,1,0:T(8,128)(2,1)}), s16[16,136,128]{2,1,0:T(8,128)(2,1)S(1)}, u32[]{:S(2)}, u32[]{:S(2)}) async-start(s16[16,136,128]{2,1,0:T(8,128)(2,1)} %bitcast.5), calls=%async_computation.1 | async-start | bytes 1114112 | tf_op jit(solution)/shard_map/all_to_all | solution.py:403

commit v8 on v7

--- a/solution.py
+++ b/solution.py
@@ -264,7 +264,7 @@
             pltpu.VMEM(total.shape, total.dtype),
             pltpu.VMEM((packed.shape[0] // 8, 8, LANES), jnp.int32),
         ],
-        compiler_params=pltpu.CompilerParams(vmem_limit_bytes=24 * 2**20),
+        compiler_params=pltpu.CompilerParams(vmem_limit_bytes=12 * 2**20),
         cost_estimate=pl.CostEstimate(
             flops=4 * count * depth * width,
             bytes_accessed=2 * depth * (width + 2 * count) + 8 * count * width * (1 + n_acc),
@@ -363,7 +363,7 @@
         out_specs=pl.BlockSpec(memory_space=pltpu.VMEM),
         out_shape=out,
         scratch_shapes=scratch,
-        compiler_params=pltpu.CompilerParams(vmem_limit_bytes=24 * 2**20),
+        compiler_params=pltpu.CompilerParams(vmem_limit_bytes=12 * 2**20),
     )(*args)
 
 

time: 91.9 us -> 91.9 us (level)
  no operation moved by 1% of the time
where the time goes in v8:
time: 91.9 us; the launch traced here: 91.6 us
  starting transfers between devices  26.5 us (29%)
  blocking collectives  23 us (25%)
  waiting for transfers between devices  21.9 us (24%)
  Pallas kernels  18.4 us (20%)
  local copies, waits for them, and re-layouts  1.68 us (2%)
    all_to_all x1, blocking collectives, exchange(): return lax.all_to_all(value, 'shell', 0, 0).reshape(parcels.shape)  23 us
    all_to_all x1, waiting for transfers between devices, exchange(): return lax.all_to_all(value, 'shell', 0, 0).reshape(parcels.shape)  14.9 us
    ppermute x7, starting transfers between devices, around(): return lax.ppermute(value, 'shell', onward)  14.4 us
    pallas_call x6, Pallas kernels, project(): pl.pallas_call(functools.partial(project_kernel, lax.axis_size('shell'),...  9.42 us
    ppermute x7, waiting for transfers between devices, around(): return lax.ppermute(value, 'shell', onward)  5.31 us
    pallas_call x1, Pallas kernels, sort_rows(): pl.pallas_call(sort_kernel, in_specs=[pl.BlockSpec(memory_space=pltpu.SME...  5.14 us
    ppermute x3, starting transfers between devices, across(): return lax.ppermute(value, 'grp', [(0, 1), (1, 0)])  4.98 us
    pallas_call x2, Pallas kernels, local_call(): pl.pallas_call(kernel, in_specs=[pl.BlockSpec(memory_space=pltpu.SMEM)] *...  3.89 us
  transfers between devices with their start and end apart: 24, of which 10 were waited for; matrix products, arithmetic and copies ran while one was open for 1% of the time, Pallas kernels for 14%

profile of v8, /device:TPU:0, one launch (start us, length us, event | category | flops | bytes accessed | tf_op | source)
XLA Modules:
  0.0 91.6 jit_solution(6175586006244549047)
XLA Ops:
  0.0 3.0 %collective-permute-start = (bf16[512,512]{1,0:T(8,128)(2,1)}, bf16[512,512]{1,0:T(8,128)(2,1)S(1)}, u32[]{:S(2)}, u32[]{:S(2)}) collective-permute-start(bf16[512,512]{1,0:T(8,128)(2,1)} %bitcast.16), channel_id=1, source_target_pairs={{0,4},{5,1},{4,8},{9,5},{8,12},{13,9},{12,14},{15,13},{14,10},{11,... | collective-permute-start | bytes 1572872 | tf_op jit(solution)/shard_map/ppermute | solution.py:385
  3.0 1.0 %dynamic-slice_bitcast_fusion = bf16[256,512]{1,0:T(8,128)(2,1)S(1)} fusion(bf16[1,512,512]{2,1,0:T(8,128)(2,1)} %param.5, s32[]{:T(128)S(6)} %select_n.22), kind=kLoop, calls=%fused_computation | loop fusion | bytes 524292 | tf_op jit(solution)/shard_map/dynamic_slice | solution.py:408
  4.0 0.7 collective-permute-start.1
  4.8 1.0 %collective-permute-start.5 = (bf16[512,512]{1,0:T(8,128)(2,1)}, bf16[512,512]{1,0:T(8,128)(2,1)S(1)}, u32[]{:S(2)}, u32[]{:S(2)}) collective-permute-start(bf16[512,512]{1,0:T(8,128)(2,1)} %bitcast.17), channel_id=1, source_target_pairs={{0,1},{1,0},{2,3},{3,2},{4,5},{5,4},{6,7},{7,6},{8,9},{9,8},{10,11... | collective-permute-start | bytes 1572872 | tf_op jit(solution)/shard_map/ppermute | solution.py:391
  5.8 0.7 copy-done.2
  6.4 5.1 %shard_map.46.rows_ref = bf16[16,256,1024]{2,1,0:T(8,128)(2,1)S(1)} custom-call(s32[8]{0:T(128)S(1)} %copy-done.2, bf16[4096,1024]{1,0:T(8,128)(2,1)} %bitcast.19), custom_call_target="tpu_custom_call" | custom-call | flops 2147483648 | bytes 16777216 | tf_op jit(solution)/shard_map/pallas_call | solution.py:137
  11.6 1.2 %collective-permute-done.1.refs_2_ = bf16[256,512]{1,0:T(8,128)(2,1)S(1)} collective-permute-done((bf16[256,512]{1,0:T(8,128)(2,1)S(1)}, bf16[256,512]{1,0:T(8,128)(2,1)S(1)}, u32[]{:S(2)}, u32[]{:S(2)}) %collective-permute-start.1) | collective-permute-done | bytes 262176 | tf_op jit(solution)/shard_map/ppermute | solution.py:388
  13.1 2.1 %collective-permute-start.2 = (bf16[512,512]{1,0:T(8,128)(2,1)S(1)}, bf16[512,512]{1,0:T(8,128)(2,1)S(1)}, u32[]{:S(2)}, u32[]{:S(2)}) collective-permute-start(bf16[512,512]{1,0:T(8,128)(2,1)S(1)} %collective-permute-done.refs_0_), channel_id=1, source_target_pairs={{0,4},{5,1},{4,8},{9,5},{8,12},{13,9},{12,14},{15,13},{14,10},{11,... | collective-permute-start | bytes 1572872 | tf_op jit(solution)/shard_map/ppermute | solution.py:385
  15.4 1.4 %collective-permute-start.8 = (bf16[256,512]{1,0:T(8,128)(2,1)S(1)}, bf16[256,512]{1,0:T(8,128)(2,1)S(1)}, u32[]{:S(2)}, u32[]{:S(2)}) collective-permute-start(bf16[256,512]{1,0:T(8,128)(2,1)S(1)} %collective-permute-done.1.refs_2_), channel_id=1, source_target_pairs={{0,4},{5,1},{4,8},{9,5},{8,12},{13,9},{12,14},{15,13},{14,10},{11,... | collective-permute-start | bytes 786440 | tf_op jit(solution)/shard_map/ppermute | solution.py:385
  16.8 1.5 %collective-permute-start.10 = (bf16[256,512]{1,0:T(8,128)(2,1)S(1)}, bf16[256,512]{1,0:T(8,128)(2,1)S(1)}, u32[]{:S(2)}, u32[]{:S(2)}) collective-permute-start(bf16[256,512]{1,0:T(8,128)(2,1)S(1)} %collective-permute-done.1.refs_2_), channel_id=1, source_target_pairs={{0,16},{16,0},{1,17},{17,1},{2,18},{18,2},{3,19},{19,3},{4,20},{20... | collective-permute-start | bytes 786440 | tf_op jit(solution)/shard_map/ppermute | solution.py:394
  18.3 1.3 %shard_map.47.refs_4_ = f32[512,512]{1,0:T(8,128)S(1)} custom-call(s32[16]{0:T(128)S(1)} %copy-done.1, bf16[16,256,1024]{2,1,0:T(8,128)(2,1)S(1)} %shard_map.46.rows_ref, bf16[512,512]{1,0:T(8,128)(2,1)S(1)} %bitcast.18, bf16[512,512]{1,0:T(8,128)(2,1)S(1)} %collective-permute-done.5.refs_1_), custom_call_target="tpu_custom_call" | custom-call | flops 536870912 | bytes 3145728 | tf_op jit(solution)/shard_map/pallas_call | solution.py:253
  19.6 1.5 %shard_map.48.refs_6_ = f32[512,512]{1,0:T(8,128)S(1)} custom-call(s32[16]{0:T(128)S(1)} %copy-done.1, bf16[16,256,1024]{2,1,0:T(8,128)(2,1)S(1)} %shard_map.46.rows_ref, bf16[512,512]{1,0:T(8,128)(2,1)S(1)} %collective-permute-done.refs_0_, bf16[512,512]{1,0:T(8,128)(2,1)S(1)} %collective-permute-done.3.refs_1_, ...), custom_call_target="tpu_custom_call" | custom-call | flops 805306368 | bytes 5242880 | tf_op jit(solution)/shard_map/pallas_call | solution.py:253
  21.1 1.2 %collective-permute-done.2.refs_0_ = bf16[512,512]{1,0:T(8,128)(2,1)S(1)} collective-permute-done((bf16[512,512]{1,0:T(8,128)(2,1)S(1)}, bf16[512,512]{1,0:T(8,128)(2,1)S(1)}, u32[]{:S(2)}, u32[]{:S(2)}) %collective-permute-start.2) | collective-permute-done | bytes 524320 | tf_op jit(solution)/shard_map/ppermute | solution.py:385
  22.3 2.1 %collective-permute-start.6 = (bf16[512,512]{1,0:T(8,128)(2,1)S(1)}, bf16[512,512]{1,0:T(8,128)(2,1)S(1)}, u32[]{:S(2)}, u32[]{:S(2)}) collective-permute-start(bf16[512,512]{1,0:T(8,128)(2,1)S(1)} %collective-permute-done.2.refs_0_), channel_id=1, source_target_pairs={{0,4},{5,1},{4,8},{9,5},{8,12},{13,9},{12,14},{15,13},{14,10},{11,... | collective-permute-start | bytes 1572872 | tf_op jit(solution)/shard_map/ppermute | solution.py:385
  24.4 0.7 collective-permute-done.8.refs_2_
  25.1 0.5 collective-permute-start.11
  25.7 2.0 %collective-permute-start.16 = (bf16[256,512]{1,0:T(8,128)(2,1)S(1)}, bf16[256,512]{1,0:T(8,128)(2,1)S(1)}, u32[]{:S(2)}, u32[]{:S(2)}) collective-permute-start(bf16[256,512]{1,0:T(8,128)(2,1)S(1)} %collective-permute-done.8.refs_2_), channel_id=1, source_target_pairs={{0,16},{16,0},{1,17},{17,1},{2,18},{18,2},{3,19},{19,3},{4,20},{20... | collective-permute-start | bytes 786440 | tf_op jit(solution)/shard_map/ppermute | solution.py:394
  27.7 1.6 %collective-permute-start.14 = (bf16[256,512]{1,0:T(8,128)(2,1)S(1)}, bf16[256,512]{1,0:T(8,128)(2,1)S(1)}, u32[]{:S(2)}, u32[]{:S(2)}) collective-permute-start(bf16[256,512]{1,0:T(8,128)(2,1)S(1)} %collective-permute-done.8.refs_2_), channel_id=1, source_target_pairs={{0,4},{5,1},{4,8},{9,5},{8,12},{13,9},{12,14},{15,13},{14,10},{11,... | collective-permute-start | bytes 786440 | tf_op jit(solution)/shard_map/ppermute | solution.py:385
  29.2 1.8 %shard_map.49.refs_6_ = f32[512,512]{1,0:T(8,128)S(1)} custom-call(s32[16]{0:T(128)S(1)} %copy-done.1, bf16[16,256,1024]{2,1,0:T(8,128)(2,1)S(1)} %shard_map.46.rows_ref, bf16[512,512]{1,0:T(8,128)(2,1)S(1)} %collective-permute-done.2.refs_0_, bf16[512,512]{1,0:T(8,128)(2,1)S(1)} %collective-permute-done.7.refs_1_, ...), custom_call_target="tpu_custom_call" | custom-call | flops 1073741824 | bytes 6291456 | tf_op jit(solution)/shard_map/pallas_call | solution.py:253
  31.5 2.1 %collective-permute-start.12 = (bf16[512,512]{1,0:T(8,128)(2,1)S(1)}, bf16[512,512]{1,0:T(8,128)(2,1)S(1)}, u32[]{:S(2)}, u32[]{:S(2)}) collective-permute-start(bf16[512,512]{1,0:T(8,128)(2,1)S(1)} %collective-permute-done.6.refs_0_), channel_id=1, source_target_pairs={{0,4},{5,1},{4,8},{9,5},{8,12},{13,9},{12,14},{15,13},{14,10},{11,... | collective-permute-start | bytes 1572872 | tf_op jit(solution)/shard_map/ppermute | solution.py:385
  33.6 0.7 collective-permute-done.14.refs_2_
  34.9 2.1 %collective-permute-start.18 = (bf16[128,512]{1,0:T(8,128)(2,1)S(1)}, bf16[128,512]{1,0:T(8,128)(2,1)S(1)}, u32[]{:S(2)}, u32[]{:S(2)}) collective-permute-start(bf16[128,512]{1,0:T(8,128)(2,1)S(1)} %slice.8), channel_id=1, source_target_pairs={{0,4},{5,1},{4,8},{9,5},{8,12},{13,9},{12,14},{15,13},{14,10},{11,... | collective-permute-start | bytes 393224 | tf_op jit(solution)/shard_map/ppermute | solution.py:385
  37.0 1.5 %collective-permute-start.19 = (bf16[128,512]{1,0:T(8,128)(2,1)S(1)}, bf16[128,512]{1,0:T(8,128)(2,1)S(1)}, u32[]{:S(2)}, u32[]{:S(2)}) collective-permute-start(bf16[128,512]{1,0:T(8,128)(2,1)S(1)} %slice.9), channel_id=1, source_target_pairs={{0,16},{16,0},{1,17},{17,1},{2,18},{18,2},{3,19},{19,3},{4,20},{20... | collective-permute-start | bytes 393224 | tf_op jit(solution)/shard_map/ppermute | solution.py:394
  38.5 1.8 %shard_map.50.refs_3_ = f32[512,512]{1,0:T(8,128)S(1)} custom-call(s32[16]{0:T(128)S(1)} %copy-done.1, bf16[16,256,1024]{2,1,0:T(8,128)(2,1)S(1)} %shard_map.46.rows_ref, bf16[512,512]{1,0:T(8,128)(2,1)S(1)} %collective-permute-done.6.refs_0_, bf16[512,512]{1,0:T(8,128)(2,1)S(1)} %collective-permute-done.13.refs_1_, ...), custom_call_target="tpu_custom_call" | custom-call | flops 1073741824 | bytes 6291456 | tf_op jit(solution)/shard_map/pallas_call | solution.py:253
  40.3 1.8 %collective-permute-done.18.refs_1_ = bf16[128,512]{1,0:T(8,128)(2,1)S(1)} collective-permute-done((bf16[128,512]{1,0:T(8,128)(2,1)S(1)}, bf16[128,512]{1,0:T(8,128)(2,1)S(1)}, u32[]{:S(2)}, u32[]{:S(2)}) %collective-permute-start.18) | collective-permute-done | bytes 131104 | tf_op jit(solution)/shard_map/ppermute | solution.py:385
  42.7 1.2 %shard_map.51.refs_3_ = f32[512,512]{1,0:T(8,128)S(1)} custom-call(s32[16]{0:T(128)S(1)} %copy-done.1, bf16[16,256,1024]{2,1,0:T(8,128)(2,1)S(1)} %shard_map.46.rows_ref, bf16[512,512]{1,0:T(8,128)(2,1)S(1)} %collective-permute-done.12.refs_0_, bf16[128,512]{1,0:T(8,128)(2,1)S(1)} %collective-permute-done.18.refs_1_, ...), custom_call_target="tpu_custom_call" | custom-call | flops 402653184 | bytes 3670016 | tf_op jit(solution)/shard_map/pallas_call | solution.py:253
  44.4 1.8 %shard_map.52 = s16[2176,128]{1,0:T(8,128)(2,1)S(1)} custom-call(s32[16]{0:T(128)S(1)} %copy-done.1, bf16[16,256,1024]{2,1,0:T(8,128)(2,1)S(1)} %shard_map.46.rows_ref, bf16[512,512]{1,0:T(8,128)(2,1)S(1)} %collective-permute-done.20.refs_0_, bf16[128,512]{1,0:T(8,128)(2,1)S(1)} %collective-permute-done.21.refs_1_, ...), custom_call_target="tpu_custom_call" | custom-call | flops 402653184 | bytes 3670016 | tf_op jit(solution)/shard_map/pallas_call | solution.py:253
  46.2 23.0 %all_to_all.10 = s16[16,136,128]{2,1,0:T(8,128)(2,1)S(1)} all-to-all(s16[16,136,128]{2,1,0:T(8,128)(2,1)S(1)} %bitcast.15), channel_id=1, replica_groups=mesh['grp'=2,'shell'=16] {'shell'}, dimensions={0} | all-to-all | bytes 1114112 | tf_op jit(solution)/shard_map/all_to_all | solution.py:403
  69.2 1.7 %shard_map.53 = s16[2176,128]{1,0:T(8,128)(2,1)} custom-call(s16[2176,128]{1,0:T(8,128)(2,1)S(1)} %bitcast.14), custom_call_target="tpu_custom_call" | custom-call | tf_op jit(solution)/shard_map/pallas_call | solution.py:359
  70.9 3.6 %all-to-all-start.1 = ((s16[16,136,128]{2,1,0:T(8,128)(2,1)}), s16[16,136,128]{2,1,0:T(8,128)(2,1)S(1)}, u32[]{:S(2)}, u32[]{:S(2)}) async-start(s16[16,136,128]{2,1,0:T(8,128)(2,1)} %bitcast.5), calls=%async_computation.1 | async-start | bytes 1114112 | tf_op jit(solution)/shard_map/all_to_all | solution.py:403
  74.5 14.9 %all-to-all-done.1 = s16[16,136,128]{2,1,0:T(8,128)(2,1)S(1)} async-done(((s16[16,136,128]{2,1,0:T(8,128)(2,1)}), s16[16,136,128]{2,1,0:T(8,128)(2,1)S(1)}, u32[]{:S(2)}, u32[]{:S(2)}) %all-to-all-start.1) | async-done | bytes 557088 | tf_op jit(solution)/shard_map/all_to_all | solution.py:403
  89.4 2.2 %shard_map.54 = f32[2048,128]{1,0:T(8,128)} custom-call(f32[2,32]{1,0:T(2,128)S(1)} %maximum_multiply_fusion.twist_ref, s16[2176,128]{1,0:T(8,128)(2,1)S(1)} %bitcast.13), custom_call_target="tpu_custom_call" | custom-call | tf_op jit(solution)/shard_map/pallas_call | solution.py:359
  (37 shorter events, 2.7 us)
Async XLA Ops:
  0.0 13.1 %collective-permute-start = (bf16[512,512]{1,0:T(8,128)(2,1)}, bf16[512,512]{1,0:T(8,128)(2,1)S(1)}, u32[]{:S(2)}, u32[]{:S(2)}) collective-permute-start(bf16[512,512]{1,0:T(8,128)(2,1)} %bitcast.16), channel_id=1, source_target_pairs={{0,4},{5,1},{4,8},{9,5},{8,12},{13,9},{12,14},{15,13},{14,10},{11,... | collective-permute-start | bytes 1572872 | tf_op jit(solution)/shard_map/ppermute | solution.py:385
  4.0 8.7 %collective-permute-start.1 = (bf16[256,512]{1,0:T(8,128)(2,1)S(1)}, bf16[256,512]{1,0:T(8,128)(2,1)S(1)}, u32[]{:S(2)}, u32[]{:S(2)}) collective-permute-start(bf16[256,512]{1,0:T(8,128)(2,1)S(1)} %dynamic-slice_bitcast_fusion), channel_id=1, source_target_pairs={{1,4},{4,1},{5,8},{8,5},{9,12},{12,9},{13,14},{14,13},{15,10},{10,... | collective-permute-start | bytes 786440 | tf_op jit(solution)/shard_map/ppermute | solution.py:388
  4.8 12.0 %collective-permute-start.5 = (bf16[512,512]{1,0:T(8,128)(2,1)}, bf16[512,512]{1,0:T(8,128)(2,1)S(1)}, u32[]{:S(2)}, u32[]{:S(2)}) collective-permute-start(bf16[512,512]{1,0:T(8,128)(2,1)} %bitcast.17), channel_id=1, source_target_pairs={{0,1},{1,0},{2,3},{3,2},{4,5},{5,4},{6,7},{7,6},{8,9},{9,8},{10,11... | collective-permute-start | bytes 1572872 | tf_op jit(solution)/shard_map/ppermute | solution.py:391
  5.8 0.7 copy-start.2
  6.4 11.9 %copy-start = (bf16[1,512,512]{2,1,0:T(8,128)(2,1)S(1)}, bf16[1,512,512]{2,1,0:T(8,128)(2,1)}, u32[]{:S(2)}) copy-start(bf16[1,512,512]{2,1,0:T(8,128)(2,1)} %param.5) | copy-start | bytes 1572868
  6.4 11.9 %copy-start.1 = (s32[16]{0:T(128)S(1)}, s32[16]{0:T(128)}, u32[]{:S(2)}) copy-start(s32[16]{0:T(128)} %owner_ref.11) | copy-start | bytes 196
  13.1 6.4 %collective-permute-start.3 = (bf16[512,512]{1,0:T(8,128)(2,1)S(1)}, bf16[512,512]{1,0:T(8,128)(2,1)S(1)}, u32[]{:S(2)}, u32[]{:S(2)}) collective-permute-start(bf16[512,512]{1,0:T(8,128)(2,1)S(1)} %collective-permute-done.refs_0_), channel_id=1, source_target_pairs={{0,1},{1,0},{2,3},{3,2},{4,5},{5,4},{6,7},{7,6},{8,9},{9,8},{10,11... | collective-permute-start | bytes 1572872 | tf_op jit(solution)/shard_map/ppermute | solution.py:391
  13.1 9.2 %collective-permute-start.2 = (bf16[512,512]{1,0:T(8,128)(2,1)S(1)}, bf16[512,512]{1,0:T(8,128)(2,1)S(1)}, u32[]{:S(2)}, u32[]{:S(2)}) collective-permute-start(bf16[512,512]{1,0:T(8,128)(2,1)S(1)} %collective-permute-done.refs_0_), channel_id=1, source_target_pairs={{0,4},{5,1},{4,8},{9,5},{8,12},{13,9},{12,14},{15,13},{14,10},{11,... | collective-permute-start | bytes 1572872 | tf_op jit(solution)/shard_map/ppermute | solution.py:385
  15.2 4.3 %collective-permute-start.4 = (bf16[256,512]{1,0:T(8,128)(2,1)S(1)}, bf16[256,512]{1,0:T(8,128)(2,1)S(1)}, u32[]{:S(2)}, u32[]{:S(2)}) collective-permute-start(bf16[256,512]{1,0:T(8,128)(2,1)S(1)} %collective-permute-done.1.refs_2_), channel_id=1, source_target_pairs={{0,1},{1,0},{2,3},{3,2},{4,5},{5,4},{6,7},{7,6},{8,9},{9,8},{10,11... | collective-permute-start | bytes 786440 | tf_op jit(solution)/shard_map/ppermute | solution.py:391
  15.4 9.7 %collective-permute-start.8 = (bf16[256,512]{1,0:T(8,128)(2,1)S(1)}, bf16[256,512]{1,0:T(8,128)(2,1)S(1)}, u32[]{:S(2)}, u32[]{:S(2)}) collective-permute-start(bf16[256,512]{1,0:T(8,128)(2,1)S(1)} %collective-permute-done.1.refs_2_), channel_id=1, source_target_pairs={{0,4},{5,1},{4,8},{9,5},{8,12},{13,9},{12,14},{15,13},{14,10},{11,... | collective-permute-start | bytes 786440 | tf_op jit(solution)/shard_map/ppermute | solution.py:385
  16.8 8.3 %collective-permute-start.10 = (bf16[256,512]{1,0:T(8,128)(2,1)S(1)}, bf16[256,512]{1,0:T(8,128)(2,1)S(1)}, u32[]{:S(2)}, u32[]{:S(2)}) collective-permute-start(bf16[256,512]{1,0:T(8,128)(2,1)S(1)} %collective-permute-done.1.refs_2_), channel_id=1, source_target_pairs={{0,16},{16,0},{1,17},{17,1},{2,18},{18,2},{3,19},{19,3},{4,20},{20... | collective-permute-start | bytes 786440 | tf_op jit(solution)/shard_map/ppermute | solution.py:394
  22.3 6.9 %collective-permute-start.7 = (bf16[512,512]{1,0:T(8,128)(2,1)S(1)}, bf16[512,512]{1,0:T(8,128)(2,1)S(1)}, u32[]{:S(2)}, u32[]{:S(2)}) collective-permute-start(bf16[512,512]{1,0:T(8,128)(2,1)S(1)} %collective-permute-done.2.refs_0_), channel_id=1, source_target_pairs={{0,1},{1,0},{2,3},{3,2},{4,5},{5,4},{6,7},{7,6},{8,9},{9,8},{10,11... | collective-permute-start | bytes 1572872 | tf_op jit(solution)/shard_map/ppermute | solution.py:391
  22.3 9.2 %collective-permute-start.6 = (bf16[512,512]{1,0:T(8,128)(2,1)S(1)}, bf16[512,512]{1,0:T(8,128)(2,1)S(1)}, u32[]{:S(2)}, u32[]{:S(2)}) collective-permute-start(bf16[512,512]{1,0:T(8,128)(2,1)S(1)} %collective-permute-done.2.refs_0_), channel_id=1, source_target_pairs={{0,4},{5,1},{4,8},{9,5},{8,12},{13,9},{12,14},{15,13},{14,10},{11,... | collective-permute-start | bytes 1572872 | tf_op jit(solution)/shard_map/ppermute | solution.py:385
  25.1 2.5 %collective-permute-start.9 = (bf16[256,512]{1,0:T(8,128)(2,1)S(1)}, bf16[256,512]{1,0:T(8,128)(2,1)S(1)}, u32[]{:S(2)}, u32[]{:S(2)}) collective-permute-start(bf16[256,512]{1,0:T(8,128)(2,1)S(1)} %collective-permute-done.8.refs_2_), channel_id=1, source_target_pairs={{0,1},{1,0},{2,3},{3,2},{4,5},{5,4},{6,7},{7,6},{8,9},{9,8},{10,11... | collective-permute-start | bytes 786440 | tf_op jit(solution)/shard_map/ppermute | solution.py:391
  25.1 4.1 %collective-permute-start.11 = (bf16[256,512]{1,0:T(8,128)(2,1)S(1)}, bf16[256,512]{1,0:T(8,128)(2,1)S(1)}, u32[]{:S(2)}, u32[]{:S(2)}) collective-permute-start(bf16[256,512]{1,0:T(8,128)(2,1)S(1)} %collective-permute-done.10.refs_4_), channel_id=1, source_target_pairs={{0,1},{1,0},{2,3},{3,2},{4,5},{5,4},{6,7},{7,6},{8,9},{9,8},{10,11... | collective-permute-start | bytes 786440 | tf_op jit(solution)/shard_map/ppermute | solution.py:391
  25.7 8.7 %collective-permute-start.16 = (bf16[256,512]{1,0:T(8,128)(2,1)S(1)}, bf16[256,512]{1,0:T(8,128)(2,1)S(1)}, u32[]{:S(2)}, u32[]{:S(2)}) collective-permute-start(bf16[256,512]{1,0:T(8,128)(2,1)S(1)} %collective-permute-done.8.refs_2_), channel_id=1, source_target_pairs={{0,16},{16,0},{1,17},{17,1},{2,18},{18,2},{3,19},{19,3},{4,20},{20... | collective-permute-start | bytes 786440 | tf_op jit(solution)/shard_map/ppermute | solution.py:394
  27.7 6.7 %collective-permute-start.14 = (bf16[256,512]{1,0:T(8,128)(2,1)S(1)}, bf16[256,512]{1,0:T(8,128)(2,1)S(1)}, u32[]{:S(2)}, u32[]{:S(2)}) collective-permute-start(bf16[256,512]{1,0:T(8,128)(2,1)S(1)} %collective-permute-done.8.refs_2_), channel_id=1, source_target_pairs={{0,4},{5,1},{4,8},{9,5},{8,12},{13,9},{12,14},{15,13},{14,10},{11,... | collective-permute-start | bytes 786440 | tf_op jit(solution)/shard_map/ppermute | solution.py:385
  31.5 7.0 %collective-permute-start.13 = (bf16[512,512]{1,0:T(8,128)(2,1)S(1)}, bf16[512,512]{1,0:T(8,128)(2,1)S(1)}, u32[]{:S(2)}, u32[]{:S(2)}) collective-permute-start(bf16[512,512]{1,0:T(8,128)(2,1)S(1)} %collective-permute-done.6.refs_0_), channel_id=1, source_target_pairs={{0,1},{1,0},{2,3},{3,2},{4,5},{5,4},{6,7},{7,6},{8,9},{9,8},{10,11... | collective-permute-start | bytes 1572872 | tf_op jit(solution)/shard_map/ppermute | solution.py:391
  31.5 10.6 %collective-permute-start.12 = (bf16[512,512]{1,0:T(8,128)(2,1)S(1)}, bf16[512,512]{1,0:T(8,128)(2,1)S(1)}, u32[]{:S(2)}, u32[]{:S(2)}) collective-permute-start(bf16[512,512]{1,0:T(8,128)(2,1)S(1)} %collective-permute-done.6.refs_0_), channel_id=1, source_target_pairs={{0,4},{5,1},{4,8},{9,5},{8,12},{13,9},{12,14},{15,13},{14,10},{11,... | collective-permute-start | bytes 1572872 | tf_op jit(solution)/shard_map/ppermute | solution.py:385
  34.3 2.7 %collective-permute-start.15 = (bf16[256,512]{1,0:T(8,128)(2,1)S(1)}, bf16[256,512]{1,0:T(8,128)(2,1)S(1)}, u32[]{:S(2)}, u32[]{:S(2)}) collective-permute-start(bf16[256,512]{1,0:T(8,128)(2,1)S(1)} %collective-permute-done.14.refs_2_), channel_id=1, source_target_pairs={{0,1},{1,0},{2,3},{3,2},{4,5},{5,4},{6,7},{7,6},{8,9},{9,8},{10,11... | collective-permute-start | bytes 786440 | tf_op jit(solution)/shard_map/ppermute | solution.py:391
  34.3 4.2 %collective-permute-start.17 = (bf16[256,512]{1,0:T(8,128)(2,1)S(1)}, bf16[256,512]{1,0:T(8,128)(2,1)S(1)}, u32[]{:S(2)}, u32[]{:S(2)}) collective-permute-start(bf16[256,512]{1,0:T(8,128)(2,1)S(1)} %collective-permute-done.16.refs_4_), channel_id=1, source_target_pairs={{0,1},{1,0},{2,3},{3,2},{4,5},{5,4},{6,7},{7,6},{8,9},{9,8},{10,11... | collective-permute-start | bytes 786440 | tf_op jit(solution)/shard_map/ppermute | solution.py:391
  34.9 7.2 %collective-permute-start.18 = (bf16[128,512]{1,0:T(8,128)(2,1)S(1)}, bf16[128,512]{1,0:T(8,128)(2,1)S(1)}, u32[]{:S(2)}, u32[]{:S(2)}) collective-permute-start(bf16[128,512]{1,0:T(8,128)(2,1)S(1)} %slice.8), channel_id=1, source_target_pairs={{0,4},{5,1},{4,8},{9,5},{8,12},{13,9},{12,14},{15,13},{14,10},{11,... | collective-permute-start | bytes 393224 | tf_op jit(solution)/shard_map/ppermute | solution.py:385
  37.0 5.1 %collective-permute-start.19 = (bf16[128,512]{1,0:T(8,128)(2,1)S(1)}, bf16[128,512]{1,0:T(8,128)(2,1)S(1)}, u32[]{:S(2)}, u32[]{:S(2)}) collective-permute-start(bf16[128,512]{1,0:T(8,128)(2,1)S(1)} %slice.9), channel_id=1, source_target_pairs={{0,16},{16,0},{1,17},{17,1},{2,18},{18,2},{3,19},{19,3},{4,20},{20... | collective-permute-start | bytes 393224 | tf_op jit(solution)/shard_map/ppermute | solution.py:394
  42.1 2.3 %collective-permute-start.20 = (bf16[512,512]{1,0:T(8,128)(2,1)S(1)}, bf16[512,512]{1,0:T(8,128)(2,1)S(1)}, u32[]{:S(2)}, u32[]{:S(2)}) collective-permute-start(bf16[512,512]{1,0:T(8,128)(2,1)S(1)} %collective-permute-done.12.refs_0_), channel_id=1, source_target_pairs={{0,1},{1,0},{2,3},{3,2},{4,5},{5,4},{6,7},{7,6},{8,9},{9,8},{10,11... | collective-permute-start | bytes 1572872 | tf_op jit(solution)/shard_map/ppermute | solution.py:391
  42.1 2.1 %collective-permute-start.21 = (bf16[128,512]{1,0:T(8,128)(2,1)S(1)}, bf16[128,512]{1,0:T(8,128)(2,1)S(1)}, u32[]{:S(2)}, u32[]{:S(2)}) collective-permute-start(bf16[128,512]{1,0:T(8,128)(2,1)S(1)} %collective-permute-done.18.refs_1_), channel_id=1, source_target_pairs={{0,1},{1,0},{2,3},{3,2},{4,5},{5,4},{6,7},{7,6},{8,9},{9,8},{10,11... | collective-permute-start | bytes 393224 | tf_op jit(solution)/shard_map/ppermute | solution.py:391
  42.6 1.8 %collective-permute-start.22 = (bf16[128,512]{1,0:T(8,128)(2,1)S(1)}, bf16[128,512]{1,0:T(8,128)(2,1)S(1)}, u32[]{:S(2)}, u32[]{:S(2)}) collective-permute-start(bf16[128,512]{1,0:T(8,128)(2,1)S(1)} %collective-permute-done.19.refs_2_), channel_id=1, source_target_pairs={{0,1},{1,0},{2,3},{3,2},{4,5},{5,4},{6,7},{7,6},{8,9},{9,8},{10,11... | collective-permute-start | bytes 393224 | tf_op jit(solution)/shard_map/ppermute | solution.py:391
  70.9 18.6 %all-to-all-start.1 = ((s16[16,136,128]{2,1,0:T(8,128)(2,1)}), s16[16,136,128]{2,1,0:T(8,128)(2,1)S(1)}, u32[]{:S(2)}, u32[]{:S(2)}) async-start(s16[16,136,128]{2,1,0:T(8,128)(2,1)} %bitcast.5), calls=%async_computation.1 | async-start | bytes 1114112 | tf_op jit(solution)/shard_map/all_to_all | solution.py:403

commit v9 on v8

--- a/solution.py
+++ b/solution.py
@@ -384,9 +384,6 @@
     def around(value):
         return lax.ppermute(value, "shell", onward)
 
-    def crosswise(value):
-        return lax.ppermute(value, "shell", [(source ^ 1, target) for source, target in onward])
-
     def sibling(value):
         return lax.ppermute(value, "shell", [(s, s ^ 1) for s in range(devices)])
 
@@ -405,11 +402,11 @@
     own = panel_pool[0]
     half = own.shape[0] // 2
     whole = around(own)
-    part = crosswise(lax.dynamic_slice_in_dim(own, half * lax.axis_index("grp"), half))
     other = sibling(own)
+    part = around(lax.dynamic_slice_in_dim(other, half * lax.axis_index("grp"), half))
     rows = sort_rows(pair_coef, batch_order)
     acc = project(None, rows, degree_owner, [own, other], [(0, 0, None), (0, 1, None)])
-    whole, part, rows = lax.optimization_barrier((whole, part, rows))
+    whole, rows = lax.optimization_barrier((whole, rows))
     late, late_from = [], []
     for step in range(1, chips // 2):
         if step > 1:

time: 91.9 us -> 89.7 us (0.976)
  waiting for transfers between devices: 21.9 us -> 25.3 us
  starting transfers between devices: 26.5 us -> 23.4 us
  blocking collectives: 23 us -> 21.5 us
  local copies, waits for them, and re-layouts: 1.68 us -> 0.71 us
    ppermute x3, waiting for transfers between devices: 0.01 us -> 2.83 us  [across(): return lax.ppermute(value, 'grp', [(0, 1), (1, 0)])]
    ppermute x12, starting transfers between devices: 2.79 us -> 1.06 us  [sibling(): return lax.ppermute(value, 'shell', [(s, s ^ 1) for s in range(devices)])]
    ppermute x7 -> x8, waiting for transfers between devices: 5.31 us -> 6.99 us  [around(): return lax.ppermute(value, 'shell', onward)]
    all_to_all x1, blocking collectives: 23 us -> 21.5 us  [exchange(): return lax.all_to_all(value, 'shell', 0, 0).reshape(parcels.shape)]
    ppermute x1 -> x0, waiting for transfers between devices: 1.17 us -> none  [crosswise(): lax.ppermute(value, 'shell', [(source ^ 1, target) for source, target in...]
    dynamic_slice x1, local copies, waits for them, and re-layouts: 1 us -> 0.03 us  [shards(): lax.dynamic_slice_in_dim(other, half * lax.axis_index('grp'), half)]
    ppermute x7 -> x8, starting transfers between devices: 14.4 us -> 14.2 us  [around(): return lax.ppermute(value, 'shell', onward)]
  transfers between devices with their start and end apart: 24 -> 24, of which waited for: 10 -> 11; matrix products, arithmetic and copies ran while one was open for 1% -> 0% of each run, Pallas kernels for 14% -> 14%
where the time goes in v9:
time: 89.7 us; the launch traced here: 89.5 us
  waiting for transfers between devices  25.3 us (28%)
  starting transfers between devices  23.4 us (26%)
  blocking collectives  21.5 us (24%)
  Pallas kernels  18.5 us (21%)
    all_to_all x1, blocking collectives, exchange(): return lax.all_to_all(value, 'shell', 0, 0).reshape(parcels.shape)  21.5 us
    all_to_all x1, waiting for transfers between devices, exchange(): return lax.all_to_all(value, 'shell', 0, 0).reshape(parcels.shape)  14.9 us
    ppermute x8, starting transfers between devices, around(): return lax.ppermute(value, 'shell', onward)  14.2 us
    pallas_call x6, Pallas kernels, project(): pl.pallas_call(functools.partial(project_kernel, lax.axis_size('shell'),...  9.43 us
    ppermute x8, waiting for transfers between devices, around(): return lax.ppermute(value, 'shell', onward)  6.99 us
    pallas_call x1, Pallas kernels, sort_rows(): pl.pallas_call(sort_kernel, in_specs=[pl.BlockSpec(memory_space=pltpu.SME...  5.14 us
    ppermute x3, starting transfers between devices, across(): return lax.ppermute(value, 'grp', [(0, 1), (1, 0)])  4.53 us
    pallas_call x2, Pallas kernels, local_call(): pl.pallas_call(kernel, in_specs=[pl.BlockSpec(memory_space=pltpu.SMEM)] *...  3.89 us
  transfers between devices with their start and end apart: 24, of which 11 were waited for; matrix products, arithmetic and copies ran while one was open for 0% of the time, Pallas kernels for 14%

profile of v9, /device:TPU:0, one launch (start us, length us, event | category | flops | bytes accessed | tf_op | source)
XLA Modules:
  0.0 89.5 jit_solution(6348858700780419694)
XLA Ops:
  0.0 0.5 collective-permute-start.3
  0.5 2.6 %collective-permute-start = (bf16[512,512]{1,0:T(8,128)(2,1)}, bf16[512,512]{1,0:T(8,128)(2,1)S(1)}, u32[]{:S(2)}, u32[]{:S(2)}) collective-permute-start(bf16[512,512]{1,0:T(8,128)(2,1)} %bitcast.15), channel_id=1, source_target_pairs={{0,4},{5,1},{4,8},{9,5},{8,12},{13,9},{12,14},{15,13},{14,10},{11,... | collective-permute-start | bytes 1572872 | tf_op jit(solution)/shard_map/ppermute | solution.py:385
  3.0 0.7 copy-done.2
  3.7 5.1 %shard_map.46.rows_ref = bf16[16,256,1024]{2,1,0:T(8,128)(2,1)S(1)} custom-call(s32[8]{0:T(128)S(1)} %copy-done.2, bf16[4096,1024]{1,0:T(8,128)(2,1)} %bitcast.17), custom_call_target="tpu_custom_call" | custom-call | flops 2147483648 | bytes 16777216 | tf_op jit(solution)/shard_map/pallas_call | solution.py:137
  8.9 1.6 %collective-permute-start.4 = (bf16[256,512]{1,0:T(8,128)(2,1)S(1)}, bf16[256,512]{1,0:T(8,128)(2,1)S(1)}, u32[]{:S(2)}, u32[]{:S(2)}) collective-permute-start(bf16[256,512]{1,0:T(8,128)(2,1)S(1)} %constant_dynamic-slice_fusion), channel_id=1, source_target_pairs={{0,4},{5,1},{4,8},{9,5},{8,12},{13,9},{12,14},{15,13},{14,10},{11,... | collective-permute-start | bytes 786440 | tf_op jit(solution)/shard_map/ppermute | solution.py:385
  10.5 1.9 %collective-permute-start.1 = (bf16[512,512]{1,0:T(8,128)(2,1)S(1)}, bf16[512,512]{1,0:T(8,128)(2,1)S(1)}, u32[]{:S(2)}, u32[]{:S(2)}) collective-permute-start(bf16[512,512]{1,0:T(8,128)(2,1)S(1)} %collective-permute-done.refs_0_), channel_id=1, source_target_pairs={{0,4},{5,1},{4,8},{9,5},{8,12},{13,9},{12,14},{15,13},{14,10},{11,... | collective-permute-start | bytes 1572872 | tf_op jit(solution)/shard_map/ppermute | solution.py:385
  12.4 2.9 %collective-permute-done.4.refs_2_ = bf16[256,512]{1,0:T(8,128)(2,1)S(1)} collective-permute-done((bf16[256,512]{1,0:T(8,128)(2,1)S(1)}, bf16[256,512]{1,0:T(8,128)(2,1)S(1)}, u32[]{:S(2)}, u32[]{:S(2)}) %collective-permute-start.4) | collective-permute-done | bytes 262176 | tf_op jit(solution)/shard_map/ppermute | solution.py:385
  15.3 1.3 %shard_map.47.refs_4_ = f32[512,512]{1,0:T(8,128)S(1)} custom-call(s32[16]{0:T(128)S(1)} %copy-done.1, bf16[16,256,1024]{2,1,0:T(8,128)(2,1)S(1)} %shard_map.46.rows_ref, bf16[512,512]{1,0:T(8,128)(2,1)S(1)} %bitcast.16, bf16[512,512]{1,0:T(8,128)(2,1)S(1)} %collective-permute-done.3.refs_1_), custom_call_target="tpu_custom_call" | custom-call | flops 536870912 | bytes 3145728 | tf_op jit(solution)/shard_map/pallas_call | solution.py:253
  16.6 1.6 %collective-permute-start.8 = (bf16[256,512]{1,0:T(8,128)(2,1)S(1)}, bf16[256,512]{1,0:T(8,128)(2,1)S(1)}, u32[]{:S(2)}, u32[]{:S(2)}) collective-permute-start(bf16[256,512]{1,0:T(8,128)(2,1)S(1)} %collective-permute-done.4.refs_2_), channel_id=1, source_target_pairs={{0,4},{5,1},{4,8},{9,5},{8,12},{13,9},{12,14},{15,13},{14,10},{11,... | collective-permute-start | bytes 786440 | tf_op jit(solution)/shard_map/ppermute | solution.py:385
  18.2 1.5 %collective-permute-start.10 = (bf16[256,512]{1,0:T(8,128)(2,1)S(1)}, bf16[256,512]{1,0:T(8,128)(2,1)S(1)}, u32[]{:S(2)}, u32[]{:S(2)}) collective-permute-start(bf16[256,512]{1,0:T(8,128)(2,1)S(1)} %collective-permute-done.4.refs_2_), channel_id=1, source_target_pairs={{0,16},{16,0},{1,17},{17,1},{2,18},{18,2},{3,19},{19,3},{4,20},{20... | collective-permute-start | bytes 786440 | tf_op jit(solution)/shard_map/ppermute | solution.py:391
  19.7 1.5 %shard_map.48.refs_6_ = f32[512,512]{1,0:T(8,128)S(1)} custom-call(s32[16]{0:T(128)S(1)} %copy-done.1, bf16[16,256,1024]{2,1,0:T(8,128)(2,1)S(1)} %shard_map.46.rows_ref, bf16[512,512]{1,0:T(8,128)(2,1)S(1)} %collective-permute-done.refs_0_, bf16[512,512]{1,0:T(8,128)(2,1)S(1)} %collective-permute-done.2.refs_1_, ...), custom_call_target="tpu_custom_call" | custom-call | flops 805306368 | bytes 5242880 | tf_op jit(solution)/shard_map/pallas_call | solution.py:253
  21.3 1.6 %collective-permute-start.6 = (bf16[512,512]{1,0:T(8,128)(2,1)S(1)}, bf16[512,512]{1,0:T(8,128)(2,1)S(1)}, u32[]{:S(2)}, u32[]{:S(2)}) collective-permute-start(bf16[512,512]{1,0:T(8,128)(2,1)S(1)} %collective-permute-done.1.refs_0_), channel_id=1, source_target_pairs={{0,4},{5,1},{4,8},{9,5},{8,12},{13,9},{12,14},{15,13},{14,10},{11,... | collective-permute-start | bytes 1572872 | tf_op jit(solution)/shard_map/ppermute | solution.py:385
  23.0 0.8 collective-permute-done.8.refs_2_
  23.7 1.7 %collective-permute-done.10.refs_4_ = bf16[256,512]{1,0:T(8,128)(2,1)S(1)} collective-permute-done((bf16[256,512]{1,0:T(8,128)(2,1)S(1)}, bf16[256,512]{1,0:T(8,128)(2,1)S(1)}, u32[]{:S(2)}, u32[]{:S(2)}) %collective-permute-start.10) | collective-permute-done | bytes 262176 | tf_op jit(solution)/shard_map/ppermute | solution.py:391
  25.5 1.6 %collective-permute-start.16 = (bf16[256,512]{1,0:T(8,128)(2,1)S(1)}, bf16[256,512]{1,0:T(8,128)(2,1)S(1)}, u32[]{:S(2)}, u32[]{:S(2)}) collective-permute-start(bf16[256,512]{1,0:T(8,128)(2,1)S(1)} %collective-permute-done.8.refs_2_), channel_id=1, source_target_pairs={{0,16},{16,0},{1,17},{17,1},{2,18},{18,2},{3,19},{19,3},{4,20},{20... | collective-permute-start | bytes 786440 | tf_op jit(solution)/shard_map/ppermute | solution.py:391
  27.0 1.6 %collective-permute-start.14 = (bf16[256,512]{1,0:T(8,128)(2,1)S(1)}, bf16[256,512]{1,0:T(8,128)(2,1)S(1)}, u32[]{:S(2)}, u32[]{:S(2)}) collective-permute-start(bf16[256,512]{1,0:T(8,128)(2,1)S(1)} %collective-permute-done.8.refs_2_), channel_id=1, source_target_pairs={{0,4},{5,1},{4,8},{9,5},{8,12},{13,9},{12,14},{15,13},{14,10},{11,... | collective-permute-start | bytes 786440 | tf_op jit(solution)/shard_map/ppermute | solution.py:385
  28.6 1.8 %shard_map.49.refs_6_ = f32[512,512]{1,0:T(8,128)S(1)} custom-call(s32[16]{0:T(128)S(1)} %copy-done.1, bf16[16,256,1024]{2,1,0:T(8,128)(2,1)S(1)} %shard_map.46.rows_ref, bf16[512,512]{1,0:T(8,128)(2,1)S(1)} %collective-permute-done.1.refs_0_, bf16[512,512]{1,0:T(8,128)(2,1)S(1)} %collective-permute-done.7.refs_1_, ...), custom_call_target="tpu_custom_call" | custom-call | flops 1073741824 | bytes 6291456 | tf_op jit(solution)/shard_map/pallas_call | solution.py:253
  30.6 1.6 %collective-permute-start.12 = (bf16[512,512]{1,0:T(8,128)(2,1)S(1)}, bf16[512,512]{1,0:T(8,128)(2,1)S(1)}, u32[]{:S(2)}, u32[]{:S(2)}) collective-permute-start(bf16[512,512]{1,0:T(8,128)(2,1)S(1)} %collective-permute-done.6.refs_0_), channel_id=1, source_target_pairs={{0,4},{5,1},{4,8},{9,5},{8,12},{13,9},{12,14},{15,13},{14,10},{11,... | collective-permute-start | bytes 1572872 | tf_op jit(solution)/shard_map/ppermute | solution.py:385
  32.1 1.2 %collective-permute-done.14.refs_2_ = bf16[256,512]{1,0:T(8,128)(2,1)S(1)} collective-permute-done((bf16[256,512]{1,0:T(8,128)(2,1)S(1)}, bf16[256,512]{1,0:T(8,128)(2,1)S(1)}, u32[]{:S(2)}, u32[]{:S(2)}) %collective-permute-start.14) | collective-permute-done | bytes 262176 | tf_op jit(solution)/shard_map/ppermute | solution.py:385
  33.4 0.8 collective-permute-done.16.refs_4_
  34.2 1.7 %collective-permute-start.18 = (bf16[128,512]{1,0:T(8,128)(2,1)S(1)}, bf16[128,512]{1,0:T(8,128)(2,1)S(1)}, u32[]{:S(2)}, u32[]{:S(2)}) collective-permute-start(bf16[128,512]{1,0:T(8,128)(2,1)S(1)} %slice.8), channel_id=1, source_target_pairs={{0,4},{5,1},{4,8},{9,5},{8,12},{13,9},{12,14},{15,13},{14,10},{11,... | collective-permute-start | bytes 393224 | tf_op jit(solution)/shard_map/ppermute | solution.py:385
  35.9 1.5 %collective-permute-start.19 = (bf16[128,512]{1,0:T(8,128)(2,1)S(1)}, bf16[128,512]{1,0:T(8,128)(2,1)S(1)}, u32[]{:S(2)}, u32[]{:S(2)}) collective-permute-start(bf16[128,512]{1,0:T(8,128)(2,1)S(1)} %slice.9), channel_id=1, source_target_pairs={{0,16},{16,0},{1,17},{17,1},{2,18},{18,2},{3,19},{19,3},{4,20},{20... | collective-permute-start | bytes 393224 | tf_op jit(solution)/shard_map/ppermute | solution.py:391
  37.4 1.8 %shard_map.50.refs_3_ = f32[512,512]{1,0:T(8,128)S(1)} custom-call(s32[16]{0:T(128)S(1)} %copy-done.1, bf16[16,256,1024]{2,1,0:T(8,128)(2,1)S(1)} %shard_map.46.rows_ref, bf16[512,512]{1,0:T(8,128)(2,1)S(1)} %collective-permute-done.6.refs_0_, bf16[512,512]{1,0:T(8,128)(2,1)S(1)} %collective-permute-done.13.refs_1_, ...), custom_call_target="tpu_custom_call" | custom-call | flops 1073741824 | bytes 6291456 | tf_op jit(solution)/shard_map/pallas_call | solution.py:253
  39.2 1.9 %collective-permute-done.18.refs_1_ = bf16[128,512]{1,0:T(8,128)(2,1)S(1)} collective-permute-done((bf16[128,512]{1,0:T(8,128)(2,1)S(1)}, bf16[128,512]{1,0:T(8,128)(2,1)S(1)}, u32[]{:S(2)}, u32[]{:S(2)}) %collective-permute-start.18) | collective-permute-done | bytes 131104 | tf_op jit(solution)/shard_map/ppermute | solution.py:385
  41.5 0.5 collective-permute-start.21
  42.0 1.2 %shard_map.51.refs_3_ = f32[512,512]{1,0:T(8,128)S(1)} custom-call(s32[16]{0:T(128)S(1)} %copy-done.1, bf16[16,256,1024]{2,1,0:T(8,128)(2,1)S(1)} %shard_map.46.rows_ref, bf16[512,512]{1,0:T(8,128)(2,1)S(1)} %collective-permute-done.12.refs_0_, bf16[128,512]{1,0:T(8,128)(2,1)S(1)} %collective-permute-done.18.refs_1_, ...), custom_call_target="tpu_custom_call" | custom-call | flops 402653184 | bytes 3670016 | tf_op jit(solution)/shard_map/pallas_call | solution.py:253
  43.8 1.8 %shard_map.52 = s16[2176,128]{1,0:T(8,128)(2,1)S(1)} custom-call(s32[16]{0:T(128)S(1)} %copy-done.1, bf16[16,256,1024]{2,1,0:T(8,128)(2,1)S(1)} %shard_map.46.rows_ref, bf16[512,512]{1,0:T(8,128)(2,1)S(1)} %collective-permute-done.20.refs_0_, bf16[128,512]{1,0:T(8,128)(2,1)S(1)} %collective-permute-done.21.refs_1_, ...), custom_call_target="tpu_custom_call" | custom-call | flops 402653184 | bytes 3670016 | tf_op jit(solution)/shard_map/pallas_call | solution.py:253
  45.6 21.5 %all_to_all.10 = s16[16,136,128]{2,1,0:T(8,128)(2,1)S(1)} all-to-all(s16[16,136,128]{2,1,0:T(8,128)(2,1)S(1)} %bitcast.13), channel_id=1, replica_groups=mesh['grp'=2,'shell'=16] {'shell'}, dimensions={0} | all-to-all | bytes 1114112 | tf_op jit(solution)/shard_map/all_to_all | solution.py:400
  67.0 1.7 %shard_map.53 = s16[2176,128]{1,0:T(8,128)(2,1)} custom-call(s16[2176,128]{1,0:T(8,128)(2,1)S(1)} %bitcast.12), custom_call_target="tpu_custom_call" | custom-call | tf_op jit(solution)/shard_map/pallas_call | solution.py:359
  68.7 3.6 %all-to-all-start.1 = ((s16[16,136,128]{2,1,0:T(8,128)(2,1)}), s16[16,136,128]{2,1,0:T(8,128)(2,1)S(1)}, u32[]{:S(2)}, u32[]{:S(2)}) async-start(s16[16,136,128]{2,1,0:T(8,128)(2,1)} %bitcast.4), calls=%async_computation.1 | async-start | bytes 1114112 | tf_op jit(solution)/shard_map/all_to_all | solution.py:400
  72.4 14.9 %all-to-all-done.1 = s16[16,136,128]{2,1,0:T(8,128)(2,1)S(1)} async-done(((s16[16,136,128]{2,1,0:T(8,128)(2,1)}), s16[16,136,128]{2,1,0:T(8,128)(2,1)S(1)}, u32[]{:S(2)}, u32[]{:S(2)}) %all-to-all-start.1) | async-done | bytes 557088 | tf_op jit(solution)/shard_map/all_to_all | solution.py:400
  87.3 2.2 %shard_map.54 = f32[2048,128]{1,0:T(8,128)} custom-call(f32[2,32]{1,0:T(2,128)S(1)} %maximum_multiply_fusion.twist_ref, s16[2176,128]{1,0:T(8,128)(2,1)S(1)} %bitcast.11), custom_call_target="tpu_custom_call" | custom-call | tf_op jit(solution)/shard_map/pallas_call | solution.py:359
  (37 shorter events, 1.2 us)
Async XLA Ops:
  0.0 8.8 %collective-permute-start.3 = (bf16[512,512]{1,0:T(8,128)(2,1)}, bf16[512,512]{1,0:T(8,128)(2,1)S(1)}, u32[]{:S(2)}, u32[]{:S(2)}) collective-permute-start(bf16[512,512]{1,0:T(8,128)(2,1)} %bitcast.14), channel_id=1, source_target_pairs={{0,1},{1,0},{2,3},{3,2},{4,5},{5,4},{6,7},{7,6},{8,9},{9,8},{10,11... | collective-permute-start | bytes 1572872 | tf_op jit(solution)/shard_map/ppermute | solution.py:388
  0.5 10.1 %collective-permute-start = (bf16[512,512]{1,0:T(8,128)(2,1)}, bf16[512,512]{1,0:T(8,128)(2,1)S(1)}, u32[]{:S(2)}, u32[]{:S(2)}) collective-permute-start(bf16[512,512]{1,0:T(8,128)(2,1)} %bitcast.15), channel_id=1, source_target_pairs={{0,4},{5,1},{4,8},{9,5},{8,12},{13,9},{12,14},{15,13},{14,10},{11,... | collective-permute-start | bytes 1572872 | tf_op jit(solution)/shard_map/ppermute | solution.py:385
  3.0 0.7 copy-start.2
  3.7 11.6 %copy-start = (bf16[1,512,512]{2,1,0:T(8,128)(2,1)S(1)}, bf16[1,512,512]{2,1,0:T(8,128)(2,1)}, u32[]{:S(2)}) copy-start(bf16[1,512,512]{2,1,0:T(8,128)(2,1)} %param.5) | copy-start | bytes 1572868
  3.7 11.6 %copy-start.1 = (s32[16]{0:T(128)S(1)}, s32[16]{0:T(128)}, u32[]{:S(2)}) copy-start(s32[16]{0:T(128)} %owner_ref.11) | copy-start | bytes 196
  8.9 6.4 %collective-permute-start.4 = (bf16[256,512]{1,0:T(8,128)(2,1)S(1)}, bf16[256,512]{1,0:T(8,128)(2,1)S(1)}, u32[]{:S(2)}, u32[]{:S(2)}) collective-permute-start(bf16[256,512]{1,0:T(8,128)(2,1)S(1)} %constant_dynamic-slice_fusion), channel_id=1, source_target_pairs={{0,4},{5,1},{4,8},{9,5},{8,12},{13,9},{12,14},{15,13},{14,10},{11,... | collective-permute-start | bytes 786440 | tf_op jit(solution)/shard_map/ppermute | solution.py:385
  10.5 9.2 %collective-permute-start.2 = (bf16[512,512]{1,0:T(8,128)(2,1)S(1)}, bf16[512,512]{1,0:T(8,128)(2,1)S(1)}, u32[]{:S(2)}, u32[]{:S(2)}) collective-permute-start(bf16[512,512]{1,0:T(8,128)(2,1)S(1)} %collective-permute-done.refs_0_), channel_id=1, source_target_pairs={{0,1},{1,0},{2,3},{3,2},{4,5},{5,4},{6,7},{7,6},{8,9},{9,8},{10,11... | collective-permute-start | bytes 1572872 | tf_op jit(solution)/shard_map/ppermute | solution.py:388
  10.5 10.7 %collective-permute-start.1 = (bf16[512,512]{1,0:T(8,128)(2,1)S(1)}, bf16[512,512]{1,0:T(8,128)(2,1)S(1)}, u32[]{:S(2)}, u32[]{:S(2)}) collective-permute-start(bf16[512,512]{1,0:T(8,128)(2,1)S(1)} %collective-permute-done.refs_0_), channel_id=1, source_target_pairs={{0,4},{5,1},{4,8},{9,5},{8,12},{13,9},{12,14},{15,13},{14,10},{11,... | collective-permute-start | bytes 1572872 | tf_op jit(solution)/shard_map/ppermute | solution.py:385
  15.3 4.4 %collective-permute-start.5 = (bf16[256,512]{1,0:T(8,128)(2,1)S(1)}, bf16[256,512]{1,0:T(8,128)(2,1)S(1)}, u32[]{:S(2)}, u32[]{:S(2)}) collective-permute-start(bf16[256,512]{1,0:T(8,128)(2,1)S(1)} %collective-permute-done.4.refs_2_), channel_id=1, source_target_pairs={{0,1},{1,0},{2,3},{3,2},{4,5},{5,4},{6,7},{7,6},{8,9},{9,8},{10,11... | collective-permute-start | bytes 786440 | tf_op jit(solution)/shard_map/ppermute | solution.py:388
  16.6 7.2 %collective-permute-start.8 = (bf16[256,512]{1,0:T(8,128)(2,1)S(1)}, bf16[256,512]{1,0:T(8,128)(2,1)S(1)}, u32[]{:S(2)}, u32[]{:S(2)}) collective-permute-start(bf16[256,512]{1,0:T(8,128)(2,1)S(1)} %collective-permute-done.4.refs_2_), channel_id=1, source_target_pairs={{0,4},{5,1},{4,8},{9,5},{8,12},{13,9},{12,14},{15,13},{14,10},{11,... | collective-permute-start | bytes 786440 | tf_op jit(solution)/shard_map/ppermute | solution.py:385
  18.2 7.2 %collective-permute-start.10 = (bf16[256,512]{1,0:T(8,128)(2,1)S(1)}, bf16[256,512]{1,0:T(8,128)(2,1)S(1)}, u32[]{:S(2)}, u32[]{:S(2)}) collective-permute-start(bf16[256,512]{1,0:T(8,128)(2,1)S(1)} %collective-permute-done.4.refs_2_), channel_id=1, source_target_pairs={{0,16},{16,0},{1,17},{17,1},{2,18},{18,2},{3,19},{19,3},{4,20},{20... | collective-permute-start | bytes 786440 | tf_op jit(solution)/shard_map/ppermute | solution.py:391
  21.2 7.4 %collective-permute-start.7 = (bf16[512,512]{1,0:T(8,128)(2,1)S(1)}, bf16[512,512]{1,0:T(8,128)(2,1)S(1)}, u32[]{:S(2)}, u32[]{:S(2)}) collective-permute-start(bf16[512,512]{1,0:T(8,128)(2,1)S(1)} %collective-permute-done.1.refs_0_), channel_id=1, source_target_pairs={{0,1},{1,0},{2,3},{3,2},{4,5},{5,4},{6,7},{7,6},{8,9},{9,8},{10,11... | collective-permute-start | bytes 1572872 | tf_op jit(solution)/shard_map/ppermute | solution.py:388
  21.3 9.2 %collective-permute-start.6 = (bf16[512,512]{1,0:T(8,128)(2,1)S(1)}, bf16[512,512]{1,0:T(8,128)(2,1)S(1)}, u32[]{:S(2)}, u32[]{:S(2)}) collective-permute-start(bf16[512,512]{1,0:T(8,128)(2,1)S(1)} %collective-permute-done.1.refs_0_), channel_id=1, source_target_pairs={{0,4},{5,1},{4,8},{9,5},{8,12},{13,9},{12,14},{15,13},{14,10},{11,... | collective-permute-start | bytes 1572872 | tf_op jit(solution)/shard_map/ppermute | solution.py:385
  23.7 3.3 %collective-permute-start.9 = (bf16[256,512]{1,0:T(8,128)(2,1)S(1)}, bf16[256,512]{1,0:T(8,128)(2,1)S(1)}, u32[]{:S(2)}, u32[]{:S(2)}) collective-permute-start(bf16[256,512]{1,0:T(8,128)(2,1)S(1)} %collective-permute-done.8.refs_2_), channel_id=1, source_target_pairs={{0,1},{1,0},{2,3},{3,2},{4,5},{5,4},{6,7},{7,6},{8,9},{9,8},{10,11... | collective-permute-start | bytes 786440 | tf_op jit(solution)/shard_map/ppermute | solution.py:388
  25.5 3.1 %collective-permute-start.11 = (bf16[256,512]{1,0:T(8,128)(2,1)S(1)}, bf16[256,512]{1,0:T(8,128)(2,1)S(1)}, u32[]{:S(2)}, u32[]{:S(2)}) collective-permute-start(bf16[256,512]{1,0:T(8,128)(2,1)S(1)} %collective-permute-done.10.refs_4_), channel_id=1, source_target_pairs={{0,1},{1,0},{2,3},{3,2},{4,5},{5,4},{6,7},{7,6},{8,9},{9,8},{10,11... | collective-permute-start | bytes 786440 | tf_op jit(solution)/shard_map/ppermute | solution.py:388
  25.5 8.7 %collective-permute-start.16 = (bf16[256,512]{1,0:T(8,128)(2,1)S(1)}, bf16[256,512]{1,0:T(8,128)(2,1)S(1)}, u32[]{:S(2)}, u32[]{:S(2)}) collective-permute-start(bf16[256,512]{1,0:T(8,128)(2,1)S(1)} %collective-permute-done.8.refs_2_), channel_id=1, source_target_pairs={{0,16},{16,0},{1,17},{17,1},{2,18},{18,2},{3,19},{19,3},{4,20},{20... | collective-permute-start | bytes 786440 | tf_op jit(solution)/shard_map/ppermute | solution.py:391
  27.0 6.4 %collective-permute-start.14 = (bf16[256,512]{1,0:T(8,128)(2,1)S(1)}, bf16[256,512]{1,0:T(8,128)(2,1)S(1)}, u32[]{:S(2)}, u32[]{:S(2)}) collective-permute-start(bf16[256,512]{1,0:T(8,128)(2,1)S(1)} %collective-permute-done.8.refs_2_), channel_id=1, source_target_pairs={{0,4},{5,1},{4,8},{9,5},{8,12},{13,9},{12,14},{15,13},{14,10},{11,... | collective-permute-start | bytes 786440 | tf_op jit(solution)/shard_map/ppermute | solution.py:385
  30.6 6.8 %collective-permute-start.13 = (bf16[512,512]{1,0:T(8,128)(2,1)S(1)}, bf16[512,512]{1,0:T(8,128)(2,1)S(1)}, u32[]{:S(2)}, u32[]{:S(2)}) collective-permute-start(bf16[512,512]{1,0:T(8,128)(2,1)S(1)} %collective-permute-done.6.refs_0_), channel_id=1, source_target_pairs={{0,1},{1,0},{2,3},{3,2},{4,5},{5,4},{6,7},{7,6},{8,9},{9,8},{10,11... | collective-permute-start | bytes 1572872 | tf_op jit(solution)/shard_map/ppermute | solution.py:388
  30.6 10.9 %collective-permute-start.12 = (bf16[512,512]{1,0:T(8,128)(2,1)S(1)}, bf16[512,512]{1,0:T(8,128)(2,1)S(1)}, u32[]{:S(2)}, u32[]{:S(2)}) collective-permute-start(bf16[512,512]{1,0:T(8,128)(2,1)S(1)} %collective-permute-done.6.refs_0_), channel_id=1, source_target_pairs={{0,4},{5,1},{4,8},{9,5},{8,12},{13,9},{12,14},{15,13},{14,10},{11,... | collective-permute-start | bytes 1572872 | tf_op jit(solution)/shard_map/ppermute | solution.py:385
  33.4 2.5 %collective-permute-start.15 = (bf16[256,512]{1,0:T(8,128)(2,1)S(1)}, bf16[256,512]{1,0:T(8,128)(2,1)S(1)}, u32[]{:S(2)}, u32[]{:S(2)}) collective-permute-start(bf16[256,512]{1,0:T(8,128)(2,1)S(1)} %collective-permute-done.14.refs_2_), channel_id=1, source_target_pairs={{0,1},{1,0},{2,3},{3,2},{4,5},{5,4},{6,7},{7,6},{8,9},{9,8},{10,11... | collective-permute-start | bytes 786440 | tf_op jit(solution)/shard_map/ppermute | solution.py:388
  34.2 3.2 %collective-permute-start.17 = (bf16[256,512]{1,0:T(8,128)(2,1)S(1)}, bf16[256,512]{1,0:T(8,128)(2,1)S(1)}, u32[]{:S(2)}, u32[]{:S(2)}) collective-permute-start(bf16[256,512]{1,0:T(8,128)(2,1)S(1)} %collective-permute-done.16.refs_4_), channel_id=1, source_target_pairs={{0,1},{1,0},{2,3},{3,2},{4,5},{5,4},{6,7},{7,6},{8,9},{9,8},{10,11... | collective-permute-start | bytes 786440 | tf_op jit(solution)/shard_map/ppermute | solution.py:388
  34.2 6.9 %collective-permute-start.18 = (bf16[128,512]{1,0:T(8,128)(2,1)S(1)}, bf16[128,512]{1,0:T(8,128)(2,1)S(1)}, u32[]{:S(2)}, u32[]{:S(2)}) collective-permute-start(bf16[128,512]{1,0:T(8,128)(2,1)S(1)} %slice.8), channel_id=1, source_target_pairs={{0,4},{5,1},{4,8},{9,5},{8,12},{13,9},{12,14},{15,13},{14,10},{11,... | collective-permute-start | bytes 393224 | tf_op jit(solution)/shard_map/ppermute | solution.py:385
  35.9 5.6 %collective-permute-start.19 = (bf16[128,512]{1,0:T(8,128)(2,1)S(1)}, bf16[128,512]{1,0:T(8,128)(2,1)S(1)}, u32[]{:S(2)}, u32[]{:S(2)}) collective-permute-start(bf16[128,512]{1,0:T(8,128)(2,1)S(1)} %slice.9), channel_id=1, source_target_pairs={{0,16},{16,0},{1,17},{17,1},{2,18},{18,2},{3,19},{19,3},{4,20},{20... | collective-permute-start | bytes 393224 | tf_op jit(solution)/shard_map/ppermute | solution.py:391
  41.5 2.3 %collective-permute-start.20 = (bf16[512,512]{1,0:T(8,128)(2,1)S(1)}, bf16[512,512]{1,0:T(8,128)(2,1)S(1)}, u32[]{:S(2)}, u32[]{:S(2)}) collective-permute-start(bf16[512,512]{1,0:T(8,128)(2,1)S(1)} %collective-permute-done.12.refs_0_), channel_id=1, source_target_pairs={{0,1},{1,0},{2,3},{3,2},{4,5},{5,4},{6,7},{7,6},{8,9},{9,8},{10,11... | collective-permute-start | bytes 1572872 | tf_op jit(solution)/shard_map/ppermute | solution.py:388
  41.5 2.1 %collective-permute-start.21 = (bf16[128,512]{1,0:T(8,128)(2,1)S(1)}, bf16[128,512]{1,0:T(8,128)(2,1)S(1)}, u32[]{:S(2)}, u32[]{:S(2)}) collective-permute-start(bf16[128,512]{1,0:T(8,128)(2,1)S(1)} %collective-permute-done.18.refs_1_), channel_id=1, source_target_pairs={{0,1},{1,0},{2,3},{3,2},{4,5},{5,4},{6,7},{7,6},{8,9},{9,8},{10,11... | collective-permute-start | bytes 393224 | tf_op jit(solution)/shard_map/ppermute | solution.py:388
  42.0 1.8 %collective-permute-start.22 = (bf16[128,512]{1,0:T(8,128)(2,1)S(1)}, bf16[128,512]{1,0:T(8,128)(2,1)S(1)}, u32[]{:S(2)}, u32[]{:S(2)}) collective-permute-start(bf16[128,512]{1,0:T(8,128)(2,1)S(1)} %collective-permute-done.19.refs_2_), channel_id=1, source_target_pairs={{0,1},{1,0},{2,3},{3,2},{4,5},{5,4},{6,7},{7,6},{8,9},{9,8},{10,11... | collective-permute-start | bytes 393224 | tf_op jit(solution)/shard_map/ppermute | solution.py:388
  68.7 18.6 %all-to-all-start.1 = ((s16[16,136,128]{2,1,0:T(8,128)(2,1)}), s16[16,136,128]{2,1,0:T(8,128)(2,1)S(1)}, u32[]{:S(2)}, u32[]{:S(2)}) async-start(s16[16,136,128]{2,1,0:T(8,128)(2,1)} %bitcast.4), calls=%async_computation.1 | async-start | bytes 1114112 | tf_op jit(solution)/shard_map/all_to_all | solution.py:400

commit v10 on v9

--- a/solution.py
+++ b/solution.py
@@ -407,6 +407,7 @@
     rows = sort_rows(pair_coef, batch_order)
     acc = project(None, rows, degree_owner, [own, other], [(0, 0, None), (0, 1, None)])
     whole, rows = lax.optimization_barrier((whole, rows))
+    part, acc = lax.optimization_barrier((part, acc))
     late, late_from = [], []
     for step in range(1, chips // 2):
         if step > 1:

time: 89.7 us -> 89.1 us (level)
  waiting for transfers between devices: 25.3 us -> 23.1 us
    ppermute x3, waiting for transfers between devices: 2.83 us -> 0.46 us  [across(): return lax.ppermute(value, 'grp', [(0, 1), (1, 0)])]
  transfers between devices with their start and end apart: 24 -> 24, of which waited for: 11 -> 9; matrix products, arithmetic and copies ran while one was open for 0% -> 0% of each run, Pallas kernels for 14% -> 14%
where the time goes in v10:
time: 89.1 us; the launch traced here: 88.8 us
  starting transfers between devices  24.2 us (27%)
  waiting for transfers between devices  23.1 us (26%)
  blocking collectives  22.2 us (25%)
  Pallas kernels  18.5 us (21%)
    all_to_all x1, blocking collectives, exchange(): return lax.all_to_all(value, 'shell', 0, 0).reshape(parcels.shape)  22.2 us
    all_to_all x1, waiting for transfers between devices, exchange(): return lax.all_to_all(value, 'shell', 0, 0).reshape(parcels.shape)  14.9 us
    ppermute x8, starting transfers between devices, around(): return lax.ppermute(value, 'shell', onward)  14.4 us
    pallas_call x6, Pallas kernels, project(): pl.pallas_call(functools.partial(project_kernel, lax.axis_size('shell'),...  9.43 us
    ppermute x8, waiting for transfers between devices, around(): return lax.ppermute(value, 'shell', onward)  7.32 us
    pallas_call x1, Pallas kernels, sort_rows(): pl.pallas_call(sort_kernel, in_specs=[pl.BlockSpec(memory_space=pltpu.SME...  5.14 us
    ppermute x3, starting transfers between devices, across(): return lax.ppermute(value, 'grp', [(0, 1), (1, 0)])  4.47 us
    pallas_call x2, Pallas kernels, local_call(): pl.pallas_call(kernel, in_specs=[pl.BlockSpec(memory_space=pltpu.SMEM)] *...  3.89 us
  transfers between devices with their start and end apart: 24, of which 9 were waited for; matrix products, arithmetic and copies ran while one was open for 0% of the time, Pallas kernels for 14%

profile of v10, /device:TPU:0, one launch (start us, length us, event | category | flops | bytes accessed | tf_op | source)
XLA Modules:
  0.0 88.8 jit_solution(11095292847030884293)
XLA Ops:
  0.5 2.6 %collective-permute-start = (bf16[512,512]{1,0:T(8,128)(2,1)}, bf16[512,512]{1,0:T(8,128)(2,1)S(1)}, u32[]{:S(2)}, u32[]{:S(2)}) collective-permute-start(bf16[512,512]{1,0:T(8,128)(2,1)} %bitcast.15), channel_id=1, source_target_pairs={{0,4},{5,1},{4,8},{9,5},{8,12},{13,9},{12,14},{15,13},{14,10},{11,... | collective-permute-start | bytes 1572872 | tf_op jit(solution)/shard_map/ppermute | solution.py:385
  3.1 2.2 %collective-permute-start.4 = (bf16[256,512]{1,0:T(8,128)(2,1)S(1)}, bf16[256,512]{1,0:T(8,128)(2,1)S(1)}, u32[]{:S(2)}, u32[]{:S(2)}) collective-permute-start(bf16[256,512]{1,0:T(8,128)(2,1)S(1)} %constant_dynamic-slice_fusion), channel_id=1, source_target_pairs={{0,4},{5,1},{4,8},{9,5},{8,12},{13,9},{12,14},{15,13},{14,10},{11,... | collective-permute-start | bytes 786440 | tf_op jit(solution)/shard_map/ppermute | solution.py:385
  5.2 0.7 copy-done.2
  5.9 5.1 %shard_map.46.rows_ref = bf16[16,256,1024]{2,1,0:T(8,128)(2,1)S(1)} custom-call(s32[8]{0:T(128)S(1)} %copy-done.2, bf16[4096,1024]{1,0:T(8,128)(2,1)} %bitcast.17), custom_call_target="tpu_custom_call" | custom-call | flops 2147483648 | bytes 16777216 | tf_op jit(solution)/shard_map/pallas_call | solution.py:137
  11.1 1.6 %collective-permute-start.1 = (bf16[512,512]{1,0:T(8,128)(2,1)S(1)}, bf16[512,512]{1,0:T(8,128)(2,1)S(1)}, u32[]{:S(2)}, u32[]{:S(2)}) collective-permute-start(bf16[512,512]{1,0:T(8,128)(2,1)S(1)} %collective-permute-done.refs_0_), channel_id=1, source_target_pairs={{0,4},{5,1},{4,8},{9,5},{8,12},{13,9},{12,14},{15,13},{14,10},{11,... | collective-permute-start | bytes 1572872 | tf_op jit(solution)/shard_map/ppermute | solution.py:385
  12.7 1.3 %shard_map.47.refs_4_ = f32[512,512]{1,0:T(8,128)S(1)} custom-call(s32[16]{0:T(128)S(1)} %copy-done.1, bf16[16,256,1024]{2,1,0:T(8,128)(2,1)S(1)} %shard_map.46.rows_ref, bf16[512,512]{1,0:T(8,128)(2,1)S(1)} %bitcast.16, bf16[512,512]{1,0:T(8,128)(2,1)S(1)} %collective-permute-done.3.refs_1_), custom_call_target="tpu_custom_call" | custom-call | flops 536870912 | bytes 3145728 | tf_op jit(solution)/shard_map/pallas_call | solution.py:253
  14.1 1.6 %collective-permute-start.8 = (bf16[256,512]{1,0:T(8,128)(2,1)S(1)}, bf16[256,512]{1,0:T(8,128)(2,1)S(1)}, u32[]{:S(2)}, u32[]{:S(2)}) collective-permute-start(bf16[256,512]{1,0:T(8,128)(2,1)S(1)} %collective-permute-done.4.refs_2_), channel_id=1, source_target_pairs={{0,4},{5,1},{4,8},{9,5},{8,12},{13,9},{12,14},{15,13},{14,10},{11,... | collective-permute-start | bytes 786440 | tf_op jit(solution)/shard_map/ppermute | solution.py:385
  15.7 1.5 %collective-permute-start.10 = (bf16[256,512]{1,0:T(8,128)(2,1)S(1)}, bf16[256,512]{1,0:T(8,128)(2,1)S(1)}, u32[]{:S(2)}, u32[]{:S(2)}) collective-permute-start(bf16[256,512]{1,0:T(8,128)(2,1)S(1)} %collective-permute-done.4.refs_2_), channel_id=1, source_target_pairs={{0,16},{16,0},{1,17},{17,1},{2,18},{18,2},{3,19},{19,3},{4,20},{20... | collective-permute-start | bytes 786440 | tf_op jit(solution)/shard_map/ppermute | solution.py:391
  17.2 1.5 %shard_map.48.refs_6_ = f32[512,512]{1,0:T(8,128)S(1)} custom-call(s32[16]{0:T(128)S(1)} %copy-done.1, bf16[16,256,1024]{2,1,0:T(8,128)(2,1)S(1)} %shard_map.46.rows_ref, bf16[512,512]{1,0:T(8,128)(2,1)S(1)} %collective-permute-done.refs_0_, bf16[512,512]{1,0:T(8,128)(2,1)S(1)} %collective-permute-done.2.refs_1_, ...), custom_call_target="tpu_custom_call" | custom-call | flops 805306368 | bytes 5242880 | tf_op jit(solution)/shard_map/pallas_call | solution.py:253
  18.8 1.6 %collective-permute-done.1.refs_0_ = bf16[512,512]{1,0:T(8,128)(2,1)S(1)} collective-permute-done((bf16[512,512]{1,0:T(8,128)(2,1)S(1)}, bf16[512,512]{1,0:T(8,128)(2,1)S(1)}, u32[]{:S(2)}, u32[]{:S(2)}) %collective-permute-start.1) | collective-permute-done | bytes 524320 | tf_op jit(solution)/shard_map/ppermute | solution.py:385
  20.4 1.6 %collective-permute-start.6 = (bf16[512,512]{1,0:T(8,128)(2,1)S(1)}, bf16[512,512]{1,0:T(8,128)(2,1)S(1)}, u32[]{:S(2)}, u32[]{:S(2)}) collective-permute-start(bf16[512,512]{1,0:T(8,128)(2,1)S(1)} %collective-permute-done.1.refs_0_), channel_id=1, source_target_pairs={{0,4},{5,1},{4,8},{9,5},{8,12},{13,9},{12,14},{15,13},{14,10},{11,... | collective-permute-start | bytes 1572872 | tf_op jit(solution)/shard_map/ppermute | solution.py:385
  21.9 1.2 %collective-permute-done.8.refs_2_ = bf16[256,512]{1,0:T(8,128)(2,1)S(1)} collective-permute-done((bf16[256,512]{1,0:T(8,128)(2,1)S(1)}, bf16[256,512]{1,0:T(8,128)(2,1)S(1)}, u32[]{:S(2)}, u32[]{:S(2)}) %collective-permute-start.8) | collective-permute-done | bytes 262176 | tf_op jit(solution)/shard_map/ppermute | solution.py:385
  23.2 0.5 collective-permute-done.10.refs_4_
  23.7 1.5 %collective-permute-start.16 = (bf16[256,512]{1,0:T(8,128)(2,1)S(1)}, bf16[256,512]{1,0:T(8,128)(2,1)S(1)}, u32[]{:S(2)}, u32[]{:S(2)}) collective-permute-start(bf16[256,512]{1,0:T(8,128)(2,1)S(1)} %collective-permute-done.8.refs_2_), channel_id=1, source_target_pairs={{0,16},{16,0},{1,17},{17,1},{2,18},{18,2},{3,19},{19,3},{4,20},{20... | collective-permute-start | bytes 786440 | tf_op jit(solution)/shard_map/ppermute | solution.py:391
  25.2 1.6 %collective-permute-start.14 = (bf16[256,512]{1,0:T(8,128)(2,1)S(1)}, bf16[256,512]{1,0:T(8,128)(2,1)S(1)}, u32[]{:S(2)}, u32[]{:S(2)}) collective-permute-start(bf16[256,512]{1,0:T(8,128)(2,1)S(1)} %collective-permute-done.8.refs_2_), channel_id=1, source_target_pairs={{0,4},{5,1},{4,8},{9,5},{8,12},{13,9},{12,14},{15,13},{14,10},{11,... | collective-permute-start | bytes 786440 | tf_op jit(solution)/shard_map/ppermute | solution.py:385
  26.7 1.8 %shard_map.49.refs_6_ = f32[512,512]{1,0:T(8,128)S(1)} custom-call(s32[16]{0:T(128)S(1)} %copy-done.1, bf16[16,256,1024]{2,1,0:T(8,128)(2,1)S(1)} %shard_map.46.rows_ref, bf16[512,512]{1,0:T(8,128)(2,1)S(1)} %collective-permute-done.1.refs_0_, bf16[512,512]{1,0:T(8,128)(2,1)S(1)} %collective-permute-done.7.refs_1_, ...), custom_call_target="tpu_custom_call" | custom-call | flops 1073741824 | bytes 6291456 | tf_op jit(solution)/shard_map/pallas_call | solution.py:253
  28.6 1.0 %collective-permute-done.6.refs_0_ = bf16[512,512]{1,0:T(8,128)(2,1)S(1)} collective-permute-done((bf16[512,512]{1,0:T(8,128)(2,1)S(1)}, bf16[512,512]{1,0:T(8,128)(2,1)S(1)}, u32[]{:S(2)}, u32[]{:S(2)}) %collective-permute-start.6) | collective-permute-done | bytes 524320 | tf_op jit(solution)/shard_map/ppermute | solution.py:385
  29.5 1.6 %collective-permute-start.12 = (bf16[512,512]{1,0:T(8,128)(2,1)S(1)}, bf16[512,512]{1,0:T(8,128)(2,1)S(1)}, u32[]{:S(2)}, u32[]{:S(2)}) collective-permute-start(bf16[512,512]{1,0:T(8,128)(2,1)S(1)} %collective-permute-done.6.refs_0_), channel_id=1, source_target_pairs={{0,4},{5,1},{4,8},{9,5},{8,12},{13,9},{12,14},{15,13},{14,10},{11,... | collective-permute-start | bytes 1572872 | tf_op jit(solution)/shard_map/ppermute | solution.py:385
  31.1 1.2 %collective-permute-done.14.refs_2_ = bf16[256,512]{1,0:T(8,128)(2,1)S(1)} collective-permute-done((bf16[256,512]{1,0:T(8,128)(2,1)S(1)}, bf16[256,512]{1,0:T(8,128)(2,1)S(1)}, u32[]{:S(2)}, u32[]{:S(2)}) %collective-permute-start.14) | collective-permute-done | bytes 262176 | tf_op jit(solution)/shard_map/ppermute | solution.py:385
  32.3 0.5 collective-permute-start.17
  32.9 1.6 %collective-permute-start.18 = (bf16[128,512]{1,0:T(8,128)(2,1)S(1)}, bf16[128,512]{1,0:T(8,128)(2,1)S(1)}, u32[]{:S(2)}, u32[]{:S(2)}) collective-permute-start(bf16[128,512]{1,0:T(8,128)(2,1)S(1)} %slice.8), channel_id=1, source_target_pairs={{0,4},{5,1},{4,8},{9,5},{8,12},{13,9},{12,14},{15,13},{14,10},{11,... | collective-permute-start | bytes 393224 | tf_op jit(solution)/shard_map/ppermute | solution.py:385
  34.5 1.5 %collective-permute-start.19 = (bf16[128,512]{1,0:T(8,128)(2,1)S(1)}, bf16[128,512]{1,0:T(8,128)(2,1)S(1)}, u32[]{:S(2)}, u32[]{:S(2)}) collective-permute-start(bf16[128,512]{1,0:T(8,128)(2,1)S(1)} %slice.9), channel_id=1, source_target_pairs={{0,16},{16,0},{1,17},{17,1},{2,18},{18,2},{3,19},{19,3},{4,20},{20... | collective-permute-start | bytes 393224 | tf_op jit(solution)/shard_map/ppermute | solution.py:391
  36.0 1.8 %shard_map.50.refs_3_ = f32[512,512]{1,0:T(8,128)S(1)} custom-call(s32[16]{0:T(128)S(1)} %copy-done.1, bf16[16,256,1024]{2,1,0:T(8,128)(2,1)S(1)} %shard_map.46.rows_ref, bf16[512,512]{1,0:T(8,128)(2,1)S(1)} %collective-permute-done.6.refs_0_, bf16[512,512]{1,0:T(8,128)(2,1)S(1)} %collective-permute-done.13.refs_1_, ...), custom_call_target="tpu_custom_call" | custom-call | flops 1073741824 | bytes 6291456 | tf_op jit(solution)/shard_map/pallas_call | solution.py:253
  37.8 2.3 %collective-permute-done.18.refs_1_ = bf16[128,512]{1,0:T(8,128)(2,1)S(1)} collective-permute-done((bf16[128,512]{1,0:T(8,128)(2,1)S(1)}, bf16[128,512]{1,0:T(8,128)(2,1)S(1)}, u32[]{:S(2)}, u32[]{:S(2)}) %collective-permute-start.18) | collective-permute-done | bytes 131104 | tf_op jit(solution)/shard_map/ppermute | solution.py:385
  40.1 0.5 collective-permute-start.21
  40.7 1.2 %shard_map.51.refs_3_ = f32[512,512]{1,0:T(8,128)S(1)} custom-call(s32[16]{0:T(128)S(1)} %copy-done.1, bf16[16,256,1024]{2,1,0:T(8,128)(2,1)S(1)} %shard_map.46.rows_ref, bf16[512,512]{1,0:T(8,128)(2,1)S(1)} %collective-permute-done.12.refs_0_, bf16[128,512]{1,0:T(8,128)(2,1)S(1)} %collective-permute-done.18.refs_1_, ...), custom_call_target="tpu_custom_call" | custom-call | flops 402653184 | bytes 3670016 | tf_op jit(solution)/shard_map/pallas_call | solution.py:253
  42.4 1.8 %shard_map.52 = s16[2176,128]{1,0:T(8,128)(2,1)S(1)} custom-call(s32[16]{0:T(128)S(1)} %copy-done.1, bf16[16,256,1024]{2,1,0:T(8,128)(2,1)S(1)} %shard_map.46.rows_ref, bf16[512,512]{1,0:T(8,128)(2,1)S(1)} %collective-permute-done.20.refs_0_, bf16[128,512]{1,0:T(8,128)(2,1)S(1)} %collective-permute-done.21.refs_1_, ...), custom_call_target="tpu_custom_call" | custom-call | flops 402653184 | bytes 3670016 | tf_op jit(solution)/shard_map/pallas_call | solution.py:253
  44.2 22.2 %all_to_all.10 = s16[16,136,128]{2,1,0:T(8,128)(2,1)S(1)} all-to-all(s16[16,136,128]{2,1,0:T(8,128)(2,1)S(1)} %bitcast.13), channel_id=1, replica_groups=mesh['grp'=2,'shell'=16] {'shell'}, dimensions={0} | all-to-all | bytes 1114112 | tf_op jit(solution)/shard_map/all_to_all | solution.py:400
  66.4 1.7 %shard_map.53 = s16[2176,128]{1,0:T(8,128)(2,1)} custom-call(s16[2176,128]{1,0:T(8,128)(2,1)S(1)} %bitcast.12), custom_call_target="tpu_custom_call" | custom-call | tf_op jit(solution)/shard_map/pallas_call | solution.py:359
  68.1 3.6 %all-to-all-start.1 = ((s16[16,136,128]{2,1,0:T(8,128)(2,1)}), s16[16,136,128]{2,1,0:T(8,128)(2,1)S(1)}, u32[]{:S(2)}, u32[]{:S(2)}) async-start(s16[16,136,128]{2,1,0:T(8,128)(2,1)} %bitcast.4), calls=%async_computation.1 | async-start | bytes 1114112 | tf_op jit(solution)/shard_map/all_to_all | solution.py:400
  71.7 14.9 %all-to-all-done.1 = s16[16,136,128]{2,1,0:T(8,128)(2,1)S(1)} async-done(((s16[16,136,128]{2,1,0:T(8,128)(2,1)}), s16[16,136,128]{2,1,0:T(8,128)(2,1)S(1)}, u32[]{:S(2)}, u32[]{:S(2)}) %all-to-all-start.1) | async-done | bytes 557088 | tf_op jit(solution)/shard_map/all_to_all | solution.py:400
  86.6 2.2 %shard_map.54 = f32[2048,128]{1,0:T(8,128)} custom-call(f32[2,32]{1,0:T(2,128)S(1)} %maximum_multiply_fusion.twist_ref, s16[2176,128]{1,0:T(8,128)(2,1)S(1)} %bitcast.11), custom_call_target="tpu_custom_call" | custom-call | tf_op jit(solution)/shard_map/pallas_call | solution.py:359
  (37 shorter events, 1.3 us)
Async XLA Ops:
  0.0 3.0 %collective-permute-start.3 = (bf16[512,512]{1,0:T(8,128)(2,1)}, bf16[512,512]{1,0:T(8,128)(2,1)S(1)}, u32[]{:S(2)}, u32[]{:S(2)}) collective-permute-start(bf16[512,512]{1,0:T(8,128)(2,1)} %bitcast.14), channel_id=1, source_target_pairs={{0,1},{1,0},{2,3},{3,2},{4,5},{5,4},{6,7},{7,6},{8,9},{9,8},{10,11... | collective-permute-start | bytes 1572872 | tf_op jit(solution)/shard_map/ppermute | solution.py:388
  0.5 10.6 %collective-permute-start = (bf16[512,512]{1,0:T(8,128)(2,1)}, bf16[512,512]{1,0:T(8,128)(2,1)S(1)}, u32[]{:S(2)}, u32[]{:S(2)}) collective-permute-start(bf16[512,512]{1,0:T(8,128)(2,1)} %bitcast.15), channel_id=1, source_target_pairs={{0,4},{5,1},{4,8},{9,5},{8,12},{13,9},{12,14},{15,13},{14,10},{11,... | collective-permute-start | bytes 1572872 | tf_op jit(solution)/shard_map/ppermute | solution.py:385
  3.1 11.0 %collective-permute-start.4 = (bf16[256,512]{1,0:T(8,128)(2,1)S(1)}, bf16[256,512]{1,0:T(8,128)(2,1)S(1)}, u32[]{:S(2)}, u32[]{:S(2)}) collective-permute-start(bf16[256,512]{1,0:T(8,128)(2,1)S(1)} %constant_dynamic-slice_fusion), channel_id=1, source_target_pairs={{0,4},{5,1},{4,8},{9,5},{8,12},{13,9},{12,14},{15,13},{14,10},{11,... | collective-permute-start | bytes 786440 | tf_op jit(solution)/shard_map/ppermute | solution.py:385
  5.2 0.7 copy-start.2
  5.9 6.9 %copy-start = (bf16[1,512,512]{2,1,0:T(8,128)(2,1)S(1)}, bf16[1,512,512]{2,1,0:T(8,128)(2,1)}, u32[]{:S(2)}) copy-start(bf16[1,512,512]{2,1,0:T(8,128)(2,1)} %param.5) | copy-start | bytes 1572868
  5.9 6.9 %copy-start.1 = (s32[16]{0:T(128)S(1)}, s32[16]{0:T(128)}, u32[]{:S(2)}) copy-start(s32[16]{0:T(128)} %owner_ref.11) | copy-start | bytes 196
  11.0 6.2 %collective-permute-start.2 = (bf16[512,512]{1,0:T(8,128)(2,1)S(1)}, bf16[512,512]{1,0:T(8,128)(2,1)S(1)}, u32[]{:S(2)}, u32[]{:S(2)}) collective-permute-start(bf16[512,512]{1,0:T(8,128)(2,1)S(1)} %collective-permute-done.refs_0_), channel_id=1, source_target_pairs={{0,1},{1,0},{2,3},{3,2},{4,5},{5,4},{6,7},{7,6},{8,9},{9,8},{10,11... | collective-permute-start | bytes 1572872 | tf_op jit(solution)/shard_map/ppermute | solution.py:388
  11.1 9.2 %collective-permute-start.1 = (bf16[512,512]{1,0:T(8,128)(2,1)S(1)}, bf16[512,512]{1,0:T(8,128)(2,1)S(1)}, u32[]{:S(2)}, u32[]{:S(2)}) collective-permute-start(bf16[512,512]{1,0:T(8,128)(2,1)S(1)} %collective-permute-done.refs_0_), channel_id=1, source_target_pairs={{0,4},{5,1},{4,8},{9,5},{8,12},{13,9},{12,14},{15,13},{14,10},{11,... | collective-permute-start | bytes 1572872 | tf_op jit(solution)/shard_map/ppermute | solution.py:385
  14.0 3.2 %collective-permute-start.5 = (bf16[256,512]{1,0:T(8,128)(2,1)S(1)}, bf16[256,512]{1,0:T(8,128)(2,1)S(1)}, u32[]{:S(2)}, u32[]{:S(2)}) collective-permute-start(bf16[256,512]{1,0:T(8,128)(2,1)S(1)} %collective-permute-done.4.refs_2_), channel_id=1, source_target_pairs={{0,1},{1,0},{2,3},{3,2},{4,5},{5,4},{6,7},{7,6},{8,9},{9,8},{10,11... | collective-permute-start | bytes 786440 | tf_op jit(solution)/shard_map/ppermute | solution.py:388
  14.1 9.1 %collective-permute-start.8 = (bf16[256,512]{1,0:T(8,128)(2,1)S(1)}, bf16[256,512]{1,0:T(8,128)(2,1)S(1)}, u32[]{:S(2)}, u32[]{:S(2)}) collective-permute-start(bf16[256,512]{1,0:T(8,128)(2,1)S(1)} %collective-permute-done.4.refs_2_), channel_id=1, source_target_pairs={{0,4},{5,1},{4,8},{9,5},{8,12},{13,9},{12,14},{15,13},{14,10},{11,... | collective-permute-start | bytes 786440 | tf_op jit(solution)/shard_map/ppermute | solution.py:385
  15.7 7.9 %collective-permute-start.10 = (bf16[256,512]{1,0:T(8,128)(2,1)S(1)}, bf16[256,512]{1,0:T(8,128)(2,1)S(1)}, u32[]{:S(2)}, u32[]{:S(2)}) collective-permute-start(bf16[256,512]{1,0:T(8,128)(2,1)S(1)} %collective-permute-done.4.refs_2_), channel_id=1, source_target_pairs={{0,16},{16,0},{1,17},{17,1},{2,18},{18,2},{3,19},{19,3},{4,20},{20... | collective-permute-start | bytes 786440 | tf_op jit(solution)/shard_map/ppermute | solution.py:391
  20.3 6.4 %collective-permute-start.7 = (bf16[512,512]{1,0:T(8,128)(2,1)S(1)}, bf16[512,512]{1,0:T(8,128)(2,1)S(1)}, u32[]{:S(2)}, u32[]{:S(2)}) collective-permute-start(bf16[512,512]{1,0:T(8,128)(2,1)S(1)} %collective-permute-done.1.refs_0_), channel_id=1, source_target_pairs={{0,1},{1,0},{2,3},{3,2},{4,5},{5,4},{6,7},{7,6},{8,9},{9,8},{10,11... | collective-permute-start | bytes 1572872 | tf_op jit(solution)/shard_map/ppermute | solution.py:388
  20.4 9.2 %collective-permute-start.6 = (bf16[512,512]{1,0:T(8,128)(2,1)S(1)}, bf16[512,512]{1,0:T(8,128)(2,1)S(1)}, u32[]{:S(2)}, u32[]{:S(2)}) collective-permute-start(bf16[512,512]{1,0:T(8,128)(2,1)S(1)} %collective-permute-done.1.refs_0_), channel_id=1, source_target_pairs={{0,4},{5,1},{4,8},{9,5},{8,12},{13,9},{12,14},{15,13},{14,10},{11,... | collective-permute-start | bytes 1572872 | tf_op jit(solution)/shard_map/ppermute | solution.py:385
  23.2 2.0 %collective-permute-start.9 = (bf16[256,512]{1,0:T(8,128)(2,1)S(1)}, bf16[256,512]{1,0:T(8,128)(2,1)S(1)}, u32[]{:S(2)}, u32[]{:S(2)}) collective-permute-start(bf16[256,512]{1,0:T(8,128)(2,1)S(1)} %collective-permute-done.8.refs_2_), channel_id=1, source_target_pairs={{0,1},{1,0},{2,3},{3,2},{4,5},{5,4},{6,7},{7,6},{8,9},{9,8},{10,11... | collective-permute-start | bytes 786440 | tf_op jit(solution)/shard_map/ppermute | solution.py:388
  23.6 3.1 %collective-permute-start.11 = (bf16[256,512]{1,0:T(8,128)(2,1)S(1)}, bf16[256,512]{1,0:T(8,128)(2,1)S(1)}, u32[]{:S(2)}, u32[]{:S(2)}) collective-permute-start(bf16[256,512]{1,0:T(8,128)(2,1)S(1)} %collective-permute-done.10.refs_4_), channel_id=1, source_target_pairs={{0,1},{1,0},{2,3},{3,2},{4,5},{5,4},{6,7},{7,6},{8,9},{9,8},{10,11... | collective-permute-start | bytes 786440 | tf_op jit(solution)/shard_map/ppermute | solution.py:388
  23.7 8.7 %collective-permute-start.16 = (bf16[256,512]{1,0:T(8,128)(2,1)S(1)}, bf16[256,512]{1,0:T(8,128)(2,1)S(1)}, u32[]{:S(2)}, u32[]{:S(2)}) collective-permute-start(bf16[256,512]{1,0:T(8,128)(2,1)S(1)} %collective-permute-done.8.refs_2_), channel_id=1, source_target_pairs={{0,16},{16,0},{1,17},{17,1},{2,18},{18,2},{3,19},{19,3},{4,20},{20... | collective-permute-start | bytes 786440 | tf_op jit(solution)/shard_map/ppermute | solution.py:391
  25.2 7.2 %collective-permute-start.14 = (bf16[256,512]{1,0:T(8,128)(2,1)S(1)}, bf16[256,512]{1,0:T(8,128)(2,1)S(1)}, u32[]{:S(2)}, u32[]{:S(2)}) collective-permute-start(bf16[256,512]{1,0:T(8,128)(2,1)S(1)} %collective-permute-done.8.refs_2_), channel_id=1, source_target_pairs={{0,4},{5,1},{4,8},{9,5},{8,12},{13,9},{12,14},{15,13},{14,10},{11,... | collective-permute-start | bytes 786440 | tf_op jit(solution)/shard_map/ppermute | solution.py:385
  29.5 6.5 %collective-permute-start.13 = (bf16[512,512]{1,0:T(8,128)(2,1)S(1)}, bf16[512,512]{1,0:T(8,128)(2,1)S(1)}, u32[]{:S(2)}, u32[]{:S(2)}) collective-permute-start(bf16[512,512]{1,0:T(8,128)(2,1)S(1)} %collective-permute-done.6.refs_0_), channel_id=1, source_target_pairs={{0,1},{1,0},{2,3},{3,2},{4,5},{5,4},{6,7},{7,6},{8,9},{9,8},{10,11... | collective-permute-start | bytes 1572872 | tf_op jit(solution)/shard_map/ppermute | solution.py:388
  29.5 10.6 %collective-permute-start.12 = (bf16[512,512]{1,0:T(8,128)(2,1)S(1)}, bf16[512,512]{1,0:T(8,128)(2,1)S(1)}, u32[]{:S(2)}, u32[]{:S(2)}) collective-permute-start(bf16[512,512]{1,0:T(8,128)(2,1)S(1)} %collective-permute-done.6.refs_0_), channel_id=1, source_target_pairs={{0,4},{5,1},{4,8},{9,5},{8,12},{13,9},{12,14},{15,13},{14,10},{11,... | collective-permute-start | bytes 1572872 | tf_op jit(solution)/shard_map/ppermute | solution.py:385
  32.3 2.2 %collective-permute-start.15 = (bf16[256,512]{1,0:T(8,128)(2,1)S(1)}, bf16[256,512]{1,0:T(8,128)(2,1)S(1)}, u32[]{:S(2)}, u32[]{:S(2)}) collective-permute-start(bf16[256,512]{1,0:T(8,128)(2,1)S(1)} %collective-permute-done.14.refs_2_), channel_id=1, source_target_pairs={{0,1},{1,0},{2,3},{3,2},{4,5},{5,4},{6,7},{7,6},{8,9},{9,8},{10,11... | collective-permute-start | bytes 786440 | tf_op jit(solution)/shard_map/ppermute | solution.py:388
  32.3 3.7 %collective-permute-start.17 = (bf16[256,512]{1,0:T(8,128)(2,1)S(1)}, bf16[256,512]{1,0:T(8,128)(2,1)S(1)}, u32[]{:S(2)}, u32[]{:S(2)}) collective-permute-start(bf16[256,512]{1,0:T(8,128)(2,1)S(1)} %collective-permute-done.16.refs_4_), channel_id=1, source_target_pairs={{0,1},{1,0},{2,3},{3,2},{4,5},{5,4},{6,7},{7,6},{8,9},{9,8},{10,11... | collective-permute-start | bytes 786440 | tf_op jit(solution)/shard_map/ppermute | solution.py:388
  32.9 7.2 %collective-permute-start.18 = (bf16[128,512]{1,0:T(8,128)(2,1)S(1)}, bf16[128,512]{1,0:T(8,128)(2,1)S(1)}, u32[]{:S(2)}, u32[]{:S(2)}) collective-permute-start(bf16[128,512]{1,0:T(8,128)(2,1)S(1)} %slice.8), channel_id=1, source_target_pairs={{0,4},{5,1},{4,8},{9,5},{8,12},{13,9},{12,14},{15,13},{14,10},{11,... | collective-permute-start | bytes 393224 | tf_op jit(solution)/shard_map/ppermute | solution.py:385
  34.5 5.6 %collective-permute-start.19 = (bf16[128,512]{1,0:T(8,128)(2,1)S(1)}, bf16[128,512]{1,0:T(8,128)(2,1)S(1)}, u32[]{:S(2)}, u32[]{:S(2)}) collective-permute-start(bf16[128,512]{1,0:T(8,128)(2,1)S(1)} %slice.9), channel_id=1, source_target_pairs={{0,16},{16,0},{1,17},{17,1},{2,18},{18,2},{3,19},{19,3},{4,20},{20... | collective-permute-start | bytes 393224 | tf_op jit(solution)/shard_map/ppermute | solution.py:391
  40.1 2.3 %collective-permute-start.20 = (bf16[512,512]{1,0:T(8,128)(2,1)S(1)}, bf16[512,512]{1,0:T(8,128)(2,1)S(1)}, u32[]{:S(2)}, u32[]{:S(2)}) collective-permute-start(bf16[512,512]{1,0:T(8,128)(2,1)S(1)} %collective-permute-done.12.refs_0_), channel_id=1, source_target_pairs={{0,1},{1,0},{2,3},{3,2},{4,5},{5,4},{6,7},{7,6},{8,9},{9,8},{10,11... | collective-permute-start | bytes 1572872 | tf_op jit(solution)/shard_map/ppermute | solution.py:388
  40.1 2.1 %collective-permute-start.21 = (bf16[128,512]{1,0:T(8,128)(2,1)S(1)}, bf16[128,512]{1,0:T(8,128)(2,1)S(1)}, u32[]{:S(2)}, u32[]{:S(2)}) collective-permute-start(bf16[128,512]{1,0:T(8,128)(2,1)S(1)} %collective-permute-done.18.refs_1_), channel_id=1, source_target_pairs={{0,1},{1,0},{2,3},{3,2},{4,5},{5,4},{6,7},{7,6},{8,9},{9,8},{10,11... | collective-permute-start | bytes 393224 | tf_op jit(solution)/shard_map/ppermute | solution.py:388
  40.6 1.8 %collective-permute-start.22 = (bf16[128,512]{1,0:T(8,128)(2,1)S(1)}, bf16[128,512]{1,0:T(8,128)(2,1)S(1)}, u32[]{:S(2)}, u32[]{:S(2)}) collective-permute-start(bf16[128,512]{1,0:T(8,128)(2,1)S(1)} %collective-permute-done.19.refs_2_), channel_id=1, source_target_pairs={{0,1},{1,0},{2,3},{3,2},{4,5},{5,4},{6,7},{7,6},{8,9},{9,8},{10,11... | collective-permute-start | bytes 393224 | tf_op jit(solution)/shard_map/ppermute | solution.py:388
  68.1 18.6 %all-to-all-start.1 = ((s16[16,136,128]{2,1,0:T(8,128)(2,1)}), s16[16,136,128]{2,1,0:T(8,128)(2,1)S(1)}, u32[]{:S(2)}, u32[]{:S(2)}) async-start(s16[16,136,128]{2,1,0:T(8,128)(2,1)} %bitcast.4), calls=%async_computation.1 | async-start | bytes 1114112 | tf_op jit(solution)/shard_map/all_to_all | solution.py:400

commit v11 on v10

--- a/solution.py
+++ b/solution.py
@@ -330,7 +330,7 @@
     ship(stage_ref, out_ref)
 
 
-def inner_kernel(twist_ref, in_ref, out_ref, gain_ref):
+def inner_kernel(twist_ref, in_ref, out_ref, gain_ref, held_ref, sems):
     n = 2 * gain_ref.shape[0]
     orders = 2 * n
     nbits = orders.bit_length() - 1
@@ -350,17 +350,23 @@
         for p in range(orders):
             h = bit_reverse(p, nbits)
             for part, value in enumerate((re[p], im[p])):
-                for b in range(2):
-                    first = (b * orders + h) * 32 + 2 * jb + part
-                    out_ref[pl.ds(first, 4, stride=8), :] = value[4 * b : 4 * b + 4]
-
-
-def local_call(kernel, out, scratch, *args, smem=0):
+                held_ref[pl.ds(64 * h + 2 * jb + part, 8, stride=8), :] = value
+    by_batch = held_ref.reshape(orders, 2, 32, LANES)
+    copies = [
+        pltpu.make_async_copy(by_batch.at[:, b], out_ref.at[b], sems.at[b]) for b in range(2)
+    ]
+    for copy in copies:
+        copy.start()
+    for copy in copies:
+        copy.wait()
+
+
+def local_call(kernel, out, scratch, *args, smem=0, place=pltpu.VMEM):
     return pl.pallas_call(
         kernel,
         in_specs=[pl.BlockSpec(memory_space=pltpu.SMEM)] * smem
         + [pl.BlockSpec(memory_space=pltpu.VMEM)] * (len(args) - smem),
-        out_specs=pl.BlockSpec(memory_space=pltpu.VMEM),
+        out_specs=pl.BlockSpec(memory_space=place),
         out_shape=out,
         scratch_shapes=scratch,
         compiler_params=pltpu.CompilerParams(vmem_limit_bytes=12 * 2**20),
@@ -453,8 +459,10 @@
     phase = lax.iota(jnp.int32, local_orders) * first % total_orders
     angle = -2.0 * math.pi * phase.astype(jnp.float32) / float(total_orders)
     twist = jnp.stack([jnp.cos(angle), jnp.sin(angle)]) * (1.0 / math.sqrt(total_orders))
-    out = jax.ShapeDtypeStruct((2 * local_orders * shells // 2 * 2 * blocks, LANES), jnp.float32)
-    scores = local_call(inner_kernel, out, [lines], twist, sent, smem=1)
+    out = jax.ShapeDtypeStruct((2, local_orders, shells * blocks, LANES), jnp.float32)
+    held = pltpu.VMEM((local_orders * shells * 2 * blocks, LANES), jnp.float32)
+    scratch = [lines, held, pltpu.SemaphoreType.DMA((2,))]
+    scores = local_call(inner_kernel, out, scratch, twist, sent, smem=1, place=pltpu.HBM)
     scores = scores.reshape(2, local_orders, shells // 2, blocks, 2, LANES)
     return scores.transpose(0, 1, 2, 4, 3, 5).reshape(2, local_orders, shells // 2, 2, width)
 

time: 89.1 us -> 89.1 us (level)
  no operation moved by 1% of the time
where the time goes in v11:
time: 89.1 us; the launch traced here: 88.8 us
  starting transfers between devices  24.2 us (27%)
  waiting for transfers between devices  23.1 us (26%)
  blocking collectives  22.2 us (25%)
  Pallas kernels  18.4 us (21%)
    all_to_all x1, blocking collectives, exchange(): return lax.all_to_all(value, 'shell', 0, 0).reshape(parcels.shape)  22.2 us
    all_to_all x1, waiting for transfers between devices, exchange(): return lax.all_to_all(value, 'shell', 0, 0).reshape(parcels.shape)  14.9 us
    ppermute x8, starting transfers between devices, around(): return lax.ppermute(value, 'shell', onward)  14.4 us
    pallas_call x6, Pallas kernels, project(): pl.pallas_call(functools.partial(project_kernel, lax.axis_size('shell'),...  9.43 us
    ppermute x8, waiting for transfers between devices, around(): return lax.ppermute(value, 'shell', onward)  7.32 us
    pallas_call x1, Pallas kernels, sort_rows(): pl.pallas_call(sort_kernel, in_specs=[pl.BlockSpec(memory_space=pltpu.SME...  5.14 us
    ppermute x3, starting transfers between devices, across(): return lax.ppermute(value, 'grp', [(0, 1), (1, 0)])  4.47 us
    pallas_call x2, Pallas kernels, local_call(): pl.pallas_call(kernel, in_specs=[pl.BlockSpec(memory_space=pltpu.SMEM)] *...  3.86 us
  transfers between devices with their start and end apart: 24, of which 9 were waited for; matrix products, arithmetic and copies ran while one was open for 0% of the time, Pallas kernels for 14%

profile of v11, /device:TPU:0, one launch (start us, length us, event | category | flops | bytes accessed | tf_op | source)
XLA Modules:
  0.0 88.8 jit_solution(17309140531275405180)
XLA Ops:
  0.5 2.6 %collective-permute-start = (bf16[512,512]{1,0:T(8,128)(2,1)}, bf16[512,512]{1,0:T(8,128)(2,1)S(1)}, u32[]{:S(2)}, u32[]{:S(2)}) collective-permute-start(bf16[512,512]{1,0:T(8,128)(2,1)} %bitcast.15), channel_id=1, source_target_pairs={{0,4},{5,1},{4,8},{9,5},{8,12},{13,9},{12,14},{15,13},{14,10},{11,... | collective-permute-start | bytes 1572872 | tf_op jit(solution)/shard_map/ppermute | solution.py:391
  3.1 2.2 %collective-permute-start.4 = (bf16[256,512]{1,0:T(8,128)(2,1)S(1)}, bf16[256,512]{1,0:T(8,128)(2,1)S(1)}, u32[]{:S(2)}, u32[]{:S(2)}) collective-permute-start(bf16[256,512]{1,0:T(8,128)(2,1)S(1)} %constant_dynamic-slice_fusion), channel_id=1, source_target_pairs={{0,4},{5,1},{4,8},{9,5},{8,12},{13,9},{12,14},{15,13},{14,10},{11,... | collective-permute-start | bytes 786440 | tf_op jit(solution)/shard_map/ppermute | solution.py:391
  5.2 0.7 copy-done.2
  5.9 5.1 %shard_map.46.rows_ref = bf16[16,256,1024]{2,1,0:T(8,128)(2,1)S(1)} custom-call(s32[8]{0:T(128)S(1)} %copy-done.2, bf16[4096,1024]{1,0:T(8,128)(2,1)} %bitcast.17), custom_call_target="tpu_custom_call" | custom-call | flops 2147483648 | bytes 16777216 | tf_op jit(solution)/shard_map/pallas_call | solution.py:137
  11.1 1.6 %collective-permute-start.1 = (bf16[512,512]{1,0:T(8,128)(2,1)S(1)}, bf16[512,512]{1,0:T(8,128)(2,1)S(1)}, u32[]{:S(2)}, u32[]{:S(2)}) collective-permute-start(bf16[512,512]{1,0:T(8,128)(2,1)S(1)} %collective-permute-done.refs_0_), channel_id=1, source_target_pairs={{0,4},{5,1},{4,8},{9,5},{8,12},{13,9},{12,14},{15,13},{14,10},{11,... | collective-permute-start | bytes 1572872 | tf_op jit(solution)/shard_map/ppermute | solution.py:391
  12.7 1.3 %shard_map.47.refs_4_ = f32[512,512]{1,0:T(8,128)S(1)} custom-call(s32[16]{0:T(128)S(1)} %copy-done.1, bf16[16,256,1024]{2,1,0:T(8,128)(2,1)S(1)} %shard_map.46.rows_ref, bf16[512,512]{1,0:T(8,128)(2,1)S(1)} %bitcast.16, bf16[512,512]{1,0:T(8,128)(2,1)S(1)} %collective-permute-done.3.refs_1_), custom_call_target="tpu_custom_call" | custom-call | flops 536870912 | bytes 3145728 | tf_op jit(solution)/shard_map/pallas_call | solution.py:253
  14.1 1.6 %collective-permute-start.8 = (bf16[256,512]{1,0:T(8,128)(2,1)S(1)}, bf16[256,512]{1,0:T(8,128)(2,1)S(1)}, u32[]{:S(2)}, u32[]{:S(2)}) collective-permute-start(bf16[256,512]{1,0:T(8,128)(2,1)S(1)} %collective-permute-done.4.refs_2_), channel_id=1, source_target_pairs={{0,4},{5,1},{4,8},{9,5},{8,12},{13,9},{12,14},{15,13},{14,10},{11,... | collective-permute-start | bytes 786440 | tf_op jit(solution)/shard_map/ppermute | solution.py:391
  15.7 1.5 %collective-permute-start.10 = (bf16[256,512]{1,0:T(8,128)(2,1)S(1)}, bf16[256,512]{1,0:T(8,128)(2,1)S(1)}, u32[]{:S(2)}, u32[]{:S(2)}) collective-permute-start(bf16[256,512]{1,0:T(8,128)(2,1)S(1)} %collective-permute-done.4.refs_2_), channel_id=1, source_target_pairs={{0,16},{16,0},{1,17},{17,1},{2,18},{18,2},{3,19},{19,3},{4,20},{20... | collective-permute-start | bytes 786440 | tf_op jit(solution)/shard_map/ppermute | solution.py:397
  17.2 1.5 %shard_map.48.refs_6_ = f32[512,512]{1,0:T(8,128)S(1)} custom-call(s32[16]{0:T(128)S(1)} %copy-done.1, bf16[16,256,1024]{2,1,0:T(8,128)(2,1)S(1)} %shard_map.46.rows_ref, bf16[512,512]{1,0:T(8,128)(2,1)S(1)} %collective-permute-done.refs_0_, bf16[512,512]{1,0:T(8,128)(2,1)S(1)} %collective-permute-done.2.refs_1_, ...), custom_call_target="tpu_custom_call" | custom-call | flops 805306368 | bytes 5242880 | tf_op jit(solution)/shard_map/pallas_call | solution.py:253
  18.8 1.6 %collective-permute-done.1.refs_0_ = bf16[512,512]{1,0:T(8,128)(2,1)S(1)} collective-permute-done((bf16[512,512]{1,0:T(8,128)(2,1)S(1)}, bf16[512,512]{1,0:T(8,128)(2,1)S(1)}, u32[]{:S(2)}, u32[]{:S(2)}) %collective-permute-start.1) | collective-permute-done | bytes 524320 | tf_op jit(solution)/shard_map/ppermute | solution.py:391
  20.4 1.6 %collective-permute-start.6 = (bf16[512,512]{1,0:T(8,128)(2,1)S(1)}, bf16[512,512]{1,0:T(8,128)(2,1)S(1)}, u32[]{:S(2)}, u32[]{:S(2)}) collective-permute-start(bf16[512,512]{1,0:T(8,128)(2,1)S(1)} %collective-permute-done.1.refs_0_), channel_id=1, source_target_pairs={{0,4},{5,1},{4,8},{9,5},{8,12},{13,9},{12,14},{15,13},{14,10},{11,... | collective-permute-start | bytes 1572872 | tf_op jit(solution)/shard_map/ppermute | solution.py:391
  21.9 1.2 %collective-permute-done.8.refs_2_ = bf16[256,512]{1,0:T(8,128)(2,1)S(1)} collective-permute-done((bf16[256,512]{1,0:T(8,128)(2,1)S(1)}, bf16[256,512]{1,0:T(8,128)(2,1)S(1)}, u32[]{:S(2)}, u32[]{:S(2)}) %collective-permute-start.8) | collective-permute-done | bytes 262176 | tf_op jit(solution)/shard_map/ppermute | solution.py:391
  23.2 0.5 collective-permute-done.10.refs_4_
  23.7 1.5 %collective-permute-start.16 = (bf16[256,512]{1,0:T(8,128)(2,1)S(1)}, bf16[256,512]{1,0:T(8,128)(2,1)S(1)}, u32[]{:S(2)}, u32[]{:S(2)}) collective-permute-start(bf16[256,512]{1,0:T(8,128)(2,1)S(1)} %collective-permute-done.8.refs_2_), channel_id=1, source_target_pairs={{0,16},{16,0},{1,17},{17,1},{2,18},{18,2},{3,19},{19,3},{4,20},{20... | collective-permute-start | bytes 786440 | tf_op jit(solution)/shard_map/ppermute | solution.py:397
  25.2 1.6 %collective-permute-start.14 = (bf16[256,512]{1,0:T(8,128)(2,1)S(1)}, bf16[256,512]{1,0:T(8,128)(2,1)S(1)}, u32[]{:S(2)}, u32[]{:S(2)}) collective-permute-start(bf16[256,512]{1,0:T(8,128)(2,1)S(1)} %collective-permute-done.8.refs_2_), channel_id=1, source_target_pairs={{0,4},{5,1},{4,8},{9,5},{8,12},{13,9},{12,14},{15,13},{14,10},{11,... | collective-permute-start | bytes 786440 | tf_op jit(solution)/shard_map/ppermute | solution.py:391
  26.7 1.8 %shard_map.49.refs_6_ = f32[512,512]{1,0:T(8,128)S(1)} custom-call(s32[16]{0:T(128)S(1)} %copy-done.1, bf16[16,256,1024]{2,1,0:T(8,128)(2,1)S(1)} %shard_map.46.rows_ref, bf16[512,512]{1,0:T(8,128)(2,1)S(1)} %collective-permute-done.1.refs_0_, bf16[512,512]{1,0:T(8,128)(2,1)S(1)} %collective-permute-done.7.refs_1_, ...), custom_call_target="tpu_custom_call" | custom-call | flops 1073741824 | bytes 6291456 | tf_op jit(solution)/shard_map/pallas_call | solution.py:253
  28.6 1.0 %collective-permute-done.6.refs_0_ = bf16[512,512]{1,0:T(8,128)(2,1)S(1)} collective-permute-done((bf16[512,512]{1,0:T(8,128)(2,1)S(1)}, bf16[512,512]{1,0:T(8,128)(2,1)S(1)}, u32[]{:S(2)}, u32[]{:S(2)}) %collective-permute-start.6) | collective-permute-done | bytes 524320 | tf_op jit(solution)/shard_map/ppermute | solution.py:391
  29.5 1.6 %collective-permute-start.12 = (bf16[512,512]{1,0:T(8,128)(2,1)S(1)}, bf16[512,512]{1,0:T(8,128)(2,1)S(1)}, u32[]{:S(2)}, u32[]{:S(2)}) collective-permute-start(bf16[512,512]{1,0:T(8,128)(2,1)S(1)} %collective-permute-done.6.refs_0_), channel_id=1, source_target_pairs={{0,4},{5,1},{4,8},{9,5},{8,12},{13,9},{12,14},{15,13},{14,10},{11,... | collective-permute-start | bytes 1572872 | tf_op jit(solution)/shard_map/ppermute | solution.py:391
  31.1 1.2 %collective-permute-done.14.refs_2_ = bf16[256,512]{1,0:T(8,128)(2,1)S(1)} collective-permute-done((bf16[256,512]{1,0:T(8,128)(2,1)S(1)}, bf16[256,512]{1,0:T(8,128)(2,1)S(1)}, u32[]{:S(2)}, u32[]{:S(2)}) %collective-permute-start.14) | collective-permute-done | bytes 262176 | tf_op jit(solution)/shard_map/ppermute | solution.py:391
  32.3 0.5 collective-permute-start.17
  32.9 1.6 %collective-permute-start.18 = (bf16[128,512]{1,0:T(8,128)(2,1)S(1)}, bf16[128,512]{1,0:T(8,128)(2,1)S(1)}, u32[]{:S(2)}, u32[]{:S(2)}) collective-permute-start(bf16[128,512]{1,0:T(8,128)(2,1)S(1)} %slice.8), channel_id=1, source_target_pairs={{0,4},{5,1},{4,8},{9,5},{8,12},{13,9},{12,14},{15,13},{14,10},{11,... | collective-permute-start | bytes 393224 | tf_op jit(solution)/shard_map/ppermute | solution.py:391
  34.5 1.5 %collective-permute-start.19 = (bf16[128,512]{1,0:T(8,128)(2,1)S(1)}, bf16[128,512]{1,0:T(8,128)(2,1)S(1)}, u32[]{:S(2)}, u32[]{:S(2)}) collective-permute-start(bf16[128,512]{1,0:T(8,128)(2,1)S(1)} %slice.9), channel_id=1, source_target_pairs={{0,16},{16,0},{1,17},{17,1},{2,18},{18,2},{3,19},{19,3},{4,20},{20... | collective-permute-start | bytes 393224 | tf_op jit(solution)/shard_map/ppermute | solution.py:397
  36.0 1.8 %shard_map.50.refs_3_ = f32[512,512]{1,0:T(8,128)S(1)} custom-call(s32[16]{0:T(128)S(1)} %copy-done.1, bf16[16,256,1024]{2,1,0:T(8,128)(2,1)S(1)} %shard_map.46.rows_ref, bf16[512,512]{1,0:T(8,128)(2,1)S(1)} %collective-permute-done.6.refs_0_, bf16[512,512]{1,0:T(8,128)(2,1)S(1)} %collective-permute-done.13.refs_1_, ...), custom_call_target="tpu_custom_call" | custom-call | flops 1073741824 | bytes 6291456 | tf_op jit(solution)/shard_map/pallas_call | solution.py:253
  37.8 2.3 %collective-permute-done.18.refs_1_ = bf16[128,512]{1,0:T(8,128)(2,1)S(1)} collective-permute-done((bf16[128,512]{1,0:T(8,128)(2,1)S(1)}, bf16[128,512]{1,0:T(8,128)(2,1)S(1)}, u32[]{:S(2)}, u32[]{:S(2)}) %collective-permute-start.18) | collective-permute-done | bytes 131104 | tf_op jit(solution)/shard_map/ppermute | solution.py:391
  40.1 0.5 collective-permute-start.21
  40.7 1.2 %shard_map.51.refs_3_ = f32[512,512]{1,0:T(8,128)S(1)} custom-call(s32[16]{0:T(128)S(1)} %copy-done.1, bf16[16,256,1024]{2,1,0:T(8,128)(2,1)S(1)} %shard_map.46.rows_ref, bf16[512,512]{1,0:T(8,128)(2,1)S(1)} %collective-permute-done.12.refs_0_, bf16[128,512]{1,0:T(8,128)(2,1)S(1)} %collective-permute-done.18.refs_1_, ...), custom_call_target="tpu_custom_call" | custom-call | flops 402653184 | bytes 3670016 | tf_op jit(solution)/shard_map/pallas_call | solution.py:253
  42.4 1.8 %shard_map.52 = s16[2176,128]{1,0:T(8,128)(2,1)S(1)} custom-call(s32[16]{0:T(128)S(1)} %copy-done.1, bf16[16,256,1024]{2,1,0:T(8,128)(2,1)S(1)} %shard_map.46.rows_ref, bf16[512,512]{1,0:T(8,128)(2,1)S(1)} %collective-permute-done.20.refs_0_, bf16[128,512]{1,0:T(8,128)(2,1)S(1)} %collective-permute-done.21.refs_1_, ...), custom_call_target="tpu_custom_call" | custom-call | flops 402653184 | bytes 3670016 | tf_op jit(solution)/shard_map/pallas_call | solution.py:253
  44.2 22.2 %all_to_all.10 = s16[16,136,128]{2,1,0:T(8,128)(2,1)S(1)} all-to-all(s16[16,136,128]{2,1,0:T(8,128)(2,1)S(1)} %bitcast.13), channel_id=1, replica_groups=mesh['grp'=2,'shell'=16] {'shell'}, dimensions={0} | all-to-all | bytes 1114112 | tf_op jit(solution)/shard_map/all_to_all | solution.py:406
  66.4 1.7 %shard_map.53 = s16[2176,128]{1,0:T(8,128)(2,1)} custom-call(s16[2176,128]{1,0:T(8,128)(2,1)S(1)} %bitcast.12), custom_call_target="tpu_custom_call" | custom-call | tf_op jit(solution)/shard_map/pallas_call | solution.py:365
  68.1 3.6 %all-to-all-start.1 = ((s16[16,136,128]{2,1,0:T(8,128)(2,1)}), s16[16,136,128]{2,1,0:T(8,128)(2,1)S(1)}, u32[]{:S(2)}, u32[]{:S(2)}) async-start(s16[16,136,128]{2,1,0:T(8,128)(2,1)} %bitcast.4), calls=%async_computation.1 | async-start | bytes 1114112 | tf_op jit(solution)/shard_map/all_to_all | solution.py:406
  71.7 14.9 %all-to-all-done.1 = s16[16,136,128]{2,1,0:T(8,128)(2,1)S(1)} async-done(((s16[16,136,128]{2,1,0:T(8,128)(2,1)}), s16[16,136,128]{2,1,0:T(8,128)(2,1)S(1)}, u32[]{:S(2)}, u32[]{:S(2)}) %all-to-all-start.1) | async-done | bytes 557088 | tf_op jit(solution)/shard_map/all_to_all | solution.py:406
  86.6 2.2 %shard_map.54 = f32[2,32,32,128]{3,2,1,0:T(8,128)} custom-call(f32[2,32]{1,0:T(2,128)S(1)} %maximum_multiply_fusion.twist_ref, s16[2176,128]{1,0:T(8,128)(2,1)S(1)} %bitcast.11), custom_call_target="tpu_custom_call" | custom-call | tf_op jit(solution)/shard_map/pallas_call | solution.py:365
  (37 shorter events, 1.3 us)
Async XLA Ops:
  0.0 3.0 %collective-permute-start.3 = (bf16[512,512]{1,0:T(8,128)(2,1)}, bf16[512,512]{1,0:T(8,128)(2,1)S(1)}, u32[]{:S(2)}, u32[]{:S(2)}) collective-permute-start(bf16[512,512]{1,0:T(8,128)(2,1)} %bitcast.14), channel_id=1, source_target_pairs={{0,1},{1,0},{2,3},{3,2},{4,5},{5,4},{6,7},{7,6},{8,9},{9,8},{10,11... | collective-permute-start | bytes 1572872 | tf_op jit(solution)/shard_map/ppermute | solution.py:394
  0.5 10.6 %collective-permute-start = (bf16[512,512]{1,0:T(8,128)(2,1)}, bf16[512,512]{1,0:T(8,128)(2,1)S(1)}, u32[]{:S(2)}, u32[]{:S(2)}) collective-permute-start(bf16[512,512]{1,0:T(8,128)(2,1)} %bitcast.15), channel_id=1, source_target_pairs={{0,4},{5,1},{4,8},{9,5},{8,12},{13,9},{12,14},{15,13},{14,10},{11,... | collective-permute-start | bytes 1572872 | tf_op jit(solution)/shard_map/ppermute | solution.py:391
  3.1 11.0 %collective-permute-start.4 = (bf16[256,512]{1,0:T(8,128)(2,1)S(1)}, bf16[256,512]{1,0:T(8,128)(2,1)S(1)}, u32[]{:S(2)}, u32[]{:S(2)}) collective-permute-start(bf16[256,512]{1,0:T(8,128)(2,1)S(1)} %constant_dynamic-slice_fusion), channel_id=1, source_target_pairs={{0,4},{5,1},{4,8},{9,5},{8,12},{13,9},{12,14},{15,13},{14,10},{11,... | collective-permute-start | bytes 786440 | tf_op jit(solution)/shard_map/ppermute | solution.py:391
  5.2 0.7 copy-start.2
  5.9 6.9 %copy-start = (bf16[1,512,512]{2,1,0:T(8,128)(2,1)S(1)}, bf16[1,512,512]{2,1,0:T(8,128)(2,1)}, u32[]{:S(2)}) copy-start(bf16[1,512,512]{2,1,0:T(8,128)(2,1)} %param.5) | copy-start | bytes 1572868
  5.9 6.9 %copy-start.1 = (s32[16]{0:T(128)S(1)}, s32[16]{0:T(128)}, u32[]{:S(2)}) copy-start(s32[16]{0:T(128)} %owner_ref.11) | copy-start | bytes 196
  11.0 6.2 %collective-permute-start.2 = (bf16[512,512]{1,0:T(8,128)(2,1)S(1)}, bf16[512,512]{1,0:T(8,128)(2,1)S(1)}, u32[]{:S(2)}, u32[]{:S(2)}) collective-permute-start(bf16[512,512]{1,0:T(8,128)(2,1)S(1)} %collective-permute-done.refs_0_), channel_id=1, source_target_pairs={{0,1},{1,0},{2,3},{3,2},{4,5},{5,4},{6,7},{7,6},{8,9},{9,8},{10,11... | collective-permute-start | bytes 1572872 | tf_op jit(solution)/shard_map/ppermute | solution.py:394
  11.1 9.2 %collective-permute-start.1 = (bf16[512,512]{1,0:T(8,128)(2,1)S(1)}, bf16[512,512]{1,0:T(8,128)(2,1)S(1)}, u32[]{:S(2)}, u32[]{:S(2)}) collective-permute-start(bf16[512,512]{1,0:T(8,128)(2,1)S(1)} %collective-permute-done.refs_0_), channel_id=1, source_target_pairs={{0,4},{5,1},{4,8},{9,5},{8,12},{13,9},{12,14},{15,13},{14,10},{11,... | collective-permute-start | bytes 1572872 | tf_op jit(solution)/shard_map/ppermute | solution.py:391
  14.0 3.2 %collective-permute-start.5 = (bf16[256,512]{1,0:T(8,128)(2,1)S(1)}, bf16[256,512]{1,0:T(8,128)(2,1)S(1)}, u32[]{:S(2)}, u32[]{:S(2)}) collective-permute-start(bf16[256,512]{1,0:T(8,128)(2,1)S(1)} %collective-permute-done.4.refs_2_), channel_id=1, source_target_pairs={{0,1},{1,0},{2,3},{3,2},{4,5},{5,4},{6,7},{7,6},{8,9},{9,8},{10,11... | collective-permute-start | bytes 786440 | tf_op jit(solution)/shard_map/ppermute | solution.py:394
  14.1 9.1 %collective-permute-start.8 = (bf16[256,512]{1,0:T(8,128)(2,1)S(1)}, bf16[256,512]{1,0:T(8,128)(2,1)S(1)}, u32[]{:S(2)}, u32[]{:S(2)}) collective-permute-start(bf16[256,512]{1,0:T(8,128)(2,1)S(1)} %collective-permute-done.4.refs_2_), channel_id=1, source_target_pairs={{0,4},{5,1},{4,8},{9,5},{8,12},{13,9},{12,14},{15,13},{14,10},{11,... | collective-permute-start | bytes 786440 | tf_op jit(solution)/shard_map/ppermute | solution.py:391
  15.7 7.9 %collective-permute-start.10 = (bf16[256,512]{1,0:T(8,128)(2,1)S(1)}, bf16[256,512]{1,0:T(8,128)(2,1)S(1)}, u32[]{:S(2)}, u32[]{:S(2)}) collective-permute-start(bf16[256,512]{1,0:T(8,128)(2,1)S(1)} %collective-permute-done.4.refs_2_), channel_id=1, source_target_pairs={{0,16},{16,0},{1,17},{17,1},{2,18},{18,2},{3,19},{19,3},{4,20},{20... | collective-permute-start | bytes 786440 | tf_op jit(solution)/shard_map/ppermute | solution.py:397
  20.3 6.4 %collective-permute-start.7 = (bf16[512,512]{1,0:T(8,128)(2,1)S(1)}, bf16[512,512]{1,0:T(8,128)(2,1)S(1)}, u32[]{:S(2)}, u32[]{:S(2)}) collective-permute-start(bf16[512,512]{1,0:T(8,128)(2,1)S(1)} %collective-permute-done.1.refs_0_), channel_id=1, source_target_pairs={{0,1},{1,0},{2,3},{3,2},{4,5},{5,4},{6,7},{7,6},{8,9},{9,8},{10,11... | collective-permute-start | bytes 1572872 | tf_op jit(solution)/shard_map/ppermute | solution.py:394
  20.4 9.2 %collective-permute-start.6 = (bf16[512,512]{1,0:T(8,128)(2,1)S(1)}, bf16[512,512]{1,0:T(8,128)(2,1)S(1)}, u32[]{:S(2)}, u32[]{:S(2)}) collective-permute-start(bf16[512,512]{1,0:T(8,128)(2,1)S(1)} %collective-permute-done.1.refs_0_), channel_id=1, source_target_pairs={{0,4},{5,1},{4,8},{9,5},{8,12},{13,9},{12,14},{15,13},{14,10},{11,... | collective-permute-start | bytes 1572872 | tf_op jit(solution)/shard_map/ppermute | solution.py:391
  23.2 2.0 %collective-permute-start.9 = (bf16[256,512]{1,0:T(8,128)(2,1)S(1)}, bf16[256,512]{1,0:T(8,128)(2,1)S(1)}, u32[]{:S(2)}, u32[]{:S(2)}) collective-permute-start(bf16[256,512]{1,0:T(8,128)(2,1)S(1)} %collective-permute-done.8.refs_2_), channel_id=1, source_target_pairs={{0,1},{1,0},{2,3},{3,2},{4,5},{5,4},{6,7},{7,6},{8,9},{9,8},{10,11... | collective-permute-start | bytes 786440 | tf_op jit(solution)/shard_map/ppermute | solution.py:394
  23.6 3.1 %collective-permute-start.11 = (bf16[256,512]{1,0:T(8,128)(2,1)S(1)}, bf16[256,512]{1,0:T(8,128)(2,1)S(1)}, u32[]{:S(2)}, u32[]{:S(2)}) collective-permute-start(bf16[256,512]{1,0:T(8,128)(2,1)S(1)} %collective-permute-done.10.refs_4_), channel_id=1, source_target_pairs={{0,1},{1,0},{2,3},{3,2},{4,5},{5,4},{6,7},{7,6},{8,9},{9,8},{10,11... | collective-permute-start | bytes 786440 | tf_op jit(solution)/shard_map/ppermute | solution.py:394
  23.7 8.7 %collective-permute-start.16 = (bf16[256,512]{1,0:T(8,128)(2,1)S(1)}, bf16[256,512]{1,0:T(8,128)(2,1)S(1)}, u32[]{:S(2)}, u32[]{:S(2)}) collective-permute-start(bf16[256,512]{1,0:T(8,128)(2,1)S(1)} %collective-permute-done.8.refs_2_), channel_id=1, source_target_pairs={{0,16},{16,0},{1,17},{17,1},{2,18},{18,2},{3,19},{19,3},{4,20},{20... | collective-permute-start | bytes 786440 | tf_op jit(solution)/shard_map/ppermute | solution.py:397
  25.2 7.2 %collective-permute-start.14 = (bf16[256,512]{1,0:T(8,128)(2,1)S(1)}, bf16[256,512]{1,0:T(8,128)(2,1)S(1)}, u32[]{:S(2)}, u32[]{:S(2)}) collective-permute-start(bf16[256,512]{1,0:T(8,128)(2,1)S(1)} %collective-permute-done.8.refs_2_), channel_id=1, source_target_pairs={{0,4},{5,1},{4,8},{9,5},{8,12},{13,9},{12,14},{15,13},{14,10},{11,... | collective-permute-start | bytes 786440 | tf_op jit(solution)/shard_map/ppermute | solution.py:391
  29.5 6.5 %collective-permute-start.13 = (bf16[512,512]{1,0:T(8,128)(2,1)S(1)}, bf16[512,512]{1,0:T(8,128)(2,1)S(1)}, u32[]{:S(2)}, u32[]{:S(2)}) collective-permute-start(bf16[512,512]{1,0:T(8,128)(2,1)S(1)} %collective-permute-done.6.refs_0_), channel_id=1, source_target_pairs={{0,1},{1,0},{2,3},{3,2},{4,5},{5,4},{6,7},{7,6},{8,9},{9,8},{10,11... | collective-permute-start | bytes 1572872 | tf_op jit(solution)/shard_map/ppermute | solution.py:394
  29.5 10.6 %collective-permute-start.12 = (bf16[512,512]{1,0:T(8,128)(2,1)S(1)}, bf16[512,512]{1,0:T(8,128)(2,1)S(1)}, u32[]{:S(2)}, u32[]{:S(2)}) collective-permute-start(bf16[512,512]{1,0:T(8,128)(2,1)S(1)} %collective-permute-done.6.refs_0_), channel_id=1, source_target_pairs={{0,4},{5,1},{4,8},{9,5},{8,12},{13,9},{12,14},{15,13},{14,10},{11,... | collective-permute-start | bytes 1572872 | tf_op jit(solution)/shard_map/ppermute | solution.py:391
  32.3 2.2 %collective-permute-start.15 = (bf16[256,512]{1,0:T(8,128)(2,1)S(1)}, bf16[256,512]{1,0:T(8,128)(2,1)S(1)}, u32[]{:S(2)}, u32[]{:S(2)}) collective-permute-start(bf16[256,512]{1,0:T(8,128)(2,1)S(1)} %collective-permute-done.14.refs_2_), channel_id=1, source_target_pairs={{0,1},{1,0},{2,3},{3,2},{4,5},{5,4},{6,7},{7,6},{8,9},{9,8},{10,11... | collective-permute-start | bytes 786440 | tf_op jit(solution)/shard_map/ppermute | solution.py:394
  32.3 3.7 %collective-permute-start.17 = (bf16[256,512]{1,0:T(8,128)(2,1)S(1)}, bf16[256,512]{1,0:T(8,128)(2,1)S(1)}, u32[]{:S(2)}, u32[]{:S(2)}) collective-permute-start(bf16[256,512]{1,0:T(8,128)(2,1)S(1)} %collective-permute-done.16.refs_4_), channel_id=1, source_target_pairs={{0,1},{1,0},{2,3},{3,2},{4,5},{5,4},{6,7},{7,6},{8,9},{9,8},{10,11... | collective-permute-start | bytes 786440 | tf_op jit(solution)/shard_map/ppermute | solution.py:394
  32.9 7.2 %collective-permute-start.18 = (bf16[128,512]{1,0:T(8,128)(2,1)S(1)}, bf16[128,512]{1,0:T(8,128)(2,1)S(1)}, u32[]{:S(2)}, u32[]{:S(2)}) collective-permute-start(bf16[128,512]{1,0:T(8,128)(2,1)S(1)} %slice.8), channel_id=1, source_target_pairs={{0,4},{5,1},{4,8},{9,5},{8,12},{13,9},{12,14},{15,13},{14,10},{11,... | collective-permute-start | bytes 393224 | tf_op jit(solution)/shard_map/ppermute | solution.py:391
  34.5 5.6 %collective-permute-start.19 = (bf16[128,512]{1,0:T(8,128)(2,1)S(1)}, bf16[128,512]{1,0:T(8,128)(2,1)S(1)}, u32[]{:S(2)}, u32[]{:S(2)}) collective-permute-start(bf16[128,512]{1,0:T(8,128)(2,1)S(1)} %slice.9), channel_id=1, source_target_pairs={{0,16},{16,0},{1,17},{17,1},{2,18},{18,2},{3,19},{19,3},{4,20},{20... | collective-permute-start | bytes 393224 | tf_op jit(solution)/shard_map/ppermute | solution.py:397
  40.1 2.3 %collective-permute-start.20 = (bf16[512,512]{1,0:T(8,128)(2,1)S(1)}, bf16[512,512]{1,0:T(8,128)(2,1)S(1)}, u32[]{:S(2)}, u32[]{:S(2)}) collective-permute-start(bf16[512,512]{1,0:T(8,128)(2,1)S(1)} %collective-permute-done.12.refs_0_), channel_id=1, source_target_pairs={{0,1},{1,0},{2,3},{3,2},{4,5},{5,4},{6,7},{7,6},{8,9},{9,8},{10,11... | collective-permute-start | bytes 1572872 | tf_op jit(solution)/shard_map/ppermute | solution.py:394
  40.1 2.1 %collective-permute-start.21 = (bf16[128,512]{1,0:T(8,128)(2,1)S(1)}, bf16[128,512]{1,0:T(8,128)(2,1)S(1)}, u32[]{:S(2)}, u32[]{:S(2)}) collective-permute-start(bf16[128,512]{1,0:T(8,128)(2,1)S(1)} %collective-permute-done.18.refs_1_), channel_id=1, source_target_pairs={{0,1},{1,0},{2,3},{3,2},{4,5},{5,4},{6,7},{7,6},{8,9},{9,8},{10,11... | collective-permute-start | bytes 393224 | tf_op jit(solution)/shard_map/ppermute | solution.py:394
  40.6 1.8 %collective-permute-start.22 = (bf16[128,512]{1,0:T(8,128)(2,1)S(1)}, bf16[128,512]{1,0:T(8,128)(2,1)S(1)}, u32[]{:S(2)}, u32[]{:S(2)}) collective-permute-start(bf16[128,512]{1,0:T(8,128)(2,1)S(1)} %collective-permute-done.19.refs_2_), channel_id=1, source_target_pairs={{0,1},{1,0},{2,3},{3,2},{4,5},{5,4},{6,7},{7,6},{8,9},{9,8},{10,11... | collective-permute-start | bytes 393224 | tf_op jit(solution)/shard_map/ppermute | solution.py:394
  68.1 18.6 %all-to-all-start.1 = ((s16[16,136,128]{2,1,0:T(8,128)(2,1)}), s16[16,136,128]{2,1,0:T(8,128)(2,1)S(1)}, u32[]{:S(2)}, u32[]{:S(2)}) async-start(s16[16,136,128]{2,1,0:T(8,128)(2,1)} %bitcast.4), calls=%async_computation.1 | async-start | bytes 1114112 | tf_op jit(solution)/shard_map/all_to_all | solution.py:406
